TPU v7x, 32 devices: a whole 2x2x4 slice. The times are simulated.
32 devices in a mesh: grp: 1, frame: 32 (over z, y, x, core).
Axes of the slice: x: 2, y: 2, z: 4, core: 2. Of those that a mesh axis runs over, the one named last changes fastest.
Arguments:
- tokens: bfloat16 [8192, 2240], P(('grp', 'frame')), may hold values from -16 to 16
- w_query: bfloat16 [1792, 2240], P('frame'), may hold values from -0.125 to 0.125
- w_keyval: bfloat16 [3584, 2240], P('frame'), may hold values from -0.125 to 0.125
- taps: float32 [3, 1792], replicated, may hold values from -1 to 1
Outputs:
- mixed: bfloat16 [8192, 1792], P(('grp', 'frame'))
All inputs are finite; a program needn't handle non-finite values.
Results may differ from a plain program's by a relative error of at most 0.0051.
Values may be sent and summed in bfloat16 or wider, within the bound.
No kernel may reach another device: no remote copies, remote signals or barrier semaphores. Data moves between devices by JAX's collectives and lax.ppermute only.
A program may use at most 128 MiB of HBM per device.

v0:
```python
import jax
import jax.numpy as jnp
from jax import lax
from jax.sharding import PartitionSpec as P

HEADS = 16
HDIM = 112
HEIGHT = 32
WIDTH = 32


epsilon = 1e-06


def from_behind(value, axis, steps):
    count = lax.axis_size(axis)
    leading, last = (max(0, -steps), min(count, count - steps))
    return lax.ppermute(value, axis, [(source, source + steps) for source in range(leading, last)])


def normalize(rows_in):
    values = rows_in.astype(jnp.float32)
    scale_inv = lax.rsqrt(jnp.mean(values * values, axis=-1, keepdims=True) + epsilon)
    return (values * scale_inv).astype(jnp.bfloat16)


def local(tokens, w_query, w_keyval, taps):
    channels = HEADS * HDIM
    rows_here = tokens.shape[0]
    normed = normalize(tokens)

    def project_rows(weight_rows):
        return lax.dot_general(
            normed, weight_rows, (((1,), (1,)), ((), ())), preferred_element_type=jnp.float32
        )

    keyval_lin = project_rows(lax.all_gather(w_keyval, "frame", axis=0, tiled=True))
    key_feats = jax.nn.relu(keyval_lin[:, :channels]).astype(jnp.bfloat16)
    value_proj = keyval_lin[:, channels:].astype(jnp.bfloat16)
    key_heads = key_feats.reshape(rows_here, HEADS, HDIM)
    value_heads = value_proj.reshape(rows_here, HEADS, HDIM)
    local_state = jnp.einsum(
        "thd,the->hde", key_heads, value_heads, preferred_element_type=jnp.float32
    )
    local_keys = jnp.sum(key_heads.astype(jnp.float32), axis=0)
    query_lin = project_rows(lax.all_gather(w_query, "frame", axis=0, tiled=True))
    query_feats = jax.nn.relu(query_lin).astype(jnp.bfloat16)
    state, key_total = lax.psum((local_state, local_keys), "frame")
    query_heads = query_feats.reshape(rows_here, HEADS, HDIM).astype(jnp.float32)
    numer = jnp.einsum("thd,hde->the", query_heads, state, precision=lax.Precision.HIGHEST)
    denom = (
        jnp.einsum("thd,hd->th", query_heads, key_total, precision=lax.Precision.HIGHEST) + epsilon
    )
    attended = (numer / denom[:, :, None]).reshape(rows_here, channels).astype(jnp.bfloat16)
    strips = HEIGHT * WIDTH // rows_here
    earlier = from_behind(attended, "frame", strips)
    later_frame = from_behind(attended, "frame", -strips)
    mixed = (
        taps[0] * earlier.astype(jnp.float32)
        + taps[1] * attended.astype(jnp.float32)
        + taps[2] * later_frame.astype(jnp.float32)
    ).astype(jnp.bfloat16)
    return mixed


def solution(mesh):
    placed = (P(("grp", "frame"), None), P("frame", None), P("frame", None), P())
    return jax.shard_map(
        local, mesh=mesh, in_specs=placed, out_specs=P(("grp", "frame"), None), check_vma=False
    )
```

profile of v0, /device:TPU:0, one launch (start us, length us, event | category | flops | bytes accessed | tf_op | source)
XLA Modules:
  0.0 409.3 jit_solution(9737158301106324964)
XLA Ops:
  6.5 0.0 copy-start.1
  6.5 0.0 all-gather.5.cloned.1.call-start
  6.5 0.7 all-gather.5.cloned.1.call-update
  7.3 0.0 all-gather.3.cloned.1.call-start
  7.3 0.7 all-gather.3.cloned.1.call-update
  8.0 0.0 all-reduce.2.cloned.1.call-start
  8.1 1.6 fusion.1
  9.7 80.0 %all-gather.5.cloned.1.call-done = bf16[1792,2240]{1,0:T(8,128)(2,1)} async-done(((bf16[56,2240]{1,0:T(8,128)(2,1)}), bf16[1792,2240]{1,0:T(8,128)(2,1)}) %all-gather.5.cloned.1.call-update) | async-done | bytes 8028176 | tf_op jit(solution)/shard_map/all_gather | solution.py:46
  89.7 0.0 copy-done.1
  89.7 5.7 %fusion = bf16[256,1792]{1,0:T(8,128)(2,1)S(1)} fusion(bf16[1792,2240]{1,0:T(8,128)(2,1)} %all-gather.5.cloned.1.call-done, bf16[256,2240]{0,1:T(8,128)(2,1)S(1)} %copy-done.1, f32[256]{0:T(256)S(1)} %add_rsqrt_fusion), kind=kOutput, calls=%fused_computation.3 | convolution fusion | flops 2057846784 | bytes 10093568 | tf_op jit(solution)/shard_map/dot_general | solution.py:33
  95.4 0.5 copy.11
  96.0 108.9 %all-gather.3.cloned.1.call-done = bf16[3584,2240]{1,0:T(8,128)(2,1)} async-done(((bf16[112,2240]{1,0:T(8,128)(2,1)}), bf16[3584,2240]{1,0:T(8,128)(2,1)}) %all-gather.3.cloned.1.call-update) | async-done | bytes 16056336 | tf_op jit(solution)/shard_map/all_gather | solution.py:37
  204.9 17.6 %fusion.6 = bf16[256,3584]{1,0:T(8,128)(2,1)} fusion(bf16[3584,2240]{1,0:T(8,128)(2,1)} %all-gather.3.cloned.1.call-done, bf16[256,2240]{0,1:T(8,128)(2,1)S(1)} %copy-done.1, f32[256]{0:T(256)S(1)} %add_rsqrt_fusion), kind=kOutput, calls=%fused_computation.13 | convolution fusion | flops 4112138240 | bytes 19039232 | tf_op jit(solution)/shard_map/dot_general | solution.py:33
  222.5 1.4 convert_reduce_fusion
  223.9 0.0 slice-start
  223.9 1.3 copy.9
  225.2 0.0 slice-done
  225.2 0.0 copy-start
  225.2 1.3 copy.10
  226.5 0.0 copy-done
  226.5 2.5 fusion.10
  229.0 0.0 all-reduce.2.cloned.1.call-update
  229.0 0.1 reduce_sum.22
  229.1 38.6 %psum.15 = f32[16,112]{1,0:T(8,128)S(1)} all-reduce(f32[16,112]{1,0:T(8,128)S(1)} %reduce_sum.22), channel_id=1, replica_groups=mesh['grp'=1,'frame'=32] {'frame'}, use_global_device_ids=true, to_apply=%region_3.4 | all-reduce | flops 1792 | bytes 14336 | tf_op jit(solution)/shard_map/psum | solution.py:48
  267.7 0.5 fusion.11
  268.1 88.9 %all-reduce.2.cloned.1.call-done = f32[16,112,112]{1,2,0:T(8,128)} async-done(((f32[16,112,112]{1,2,0:T(8,128)}), f32[16,112,112]{1,2,0:T(8,128)}) %all-reduce.2.cloned.1.call-update) | async-done | bytes 802832 | tf_op jit(solution)/shard_map/psum | solution.py:48
  357.0 2.1 fusion.4
  359.1 0.0 copy-start.2
  359.1 0.6 copy.12
  359.7 3.4 collective-permute-start
  363.1 1.3 collective-permute-start.1
  364.4 0.0 copy-done.2
  364.4 0.1 slice_reduce_fusion.2
  364.5 36.9 %collective-permute-done = bf16[256,1792]{1,0:T(8,128)(2,1)S(1)} collective-permute-done((bf16[256,1792]{1,0:T(8,128)(2,1)S(1)}, bf16[256,1792]{1,0:T(8,128)(2,1)S(1)}, u32[]{:S(2)}, u32[]{:S(2)}) %collective-permute-start) | collective-permute-done | bytes 917536 | tf_op jit(solution)/shard_map/ppermute | solution.py:18
  401.4 0.0 collective-permute-done.1
  401.4 1.4 add_convert_fusion
  (2 shorter events, 0.0 us)
Async XLA Ops:
  6.5 83.2 %copy-start.1 = (bf16[256,2240]{0,1:T(8,128)(2,1)S(1)}, bf16[256,2240]{0,1:T(8,128)(2,1)}, u32[]{:S(2)}) copy-start(bf16[256,2240]{0,1:T(8,128)(2,1)} %param.4) | copy-start | bytes 3440644
  6.5 83.2 %all-gather.5.cloned.1.call-start = ((), (), s32[]{:S(2)}) async-start(), calls=%async_computation.2 | async-start | bytes 8515584 | tf_op jit(solution)/shard_map/all_gather | solution.py:46
  7.3 197.6 %all-gather.3.cloned.1.call-start = ((), (), s32[]{:S(2)}) async-start(), calls=%async_computation | async-start | bytes 17031168 | tf_op jit(solution)/shard_map/all_gather | solution.py:37
  8.0 349.0 %all-reduce.2.cloned.1.call-start = ((), (), s32[]{:S(2)}) async-start(), calls=%async_computation.1 | async-start | bytes 1835008 | tf_op jit(solution)/shard_map/psum | solution.py:48
  223.9 1.3 slice-start
  225.2 1.3 copy-start
  359.1 5.3 %copy-start.2 = (f32[3,1792]{1,0:T(4,128)S(1)}, f32[3,1792]{1,0:T(4,128)}, u32[]{:S(2)}) copy-start(f32[3,1792]{1,0:T(4,128)} %param.7) | copy-start | bytes 64516
  359.7 41.7 %collective-permute-start = (bf16[256,1792]{1,0:T(8,128)(2,1)S(1)}, bf16[256,1792]{1,0:T(8,128)(2,1)S(1)}, u32[]{:S(2)}, u32[]{:S(2)}) collective-permute-start(bf16[256,1792]{1,0:T(8,128)(2,1)S(1)} %copy.12), channel_id=1, source_target_pairs={{0,4},{1,5},{2,6},{3,7},{4,8},{5,9},{6,10},{7,11},{8,12},{9,13},{1... | collective-permute-start | bytes 2752520 | tf_op jit(solution)/shard_map/ppermute | solution.py:18
  363.1 38.3 %collective-permute-start.1 = (bf16[256,1792]{1,0:T(8,128)(2,1)S(1)}, bf16[256,1792]{1,0:T(8,128)(2,1)S(1)}, u32[]{:S(2)}, u32[]{:S(2)}) collective-permute-start(bf16[256,1792]{1,0:T(8,128)(2,1)S(1)} %copy.12), channel_id=1, source_target_pairs={{4,0},{5,1},{6,2},{7,3},{8,4},{9,5},{10,6},{11,7},{12,8},{13,9},{1... | collective-permute-start | bytes 2752520 | tf_op jit(solution)/shard_map/ppermute | solution.py:18
Sparse Core Ops, SparseCore 0:
  10.3 79.3 all-gather.4
  92.6 112.2 all-gather.2
  229.1 127.8 all-reduce.1
where the time goes:
time: 410 us; the launch traced here: 409 us
  waiting for transfers between devices  316 us (77%)
  blocking collectives  38.6 us (9%)
  matrix products  28.4 us (7%)
  between operations  13.2 us (3%)
  starting transfers between devices  4.73 us (1%)
  other arithmetic  4.45 us (1%)
    all_gather x1, waiting for transfers between devices, local(): lax.all_gather(w_keyval, 'frame', axis=0, tiled=True)  109 us
    psum x1, waiting for transfers between devices, local(): state, key_total = lax.psum((local_state, local_keys), 'frame')  88.9 us
    all_gather x1, waiting for transfers between devices, local(): lax.all_gather(w_query, 'frame', axis=0, tiled=True)  80 us
    psum x1, blocking collectives, local(): state, key_total = lax.psum((local_state, local_keys), 'frame')  38.6 us
    ppermute x2, waiting for transfers between devices, from_behind(): lax.ppermute(value, axis, [(source, source + steps) for source in range(l...  36.9 us
    dot_general x2, matrix products, project_rows(): lax.dot_general(normed, weight_rows, (((1,), (1,)), ((), ())), preferred_...  23.3 us
  transfers between devices with their start and end apart: 5, of which 4 were waited for; matrix products, arithmetic and copies ran while one was open for 2% of the time, Pallas kernels for 0%

commit v1 on v0

--- a/solution.py
+++ b/solution.py
@@ -24,17 +24,17 @@
     return (values * scale_inv).astype(jnp.bfloat16)
 
 
-def local(tokens, w_query, w_keyval, taps):
+def project(rows, weight_rows):
+    return lax.dot_general(
+        rows, weight_rows, (((1,), (1,)), ((), ())), preferred_element_type=jnp.float32
+    )
+
+
+def gathered(tokens, w_query, w_keyval, taps):
     channels = HEADS * HDIM
     rows_here = tokens.shape[0]
     normed = normalize(tokens)
-
-    def project_rows(weight_rows):
-        return lax.dot_general(
-            normed, weight_rows, (((1,), (1,)), ((), ())), preferred_element_type=jnp.float32
-        )
-
-    keyval_lin = project_rows(lax.all_gather(w_keyval, "frame", axis=0, tiled=True))
+    keyval_lin = project(normed, lax.all_gather(w_keyval, "frame", axis=0, tiled=True))
     key_feats = jax.nn.relu(keyval_lin[:, :channels]).astype(jnp.bfloat16)
     value_proj = keyval_lin[:, channels:].astype(jnp.bfloat16)
     key_heads = key_feats.reshape(rows_here, HEADS, HDIM)
@@ -43,7 +43,7 @@
         "thd,the->hde", key_heads, value_heads, preferred_element_type=jnp.float32
     )
     local_keys = jnp.sum(key_heads.astype(jnp.float32), axis=0)
-    query_lin = project_rows(lax.all_gather(w_query, "frame", axis=0, tiled=True))
+    query_lin = project(normed, lax.all_gather(w_query, "frame", axis=0, tiled=True))
     query_feats = jax.nn.relu(query_lin).astype(jnp.bfloat16)
     state, key_total = lax.psum((local_state, local_keys), "frame")
     query_heads = query_feats.reshape(rows_here, HEADS, HDIM).astype(jnp.float32)
@@ -63,6 +63,177 @@
     return mixed
 
 
+LAYERS = 4
+PLANE = 8
+
+
+def send(value, place):
+    pairs = []
+    for z in range(LAYERS):
+        for slot in range(PLANE):
+            to = place(z, slot)
+            if to is not None:
+                pairs.append((z * PLANE + slot, to[0] * PLANE + to[1]))
+    return lax.ppermute(value, "frame", pairs)
+
+
+def swap(value, bits):
+    return send(value, lambda z, slot: (z, slot ^ bits))
+
+
+def between(value, steps):
+    return send(value, lambda z, slot: (steps[z], slot) if z in steps else None)
+
+
+def pick(flag, first, second):
+    return jnp.where(flag, first, second)
+
+
+def attend(query, state):
+    high = state.astype(jnp.bfloat16)
+    low = (state - high.astype(jnp.float32)).astype(jnp.bfloat16)
+    both = jnp.dot(query, high, preferred_element_type=jnp.float32) + jnp.dot(
+        query, low, preferred_element_type=jnp.float32
+    )
+    return (both[:, :HDIM] / (both[:, HDIM:] + epsilon)).astype(jnp.bfloat16)
+
+
+def planes(tokens, w_query, w_keyval, taps):
+    me = lax.axis_index("frame")
+    z, slot = me // PLANE, me % PLANE
+    y = slot // 4
+    rows_here = tokens.shape[0]
+
+    keyval = [w_keyval, None, None, None]
+    keyval[2] = between(w_keyval, {0: 2, 2: 0, 1: 3, 3: 1})
+    keyval[1] = between(w_keyval, {0: 1, 1: 0, 2: 3, 3: 2})
+    inner = between(w_keyval, {1: 2, 2: 1})
+
+    blocks = [None] * PLANE
+    blocks[0] = normalize(tokens)
+    blocks[2] = swap(blocks[0], 2)
+    blocks[4] = swap(blocks[0], 4)
+    blocks[1] = swap(blocks[0], 1)
+
+    def home(z, slot, half):
+        head = (z * PLANE + slot) // 2
+        return (z, head % PLANE) if slot % 2 == half else None
+
+    halves = [send(w_query, lambda z, slot, half=half: home(z, slot, half)) for half in range(2)]
+    query_here = jnp.concatenate(halves, axis=0)
+
+    outer = between(keyval[2], {1: 0, 2: 3})
+    keyval[3] = inner + outer
+
+    half_rows = rows_here // 2
+    low = swap(blocks[2][:half_rows], 4)
+    high = swap(blocks[4][half_rows:], 2)
+    blocks[3] = swap(blocks[2], 1)
+    blocks[5] = swap(blocks[4], 1)
+
+    def query_out(z, slot):
+        return (z ^ 1, slot) if z % 2 == slot // 4 else None
+
+    query_near = query_here + send(query_here, query_out)
+    query_inner = between(query_near, {1: 2, 2: 1})
+    query_far = query_inner + between(query_inner, {1: 0, 2: 3})
+
+    blocks[6] = jnp.concatenate([low, high], axis=0)
+    blocks[7] = jnp.concatenate([swap(low, 1), swap(high, 1)], axis=0)
+
+    ones = jnp.ones((2 * rows_here, 1), jnp.bfloat16)
+    partial = [0.0, 0.0]
+    chunks = [
+        jnp.concatenate([blocks[k], blocks[k + 1]], axis=0) for k in range(0, PLANE, 2)
+    ]
+    keys_first = z < 2
+    for chunk in chunks:
+        lin = [project(chunk, rows) for rows in keyval]
+        for pair in range(2):
+            key = jax.nn.relu(pick(keys_first, lin[pair], lin[pair + 2])).astype(jnp.bfloat16)
+            value = pick(keys_first, lin[pair + 2], lin[pair]).astype(jnp.bfloat16)
+            partial[pair] += lax.dot_general(
+                key,
+                jnp.concatenate([value, ones], axis=1),
+                (((0,), (0,)), ((), ())),
+                preferred_element_type=jnp.float32,
+            )
+    odd = z % 2 == 1
+    state = jnp.stack([pick(odd, partial[1], partial[0]), pick(odd, partial[0], partial[1])])
+    state = state + between(state, {0: 1, 1: 0, 2: 3, 3: 2})
+    state = state + between(state, {0: 2, 2: 0, 1: 3, 3: 1})
+
+    near_first = z < 2
+    queries = []
+    for rows in (pick(near_first, query_near, query_far), pick(near_first, query_far, query_near)):
+        queries.append(
+            [jax.nn.relu(project(chunk, rows)).astype(jnp.bfloat16) for chunk in chunks]
+        )
+    mine = [jnp.concatenate(parts[:2], axis=0) for parts in queries]
+    other = [jnp.concatenate(parts[2:], axis=0) for parts in queries]
+    even_row = y == 0
+    frame_a = jnp.concatenate([pick(even_row, m, o) for m, o in zip(mine, other)], axis=1)
+    frame_b = jnp.concatenate([pick(even_row, o, m) for m, o in zip(mine, other)], axis=1)
+    before = between(frame_b, {0: 1, 1: 2, 2: 3})
+    after = between(frame_a, {1: 0, 2: 1, 3: 2})
+
+    def attended(frame):
+        return jnp.concatenate(
+            [attend(frame[:, HDIM * i : HDIM * (i + 1)], state[i]) for i in range(2)], axis=1
+        ).astype(jnp.float32)
+
+    there_before, there_after = z > 0, z < LAYERS - 1
+    att_before = pick(there_before, attended(before), 0.0)
+    att_a, att_b = attended(frame_a), attended(frame_b)
+    att_after = pick(there_after, attended(after), 0.0)
+    by_head = taps.reshape(3, HEADS, HDIM)
+    tap = jnp.concatenate(
+        [
+            lax.dynamic_slice_in_dim(by_head, slot + PLANE * i, 1, axis=1)[:, 0]
+            for i in range(2)
+        ],
+        axis=1,
+    )
+    mixed_a = (tap[0] * att_before + tap[1] * att_a + tap[2] * att_b).astype(jnp.bfloat16)
+    mixed_b = (tap[0] * att_a + tap[1] * att_b + tap[2] * att_after).astype(jnp.bfloat16)
+    same = pick(even_row, mixed_a, mixed_b).reshape(2, 2, rows_here, 2 * HDIM)
+    cross = pick(even_row, mixed_b, mixed_a).reshape(2, 2, rows_here, 2 * HDIM)
+    by_place = jnp.stack([same, cross])
+    kept = by_place[:, :, 0]
+    given = swap(by_place[:, :, 1], 1)
+    odd_core = slot % 2 == 1
+    first, second = pick(odd_core, given, kept), pick(odd_core, kept, given)
+    whole = jnp.stack(
+        [
+            jnp.stack([part[..., HDIM * i : HDIM * (i + 1)] for part in (first, second)], axis=3)
+            for i in range(2)
+        ],
+        axis=3,
+    ).reshape(2, 2, rows_here, 4 * HDIM)
+    got = [
+        [whole[0, 0], swap(whole[0, 1], 2)],
+        [swap(whole[1, 0], 4), swap(whole[1, 1], 6)],
+    ]
+    right = (slot // 2) % 2 == 1
+    rows = [[pick(right, g[1], g[0]), pick(right, g[0], g[1])] for g in got]
+    placed = [pick(even_row, rows[0][i], rows[1][i]) for i in range(2)] + [
+        pick(even_row, rows[1][i], rows[0][i]) for i in range(2)
+    ]
+    out = [part[:, : 2 * HDIM] for part in placed] + [part[:, 2 * HDIM :] for part in placed]
+    return jnp.concatenate(out, axis=1)
+
+
+def local(tokens, w_query, w_keyval, taps):
+    fits = (
+        lax.axis_size("frame") == LAYERS * PLANE
+        and HEADS == 2 * PLANE
+        and w_keyval.shape[0] == HDIM
+        and 2 * w_query.shape[0] == HDIM
+        and PLANE * tokens.shape[0] == 2 * HEIGHT * WIDTH
+    )
+    return (planes if fits else gathered)(tokens, w_query, w_keyval, taps)
+
+
 def solution(mesh):
     placed = (P(("grp", "frame"), None), P("frame", None), P("frame", None), P())
     return jax.shard_map(

time: 410 us -> 162 us (0.40)
  waiting for transfers between devices: 316 us -> 38.8 us
  starting transfers between devices: 4.73 us -> 78.3 us
  blocking collectives: 38.6 us -> 0 us
  between operations: 13.2 us -> 1.28 us
  other arithmetic: 4.45 us -> 10.8 us
    all_gather x2 -> x0, waiting for transfers between devices: 189 us -> none  [the longest x1 109 us: local(): lax.all_gather(w_keyval, 'frame', axis=0, tiled=True)]
    psum x1 -> x0, waiting for transfers between devices: 88.9 us -> none  [local(): state, key_total = lax.psum((local_state, local_keys), 'frame')]
    ppermute x2 -> x26, starting transfers between devices: 4.66 us -> 78.3 us  [send(): return lax.ppermute(value, 'frame', pairs)]
    psum x1 -> x0, blocking collectives: 38.6 us -> none  [local(): state, key_total = lax.psum((local_state, local_keys), 'frame')]
    ppermute x2 -> x26, waiting for transfers between devices: 36.9 us -> 38.8 us  [send(): return lax.ppermute(value, 'frame', pairs)]
    dot_general x5 -> x48, matrix products: 28.4 us -> 27.5 us  [the longest x24 21.2 us: project(): lax.dot_general(rows, weight_rows, (((1,), (1,)), ((), ())), preferred_el...]
  transfers between devices with their start and end apart: 5 -> 26, of which waited for: 4 -> 7; matrix products, arithmetic and copies ran while one was open for 2% -> 19% of each run, Pallas kernels for 0% -> 0%
where the time goes in v1:
time: 162 us; the launch traced here: 161 us
  starting transfers between devices  78.3 us (48%)
  waiting for transfers between devices  38.8 us (24%)
  matrix products  27.5 us (17%)
  other arithmetic  10.8 us (7%)
  local copies, waits for them, and re-layouts  4.27 us (3%)
    ppermute x26, starting transfers between devices, send(): return lax.ppermute(value, 'frame', pairs)  78.3 us
    ppermute x26, waiting for transfers between devices, send(): return lax.ppermute(value, 'frame', pairs)  38.8 us
    dot_general x24, matrix products, project(): lax.dot_general(rows, weight_rows, (((1,), (1,)), ((), ())), preferred_el...  21.2 us
  transfers between devices with their start and end apart: 26, of which 7 were waited for; matrix products, arithmetic and copies ran while one was open for 19% of the time, Pallas kernels for 0%

profile of v1, /device:TPU:0, one launch (start us, length us, event | category | flops | bytes accessed | tf_op | source)
XLA Modules:
  0.0 161.0 jit_solution(751523236733626845)
XLA Ops:
  0.0 1.7 %collective-permute-start.2 = (bf16[56,2240]{1,0:T(8,128)(2,1)}, bf16[56,2240]{1,0:T(8,128)(2,1)S(1)}, u32[]{:S(2)}, u32[]{:S(2)}) collective-permute-start(bf16[56,2240]{1,0:T(8,128)(2,1)} %param.5), channel_id=1, source_target_pairs={{0,0},{2,1},{4,2},{6,3},{8,12},{10,13},{12,14},{14,15},{16,16},{18... | collective-permute-start | bytes 752648 | tf_op jit(solution)/shard_map/ppermute | solution.py:77
  1.7 1.6 fusion
  3.3 2.5 %fusion.1 = bf16[256,2240]{0,1:T(8,128)(2,1)} fusion(bf16[256,2240]{0,1:T(8,128)(2,1)} %param.4, f32[256]{0:T(256)S(1)} %add_rsqrt_fusion), kind=kLoop, calls=%fused_computation.3 | loop fusion | flops 1720320 | bytes 2294784 | tf_op jit(solution)/shard_map/convert_element_type | solution.py:24
  5.9 3.3 %collective-permute-start.7 = (bf16[256,2240]{0,1:T(8,128)(2,1)}, bf16[256,2240]{0,1:T(8,128)(2,1)S(1)}, u32[]{:S(2)}, u32[]{:S(2)}) collective-permute-start(bf16[256,2240]{0,1:T(8,128)(2,1)} %fusion.1), channel_id=1, source_target_pairs={{0,2},{1,3},{2,0},{3,1},{4,6},{5,7},{6,4},{7,5},{8,10},{9,11},{10,... | collective-permute-start | bytes 3440648 | tf_op jit(solution)/shard_map/ppermute | solution.py:77
  9.2 1.5 collective-permute-start
  10.6 1.3 collective-permute-start.3
  11.9 2.7 %collective-permute-start.17 = (bf16[112,2240]{1,0:T(8,128)(2,1)S(1)}, bf16[112,2240]{1,0:T(8,128)(2,1)S(1)}, u32[]{:S(2)}, u32[]{:S(2)}) collective-permute-start(bf16[112,2240]{1,0:T(8,128)(2,1)S(1)} %copy-done), channel_id=1, source_target_pairs={{0,16},{1,17},{2,18},{3,19},{4,20},{5,21},{6,22},{7,23},{8,24},{9,... | collective-permute-start | bytes 1505288 | tf_op jit(solution)/shard_map/ppermute | solution.py:77
  14.6 3.7 %collective-permute-start.4 = (bf16[112,2240]{1,0:T(8,128)(2,1)S(1)}, bf16[112,2240]{1,0:T(8,128)(2,1)}, u32[]{:S(2)}, u32[]{:S(2)}) collective-permute-start(bf16[112,2240]{1,0:T(8,128)(2,1)S(1)} %constant_dynamic-update-slice_fusion), channel_id=1, source_target_pairs={{0,8},{1,9},{2,10},{3,11},{12,4},{13,5},{14,6},{15,7},{16,24},{17,... | collective-permute-start | bytes 1505288 | tf_op jit(solution)/shard_map/ppermute | solution.py:77
  18.4 27.7 %collective-permute-start.12 = (bf16[256,2240]{0,1:T(8,128)(2,1)}, bf16[256,2240]{0,1:T(8,128)(2,1)}, u32[]{:S(2)}, u32[]{:S(2)}) collective-permute-start(bf16[256,2240]{0,1:T(8,128)(2,1)} %fusion.1), channel_id=1, source_target_pairs={{0,1},{1,0},{2,3},{3,2},{4,5},{5,4},{6,7},{7,6},{8,9},{9,8},{10,11... | collective-permute-start | bytes 3440648 | tf_op jit(solution)/shard_map/ppermute | solution.py:77
  46.1 1.4 collective-permute-start.16
  47.5 1.3 collective-permute-start.18
  49.1 1.3 add.199
  50.4 12.7 %collective-permute-start.15 = (bf16[112,2240]{1,0:T(8,128)(2,1)S(1)}, bf16[112,2240]{1,0:T(8,128)(2,1)S(1)}, u32[]{:S(2)}, u32[]{:S(2)}) collective-permute-start(bf16[112,2240]{1,0:T(8,128)(2,1)S(1)} %copy-done), channel_id=1, source_target_pairs={{0,8},{1,9},{2,10},{3,11},{4,12},{5,13},{6,14},{7,15},{8,0},{9,1},... | collective-permute-start | bytes 1505288 | tf_op jit(solution)/shard_map/ppermute | solution.py:77
  63.2 0.7 collective-permute-start.5
  63.8 1.3 add.202
  65.2 5.9 %collective-permute-start.8 = (bf16[128,2240]{0,1:T(8,128)(2,1)S(1)}, bf16[128,2240]{0,1:T(8,128)(2,1)S(1)}, u32[]{:S(2)}, u32[]{:S(2)}) collective-permute-start(bf16[128,2240]{0,1:T(8,128)(2,1)S(1)} %slice.189), channel_id=1, source_target_pairs={{0,4},{1,5},{2,6},{3,7},{4,0},{5,1},{6,2},{7,3},{8,12},{9,13},{10,... | collective-permute-start | bytes 1720328 | tf_op jit(solution)/shard_map/ppermute | solution.py:77
  71.3 2.0 %collective-permute-start.13 = (bf16[256,2240]{0,1:T(8,128)(2,1)S(1)}, bf16[256,2240]{0,1:T(8,128)(2,1)S(1)}, u32[]{:S(2)}, u32[]{:S(2)}) collective-permute-start(bf16[256,2240]{0,1:T(8,128)(2,1)S(1)} %collective-permute-done.7), channel_id=1, source_target_pairs={{0,1},{1,0},{2,3},{3,2},{4,5},{5,4},{6,7},{7,6},{8,9},{9,8},{10,11... | collective-permute-start | bytes 3440648 | tf_op jit(solution)/shard_map/ppermute | solution.py:77
  73.4 2.1 %fusion.86 = bf16[512,112]{0,1:T(8,128)(2,1)S(1)} fusion(bf16[112,2240]{1,0:T(8,128)(2,1)S(1)} %copy-done, bf16[256,2240]{0,1:T(8,128)(2,1)} %collective-permute-done.12, bf16[256,2240]{0,1:T(8,128)(2,1)} %fusion.1), kind=kOutput, calls=%fused_computation.220 | convolution fusion | flops 261488640 | bytes 2910208 | tf_op jit(solution)/shard_map/dot_general | solution.py:28
  75.4 2.1 %select_convert_fusion.3 = (bf16[512,112]{0,1:T(8,128)(2,1)S(1)}, bf16[512,112]{0,1:T(8,128)(2,1)S(1)}) fusion(bf16[512,112]{0,1:T(8,128)(2,1)S(1)} %fusion.86, pred[]{:T(512)S(6)} %lt.33, bf16[112,2240]{1,0:T(8,128)(2,1)S(1)} %collective-permute-done.17, bf16[256,2240]{0,1:T(8,128)(2,1)} %collective-permute-done.12, bf16[256,2240]{0,1:T(8,128)(2,1)} %fusion.1), kind=kOutput, calls=%fused_computation.98 | convolution fusion | flops 261545984 | bytes 3139585 | tf_op jit(solution)/shard_map/dot_general | solution.py:28
  77.9 2.1 %fusion.84 = bf16[512,112]{0,1:T(8,128)(2,1)S(1)} fusion(bf16[112,2240]{1,0:T(8,128)(2,1)S(1)} %collective-permute-done.15, bf16[256,2240]{0,1:T(8,128)(2,1)} %collective-permute-done.12, bf16[256,2240]{0,1:T(8,128)(2,1)} %fusion.1), kind=kOutput, calls=%fused_computation.218 | convolution fusion | flops 261488640 | bytes 2910208 | tf_op jit(solution)/shard_map/dot_general | solution.py:28
  80.0 2.1 %select_convert_fusion.7 = (bf16[512,112]{0,1:T(8,128)(2,1)S(1)}, bf16[512,112]{0,1:T(8,128)(2,1)S(1)}) fusion(bf16[512,112]{0,1:T(8,128)(2,1)S(1)} %fusion.84, pred[]{:T(512)S(6)} %lt.33, bf16[112,2240]{1,0:T(8,128)(2,1)S(1)} %add.202, bf16[256,2240]{0,1:T(8,128)(2,1)} %collective-permute-done.12, bf16[256,2240]{0,1:T(8,128)(2,1)} %fusion.1), kind=kOutput, calls=%fused_computation.106 | convolution fusion | flops 261545984 | bytes 3139585 | tf_op jit(solution)/shard_map/dot_general | solution.py:28
  82.3 1.3 collective-permute-start.6
  83.7 0.6 collective-permute-start.10
  84.3 2.3 %collective-permute-done.9 = bf16[128,2240]{0,1:T(8,128)(2,1)S(1)} collective-permute-done((bf16[128,2240]{0,1:T(8,128)(2,1)S(1)}, bf16[128,2240]{0,1:T(8,128)(2,1)S(1)}, u32[]{:S(2)}, u32[]{:S(2)}) %collective-permute-start.9) | collective-permute-done | bytes 573472 | tf_op jit(solution)/shard_map/ppermute | solution.py:77
  86.8 11.6 %collective-permute-done.6 = bf16[112,2240]{1,0:T(8,128)(2,1)S(1)} collective-permute-done((bf16[112,2240]{1,0:T(8,128)(2,1)S(1)}, bf16[112,2240]{1,0:T(8,128)(2,1)S(1)}, u32[]{:S(2)}, u32[]{:S(2)}) %collective-permute-start.6) | collective-permute-done | bytes 501792 | tf_op jit(solution)/shard_map/ppermute | solution.py:77
  98.4 2.1 %fusion.8 = bf16[512,112]{0,1:T(8,128)(2,1)S(1)} fusion(bf16[112,2240]{1,0:T(8,128)(2,1)S(1)} %get-tuple-element.17, bf16[256,2240]{0,1:T(8,128)(2,1)} %collective-permute-done.12, bf16[256,2240]{0,1:T(8,128)(2,1)} %fusion.1), kind=kOutput, calls=%fused_computation.27 | convolution fusion | flops 261603328 | bytes 2910208 | tf_op jit(solution)/shard_map/dot_general | solution.py:28
  100.5 2.1 %fusion.4 = bf16[512,112]{0,1:T(8,128)(2,1)S(1)} fusion(bf16[112,2240]{1,0:T(8,128)(2,1)S(1)} %get-tuple-element.16, bf16[256,2240]{0,1:T(8,128)(2,1)} %collective-permute-done.12, bf16[256,2240]{0,1:T(8,128)(2,1)} %fusion.1), kind=kOutput, calls=%fused_computation.23 | convolution fusion | flops 261603328 | bytes 2910208 | tf_op jit(solution)/shard_map/dot_general | solution.py:28
  108.0 0.5 select_convert_fusion.6
  110.0 0.5 select_convert_fusion.4
  111.2 0.5 select_convert_fusion.1
  111.8 0.5 select_convert_fusion
  113.4 0.8 pad_maximum_fusion.6
  114.2 1.5 collective-permute-start.21
  115.7 2.3 %collective-permute-done.19 = f32[2,112,113]{2,1,0:T(8,128)S(1)} collective-permute-done((f32[2,112,113]{2,1,0:T(8,128)S(1)}, f32[2,112,113]{2,1,0:T(8,128)S(1)}, u32[]{:S(2)}, u32[]{:S(2)}) %collective-permute-start.19) | collective-permute-done | bytes 101280 | tf_op jit(solution)/shard_map/ppermute | solution.py:77
  118.0 1.9 %collective-permute-start.20 = (f32[2,112,113]{2,1,0:T(8,128)S(1)}, f32[2,112,113]{2,1,0:T(8,128)S(1)}, u32[]{:S(2)}, u32[]{:S(2)}) collective-permute-start(f32[2,112,113]{2,1,0:T(8,128)S(1)} %fusion.83), channel_id=1, source_target_pairs={{0,16},{1,17},{2,18},{3,19},{4,20},{5,21},{6,22},{7,23},{8,24},{9,... | collective-permute-start | bytes 303752 | tf_op jit(solution)/shard_map/ppermute | solution.py:77
  119.9 0.8 pad_maximum_fusion.3
  120.7 3.4 %collective-permute-start.14 = (bf16[1024,224]{0,1:T(8,128)(2,1)}, bf16[1024,224]{0,1:T(8,128)(2,1)S(1)}, u32[]{:S(2)}, u32[]{:S(2)}) collective-permute-start(bf16[1024,224]{0,1:T(8,128)(2,1)} %pad_maximum_fusion.3), channel_id=1, source_target_pairs={{0,8},{1,9},{2,10},{3,11},{4,12},{5,13},{6,14},{7,15},{8,16},{9,17... | collective-permute-start | bytes 1376264 | tf_op jit(solution)/shard_map/ppermute | solution.py:77
  124.0 10.5 %collective-permute-done.20 = f32[2,112,113]{2,1,0:T(8,128)S(1)} collective-permute-done((f32[2,112,113]{2,1,0:T(8,128)S(1)}, f32[2,112,113]{2,1,0:T(8,128)S(1)}, u32[]{:S(2)}, u32[]{:S(2)}) %collective-permute-start.20) | collective-permute-done | bytes 101280 | tf_op jit(solution)/shard_map/ppermute | solution.py:77
  134.5 0.6 subtract_convert_fusion.1
  136.8 1.0 convolution_add_fusion.3
  142.4 0.6 broadcast_select_fusion.2
  143.3 1.8 %collective-permute-done.22 = bf16[2,2,256,224]{2,3,1,0:T(8,128)(2,1)S(1)} collective-permute-done((bf16[2,2,256,224]{2,3,1,0:T(8,128)(2,1)S(1)}, bf16[2,2,256,224]{2,3,1,0:T(8,128)(2,1)S(1)}, u32[]{:S(2)}, u32[]{:S(2)}) %collective-permute-start.22) | collective-permute-done | bytes 458784 | tf_op jit(solution)/shard_map/ppermute | solution.py:77
  145.5 1.5 collective-permute-start.25
  147.1 0.9 collective-permute-start.24
  148.0 1.1 collective-permute-start.23
  149.1 9.1 %collective-permute-done.25 = bf16[256,448]{0,1:T(8,128)(2,1)S(1)} collective-permute-done((bf16[256,448]{0,1:T(8,128)(2,1)S(1)}, bf16[256,448]{0,1:T(8,128)(2,1)S(1)}, u32[]{:S(2)}, u32[]{:S(2)}) %collective-permute-start.25) | collective-permute-done | bytes 229408 | tf_op jit(solution)/shard_map/ppermute | solution.py:77
  158.2 1.2 collective-permute-done.23
  159.6 1.4 copy.16
  (156 shorter events, 16.5 us)
Async XLA Ops:
  0.0 10.6 %copy-start.10 = (bf16[56,2240]{1,0:T(8,128)(2,1)S(1)}, bf16[56,2240]{1,0:T(8,128)(2,1)}, u32[]{:S(2)}) copy-start(bf16[56,2240]{1,0:T(8,128)(2,1)} %param.5) | copy-start | bytes 752644
  0.0 11.9 %copy-start = (bf16[112,2240]{1,0:T(8,128)(2,1)S(1)}, bf16[112,2240]{1,0:T(8,128)(2,1)}, u32[]{:S(2)}) copy-start(bf16[112,2240]{1,0:T(8,128)(2,1)} %param.6) | copy-start | bytes 1505284
  0.0 48.9 %copy-start.9 = (f32[3,1792]{1,0:T(4,128)S(1)}, f32[3,1792]{1,0:T(4,128)}, u32[]{:S(2)}) copy-start(f32[3,1792]{1,0:T(4,128)} %param.7) | copy-start | bytes 64516
  0.0 14.6 %collective-permute-start.2 = (bf16[56,2240]{1,0:T(8,128)(2,1)}, bf16[56,2240]{1,0:T(8,128)(2,1)S(1)}, u32[]{:S(2)}, u32[]{:S(2)}) collective-permute-start(bf16[56,2240]{1,0:T(8,128)(2,1)} %param.5), channel_id=1, source_target_pairs={{0,0},{2,1},{4,2},{6,3},{8,12},{10,13},{12,14},{14,15},{16,16},{18... | collective-permute-start | bytes 752648 | tf_op jit(solution)/shard_map/ppermute | solution.py:77
  5.9 59.3 %collective-permute-start.7 = (bf16[256,2240]{0,1:T(8,128)(2,1)}, bf16[256,2240]{0,1:T(8,128)(2,1)S(1)}, u32[]{:S(2)}, u32[]{:S(2)}) collective-permute-start(bf16[256,2240]{0,1:T(8,128)(2,1)} %fusion.1), channel_id=1, source_target_pairs={{0,2},{1,3},{2,0},{3,1},{4,6},{5,7},{6,4},{7,5},{8,10},{9,11},{10,... | collective-permute-start | bytes 3440648 | tf_op jit(solution)/shard_map/ppermute | solution.py:77
  9.2 62.0 %collective-permute-start = (bf16[256,2240]{0,1:T(8,128)(2,1)}, bf16[256,2240]{0,1:T(8,128)(2,1)S(1)}, u32[]{:S(2)}, u32[]{:S(2)}) collective-permute-start(bf16[256,2240]{0,1:T(8,128)(2,1)} %fusion.1), channel_id=1, source_target_pairs={{0,4},{1,5},{2,6},{3,7},{4,0},{5,1},{6,2},{7,3},{8,12},{9,13},{10,... | collective-permute-start | bytes 3440648 | tf_op jit(solution)/shard_map/ppermute | solution.py:77
  10.6 4.0 %collective-permute-start.3 = (bf16[56,2240]{1,0:T(8,128)(2,1)S(1)}, bf16[56,2240]{1,0:T(8,128)(2,1)S(1)}, u32[]{:S(2)}, u32[]{:S(2)}) collective-permute-start(bf16[56,2240]{1,0:T(8,128)(2,1)S(1)} %copy-done.10), channel_id=1, source_target_pairs={{1,0},{3,1},{5,2},{7,3},{9,12},{11,13},{13,14},{15,15},{17,16},{19... | collective-permute-start | bytes 752648 | tf_op jit(solution)/shard_map/ppermute | solution.py:77
  11.9 34.2 %collective-permute-start.17 = (bf16[112,2240]{1,0:T(8,128)(2,1)S(1)}, bf16[112,2240]{1,0:T(8,128)(2,1)S(1)}, u32[]{:S(2)}, u32[]{:S(2)}) collective-permute-start(bf16[112,2240]{1,0:T(8,128)(2,1)S(1)} %copy-done), channel_id=1, source_target_pairs={{0,16},{1,17},{2,18},{3,19},{4,20},{5,21},{6,22},{7,23},{8,24},{9,... | collective-permute-start | bytes 1505288 | tf_op jit(solution)/shard_map/ppermute | solution.py:77
  14.6 32.9 %copy-start.1 = (bf16[112,2240]{1,0:T(8,128)(2,1)}, bf16[112,2240]{1,0:T(8,128)(2,1)S(1)}, u32[]{:S(2)}) copy-start(bf16[112,2240]{1,0:T(8,128)(2,1)S(1)} %constant_dynamic-update-slice_fusion) | copy-start | bytes 1505284
  14.6 32.9 %collective-permute-start.4 = (bf16[112,2240]{1,0:T(8,128)(2,1)S(1)}, bf16[112,2240]{1,0:T(8,128)(2,1)}, u32[]{:S(2)}, u32[]{:S(2)}) collective-permute-start(bf16[112,2240]{1,0:T(8,128)(2,1)S(1)} %constant_dynamic-update-slice_fusion), channel_id=1, source_target_pairs={{0,8},{1,9},{2,10},{3,11},{12,4},{13,5},{14,6},{15,7},{16,24},{17,... | collective-permute-start | bytes 1505288 | tf_op jit(solution)/shard_map/ppermute | solution.py:77
  18.4 53.0 %collective-permute-start.12 = (bf16[256,2240]{0,1:T(8,128)(2,1)}, bf16[256,2240]{0,1:T(8,128)(2,1)}, u32[]{:S(2)}, u32[]{:S(2)}) collective-permute-start(bf16[256,2240]{0,1:T(8,128)(2,1)} %fusion.1), channel_id=1, source_target_pairs={{0,1},{1,0},{2,3},{3,2},{4,5},{5,4},{6,7},{7,6},{8,9},{9,8},{10,11... | collective-permute-start | bytes 3440648 | tf_op jit(solution)/shard_map/ppermute | solution.py:77
  46.1 4.3 %collective-permute-start.16 = (bf16[112,2240]{1,0:T(8,128)(2,1)S(1)}, bf16[112,2240]{1,0:T(8,128)(2,1)}, u32[]{:S(2)}, u32[]{:S(2)}) collective-permute-start(bf16[112,2240]{1,0:T(8,128)(2,1)S(1)} %copy-done), channel_id=1, source_target_pairs={{8,16},{9,17},{10,18},{11,19},{12,20},{13,21},{14,22},{15,23},{16,... | collective-permute-start | bytes 1505288 | tf_op jit(solution)/shard_map/ppermute | solution.py:77
  47.5 15.6 %collective-permute-start.18 = (bf16[112,2240]{1,0:T(8,128)(2,1)S(1)}, bf16[112,2240]{1,0:T(8,128)(2,1)}, u32[]{:S(2)}, u32[]{:S(2)}) collective-permute-start(bf16[112,2240]{1,0:T(8,128)(2,1)S(1)} %collective-permute-done.17), channel_id=1, source_target_pairs={{8,0},{9,1},{10,2},{11,3},{12,4},{13,5},{14,6},{15,7},{16,24},{17,... | collective-permute-start | bytes 1505288 | tf_op jit(solution)/shard_map/ppermute | solution.py:77
  50.4 27.4 %collective-permute-start.15 = (bf16[112,2240]{1,0:T(8,128)(2,1)S(1)}, bf16[112,2240]{1,0:T(8,128)(2,1)S(1)}, u32[]{:S(2)}, u32[]{:S(2)}) collective-permute-start(bf16[112,2240]{1,0:T(8,128)(2,1)S(1)} %copy-done), channel_id=1, source_target_pairs={{0,8},{1,9},{2,10},{3,11},{4,12},{5,13},{6,14},{7,15},{8,0},{9,1},... | collective-permute-start | bytes 1505288 | tf_op jit(solution)/shard_map/ppermute | solution.py:77
  63.2 19.1 %collective-permute-start.5 = (bf16[112,2240]{1,0:T(8,128)(2,1)S(1)}, bf16[112,2240]{1,0:T(8,128)(2,1)S(1)}, u32[]{:S(2)}, u32[]{:S(2)}) collective-permute-start(bf16[112,2240]{1,0:T(8,128)(2,1)S(1)} %add.199), channel_id=1, source_target_pairs={{8,16},{9,17},{10,18},{11,19},{12,20},{13,21},{14,22},{15,23},{16,... | collective-permute-start | bytes 1505288 | tf_op jit(solution)/shard_map/ppermute | solution.py:77
  65.2 18.4 %collective-permute-start.8 = (bf16[128,2240]{0,1:T(8,128)(2,1)S(1)}, bf16[128,2240]{0,1:T(8,128)(2,1)S(1)}, u32[]{:S(2)}, u32[]{:S(2)}) collective-permute-start(bf16[128,2240]{0,1:T(8,128)(2,1)S(1)} %slice.189), channel_id=1, source_target_pairs={{0,4},{1,5},{2,6},{3,7},{4,0},{5,1},{6,2},{7,3},{8,12},{9,13},{10,... | collective-permute-start | bytes 1720328 | tf_op jit(solution)/shard_map/ppermute | solution.py:77
  71.2 15.5 %collective-permute-start.9 = (bf16[128,2240]{0,1:T(8,128)(2,1)S(1)}, bf16[128,2240]{0,1:T(8,128)(2,1)S(1)}, u32[]{:S(2)}, u32[]{:S(2)}) collective-permute-start(bf16[128,2240]{0,1:T(8,128)(2,1)S(1)} %slice.190), channel_id=1, source_target_pairs={{0,2},{1,3},{2,0},{3,1},{4,6},{5,7},{6,4},{7,5},{8,10},{9,11},{10,... | collective-permute-start | bytes 1720328 | tf_op jit(solution)/shard_map/ppermute | solution.py:77
  71.3 31.3 %collective-permute-start.13 = (bf16[256,2240]{0,1:T(8,128)(2,1)S(1)}, bf16[256,2240]{0,1:T(8,128)(2,1)S(1)}, u32[]{:S(2)}, u32[]{:S(2)}) collective-permute-start(bf16[256,2240]{0,1:T(8,128)(2,1)S(1)} %collective-permute-done.7), channel_id=1, source_target_pairs={{0,1},{1,0},{2,3},{3,2},{4,5},{5,4},{6,7},{7,6},{8,9},{9,8},{10,11... | collective-permute-start | bytes 3440648 | tf_op jit(solution)/shard_map/ppermute | solution.py:77
  77.8 27.2 %collective-permute-start.1 = (bf16[256,2240]{0,1:T(8,128)(2,1)S(1)}, bf16[256,2240]{0,1:T(8,128)(2,1)S(1)}, u32[]{:S(2)}, u32[]{:S(2)}) collective-permute-start(bf16[256,2240]{0,1:T(8,128)(2,1)S(1)} %collective-permute-done), channel_id=1, source_target_pairs={{0,1},{1,0},{2,3},{3,2},{4,5},{5,4},{6,7},{7,6},{8,9},{9,8},{10,11... | collective-permute-start | bytes 3440648 | tf_op jit(solution)/shard_map/ppermute | solution.py:77
  82.3 16.0 %collective-permute-start.6 = (bf16[112,2240]{1,0:T(8,128)(2,1)S(1)}, bf16[112,2240]{1,0:T(8,128)(2,1)S(1)}, u32[]{:S(2)}, u32[]{:S(2)}) collective-permute-start(bf16[112,2240]{1,0:T(8,128)(2,1)S(1)} %collective-permute-done.5), channel_id=1, source_target_pairs={{8,0},{9,1},{10,2},{11,3},{12,4},{13,5},{14,6},{15,7},{16,24},{17,... | collective-permute-start | bytes 1505288 | tf_op jit(solution)/shard_map/ppermute | solution.py:77
  83.7 19.0 %collective-permute-start.10 = (bf16[128,2240]{0,1:T(8,128)(2,1)S(1)}, bf16[128,2240]{0,1:T(8,128)(2,1)S(1)}, u32[]{:S(2)}, u32[]{:S(2)}) collective-permute-start(bf16[128,2240]{0,1:T(8,128)(2,1)S(1)} %collective-permute-done.8), channel_id=1, source_target_pairs={{0,1},{1,0},{2,3},{3,2},{4,5},{5,4},{6,7},{7,6},{8,9},{9,8},{10,11... | collective-permute-start | bytes 1720328 | tf_op jit(solution)/shard_map/ppermute | solution.py:77
  86.6 17.3 %collective-permute-start.11 = (bf16[128,2240]{0,1:T(8,128)(2,1)S(1)}, bf16[128,2240]{0,1:T(8,128)(2,1)S(1)}, u32[]{:S(2)}, u32[]{:S(2)}) collective-permute-start(bf16[128,2240]{0,1:T(8,128)(2,1)S(1)} %collective-permute-done.9), channel_id=1, source_target_pairs={{0,1},{1,0},{2,3},{3,2},{4,5},{5,4},{6,7},{7,6},{8,9},{9,8},{10,11... | collective-permute-start | bytes 1720328 | tf_op jit(solution)/shard_map/ppermute | solution.py:77
  113.1 4.9 %collective-permute-start.19 = (f32[2,112,113]{2,1,0:T(8,128)S(1)}, f32[2,112,113]{2,1,0:T(8,128)S(1)}, u32[]{:S(2)}, u32[]{:S(2)}) collective-permute-start(f32[2,112,113]{2,1,0:T(8,128)S(1)} %pad_maximum_fusion.11), channel_id=1, source_target_pairs={{0,8},{1,9},{2,10},{3,11},{4,12},{5,13},{6,14},{7,15},{8,0},{9,1},... | collective-permute-start | bytes 303752 | tf_op jit(solution)/shard_map/ppermute | solution.py:77
  114.2 25.0 %collective-permute-start.21 = (bf16[1024,224]{0,1:T(8,128)(2,1)}, bf16[1024,224]{0,1:T(8,128)(2,1)S(1)}, u32[]{:S(2)}, u32[]{:S(2)}) collective-permute-start(bf16[1024,224]{0,1:T(8,128)(2,1)} %pad_maximum_fusion.6), channel_id=1, source_target_pairs={{8,0},{9,1},{10,2},{11,3},{12,4},{13,5},{14,6},{15,7},{16,8},{17,9... | collective-permute-start | bytes 1376264 | tf_op jit(solution)/shard_map/ppermute | solution.py:77
  118.0 16.5 %collective-permute-start.20 = (f32[2,112,113]{2,1,0:T(8,128)S(1)}, f32[2,112,113]{2,1,0:T(8,128)S(1)}, u32[]{:S(2)}, u32[]{:S(2)}) collective-permute-start(f32[2,112,113]{2,1,0:T(8,128)S(1)} %fusion.83), channel_id=1, source_target_pairs={{0,16},{1,17},{2,18},{3,19},{4,20},{5,21},{6,22},{7,23},{8,24},{9,... | collective-permute-start | bytes 303752 | tf_op jit(solution)/shard_map/ppermute | solution.py:77
  120.7 20.2 %collective-permute-start.14 = (bf16[1024,224]{0,1:T(8,128)(2,1)}, bf16[1024,224]{0,1:T(8,128)(2,1)S(1)}, u32[]{:S(2)}, u32[]{:S(2)}) collective-permute-start(bf16[1024,224]{0,1:T(8,128)(2,1)} %pad_maximum_fusion.3), channel_id=1, source_target_pairs={{0,8},{1,9},{2,10},{3,11},{4,12},{5,13},{6,14},{7,15},{8,16},{9,17... | collective-permute-start | bytes 1376264 | tf_op jit(solution)/shard_map/ppermute | solution.py:77
  135.2 0.6 copy-start.7
  135.2 1.4 copy-start.3
  135.2 1.4 copy-start.5
  136.8 1.3 copy-start.6
  137.9 0.8 copy-start.2
  138.4 0.8 copy-start.8
  139.0 1.0 copy-start.4
  143.2 1.9 %collective-permute-start.22 = (bf16[2,2,256,224]{2,3,1,0:T(8,128)(2,1)S(1)}, bf16[2,2,256,224]{2,3,1,0:T(8,128)(2,1)S(1)}, u32[]{:S(2)}, u32[]{:S(2)}) collective-permute-start(bf16[2,2,256,224]{2,3,1,0:T(8,128)(2,1)S(1)} %fusion.17), channel_id=1, source_target_pairs={{0,1},{1,0},{2,3},{3,2},{4,5},{5,4},{6,7},{7,6},{8,9},{9,8},{10,11... | collective-permute-start | bytes 1376264 | tf_op jit(solution)/shard_map/ppermute | solution.py:77
  145.5 12.6 %collective-permute-start.25 = (bf16[256,448]{0,1:T(8,128)(2,1)S(1)}, bf16[256,448]{0,1:T(8,128)(2,1)S(1)}, u32[]{:S(2)}, u32[]{:S(2)}) collective-permute-start(bf16[256,448]{0,1:T(8,128)(2,1)S(1)} %get-tuple-element.21), channel_id=1, source_target_pairs={{0,4},{1,5},{2,6},{3,7},{4,0},{5,1},{6,2},{7,3},{8,12},{9,13},{10,... | collective-permute-start | bytes 688136 | tf_op jit(solution)/shard_map/ppermute | solution.py:77
  147.1 11.1 %collective-permute-start.24 = (bf16[256,448]{0,1:T(8,128)(2,1)S(1)}, bf16[256,448]{0,1:T(8,128)(2,1)S(1)}, u32[]{:S(2)}, u32[]{:S(2)}) collective-permute-start(bf16[256,448]{0,1:T(8,128)(2,1)S(1)} %get-tuple-element.22), channel_id=1, source_target_pairs={{0,6},{1,7},{2,4},{3,5},{4,2},{5,3},{6,0},{7,1},{8,14},{9,15},{10,... | collective-permute-start | bytes 688136 | tf_op jit(solution)/shard_map/ppermute | solution.py:77
  148.0 11.4 %collective-permute-start.23 = (bf16[256,448]{0,1:T(8,128)(2,1)S(1)}, bf16[256,448]{0,1:T(8,128)(2,1)S(1)}, u32[]{:S(2)}, u32[]{:S(2)}) collective-permute-start(bf16[256,448]{0,1:T(8,128)(2,1)S(1)} %get-tuple-element.20), channel_id=1, source_target_pairs={{0,2},{1,3},{2,0},{3,1},{4,6},{5,7},{6,4},{7,5},{8,10},{9,11},{10,... | collective-permute-start | bytes 688136 | tf_op jit(solution)/shard_map/ppermute | solution.py:77

commit v2 on v0

--- a/solution.py
+++ b/solution.py
@@ -1,6 +1,10 @@
+import functools
+
 import jax
 import jax.numpy as jnp
 from jax import lax
+from jax.experimental import pallas as pl
+from jax.experimental.pallas import tpu as pltpu
 from jax.sharding import PartitionSpec as P
 
 HEADS = 16
@@ -24,7 +28,7 @@
     return (values * scale_inv).astype(jnp.bfloat16)
 
 
-def local(tokens, w_query, w_keyval, taps):
+def gathered(tokens, w_query, w_keyval, taps):
     channels = HEADS * HDIM
     rows_here = tokens.shape[0]
     normed = normalize(tokens)
@@ -63,6 +67,320 @@
     return mixed
 
 
+VMEM = pl.BlockSpec(memory_space=pltpu.VMEM)
+SMEM = pl.BlockSpec(memory_space=pltpu.SMEM)
+PARAMS = pltpu.CompilerParams(vmem_limit_bytes=48 * 2**20)
+
+
+def kernel_call(body, outs, *operands, scalars=1, scratch=()):
+    return pl.pallas_call(
+        body,
+        out_shape=outs,
+        in_specs=[SMEM] * scalars + [VMEM] * (len(operands) - scalars),
+        out_specs=jax.tree.map(lambda _: VMEM, outs),
+        scratch_shapes=list(scratch),
+        compiler_params=PARAMS,
+    )(*operands)
+
+
+def like(shape, dtype=jnp.bfloat16):
+    return jax.ShapeDtypeStruct(shape, dtype)
+
+
+def begin_kernel(tokens, w_query, w_keyval, normed, weights):
+    split = w_keyval.shape[0]
+    weights[:split] = w_keyval[...]
+    weights[split:] = w_query[...]
+    depth = tokens.shape[0]
+    step = depth // 10
+    total = jnp.zeros((1, tokens.shape[1]), jnp.float32)
+    for start in range(0, depth, step):
+        values = tokens[start : start + step].astype(jnp.float32)
+        total += jnp.sum(values * values, axis=0, keepdims=True)
+    scale_inv = lax.rsqrt(total / depth + epsilon)
+    for start in range(0, depth, step):
+        values = tokens[start : start + step].astype(jnp.float32)
+        normed[start : start + step] = (values * scale_inv).astype(jnp.bfloat16)
+
+
+def begin(tokens, w_query, w_keyval):
+    rows = w_keyval.shape[0] + w_query.shape[0]
+    outs = (like(tokens.shape), like((rows, w_query.shape[1])))
+    return kernel_call(begin_kernel, outs, tokens, w_query, w_keyval, scalars=0)
+
+
+def product(rows, block):
+    at, total = 0, None
+    for part in block:
+        depth = part.shape[0]
+        one = jnp.dot(rows[:, at : at + depth], part[...], preferred_element_type=jnp.float32)
+        at, total = at + depth, one if total is None else total + one
+    return total
+
+
+def parts_of(refs, shape):
+    refs = list(refs)
+    return [[refs.pop(0) for _ in block] for block in shape], refs
+
+
+def state_kernel(pairs, shape, place, *refs):
+    rows, refs = parts_of(refs, pairs)
+    blocks, (out, held) = parts_of(refs, shape)
+    z = place[0]
+    for i, row in enumerate(rows):
+        to = pl.ds(HDIM * i, HDIM)
+        if len(row) == 1:
+            held[to] = row[0][:HDIM]
+        else:
+            middle = (z == 1) | (z == 2)
+
+            @pl.when(middle)
+            def _():
+                held[to] = row[0][:HDIM]
+
+            @pl.when(jnp.logical_not(middle))
+            def _():
+                held[to] = row[1][:HDIM]
+
+    keys_first = z < 2
+    count = len(rows) // 2
+    totals = [0.0] * count
+    tokens = blocks[0][0].shape[1]
+    ones = (lax.broadcasted_iota(jnp.int32, (16, tokens), 0) == 0).astype(jnp.bfloat16)
+    for block in blocks:
+        lin = product(held, block)
+        for i in range(count):
+            one = lin[2 * i * HDIM : (2 * i + 1) * HDIM]
+            two = lin[(2 * i + 1) * HDIM : (2 * i + 2) * HDIM]
+            key = jnp.maximum(jnp.where(keys_first, one, two), 0.0).astype(jnp.bfloat16)
+            value = jnp.where(keys_first, two, one).astype(jnp.bfloat16)
+            totals[i] += lax.dot_general(
+                jnp.concatenate([value, ones], axis=0),
+                key,
+                (((1,), (1,)), ((), ())),
+                preferred_element_type=jnp.float32,
+            )
+    for i in range(count):
+        out[i] = totals[i]
+
+
+def states_of(place, rows, blocks):
+    depth = rows[0][0].shape[1]
+    return kernel_call(
+        functools.partial(
+            state_kernel, [(0,) * len(row) for row in rows], [(0,) * len(block) for block in blocks]
+        ),
+        like((len(rows) // 2, HDIM + 16, HDIM), jnp.float32),
+        place,
+        *[one for row in rows for one in row],
+        *[part for block in blocks for part in block],
+        scratch=[pltpu.VMEM((len(rows) * HDIM, depth), jnp.bfloat16)],
+    )
+
+
+def query_kernel(shape, place, mine, there, *refs):
+    blocks, (frame_a, frame_b) = parts_of(refs, shape)
+    y = place[1] // 4
+    half = HDIM // 2
+    tokens = blocks[0][0].shape[1]
+    for k, block in enumerate(blocks):
+        one, two = product(mine, block), product(there, block)
+        heads = []
+        for at in range(0, mine.shape[0], half):
+            head = jnp.concatenate([one[at : at + half], two[at : at + half]], axis=0)
+            heads.append(jnp.maximum(head, 0.0).astype(jnp.bfloat16))
+        feats = jnp.concatenate(heads, axis=0)
+        to = slice(tokens * (k % 2), tokens * (k % 2 + 1))
+
+        @pl.when(y == k // 2)
+        def _():
+            frame_a[:, to] = feats
+
+        @pl.when(y != k // 2)
+        def _():
+            frame_b[:, to] = feats
+
+
+def queries_of(place, mine, there, blocks):
+    tokens = blocks[0][0].shape[1]
+    frame = like((2 * mine.shape[0], 2 * tokens))
+    return kernel_call(
+        functools.partial(query_kernel, [(0,) * len(block) for block in blocks]),
+        (frame, frame),
+        place,
+        mine,
+        there,
+        *[part for block in blocks for part in block],
+    )
+
+
+def attend_kernel(place, mine, there, taps, frame_a, frame_b, before, later, *outs):
+    z, slot = place[0], place[1]
+    y, core = slot // 4, slot % 2
+    tokens = outs[0].shape[1]
+    half = HDIM // 2
+    row = lax.broadcasted_iota(jnp.int32, (HDIM, HDIM), 0)
+    column = lax.broadcasted_iota(jnp.int32, (HDIM, HDIM), 1)
+    turned = jnp.where(row < half, row + half, row - half)
+    order = (column == jnp.where(core == 0, row, turned)).astype(jnp.bfloat16)
+    for m in range(LAYERS):
+        own, other = mine[m // 2], there[m // 2]
+        state = jnp.where(core == m % 2, own, other)
+        high = state.astype(jnp.bfloat16)
+        low = (state - high.astype(jnp.float32)).astype(jnp.bfloat16)
+        both = jnp.concatenate([high, low], axis=0)
+        both = jnp.dot(both, order, preferred_element_type=jnp.float32).astype(jnp.bfloat16)
+        rows = pl.ds(HDIM * m, HDIM)
+
+        def attended(frame, there=None):
+            sums = jnp.dot(both, frame[rows], preferred_element_type=jnp.float32)
+            sums = sums[: HDIM + 16] + sums[HDIM + 16 :]
+            result = sums[:HDIM] * (1.0 / (sums[HDIM : HDIM + 1] + epsilon))
+            result = result.astype(jnp.bfloat16).astype(jnp.float32)
+            return result if there is None else jnp.where(there, result, 0.0)
+
+        tap = taps[rows]
+        att_before = attended(before, z > 0)
+        att_a, att_b = attended(frame_a), attended(frame_b)
+        att_later = attended(later, z < LAYERS - 1)
+        mixed_a = tap[:, 0:1] * att_before + tap[:, 1:2] * att_a + tap[:, 2:3] * att_b
+        mixed_b = tap[:, 0:1] * att_a + tap[:, 1:2] * att_b + tap[:, 2:3] * att_later
+        mixed = (jnp.where(y == 0, mixed_a, mixed_b), jnp.where(y == 0, mixed_b, mixed_a))
+        for i in range(4):
+            at = tokens * (i % 2)
+            outs[i][rows] = mixed[i // 2][:, at : at + tokens].astype(jnp.bfloat16)
+
+
+def attend(place, mine, there, taps, frames):
+    channels, tokens = frames[0].shape
+    outs = (like((channels, tokens // 2)),) * 4
+    return kernel_call(attend_kernel, outs, place, mine, there, taps, *frames)
+
+
+def finish_kernel(place, *refs):
+    parts, (out, held) = refs[:4], refs[4:]
+    chip = place[1] // 2
+    tokens = out.shape[0]
+    for k, part in enumerate(parts):
+        for m in range(LAYERS):
+            to = pl.multiple_of((4 * m + (chip ^ k)) * HDIM, 16)
+            held[pl.ds(to, HDIM)] = part[pl.ds(HDIM * m, HDIM)]
+    row = lax.broadcasted_iota(jnp.int32, (tokens, tokens), 0)
+    column = lax.broadcasted_iota(jnp.int32, (tokens, tokens), 1)
+    same = (row == column).astype(jnp.bfloat16)
+    step = 256
+    for at in range(0, out.shape[1], step):
+        out[:, at : at + step] = lax.dot_general(
+            same, held[at : at + step], (((1,), (1,)), ((), ())), preferred_element_type=jnp.float32
+        ).astype(jnp.bfloat16)
+
+
+def finish(place, parts):
+    channels, tokens = parts[0].shape
+    return kernel_call(
+        finish_kernel,
+        like((tokens, 4 * channels)),
+        place,
+        *parts,
+        scratch=[pltpu.VMEM((4 * channels, tokens), jnp.bfloat16)],
+    )
+
+
+LAYERS = 4
+PLANE = 8
+
+
+def send(value, place):
+    pairs = []
+    for z in range(LAYERS):
+        for slot in range(PLANE):
+            to = place(z, slot)
+            if to is not None:
+                pairs.append((z * PLANE + slot, to[0] * PLANE + to[1]))
+    return lax.ppermute(value, "frame", pairs)
+
+
+def swap(value, bits):
+    return send(value, lambda z, slot: (z, slot ^ bits))
+
+
+def between(value, steps):
+    return send(value, lambda z, slot: (steps[z], slot) if z in steps else None)
+
+
+def after(value, *others):
+    return lax.optimization_barrier((value,) + others)[0]
+
+
+def planes(tokens, w_query, w_keyval, taps):
+    me = lax.axis_index("frame")
+    z, slot = me // PLANE, me % PLANE
+    chip = slot // 2
+    place = jnp.stack([z, slot]).astype(jnp.int32)
+
+    cross = [{i: i ^ k for i in range(LAYERS)} for k in range(LAYERS)]
+    inner, outer = {1: 2, 2: 1}, {1: 0, 2: 3}
+
+    blocks = [None] * PLANE
+    weights = [None] * LAYERS
+    own, weights[0] = begin(tokens.T, w_query, w_keyval)
+    weights[2] = between(weights[0], cross[2])
+    beside, across = swap(own, 2), swap(own, 4)
+    weights[1] = between(weights[0], cross[1])
+    own_there = swap(own, 1)
+    split = (own.shape[0] // 256) * 128
+    low, high = swap(beside[:split], 4), swap(across[split:], 2)
+    beside_there = swap(beside, 1)
+    weights_inner = between(after(weights[0], weights[2]), inner)
+    weights_outer = between(weights[2], outer)
+    across_there = swap(across, 1)
+    low_there, high_there = swap(low, 1), swap(high, 1)
+    early = [(own,), (own_there,), (beside,), (beside_there,), (across,), (across_there,)]
+    late = [(low, high), (low_there, high_there)]
+
+    pair_0 = [(weights[0],), (weights[2],)]
+    pair_1 = [(weights[1],), (weights_inner, weights_outer)]
+    part_0 = states_of(place, pair_0, early) + states_of(place, pair_0, late)
+    part_1 = states_of(place, pair_1, early + late)
+
+    key_rows = w_keyval.shape[0]
+    middle = (z == 1) | (z == 2)
+    mine = jnp.zeros((LAYERS,) + w_query.shape, jnp.bfloat16)
+    last = jnp.where(middle, weights_inner[key_rows:], weights_outer[key_rows:])
+    for k, rows in enumerate([weights[i][key_rows:] for i in range(3)] + [last]):
+        mine = lax.dynamic_update_slice_in_dim(mine, rows[None], z ^ k, axis=0)
+    mine = mine.reshape(LAYERS * w_query.shape[0], -1)
+    there = swap(mine, 1)
+    frame_a, frame_b = queries_of(
+        place, mine, there, [(own,), (beside,), (across,), (low, high)]
+    )
+    frame_before = between(frame_b, {0: 1, 1: 2, 2: 3})
+    frame_after = between(frame_a, {1: 0, 2: 1, 3: 2})
+
+    odd = z % 2 == 1
+    part = jnp.concatenate([jnp.where(odd, part_1, part_0), jnp.where(odd, part_0, part_1)])
+    state = sum(
+        send(part, lambda z, slot, k=k: (z ^ k, 2 * (slot % 4) + slot // 4)) for k in range(LAYERS)
+    )
+    state_there = swap(state, 1)
+    by_head = taps.reshape(3, LAYERS, 4, HDIM)
+    tap = lax.dynamic_index_in_dim(by_head, chip, axis=2, keepdims=False).reshape(3, -1).T
+    pieces = attend(place, state, state_there, tap, (frame_a, frame_b, frame_before, frame_after))
+    got = [pieces[0]] + [swap(pieces[k], 2 * k) for k in range(1, 4)]
+    return finish(place, got)
+
+
+def local(tokens, w_query, w_keyval, taps):
+    fits = (
+        lax.axis_size("frame") == LAYERS * PLANE
+        and HEADS == 2 * PLANE
+        and w_keyval.shape[0] == HDIM
+        and 2 * w_query.shape[0] == HDIM
+        and PLANE * tokens.shape[0] == 2 * HEIGHT * WIDTH
+    )
+    return (planes if fits else gathered)(tokens, w_query, w_keyval, taps)
+
+
 def solution(mesh):
     placed = (P(("grp", "frame"), None), P("frame", None), P("frame", None), P())
     return jax.shard_map(

time: 410 us -> 134 us (0.33)
  waiting for transfers between devices: 316 us -> 56.4 us
  blocking collectives: 38.6 us -> 0 us
  starting transfers between devices: 4.73 us -> 35.7 us
  matrix products: 28.4 us -> 0 us
  Pallas kernels: 0 us -> 27.3 us
  between operations: 13.2 us -> 0.25 us
  local copies, waits for them, and re-layouts: 3.89 us -> 12.4 us
    all_gather x2 -> x0, waiting for transfers between devices: 189 us -> none  [the longest x1 109 us: local(): lax.all_gather(w_keyval, 'frame', axis=0, tiled=True)]
    psum x1 -> x0, waiting for transfers between devices: 88.9 us -> none  [local(): state, key_total = lax.psum((local_state, local_keys), 'frame')]
    psum x1 -> x0, blocking collectives: 38.6 us -> none  [local(): state, key_total = lax.psum((local_state, local_keys), 'frame')]
    ppermute x2 -> x24, starting transfers between devices: 4.66 us -> 35.7 us  [send(): return lax.ppermute(value, 'frame', pairs)]
    dot_general x5 -> x0, matrix products: 28.4 us -> none  [the longest x2 23.3 us: project_rows(): lax.dot_general(normed, weight_rows, (((1,), (1,)), ((), ())), preferred_...]
    pallas_call x0 -> x7, Pallas kernels: none -> 27.3 us  [kernel_call(): pl.pallas_call(body, out_shape=outs, in_specs=[SMEM] * scalars + [VMEM] *...]
    ppermute x2 -> x24, waiting for transfers between devices: 36.9 us -> 56.4 us  [send(): return lax.ppermute(value, 'frame', pairs)]
    unnamed x6 -> x23, local copies, waits for them, and re-layouts: 0.01 us -> 6.05 us
  transfers between devices with their start and end apart: 5 -> 24, of which waited for: 4 -> 8; matrix products, arithmetic and copies ran while one was open for 2% -> 6% of each run, Pallas kernels for 0% -> 16%
where the time goes in v2:
time: 134 us; the launch traced here: 133 us
  waiting for transfers between devices  56.4 us (42%)
  starting transfers between devices  35.7 us (27%)
  Pallas kernels  27.3 us (20%)
  local copies, waits for them, and re-layouts  12.4 us (9%)
    ppermute x24, waiting for transfers between devices, send(): return lax.ppermute(value, 'frame', pairs)  56.4 us
    ppermute x24, starting transfers between devices, send(): return lax.ppermute(value, 'frame', pairs)  35.7 us
    pallas_call x7, Pallas kernels, kernel_call(): pl.pallas_call(body, out_shape=outs, in_specs=[SMEM] * scalars + [VMEM] *...  27.3 us
    unnamed x23, local copies, waits for them, and re-layouts  6.05 us
    dynamic_update_slice x3, local copies, waits for them, and re-layouts, planes(): mine = lax.dynamic_update_slice_in_dim(mine, rows[None], z ^ k, axis=0)  4.05 us
  transfers between devices with their start and end apart: 24, of which 8 were waited for; matrix products, arithmetic and copies ran while one was open for 6% of the time, Pallas kernels for 16%

profile of v2, /device:TPU:0, one launch (start us, length us, event | category | flops | bytes accessed | tf_op | source)
XLA Modules:
  0.0 133.0 jit_solution(1926639074506915862)
XLA Ops:
  0.0 1.3 copy-done.7
  1.3 1.0 copy-done.8
  2.3 0.9 copy-done.9
  3.2 1.2 shard_map.46
  4.4 4.0 %collective-permute-start.1 = (bf16[168,2240]{1,0:T(8,128)(2,1)}, bf16[168,2240]{1,0:T(8,128)(2,1)}, u32[]{:S(2)}, u32[]{:S(2)}) collective-permute-start(bf16[168,2240]{1,0:T(8,128)(2,1)} %get-tuple-element.15.refs_0_), channel_id=1, source_target_pairs={{0,16},{1,17},{2,18},{3,19},{4,20},{5,21},{6,22},{7,23},{8,24},{9,... | collective-permute-start | bytes 2257928 | tf_op jit(solution)/shard_map/ppermute | solution.py:300
  8.5 1.6 %collective-permute-start = (bf16[168,2240]{1,0:T(8,128)(2,1)}, bf16[168,2240]{1,0:T(8,128)(2,1)S(1)}, u32[]{:S(2)}, u32[]{:S(2)}) collective-permute-start(bf16[168,2240]{1,0:T(8,128)(2,1)} %get-tuple-element.15.refs_0_), channel_id=1, source_target_pairs={{0,8},{1,9},{2,10},{3,11},{4,12},{5,13},{6,14},{7,15},{8,0},{9,1},... | collective-permute-start | bytes 2257928 | tf_op jit(solution)/shard_map/ppermute | solution.py:300
  10.1 1.5 %collective-permute-start.5 = (bf16[2240,256]{1,0:T(8,128)(2,1)S(1)}, bf16[2240,256]{1,0:T(8,128)(2,1)S(1)}, u32[]{:S(2)}, u32[]{:S(2)}) collective-permute-start(bf16[2240,256]{1,0:T(8,128)(2,1)S(1)} %get-tuple-element.16.refs_3_.refs_2_.refs_0_), channel_id=1, source_target_pairs={{0,2},{1,3},{2,0},{3,1},{4,6},{5,7},{6,4},{7,5},{8,10},{9,11},{10,... | collective-permute-start | bytes 3440648 | tf_op jit(solution)/shard_map/ppermute | solution.py:300
  11.5 1.5 %collective-permute-start.7 = (bf16[2240,256]{1,0:T(8,128)(2,1)S(1)}, bf16[2240,256]{1,0:T(8,128)(2,1)}, u32[]{:S(2)}, u32[]{:S(2)}) collective-permute-start(bf16[2240,256]{1,0:T(8,128)(2,1)S(1)} %get-tuple-element.16.refs_3_.refs_2_.refs_0_), channel_id=1, source_target_pairs={{0,4},{1,5},{2,6},{3,7},{4,0},{5,1},{6,2},{7,3},{8,12},{9,13},{10,... | collective-permute-start | bytes 3440648 | tf_op jit(solution)/shard_map/ppermute | solution.py:300
  13.1 1.1 broadcast_in_dim.15
  14.1 1.7 %bitcast_dynamic-update-slice_fusion = bf16[4,56,2240]{2,1,0:T(8,128)(2,1)} fusion(bf16[4,56,2240]{2,1,0:T(8,128)(2,1)} %broadcast_in_dim.15, s32[]{:T(128)S(6)} %select_n.62, bf16[168,2240]{1,0:T(8,128)(2,1)} %get-tuple-element.15.refs_0_), kind=kLoop, calls=%fused_computation.7 | loop fusion | bytes 516100 | tf_op jit(solution)/shard_map/dynamic_update_slice | solution.py:351
  15.8 27.0 %collective-permute-done.1.refs_1_ = bf16[168,2240]{1,0:T(8,128)(2,1)} collective-permute-done((bf16[168,2240]{1,0:T(8,128)(2,1)}, bf16[168,2240]{1,0:T(8,128)(2,1)}, u32[]{:S(2)}, u32[]{:S(2)}) %collective-permute-start.1) | collective-permute-done | bytes 752672 | tf_op jit(solution)/shard_map/ppermute | solution.py:300
  42.8 0.7 collective-permute-start.2
  43.5 1.3 collective-permute-start.3
  44.8 0.7 fusion.3
  45.5 0.9 copy-done.1
  46.4 1.1 slice.29
  47.5 1.6 %collective-permute-start.10 = (bf16[1216,256]{1,0:T(8,128)(2,1)S(1)}, bf16[1216,256]{1,0:T(8,128)(2,1)S(1)}, u32[]{:S(2)}, u32[]{:S(2)}) collective-permute-start(bf16[1216,256]{1,0:T(8,128)(2,1)S(1)} %slice.29), channel_id=1, source_target_pairs={{0,2},{1,3},{2,0},{3,1},{4,6},{5,7},{6,4},{7,5},{8,10},{9,11},{10,... | collective-permute-start | bytes 1867784 | tf_op jit(solution)/shard_map/ppermute | solution.py:300
  49.1 1.7 %fusion.2 = bf16[4,56,2240]{2,1,0:T(8,128)(2,1)} fusion(bf16[4,56,2240]{2,1,0:T(8,128)(2,1)} %fusion.3, s32[]{:T(128)S(6)} %select_n.64, bf16[168,2240]{1,0:T(8,128)(2,1)} %collective-permute-done.1.refs_1_), kind=kLoop, calls=%fused_computation.4 | loop fusion | bytes 516100 | tf_op jit(solution)/shard_map/dynamic_update_slice | solution.py:351
  50.8 1.6 %collective-permute-start.9 = (bf16[1024,256]{1,0:T(8,128)(2,1)S(1)}, bf16[1024,256]{1,0:T(8,128)(2,1)S(1)}, u32[]{:S(2)}, u32[]{:S(2)}) collective-permute-start(bf16[1024,256]{1,0:T(8,128)(2,1)S(1)} %slice.28), channel_id=1, source_target_pairs={{0,4},{1,5},{2,6},{3,7},{4,0},{5,1},{6,2},{7,3},{8,12},{9,13},{10,... | collective-permute-start | bytes 1572872 | tf_op jit(solution)/shard_map/ppermute | solution.py:300
  52.4 11.8 %collective-permute-done.3.refs_2_ = bf16[168,2240]{1,0:T(8,128)(2,1)S(1)} collective-permute-done((bf16[168,2240]{1,0:T(8,128)(2,1)}, bf16[168,2240]{1,0:T(8,128)(2,1)S(1)}, u32[]{:S(2)}, u32[]{:S(2)}) %collective-permute-start.3) | collective-permute-done | bytes 752672 | tf_op jit(solution)/shard_map/ppermute | solution.py:300
  64.3 0.5 collective-permute-start.12
  64.8 0.8 fusion.1
  65.6 0.9 copy-done.3
  66.5 0.9 copy-done.5
  67.3 0.5 collective-permute-start.11
  67.9 0.1 pad_add_fusion.place
  67.9 0.3 collective-permute-done.8.refs_8_.refs_7_
  68.3 5.8 %shard_map.48 = f32[1,128,112]{2,1,0:T(8,128)S(1)} custom-call(s32[2]{0:T(128)S(1)} %pad_add_fusion.place, bf16[168,2240]{1,0:T(8,128)(2,1)} %get-tuple-element.15.refs_0_, bf16[168,2240]{1,0:T(8,128)(2,1)} %collective-permute-done.1.refs_1_, bf16[2240,256]{1,0:T(8,128)(2,1)S(1)} %get-tuple-element.16.refs_3_.refs_2_.refs_0_, ...), custom_call_target="tpu_custom_call" | custom-call | tf_op jit(solution)/shard_map/pallas_call | solution.py:76
  74.2 6.6 %shard_map.47 = f32[1,128,112]{2,1,0:T(8,128)S(1)} custom-call(s32[2]{0:T(128)S(1)} %pad_add_fusion.place, bf16[168,2240]{1,0:T(8,128)(2,1)S(1)} %copy-done.2, bf16[168,2240]{1,0:T(8,128)(2,1)S(1)} %copy-done.4, bf16[168,2240]{1,0:T(8,128)(2,1)S(1)} %copy-done.6, bf16[2240,256]{1,0:T(8,128)(2,1)S(1)} %get-tuple-element.16.refs_3_.refs_2_.refs_0_, ...), custom_call_target="tpu_custom_call" | custom-call | tf_op jit(solution)/shard_map/pallas_call | solution.py:76
  80.8 2.6 %shard_map.49 = f32[1,128,112]{2,1,0:T(8,128)S(1)} custom-call(s32[2]{0:T(128)S(1)} %pad_add_fusion.place, bf16[168,2240]{1,0:T(8,128)(2,1)} %get-tuple-element.15.refs_0_, bf16[168,2240]{1,0:T(8,128)(2,1)} %collective-permute-done.1.refs_1_, bf16[1024,256]{1,0:T(8,128)(2,1)S(1)} %collective-permute-done.9.refs_9_.refs_2_.refs_3_, ...), custom_call_target="tpu_custom_call" | custom-call | tf_op jit(solution)/shard_map/pallas_call | solution.py:76
  83.5 4.0 %collective-permute-start.16 = (f32[2,128,112]{2,1,0:T(8,128)S(1)}, f32[2,128,112]{2,1,0:T(8,128)S(1)}, u32[]{:S(2)}, u32[]{:S(2)}) collective-permute-start(f32[2,128,112]{2,1,0:T(8,128)S(1)} %pad_maximum_fusion), channel_id=1, source_target_pairs={{0,24},{1,26},{2,28},{3,30},{4,25},{5,27},{6,29},{7,31},{8,16},{9,... | collective-permute-start | bytes 344072 | tf_op jit(solution)/shard_map/ppermute | solution.py:300
  87.6 0.7 collective-permute-start.13
  88.2 0.7 collective-permute-start.14
  88.9 5.9 %shard_map.50 = (bf16[448,512]{1,0:T(8,128)(2,1)S(1)}, bf16[448,512]{1,0:T(8,128)(2,1)}) custom-call(s32[2]{0:T(128)S(1)} %pad_add_fusion.place, bf16[224,2240]{1,0:T(8,128)(2,1)} %bitcast.9.mine, bf16[224,2240]{1,0:T(8,128)(2,1)} %collective-permute-done.18.there, bf16[2240,256]{1,0:T(8,128)(2,1)S(1)} %get-tuple-element.16.refs_3_.refs_2_.refs_0_, ...), custom_call_target="tpu_custom_call" | custom-call | tf_op jit(solution)/shard_map/pallas_call | solution.py:76
  94.8 3.3 %collective-permute-start.19 = (bf16[448,512]{1,0:T(8,128)(2,1)}, bf16[448,512]{1,0:T(8,128)(2,1)S(1)}, u32[]{:S(2)}, u32[]{:S(2)}) collective-permute-start(bf16[448,512]{1,0:T(8,128)(2,1)} %get-tuple-element.18.frame_b), channel_id=1, source_target_pairs={{0,8},{1,9},{2,10},{3,11},{4,12},{5,13},{6,14},{7,15},{8,16},{9,17... | collective-permute-start | bytes 1376264 | tf_op jit(solution)/shard_map/ppermute | solution.py:300
  98.1 1.5 %collective-permute-start.20 = (bf16[448,512]{1,0:T(8,128)(2,1)S(1)}, bf16[448,512]{1,0:T(8,128)(2,1)S(1)}, u32[]{:S(2)}, u32[]{:S(2)}) collective-permute-start(bf16[448,512]{1,0:T(8,128)(2,1)S(1)} %get-tuple-element.17.frame_a), channel_id=1, source_target_pairs={{8,0},{9,1},{10,2},{11,3},{12,4},{13,5},{14,6},{15,7},{16,8},{17,9... | collective-permute-start | bytes 1376264 | tf_op jit(solution)/shard_map/ppermute | solution.py:300
  99.7 3.3 %collective-permute-start.17 = (f32[2,128,112]{2,1,0:T(8,128)S(1)}, f32[2,128,112]{2,1,0:T(8,128)S(1)}, u32[]{:S(2)}, u32[]{:S(2)}) collective-permute-start(f32[2,128,112]{2,1,0:T(8,128)S(1)} %add_add_fusion.mine), channel_id=1, source_target_pairs={{0,1},{1,0},{2,3},{3,2},{4,5},{5,4},{6,7},{7,6},{8,9},{9,8},{10,11... | collective-permute-start | bytes 344072 | tf_op jit(solution)/shard_map/ppermute | solution.py:300
  103.0 0.1 reshape.10
  103.1 0.1 copy.6
  103.2 0.7 collective-permute-done.17.there
  104.0 2.8 %collective-permute-done.19.before = bf16[448,512]{1,0:T(8,128)(2,1)S(1)} collective-permute-done((bf16[448,512]{1,0:T(8,128)(2,1)}, bf16[448,512]{1,0:T(8,128)(2,1)S(1)}, u32[]{:S(2)}, u32[]{:S(2)}) %collective-permute-start.19) | collective-permute-done | bytes 458784 | tf_op jit(solution)/shard_map/ppermute | solution.py:300
  106.7 4.4 %collective-permute-done.20.later = bf16[448,512]{1,0:T(8,128)(2,1)S(1)} collective-permute-done((bf16[448,512]{1,0:T(8,128)(2,1)S(1)}, bf16[448,512]{1,0:T(8,128)(2,1)S(1)}, u32[]{:S(2)}, u32[]{:S(2)}) %collective-permute-start.20) | collective-permute-done | bytes 458784 | tf_op jit(solution)/shard_map/ppermute | solution.py:300
  111.1 3.1 %shard_map.51 = (bf16[448,256]{1,0:T(8,128)(2,1)S(1)}, bf16[448,256]{1,0:T(8,128)(2,1)S(1)}, bf16[448,256]{1,0:T(8,128)(2,1)S(1)}, bf16[448,256]{1,0:T(8,128)(2,1)S(1)}) custom-call(s32[2]{0:T(128)S(1)} %pad_add_fusion.place, f32[2,128,112]{2,1,0:T(8,128)S(1)} %add_add_fusion.mine, f32[2,128,112]{2,1,0:T(8,128)S(1)} %collective-permute-done.17.there, ...), custom_call_target="tpu_custom_call" | custom-call | tf_op jit(solution)/shard_map/pallas_call | solution.py:76
  114.2 5.9 %collective-permute-start.21 = (bf16[448,256]{1,0:T(8,128)(2,1)S(1)}, bf16[448,256]{1,0:T(8,128)(2,1)S(1)}, u32[]{:S(2)}, u32[]{:S(2)}) collective-permute-start(bf16[448,256]{1,0:T(8,128)(2,1)S(1)} %get-tuple-element.20), channel_id=1, source_target_pairs={{0,2},{1,3},{2,0},{3,1},{4,6},{5,7},{6,4},{7,5},{8,10},{9,11},{10,... | collective-permute-start | bytes 688136 | tf_op jit(solution)/shard_map/ppermute | solution.py:300
  120.2 1.5 %collective-permute-start.23 = (bf16[448,256]{1,0:T(8,128)(2,1)S(1)}, bf16[448,256]{1,0:T(8,128)(2,1)S(1)}, u32[]{:S(2)}, u32[]{:S(2)}) collective-permute-start(bf16[448,256]{1,0:T(8,128)(2,1)S(1)} %get-tuple-element.22), channel_id=1, source_target_pairs={{0,6},{1,7},{2,4},{3,5},{4,2},{5,3},{6,0},{7,1},{8,14},{9,15},{10,... | collective-permute-start | bytes 688136 | tf_op jit(solution)/shard_map/ppermute | solution.py:300
  121.7 5.0 %collective-permute-done.21.refs_1_ = bf16[448,256]{1,0:T(8,128)(2,1)S(1)} collective-permute-done((bf16[448,256]{1,0:T(8,128)(2,1)S(1)}, bf16[448,256]{1,0:T(8,128)(2,1)S(1)}, u32[]{:S(2)}, u32[]{:S(2)}) %collective-permute-start.21) | collective-permute-done | bytes 229408 | tf_op jit(solution)/shard_map/ppermute | solution.py:300
  126.6 4.4 %collective-permute-done.22.refs_2_ = bf16[448,256]{1,0:T(8,128)(2,1)S(1)} collective-permute-done((bf16[448,256]{1,0:T(8,128)(2,1)S(1)}, bf16[448,256]{1,0:T(8,128)(2,1)S(1)}, u32[]{:S(2)}, u32[]{:S(2)}) %collective-permute-start.22) | collective-permute-done | bytes 229408 | tf_op jit(solution)/shard_map/ppermute | solution.py:300
  131.0 2.0 %shard_map.52 = bf16[256,1792]{1,0:T(8,128)(2,1)} custom-call(s32[2]{0:T(128)S(1)} %pad_add_fusion.place, bf16[448,256]{1,0:T(8,128)(2,1)S(1)} %get-tuple-element.19.refs_0_, bf16[448,256]{1,0:T(8,128)(2,1)S(1)} %collective-permute-done.21.refs_1_, bf16[448,256]{1,0:T(8,128)(2,1)S(1)} %collective-permute-done.22.refs_2_, ...), custom_call_target="tpu_custom_call" | custom-call | tf_op jit(solution)/shard_map/pallas_call | solution.py:76
  (43 shorter events, 0.3 us)
Async XLA Ops:
  0.0 1.3 copy-start.7
  1.3 1.0 copy-start.8
  2.3 0.9 copy-start.9
  4.4 38.3 %collective-permute-start.1 = (bf16[168,2240]{1,0:T(8,128)(2,1)}, bf16[168,2240]{1,0:T(8,128)(2,1)}, u32[]{:S(2)}, u32[]{:S(2)}) collective-permute-start(bf16[168,2240]{1,0:T(8,128)(2,1)} %get-tuple-element.15.refs_0_), channel_id=1, source_target_pairs={{0,16},{1,17},{2,18},{3,19},{4,20},{5,21},{6,22},{7,23},{8,24},{9,... | collective-permute-start | bytes 2257928 | tf_op jit(solution)/shard_map/ppermute | solution.py:300
  8.5 35.0 %collective-permute-start = (bf16[168,2240]{1,0:T(8,128)(2,1)}, bf16[168,2240]{1,0:T(8,128)(2,1)S(1)}, u32[]{:S(2)}, u32[]{:S(2)}) collective-permute-start(bf16[168,2240]{1,0:T(8,128)(2,1)} %get-tuple-element.15.refs_0_), channel_id=1, source_target_pairs={{0,8},{1,9},{2,10},{3,11},{4,12},{5,13},{6,14},{7,15},{8,0},{9,1},... | collective-permute-start | bytes 2257928 | tf_op jit(solution)/shard_map/ppermute | solution.py:300
  10.0 57.3 %collective-permute-start.4 = (bf16[2240,256]{1,0:T(8,128)(2,1)S(1)}, bf16[2240,256]{1,0:T(8,128)(2,1)}, u32[]{:S(2)}, u32[]{:S(2)}) collective-permute-start(bf16[2240,256]{1,0:T(8,128)(2,1)S(1)} %get-tuple-element.16.refs_3_.refs_2_.refs_0_), channel_id=1, source_target_pairs={{0,1},{1,0},{2,3},{3,2},{4,5},{5,4},{6,7},{7,6},{8,9},{9,8},{10,11... | collective-permute-start | bytes 3440648 | tf_op jit(solution)/shard_map/ppermute | solution.py:300
  10.1 40.7 %collective-permute-start.5 = (bf16[2240,256]{1,0:T(8,128)(2,1)S(1)}, bf16[2240,256]{1,0:T(8,128)(2,1)S(1)}, u32[]{:S(2)}, u32[]{:S(2)}) collective-permute-start(bf16[2240,256]{1,0:T(8,128)(2,1)S(1)} %get-tuple-element.16.refs_3_.refs_2_.refs_0_), channel_id=1, source_target_pairs={{0,2},{1,3},{2,0},{3,1},{4,6},{5,7},{6,4},{7,5},{8,10},{9,11},{10,... | collective-permute-start | bytes 3440648 | tf_op jit(solution)/shard_map/ppermute | solution.py:300
  11.5 34.8 %collective-permute-start.7 = (bf16[2240,256]{1,0:T(8,128)(2,1)S(1)}, bf16[2240,256]{1,0:T(8,128)(2,1)}, u32[]{:S(2)}, u32[]{:S(2)}) collective-permute-start(bf16[2240,256]{1,0:T(8,128)(2,1)S(1)} %get-tuple-element.16.refs_3_.refs_2_.refs_0_), channel_id=1, source_target_pairs={{0,4},{1,5},{2,6},{3,7},{4,0},{5,1},{6,2},{7,3},{8,12},{9,13},{10,... | collective-permute-start | bytes 3440648 | tf_op jit(solution)/shard_map/ppermute | solution.py:300
  42.8 9.7 %collective-permute-start.2 = (bf16[168,2240]{1,0:T(8,128)(2,1)}, bf16[168,2240]{1,0:T(8,128)(2,1)S(1)}, u32[]{:S(2)}, u32[]{:S(2)}) collective-permute-start(bf16[168,2240]{1,0:T(8,128)(2,1)} %get-tuple-element.15.refs_0_), channel_id=1, source_target_pairs={{8,16},{9,17},{10,18},{11,19},{12,20},{13,21},{14,22},{15,23},{16,... | collective-permute-start | bytes 2257928 | tf_op jit(solution)/shard_map/ppermute | solution.py:300
  43.5 20.8 %collective-permute-start.3 = (bf16[168,2240]{1,0:T(8,128)(2,1)}, bf16[168,2240]{1,0:T(8,128)(2,1)S(1)}, u32[]{:S(2)}, u32[]{:S(2)}) collective-permute-start(bf16[168,2240]{1,0:T(8,128)(2,1)} %collective-permute-done.1.refs_1_), channel_id=1, source_target_pairs={{8,0},{9,1},{10,2},{11,3},{12,4},{13,5},{14,6},{15,7},{16,24},{17,... | collective-permute-start | bytes 2257928 | tf_op jit(solution)/shard_map/ppermute | solution.py:300
  45.5 0.9 copy-start.1
  47.5 16.7 %collective-permute-start.10 = (bf16[1216,256]{1,0:T(8,128)(2,1)S(1)}, bf16[1216,256]{1,0:T(8,128)(2,1)S(1)}, u32[]{:S(2)}, u32[]{:S(2)}) collective-permute-start(bf16[1216,256]{1,0:T(8,128)(2,1)S(1)} %slice.29), channel_id=1, source_target_pairs={{0,2},{1,3},{2,0},{3,1},{4,6},{5,7},{6,4},{7,5},{8,10},{9,11},{10,... | collective-permute-start | bytes 1867784 | tf_op jit(solution)/shard_map/ppermute | solution.py:300
  50.8 23.3 %copy-start = (bf16[2240,256]{1,0:T(8,128)(2,1)}, bf16[2240,256]{1,0:T(8,128)(2,1)S(1)}, u32[]{:S(2)}) copy-start(bf16[2240,256]{1,0:T(8,128)(2,1)S(1)} %collective-permute-done.5.refs_5_.refs_4_.refs_1_) | copy-start | bytes 3440644
  50.8 16.5 %collective-permute-start.9 = (bf16[1024,256]{1,0:T(8,128)(2,1)S(1)}, bf16[1024,256]{1,0:T(8,128)(2,1)S(1)}, u32[]{:S(2)}, u32[]{:S(2)}) collective-permute-start(bf16[1024,256]{1,0:T(8,128)(2,1)S(1)} %slice.28), channel_id=1, source_target_pairs={{0,4},{1,5},{2,6},{3,7},{4,0},{5,1},{6,2},{7,3},{8,12},{9,13},{10,... | collective-permute-start | bytes 1572872 | tf_op jit(solution)/shard_map/ppermute | solution.py:300
  52.4 15.5 %collective-permute-start.6 = (bf16[2240,256]{1,0:T(8,128)(2,1)S(1)}, bf16[2240,256]{1,0:T(8,128)(2,1)}, u32[]{:S(2)}, u32[]{:S(2)}) collective-permute-start(bf16[2240,256]{1,0:T(8,128)(2,1)S(1)} %collective-permute-done.5.refs_5_.refs_4_.refs_1_), channel_id=1, source_target_pairs={{0,1},{1,0},{2,3},{3,2},{4,5},{5,4},{6,7},{7,6},{8,9},{9,8},{10,11... | collective-permute-start | bytes 3440648 | tf_op jit(solution)/shard_map/ppermute | solution.py:300
  64.2 4.0 %collective-permute-start.8 = (bf16[2240,256]{1,0:T(8,128)(2,1)}, bf16[2240,256]{1,0:T(8,128)(2,1)}, u32[]{:S(2)}, u32[]{:S(2)}) collective-permute-start(bf16[2240,256]{1,0:T(8,128)(2,1)} %collective-permute-done.7.refs_7_.refs_6_.refs_2_), channel_id=1, source_target_pairs={{0,1},{1,0},{2,3},{3,2},{4,5},{5,4},{6,7},{7,6},{8,9},{9,8},{10,11... | collective-permute-start | bytes 3440648 | tf_op jit(solution)/shard_map/ppermute | solution.py:300
  64.3 9.9 %collective-permute-start.12 = (bf16[1216,256]{1,0:T(8,128)(2,1)S(1)}, bf16[1216,256]{1,0:T(8,128)(2,1)}, u32[]{:S(2)}, u32[]{:S(2)}) collective-permute-start(bf16[1216,256]{1,0:T(8,128)(2,1)S(1)} %collective-permute-done.10.refs_10_.refs_3_.refs_4_), channel_id=1, source_target_pairs={{0,1},{1,0},{2,3},{3,2},{4,5},{5,4},{6,7},{7,6},{8,9},{9,8},{10,11... | collective-permute-start | bytes 1867784 | tf_op jit(solution)/shard_map/ppermute | solution.py:300
  65.6 0.9 copy-start.3
  66.5 0.9 copy-start.5
  67.3 21.6 %collective-permute-start.18 = (bf16[224,2240]{1,0:T(8,128)(2,1)}, bf16[224,2240]{1,0:T(8,128)(2,1)}, u32[]{:S(2)}, u32[]{:S(2)}) collective-permute-start(bf16[224,2240]{1,0:T(8,128)(2,1)} %bitcast.9.mine), channel_id=1, source_target_pairs={{0,1},{1,0},{2,3},{3,2},{4,5},{5,4},{6,7},{7,6},{8,9},{9,8},{10,11... | collective-permute-start | bytes 3010568 | tf_op jit(solution)/shard_map/ppermute | solution.py:300
  67.3 6.8 %collective-permute-start.11 = (bf16[1024,256]{1,0:T(8,128)(2,1)S(1)}, bf16[1024,256]{1,0:T(8,128)(2,1)}, u32[]{:S(2)}, u32[]{:S(2)}) collective-permute-start(bf16[1024,256]{1,0:T(8,128)(2,1)S(1)} %collective-permute-done.9.refs_9_.refs_2_.refs_3_), channel_id=1, source_target_pairs={{0,1},{1,0},{2,3},{3,2},{4,5},{5,4},{6,7},{7,6},{8,9},{9,8},{10,11... | collective-permute-start | bytes 1572872 | tf_op jit(solution)/shard_map/ppermute | solution.py:300
  67.9 6.2 %copy-start.2 = (bf16[168,2240]{1,0:T(8,128)(2,1)S(1)}, bf16[168,2240]{1,0:T(8,128)(2,1)}, u32[]{:S(2)}) copy-start(bf16[168,2240]{1,0:T(8,128)(2,1)} %copy-done.1) | copy-start | bytes 2257924
  67.9 6.2 %copy-start.4 = (bf16[168,2240]{1,0:T(8,128)(2,1)S(1)}, bf16[168,2240]{1,0:T(8,128)(2,1)}, u32[]{:S(2)}) copy-start(bf16[168,2240]{1,0:T(8,128)(2,1)} %copy-done.3) | copy-start | bytes 2257924
  67.9 6.2 %copy-start.6 = (bf16[168,2240]{1,0:T(8,128)(2,1)S(1)}, bf16[168,2240]{1,0:T(8,128)(2,1)}, u32[]{:S(2)}) copy-start(bf16[168,2240]{1,0:T(8,128)(2,1)} %copy-done.5) | copy-start | bytes 2257924
  83.5 19.5 %copy-start.10 = (f32[3,1792]{1,0:T(4,128)S(1)}, f32[3,1792]{1,0:T(4,128)}, u32[]{:S(2)}) copy-start(f32[3,1792]{1,0:T(4,128)} %param.7) | copy-start | bytes 64516
  83.5 14.6 %collective-permute-start.16 = (f32[2,128,112]{2,1,0:T(8,128)S(1)}, f32[2,128,112]{2,1,0:T(8,128)S(1)}, u32[]{:S(2)}, u32[]{:S(2)}) collective-permute-start(f32[2,128,112]{2,1,0:T(8,128)S(1)} %pad_maximum_fusion), channel_id=1, source_target_pairs={{0,24},{1,26},{2,28},{3,30},{4,25},{5,27},{6,29},{7,31},{8,16},{9,... | collective-permute-start | bytes 344072 | tf_op jit(solution)/shard_map/ppermute | solution.py:300
  87.6 12.1 %collective-permute-start.15 = (f32[2,128,112]{2,1,0:T(8,128)S(1)}, f32[2,128,112]{2,1,0:T(8,128)S(1)}, u32[]{:S(2)}, u32[]{:S(2)}) collective-permute-start(f32[2,128,112]{2,1,0:T(8,128)S(1)} %pad_maximum_fusion), channel_id=1, source_target_pairs={{0,16},{1,18},{2,20},{3,22},{4,17},{5,19},{6,21},{7,23},{8,24},{9,... | collective-permute-start | bytes 344072 | tf_op jit(solution)/shard_map/ppermute | solution.py:300
  87.6 12.1 %collective-permute-start.13 = (f32[2,128,112]{2,1,0:T(8,128)S(1)}, f32[2,128,112]{2,1,0:T(8,128)S(1)}, u32[]{:S(2)}, u32[]{:S(2)}) collective-permute-start(f32[2,128,112]{2,1,0:T(8,128)S(1)} %pad_maximum_fusion), channel_id=1, source_target_pairs={{0,0},{1,2},{2,4},{3,6},{4,1},{5,3},{6,5},{7,7},{8,8},{9,10},{10,1... | collective-permute-start | bytes 344072 | tf_op jit(solution)/shard_map/ppermute | solution.py:300
  88.2 11.4 %collective-permute-start.14 = (f32[2,128,112]{2,1,0:T(8,128)S(1)}, f32[2,128,112]{2,1,0:T(8,128)S(1)}, u32[]{:S(2)}, u32[]{:S(2)}) collective-permute-start(f32[2,128,112]{2,1,0:T(8,128)S(1)} %pad_maximum_fusion), channel_id=1, source_target_pairs={{0,8},{1,10},{2,12},{3,14},{4,9},{5,11},{6,13},{7,15},{8,0},{9,2},... | collective-permute-start | bytes 344072 | tf_op jit(solution)/shard_map/ppermute | solution.py:300
  94.8 11.9 %collective-permute-start.19 = (bf16[448,512]{1,0:T(8,128)(2,1)}, bf16[448,512]{1,0:T(8,128)(2,1)S(1)}, u32[]{:S(2)}, u32[]{:S(2)}) collective-permute-start(bf16[448,512]{1,0:T(8,128)(2,1)} %get-tuple-element.18.frame_b), channel_id=1, source_target_pairs={{0,8},{1,9},{2,10},{3,11},{4,12},{5,13},{6,14},{7,15},{8,16},{9,17... | collective-permute-start | bytes 1376264 | tf_op jit(solution)/shard_map/ppermute | solution.py:300
  98.1 13.0 %collective-permute-start.20 = (bf16[448,512]{1,0:T(8,128)(2,1)S(1)}, bf16[448,512]{1,0:T(8,128)(2,1)S(1)}, u32[]{:S(2)}, u32[]{:S(2)}) collective-permute-start(bf16[448,512]{1,0:T(8,128)(2,1)S(1)} %get-tuple-element.17.frame_a), channel_id=1, source_target_pairs={{8,0},{9,1},{10,2},{11,3},{12,4},{13,5},{14,6},{15,7},{16,8},{17,9... | collective-permute-start | bytes 1376264 | tf_op jit(solution)/shard_map/ppermute | solution.py:300
  99.7 4.3 %collective-permute-start.17 = (f32[2,128,112]{2,1,0:T(8,128)S(1)}, f32[2,128,112]{2,1,0:T(8,128)S(1)}, u32[]{:S(2)}, u32[]{:S(2)}) collective-permute-start(f32[2,128,112]{2,1,0:T(8,128)S(1)} %add_add_fusion.mine), channel_id=1, source_target_pairs={{0,1},{1,0},{2,3},{3,2},{4,5},{5,4},{6,7},{7,6},{8,9},{9,8},{10,11... | collective-permute-start | bytes 344072 | tf_op jit(solution)/shard_map/ppermute | solution.py:300
  114.2 12.4 %collective-permute-start.21 = (bf16[448,256]{1,0:T(8,128)(2,1)S(1)}, bf16[448,256]{1,0:T(8,128)(2,1)S(1)}, u32[]{:S(2)}, u32[]{:S(2)}) collective-permute-start(bf16[448,256]{1,0:T(8,128)(2,1)S(1)} %get-tuple-element.20), channel_id=1, source_target_pairs={{0,2},{1,3},{2,0},{3,1},{4,6},{5,7},{6,4},{7,5},{8,10},{9,11},{10,... | collective-permute-start | bytes 688136 | tf_op jit(solution)/shard_map/ppermute | solution.py:300
  120.1 10.9 %collective-permute-start.22 = (bf16[448,256]{1,0:T(8,128)(2,1)S(1)}, bf16[448,256]{1,0:T(8,128)(2,1)S(1)}, u32[]{:S(2)}, u32[]{:S(2)}) collective-permute-start(bf16[448,256]{1,0:T(8,128)(2,1)S(1)} %get-tuple-element.21), channel_id=1, source_target_pairs={{0,4},{1,5},{2,6},{3,7},{4,0},{5,1},{6,2},{7,3},{8,12},{9,13},{10,... | collective-permute-start | bytes 688136 | tf_op jit(solution)/shard_map/ppermute | solution.py:300
  120.2 10.8 %collective-permute-start.23 = (bf16[448,256]{1,0:T(8,128)(2,1)S(1)}, bf16[448,256]{1,0:T(8,128)(2,1)S(1)}, u32[]{:S(2)}, u32[]{:S(2)}) collective-permute-start(bf16[448,256]{1,0:T(8,128)(2,1)S(1)} %get-tuple-element.22), channel_id=1, source_target_pairs={{0,6},{1,7},{2,4},{3,5},{4,2},{5,3},{6,0},{7,1},{8,14},{9,15},{10,... | collective-permute-start | bytes 688136 | tf_op jit(solution)/shard_map/ppermute | solution.py:300

commit v3 on v0

--- a/solution.py
+++ b/solution.py
@@ -1,6 +1,10 @@
+import functools
+
 import jax
 import jax.numpy as jnp
 from jax import lax
+from jax.experimental import pallas as pl
+from jax.experimental.pallas import tpu as pltpu
 from jax.sharding import PartitionSpec as P
 
 HEADS = 16
@@ -24,7 +28,7 @@
     return (values * scale_inv).astype(jnp.bfloat16)
 
 
-def local(tokens, w_query, w_keyval, taps):
+def gathered(tokens, w_query, w_keyval, taps):
     channels = HEADS * HDIM
     rows_here = tokens.shape[0]
     normed = normalize(tokens)
@@ -63,6 +67,439 @@
     return mixed
 
 
+VMEM = pl.BlockSpec(memory_space=pltpu.VMEM)
+SMEM = pl.BlockSpec(memory_space=pltpu.SMEM)
+ANY = pl.BlockSpec(memory_space=pl.ANY)
+ANY = pl.BlockSpec(memory_space=pl.ANY)
+PARAMS = pltpu.CompilerParams(vmem_limit_bytes=16 * 2**20)
+
+
+def kernel_call(body, outs, *operands, scalars=1, scratch=(), flops=0):
+    moved = sum(one.size * one.dtype.itemsize for one in operands)
+    return pl.pallas_call(
+        body,
+        out_shape=outs,
+        in_specs=[SMEM] * scalars + [VMEM] * (len(operands) - scalars),
+        out_specs=jax.tree.map(lambda _: VMEM, outs),
+        scratch_shapes=list(scratch),
+        compiler_params=PARAMS,
+        cost_estimate=pl.CostEstimate(flops=flops, bytes_accessed=moved, transcendentals=0),
+    )(*operands)
+
+
+def like(shape, dtype=jnp.bfloat16):
+    return jax.ShapeDtypeStruct(shape, dtype)
+
+
+def begin_kernel(tokens, normed):
+    depth = tokens.shape[0]
+    step = depth // 10
+    total = jnp.zeros((1, tokens.shape[1]), jnp.float32)
+    for start in range(0, depth, step):
+        values = tokens[start : start + step].astype(jnp.float32)
+        total += jnp.sum(values * values, axis=0, keepdims=True)
+    scale_inv = lax.rsqrt(total / depth + epsilon)
+    for start in range(0, depth, step):
+        values = tokens[start : start + step].astype(jnp.float32)
+        normed[start : start + step] = (values * scale_inv).astype(jnp.bfloat16)
+
+
+def begin(tokens):
+    return kernel_call(begin_kernel, like(tokens.shape), tokens, scalars=0)
+
+
+def relay_kernel(place, beside, across, out):
+    core = place[1] % 2
+    for k, block in enumerate((across, beside)):
+
+        @pl.when(core == k)
+        def _():
+            out[...] = block[...]
+
+
+def relay(place, beside, across):
+    return kernel_call(relay_kernel, like(beside.shape), place, beside, across)
+
+
+def spaced(rows):
+    gap = -rows.shape[0] % 16
+    return jnp.concatenate([rows, jnp.zeros((gap, rows.shape[1]), rows.dtype)], axis=0)
+
+
+def room_of(rows):
+    return (rows + 15) // 16 * 16
+
+
+def weights_kernel(w_keyval, w_query, out, held, sems):
+    split = w_keyval.shape[0]
+    copies = [
+        pltpu.make_async_copy(w_keyval, out.at[pl.ds(0, split)], sems.at[0]),
+        pltpu.make_async_copy(w_query, held, sems.at[1]),
+    ]
+    for copy in copies:
+        copy.start()
+    copies[1].wait()
+    out[split:] = held[...]
+    copies[0].wait()
+
+
+def weights_of(w_keyval, w_query):
+    rows, depth = w_keyval.shape[0] + w_query.shape[0], w_query.shape[1]
+    return pl.pallas_call(
+        weights_kernel,
+        out_shape=like((rows, depth)),
+        in_specs=[ANY, ANY],
+        out_specs=VMEM,
+        scratch_shapes=[
+            pltpu.VMEM(w_query.shape, w_query.dtype),
+            pltpu.SemaphoreType.DMA((2,)),
+        ],
+        compiler_params=PARAMS,
+    )(w_keyval, w_query)
+
+
+def last_kernel(place, inner, outer, out):
+    z = place[0]
+    middle = (z == 1) | (z == 2)
+    for flag, rows in ((middle, inner), (jnp.logical_not(middle), outer)):
+
+        @pl.when(flag)
+        def _():
+            out[...] = rows[...]
+
+
+def last_of(place, inner, outer):
+    return kernel_call(last_kernel, like(inner.shape), place, inner, outer)
+
+
+def add_states(z, totals, lin):
+    keys_first = z < 2
+    tokens = lin.shape[1]
+    ones = (lax.broadcasted_iota(jnp.int32, (16, tokens), 0) == 0).astype(jnp.bfloat16)
+    one, two = lin[:HDIM], lin[HDIM:]
+    key = jnp.maximum(jnp.where(keys_first, one, two), 0.0).astype(jnp.bfloat16)
+    value = jnp.where(keys_first, two, one).astype(jnp.bfloat16)
+    return totals + lax.dot_general(
+        jnp.concatenate([value, ones], axis=0),
+        key,
+        (((1,), (1,)), ((), ())),
+        preferred_element_type=jnp.float32,
+    )
+
+
+def ready_kernel(*refs):
+    *blocks, keyval, keyval_there, query = refs
+    own, first, second = range(3)
+    room = query.shape[0] // 6
+    for i, out in enumerate((keyval, keyval_there)):
+        rows = blocks[3 * i : 3 * i + 3]
+        for k, one in enumerate((first, own, second)):
+            out[HDIM * k : HDIM * (k + 1)] = rows[one][:HDIM]
+        for k in range(3):
+            at = (3 * i + k) * room
+            query[at : at + room] = spaced(rows[k][HDIM:])
+
+
+def ready_rows(mine, there):
+    rows, depth = mine[0].shape
+    outs = (like((3 * HDIM, depth)),) * 2 + (like((6 * room_of(rows - HDIM), depth)),)
+    return kernel_call(ready_kernel, outs, *mine, *there, scalars=0)
+
+
+def state_kernel(place, mine, there, *refs):
+    *blocks, out = refs
+    for i, rows in enumerate((mine, there)):
+        total = 0.0
+        for block in blocks:
+            lin = jnp.dot(rows[HDIM:], block[...], preferred_element_type=jnp.float32)
+            total = add_states(place[0], total, lin)
+        out[i] = total
+
+
+def states_of(place, mine, there, blocks):
+    depth, tokens = blocks[0].shape
+    return kernel_call(
+        state_kernel,
+        like((2, HDIM + 16, HDIM), jnp.float32),
+        place,
+        mine,
+        there,
+        *blocks,
+        flops=8 * HDIM * depth * len(blocks) * tokens,
+    )
+
+
+def late_kernel(core, place, part, *refs):
+    rows, last, *blocks, out, held, keys, values = refs
+    z = place[0]
+    odd, keys_first = z % 2 == 1, z < 2
+    held[:HDIM] = rows[:HDIM]
+    held[HDIM : 2 * HDIM] = last[:HDIM]
+    held[2 * HDIM :] = rows[HDIM:]
+    tokens = blocks[0].shape[1]
+    ones = (lax.broadcasted_iota(jnp.int32, (16, tokens), 0) == 0).astype(jnp.bfloat16)
+    contract = (((1,), (1,)), ((), ()))
+    for k, block in enumerate(blocks):
+        final = k == len(blocks) - 1
+        weights = held[...] if final else held[: 2 * HDIM]
+        lin = jnp.dot(weights, block[...], preferred_element_type=jnp.float32)
+        to = slice(tokens * k, tokens * (k + 1))
+        for i in range(2 if final else 1):
+            one, two = (lin[HDIM * j : HDIM * (j + 1)] for j in (2 * i, 2 * i + 1))
+            key = jnp.maximum(jnp.where(keys_first, one, two), 0.0).astype(jnp.bfloat16)
+            value = jnp.where(keys_first, two, one).astype(jnp.bfloat16)
+            if i == 0:
+                keys[:, to] = key
+                values[:HDIM, to] = value
+                values[HDIM:, to] = ones
+            else:
+                value = jnp.concatenate([value, ones], axis=0)
+                first = part[core] + lax.dot_general(
+                    value, key, contract, preferred_element_type=jnp.float32
+                )
+    total = lax.dot_general(values[...], keys[...], contract, preferred_element_type=jnp.float32)
+    out[0] = jnp.where(odd, total, first)
+    out[1] = jnp.where(odd, first, total)
+
+
+def late_states(core, place, part, rows, last, blocks):
+    depth, tokens = blocks[0].shape
+    columns = len(blocks) * tokens
+    return kernel_call(
+        functools.partial(late_kernel, core),
+        like(part.shape, part.dtype),
+        place,
+        part,
+        rows,
+        last,
+        *blocks,
+        scratch=[
+            pltpu.VMEM((4 * HDIM, depth), jnp.bfloat16),
+            pltpu.VMEM((HDIM, columns), jnp.bfloat16),
+            pltpu.VMEM((HDIM + 16, columns), jnp.bfloat16),
+        ],
+        flops=4 * HDIM * depth * (columns + tokens),
+    )
+
+
+def sum_kernel(*refs):
+    total = refs[0][...].astype(jnp.float32)
+    for one in refs[1:-1]:
+        total += one[...].astype(jnp.float32)
+    refs[-1][...] = total.astype(refs[-1].dtype)
+
+
+def sum_of(parts, dtype):
+    return kernel_call(sum_kernel, like(parts[0].shape, dtype), *parts, scalars=0)
+
+
+def query_kernel(place, *refs):
+    rows, last, last_there, block_0, block_1, out, held = refs
+    z = place[0]
+    half = HDIM // 2
+    step = room_of(half)
+    for i, one in enumerate((last, last_there)):
+        at = LAYERS * step * i
+        held[at : at + 3 * step] = rows[3 * step * i : 3 * step * (i + 1)]
+        held[at + 3 * step : at + 4 * step] = spaced(one[HDIM:])
+    tokens = block_0.shape[1]
+    for k, block in enumerate((block_0, block_1)):
+        lin = jnp.dot(held[...], block[...], preferred_element_type=jnp.float32)
+        for i in range(LAYERS):
+            one = lin[step * i : step * i + half]
+            two = lin[step * (LAYERS + i) : step * (LAYERS + i) + half]
+            head = jnp.maximum(jnp.concatenate([one, two], axis=0), 0.0).astype(jnp.bfloat16)
+            rows = pl.ds(pl.multiple_of((z ^ i) * HDIM, 16), HDIM)
+            out[rows, tokens * k : tokens * (k + 1)] = head
+
+
+def queries_of(place, rows, blocks):
+    depth, tokens = blocks[0].shape
+    height = 2 * LAYERS * room_of(HDIM // 2)
+    return kernel_call(
+        query_kernel,
+        like((LAYERS * HDIM, 2 * tokens)),
+        place,
+        *rows,
+        *blocks,
+        scratch=[pltpu.VMEM((height, depth), jnp.bfloat16)],
+        flops=2 * height * depth * 2 * tokens,
+    )
+
+
+def attend_kernel(row, place, mine, there, taps, center, side, halo, *outs):
+    z, slot = place[0], place[1]
+    y, core = slot // 4, slot % 2
+    tokens = outs[0].shape[1]
+    half = HDIM // 2
+    halo_later = y == row
+    halo_there = jnp.where(halo_later, z < LAYERS - 1, z > 0)
+    to = lax.broadcasted_iota(jnp.int32, (HDIM, HDIM), 0)
+    column = lax.broadcasted_iota(jnp.int32, (HDIM, HDIM), 1)
+    turned = jnp.where(to < half, to + half, to - half)
+    order = (column == jnp.where(core == 0, to, turned)).astype(jnp.bfloat16)
+    for m in range(LAYERS):
+        own, other = mine[m // 2], there[m // 2]
+        state = jnp.where(core == m % 2, own, other)
+        high = state.astype(jnp.bfloat16)
+        low = (state - high.astype(jnp.float32)).astype(jnp.bfloat16)
+        both = jnp.concatenate([high, low], axis=0)
+        both = jnp.dot(both, order, preferred_element_type=jnp.float32).astype(jnp.bfloat16)
+        rows = pl.ds(HDIM * m, HDIM)
+
+        def attended(frame):
+            sums = jnp.dot(both, frame[rows], preferred_element_type=jnp.float32)
+            sums = sums[: HDIM + 16] + sums[HDIM + 16 :]
+            result = sums[:HDIM] * (1.0 / (sums[HDIM : HDIM + 1] + epsilon))
+            return result.astype(jnp.bfloat16).astype(jnp.float32)
+
+        tap = taps[rows]
+        tap_side = jnp.where(halo_later, tap[:, 0:1], tap[:, 2:3])
+        tap_halo = jnp.where(halo_later, tap[:, 2:3], tap[:, 0:1])
+        mixed = tap_side * attended(side) + tap[:, 1:2] * attended(center)
+        mixed += tap_halo * jnp.where(halo_there, attended(halo), 0.0)
+        for i, out in enumerate(outs):
+            out[rows] = mixed[:, tokens * i : tokens * (i + 1)].astype(jnp.bfloat16)
+
+
+def attend(row, place, mine, there, taps, *frames):
+    channels, tokens = frames[0].shape
+    outs = (like((channels, tokens // 2)),) * 2
+    body = functools.partial(attend_kernel, row)
+    return kernel_call(body, outs, place, mine, there, taps, *frames)
+
+
+def finish_kernel(place, *refs):
+    parts, (out, held) = refs[:4], refs[4:]
+    chip = place[1] // 2
+    tokens = out.shape[0]
+    for k, part in enumerate(parts):
+        for m in range(LAYERS):
+            to = pl.multiple_of((4 * m + (chip ^ k)) * HDIM, 16)
+            held[pl.ds(to, HDIM)] = part[pl.ds(HDIM * m, HDIM)]
+    row = lax.broadcasted_iota(jnp.int32, (tokens, tokens), 0)
+    column = lax.broadcasted_iota(jnp.int32, (tokens, tokens), 1)
+    same = (row == column).astype(jnp.bfloat16)
+    step = 256
+    for at in range(0, out.shape[1], step):
+        out[:, at : at + step] = lax.dot_general(
+            same, held[at : at + step], (((1,), (1,)), ((), ())), preferred_element_type=jnp.float32
+        ).astype(jnp.bfloat16)
+
+
+def finish(place, parts):
+    channels, tokens = parts[0].shape
+    return kernel_call(
+        finish_kernel,
+        like((tokens, 4 * channels)),
+        place,
+        *parts,
+        scratch=[pltpu.VMEM((4 * channels, tokens), jnp.bfloat16)],
+    )
+
+
+STATE_SENT = jnp.bfloat16
+LAYERS = 4
+PLANE = 8
+
+
+def send(value, place):
+    pairs = []
+    for z in range(LAYERS):
+        for slot in range(PLANE):
+            to = place(z, slot)
+            if to is not None:
+                pairs.append((z * PLANE + slot, to[0] * PLANE + to[1]))
+    return lax.ppermute(value, "frame", pairs)
+
+
+def swap(value, bits):
+    return send(value, lambda z, slot: (z, slot ^ bits))
+
+
+def between(value, steps):
+    return send(value, lambda z, slot: (steps[z], slot) if z in steps else None)
+
+
+def together(*values):
+    return lax.optimization_barrier(values)
+
+
+def planes(tokens, w_query, w_keyval, taps):
+    me = lax.axis_index("frame")
+    z, slot = me // PLANE, me % PLANE
+    chip = slot // 2
+    place = jnp.stack([z, slot]).astype(jnp.int32)
+
+    cross = [{i: i ^ k for i in range(LAYERS)} for k in range(LAYERS)]
+    inner, outer = {1: 2, 2: 1}, {1: 0, 2: 3}
+
+    by_head = taps.reshape(3, LAYERS, 4, HDIM)
+    tap = lax.dynamic_index_in_dim(by_head, chip, axis=2, keepdims=False).reshape(3, -1).T
+    weights = weights_of(w_keyval, w_query)
+    weights_2 = between(weights, cross[2])
+    weights_1 = between(weights, cross[1])
+    own = begin(tokens.T)
+    beside, across = swap(own, 2), swap(own, 4)
+    weights_there = swap(weights, 1)
+    own, beside, across, weights, weights_1, weights_2, weights_there, tap = together(
+        own, beside, across, weights, weights_1, weights_2, weights_there, tap
+    )
+
+    weights_inner = between(weights, inner)
+    weights_outer = between(weights_2, outer)
+    passed = relay(place, beside, across)
+    diagonal = send(passed, lambda z, slot: (z, slot ^ (4 if slot % 2 else 2)))
+    there_2, there_1 = swap(weights_2, 1), swap(weights_1, 1)
+    keyval, keyval_there, query = ready_rows(
+        (weights, weights_1, weights_2), (weights_there, there_1, there_2)
+    )
+    part = states_of(place, keyval, keyval_there, (own, beside, across))
+    diagonal, weights_inner, weights_outer, part = together(
+        diagonal, weights_inner, weights_outer, part
+    )
+
+    weights_3 = last_of(place, weights_inner, weights_outer)
+    there_3 = swap(weights_3, 1)
+    blocks = (own, beside, across, diagonal)
+    kept = late_states(0, place, part, keyval, weights_3, blocks)
+    rows = (query, weights_3, there_3)
+    here = queries_of(place, rows, (own, beside))
+    there = queries_of(place, rows, (across, diagonal))
+    there, part = together(there, part)
+    given = late_states(1, place, part, keyval_there, there_3, blocks)
+    part = sum_of([kept, swap(given, 1)], STATE_SENT)
+    part = send(part, lambda z, slot: (z, 2 * (slot % 4) + slot // 4))
+    state = sum_of([part] + [between(part, cross[k]) for k in range(1, LAYERS)], jnp.float32)
+    state_there = swap(state, 1)
+
+    def aside(value, row):
+        def to(z, slot):
+            z += 1 if slot // 4 == row else -1
+            return (z, slot) if 0 <= z < LAYERS else None
+
+        return send(value, to)
+
+
+    halo_there, halo_here = aside(here, 1), aside(there, 0)
+    out_across = attend(0, place, state, state_there, tap, there, here, halo_there)
+    got_across = swap(out_across[0], 4), swap(out_across[1], 6)
+    out_here = attend(1, place, state, state_there, tap, here, there, halo_here)
+    got_beside = swap(out_here[1], 2)
+    return finish(place, [out_here[0], got_beside, *got_across])
+
+
+def local(tokens, w_query, w_keyval, taps):
+    fits = (
+        lax.axis_size("frame") == LAYERS * PLANE
+        and HEADS == 2 * PLANE
+        and w_keyval.shape[0] == HDIM
+        and 2 * w_query.shape[0] == HDIM
+        and PLANE * tokens.shape[0] == 2 * HEIGHT * WIDTH
+    )
+    return (planes if fits else gathered)(tokens, w_query, w_keyval, taps)
+
+
 def solution(mesh):
     placed = (P(("grp", "frame"), None), P("frame", None), P("frame", None), P())
     return jax.shard_map(

time: 410 us -> 122 us (0.30)
  waiting for transfers between devices: 316 us -> 61.4 us
  blocking collectives: 38.6 us -> 0 us
  starting transfers between devices: 4.73 us -> 33.8 us
  matrix products: 28.4 us -> 0 us
  Pallas kernels: 0 us -> 23.9 us
  between operations: 13.2 us -> 0.25 us
  other arithmetic: 4.45 us -> 0.07 us
    all_gather x2 -> x0, waiting for transfers between devices: 189 us -> none  [the longest x1 109 us: local(): lax.all_gather(w_keyval, 'frame', axis=0, tiled=True)]
    psum x1 -> x0, waiting for transfers between devices: 88.9 us -> none  [local(): state, key_total = lax.psum((local_state, local_keys), 'frame')]
    psum x1 -> x0, blocking collectives: 38.6 us -> none  [local(): state, key_total = lax.psum((local_state, local_keys), 'frame')]
    ppermute x2 -> x22, starting transfers between devices: 4.66 us -> 33.8 us  [send(): return lax.ppermute(value, 'frame', pairs)]
    dot_general x5 -> x0, matrix products: 28.4 us -> none  [the longest x2 23.3 us: project_rows(): lax.dot_general(normed, weight_rows, (((1,), (1,)), ((), ())), preferred_...]
    ppermute x2 -> x22, waiting for transfers between devices: 36.9 us -> 61.4 us  [send(): return lax.ppermute(value, 'frame', pairs)]
    pallas_call x0 -> x15, Pallas kernels: none -> 23.9 us  [the longest x14 22.3 us: kernel_call(): pl.pallas_call(body, out_shape=outs, in_specs=[SMEM] * scalars + [VMEM] *...]
  transfers between devices with their start and end apart: 5 -> 22, of which waited for: 4 -> 11; matrix products, arithmetic and copies ran while one was open for 2% -> 1% of each run, Pallas kernels for 0% -> 15%
where the time goes in v3:
time: 122 us
  waiting for transfers between devices  61.4 us (50%)
  starting transfers between devices  33.8 us (28%)
  Pallas kernels  23.9 us (20%)
  local copies, waits for them, and re-layouts  2.23 us (2%)
    ppermute x22, waiting for transfers between devices, send(): return lax.ppermute(value, 'frame', pairs)  61.4 us
    ppermute x22, starting transfers between devices, send(): return lax.ppermute(value, 'frame', pairs)  33.8 us
    pallas_call x14, Pallas kernels, kernel_call(): pl.pallas_call(body, out_shape=outs, in_specs=[SMEM] * scalars + [VMEM] *...  22.3 us
  transfers between devices with their start and end apart: 22, of which 11 were waited for; matrix products, arithmetic and copies ran while one was open for 1% of the time, Pallas kernels for 15%

profile of v3, /device:TPU:0, one launch (start us, length us, event | category | flops | bytes accessed | tf_op | source)
XLA Modules:
  0.0 121.7 jit_solution(17183805618219543921)
XLA Ops:
  0.0 1.3 %copy-done.1 = bf16[256,2240]{0,1:T(8,128)(2,1)S(1)} copy-done((bf16[256,2240]{0,1:T(8,128)(2,1)S(1)}, bf16[256,2240]{0,1:T(8,128)(2,1)}, u32[]{:S(2)}) %copy-start.1) | copy-done | bytes 1146904
  1.3 0.3 shard_map.46.refs_0_.refs_2_.refs_3_
  1.6 3.0 %collective-permute-start = (bf16[2240,256]{1,0:T(8,128)(2,1)S(1)}, bf16[2240,256]{1,0:T(8,128)(2,1)S(1)}, u32[]{:S(2)}, u32[]{:S(2)}) collective-permute-start(bf16[2240,256]{1,0:T(8,128)(2,1)S(1)} %shard_map.46.refs_0_.refs_2_.refs_3_), channel_id=1, source_target_pairs={{0,2},{1,3},{2,0},{3,1},{4,6},{5,7},{6,4},{7,5},{8,10},{9,11},{10,... | collective-permute-start | bytes 3440648 | tf_op jit(solution)/shard_map/ppermute | solution.py:413
  4.6 1.5 %collective-permute-start.1 = (bf16[2240,256]{1,0:T(8,128)(2,1)S(1)}, bf16[2240,256]{1,0:T(8,128)(2,1)S(1)}, u32[]{:S(2)}, u32[]{:S(2)}) collective-permute-start(bf16[2240,256]{1,0:T(8,128)(2,1)S(1)} %shard_map.46.refs_0_.refs_2_.refs_3_), channel_id=1, source_target_pairs={{0,4},{1,5},{2,6},{3,7},{4,0},{5,1},{6,2},{7,3},{8,12},{9,13},{10,... | collective-permute-start | bytes 3440648 | tf_op jit(solution)/shard_map/ppermute | solution.py:413
  6.1 1.6 %shard_map.47.refs_0_ = bf16[168,2240]{1,0:T(8,128)(2,1)} custom-call(bf16[112,2240]{1,0:T(8,128)(2,1)S(1)} %copy-done.2, bf16[56,2240]{1,0:T(8,128)(2,1)S(1)} %copy-done.3), custom_call_target="tpu_custom_call" | custom-call | tf_op jit(solution)/shard_map/pallas_call | solution.py:148
  7.7 1.6 %collective-permute-start.2 = (bf16[168,2240]{1,0:T(8,128)(2,1)}, bf16[168,2240]{1,0:T(8,128)(2,1)}, u32[]{:S(2)}, u32[]{:S(2)}) collective-permute-start(bf16[168,2240]{1,0:T(8,128)(2,1)} %shard_map.47.refs_0_), channel_id=1, source_target_pairs={{0,8},{1,9},{2,10},{3,11},{4,12},{5,13},{6,14},{7,15},{8,0},{9,1},... | collective-permute-start | bytes 2257928 | tf_op jit(solution)/shard_map/ppermute | solution.py:413
  9.3 2.6 %collective-permute-start.3 = (bf16[168,2240]{1,0:T(8,128)(2,1)}, bf16[168,2240]{1,0:T(8,128)(2,1)}, u32[]{:S(2)}, u32[]{:S(2)}) collective-permute-start(bf16[168,2240]{1,0:T(8,128)(2,1)} %shard_map.47.refs_0_), channel_id=1, source_target_pairs={{0,16},{1,17},{2,18},{3,19},{4,20},{5,21},{6,22},{7,23},{8,24},{9,... | collective-permute-start | bytes 2257928 | tf_op jit(solution)/shard_map/ppermute | solution.py:413
  11.9 0.1 reshape.7
  12.0 0.8 copy.6
  12.9 0.1 pad_add_fusion.place
  13.0 30.0 %collective-permute-done.2.refs_1_ = bf16[168,2240]{1,0:T(8,128)(2,1)} collective-permute-done((bf16[168,2240]{1,0:T(8,128)(2,1)}, bf16[168,2240]{1,0:T(8,128)(2,1)}, u32[]{:S(2)}, u32[]{:S(2)}) %collective-permute-start.2) | collective-permute-done | bytes 752672 | tf_op jit(solution)/shard_map/ppermute | solution.py:413
  43.0 2.4 %collective-permute-done.3.refs_2_ = bf16[168,2240]{1,0:T(8,128)(2,1)} collective-permute-done((bf16[168,2240]{1,0:T(8,128)(2,1)}, bf16[168,2240]{1,0:T(8,128)(2,1)}, u32[]{:S(2)}, u32[]{:S(2)}) %collective-permute-start.3) | collective-permute-done | bytes 752672 | tf_op jit(solution)/shard_map/ppermute | solution.py:413
  45.4 0.6 shard_map.48
  46.0 0.6 collective-permute-start.5
  46.6 0.5 collective-permute-start.9
  47.1 0.7 collective-permute-start.6
  47.8 1.3 %collective-permute-start.7 = (bf16[168,2240]{1,0:T(8,128)(2,1)}, bf16[168,2240]{1,0:T(8,128)(2,1)S(1)}, u32[]{:S(2)}, u32[]{:S(2)}) collective-permute-start(bf16[168,2240]{1,0:T(8,128)(2,1)} %collective-permute-done.3.refs_2_), channel_id=1, source_target_pairs={{8,0},{9,1},{10,2},{11,3},{12,4},{13,5},{14,6},{15,7},{16,24},{17,... | collective-permute-start | bytes 2257928 | tf_op jit(solution)/shard_map/ppermute | solution.py:413
  49.1 1.1 collective-permute-done.9.refs_5_
  50.2 2.1 %shard_map.49 = (bf16[336,2240]{1,0:T(8,128)(2,1)S(1)}, bf16[336,2240]{1,0:T(8,128)(2,1)S(1)}, bf16[384,2240]{1,0:T(8,128)(2,1)S(1)}) custom-call(bf16[168,2240]{1,0:T(8,128)(2,1)} %shard_map.47.refs_0_, bf16[168,2240]{1,0:T(8,128)(2,1)} %collective-permute-done.2.refs_1_, bf16[168,2240]{1,0:T(8,128)(2,1)} %collective-permute-done.3.refs_2_, ...), custom_call_target="tpu_custom_call" | custom-call | bytes 4515840 | tf_op jit(solution)/shard_map/pallas_call | solution.py:79
  52.4 3.4 %shard_map.50.part = f32[2,128,112]{2,1,0:T(8,128)S(1)} custom-call(s32[2]{0:T(128)S(1)} %pad_add_fusion.place, bf16[336,2240]{1,0:T(8,128)(2,1)S(1)} %get-tuple-element.32.mine.refs_0_, bf16[336,2240]{1,0:T(8,128)(2,1)S(1)} %get-tuple-element.33.there.refs_0_, bf16[2240,256]{1,0:T(8,128)(2,1)S(1)} %shard_map.46.refs_0_.refs_2_.refs_3_, ...), custom_call_target="tpu_custom_call" | custom-call | flops 1541406720 | bytes 6451208 | tf_op jit(solution)/shard_map/pallas_call | solution.py:79
  55.8 13.4 %collective-permute-done.7.outer = bf16[168,2240]{1,0:T(8,128)(2,1)S(1)} collective-permute-done((bf16[168,2240]{1,0:T(8,128)(2,1)}, bf16[168,2240]{1,0:T(8,128)(2,1)S(1)}, u32[]{:S(2)}, u32[]{:S(2)}) %collective-permute-start.7) | collective-permute-done | bytes 752672 | tf_op jit(solution)/shard_map/ppermute | solution.py:413
  69.1 0.6 shard_map.51.refs_1_
  69.7 0.1 collective-permute-start.10
  69.8 2.3 %collective-permute-done.10.refs_2_.refs_1_ = bf16[168,2240]{1,0:T(8,128)(2,1)S(1)} collective-permute-done((bf16[168,2240]{1,0:T(8,128)(2,1)S(1)}, bf16[168,2240]{1,0:T(8,128)(2,1)S(1)}, u32[]{:S(2)}, u32[]{:S(2)}) %collective-permute-start.10) | collective-permute-done | bytes 752672 | tf_op jit(solution)/shard_map/ppermute | solution.py:413
  72.1 2.0 %shard_map.57.center.side = bf16[448,512]{1,0:T(8,128)(2,1)S(1)} custom-call(s32[2]{0:T(128)S(1)} %pad_add_fusion.place, bf16[384,2240]{1,0:T(8,128)(2,1)S(1)} %get-tuple-element.39.refs_0_, bf16[168,2240]{1,0:T(8,128)(2,1)S(1)} %shard_map.51.refs_1_, bf16[168,2240]{1,0:T(8,128)(2,1)S(1)} %collective-permute-done.10.refs_2_.refs_1_, ...), custom_call_target="tpu_custom_call" | custom-call | flops 1174405120 | bytes 5519368 | tf_op jit(solution)/shard_map/pallas_call | solution.py:79
  74.0 1.3 %collective-permute-start.19 = (bf16[448,512]{1,0:T(8,128)(2,1)S(1)}, bf16[448,512]{1,0:T(8,128)(2,1)S(1)}, u32[]{:S(2)}, u32[]{:S(2)}) collective-permute-start(bf16[448,512]{1,0:T(8,128)(2,1)S(1)} %shard_map.57.center.side), channel_id=1, source_target_pairs={{4,12},{5,13},{6,14},{7,15},{8,0},{9,1},{10,2},{11,3},{12,20},{13,... | collective-permute-start | bytes 1376264 | tf_op jit(solution)/shard_map/ppermute | solution.py:413
  75.3 2.0 %shard_map.53.side.center = bf16[448,512]{1,0:T(8,128)(2,1)S(1)} custom-call(s32[2]{0:T(128)S(1)} %pad_add_fusion.place, bf16[384,2240]{1,0:T(8,128)(2,1)S(1)} %get-tuple-element.39.refs_0_, bf16[168,2240]{1,0:T(8,128)(2,1)S(1)} %shard_map.51.refs_1_, bf16[168,2240]{1,0:T(8,128)(2,1)S(1)} %collective-permute-done.10.refs_2_.refs_1_, ...), custom_call_target="tpu_custom_call" | custom-call | flops 1174405120 | bytes 5519368 | tf_op jit(solution)/shard_map/pallas_call | solution.py:79
  77.3 4.6 %collective-permute-start.17 = (bf16[448,512]{1,0:T(8,128)(2,1)S(1)}, bf16[448,512]{1,0:T(8,128)(2,1)S(1)}, u32[]{:S(2)}, u32[]{:S(2)}) collective-permute-start(bf16[448,512]{1,0:T(8,128)(2,1)S(1)} %shard_map.53.side.center), channel_id=1, source_target_pairs={{0,8},{1,9},{2,10},{3,11},{8,16},{9,17},{10,18},{11,19},{12,4},{13... | collective-permute-start | bytes 1376264 | tf_op jit(solution)/shard_map/ppermute | solution.py:413
  81.9 2.4 %shard_map.54 = f32[2,128,112]{2,1,0:T(8,128)S(1)} custom-call(s32[2]{0:T(128)S(1)} %pad_add_fusion.place, f32[2,128,112]{2,1,0:T(8,128)S(1)} %shard_map.50.part, bf16[336,2240]{1,0:T(8,128)(2,1)S(1)} %get-tuple-element.33.there.refs_0_, bf16[168,2240]{1,0:T(8,128)(2,1)S(1)} %collective-permute-done.10.refs_2_.refs_1_, ...), custom_call_target="tpu_custom_call" | custom-call | flops 1284505600 | bytes 6960136 | tf_op jit(solution)/shard_map/pallas_call | solution.py:79
  84.4 0.1 collective-permute-start.11
  84.4 2.5 %shard_map.52.refs_0_ = f32[2,128,112]{2,1,0:T(8,128)S(1)} custom-call(s32[2]{0:T(128)S(1)} %pad_add_fusion.place, f32[2,128,112]{2,1,0:T(8,128)S(1)} %shard_map.50.part, bf16[336,2240]{1,0:T(8,128)(2,1)S(1)} %get-tuple-element.32.mine.refs_0_, bf16[168,2240]{1,0:T(8,128)(2,1)S(1)} %shard_map.51.refs_1_, ...), custom_call_target="tpu_custom_call" | custom-call | flops 1284505600 | bytes 6960136 | tf_op jit(solution)/shard_map/pallas_call | solution.py:79
  86.9 0.8 collective-permute-start.12
  87.8 0.1 collective-permute-start.13
  87.9 0.7 collective-permute-start.14
  88.6 3.7 %collective-permute-start.15 = (bf16[2,128,112]{2,1,0:T(8,128)(2,1)S(1)}, bf16[2,128,112]{2,1,0:T(8,128)(2,1)S(1)}, u32[]{:S(2)}, u32[]{:S(2)}) collective-permute-start(bf16[2,128,112]{2,1,0:T(8,128)(2,1)S(1)} %collective-permute-done.12.refs_0_), channel_id=1, source_target_pairs={{0,24},{1,25},{2,26},{3,27},{4,28},{5,29},{6,30},{7,31},{8,16},{9,... | collective-permute-start | bytes 172040 | tf_op jit(solution)/shard_map/ppermute | solution.py:413
  92.2 0.1 collective-permute-done.13.refs_1_
  92.4 0.7 collective-permute-done.14.refs_2_
  93.1 2.2 %collective-permute-done.15.refs_3_ = bf16[2,128,112]{2,1,0:T(8,128)(2,1)S(1)} collective-permute-done((bf16[2,128,112]{2,1,0:T(8,128)(2,1)S(1)}, bf16[2,128,112]{2,1,0:T(8,128)(2,1)S(1)}, u32[]{:S(2)}, u32[]{:S(2)}) %collective-permute-start.15) | collective-permute-done | bytes 57376 | tf_op jit(solution)/shard_map/ppermute | solution.py:413
  95.3 4.1 %collective-permute-start.16 = (f32[2,128,112]{2,1,0:T(8,128)S(1)}, f32[2,128,112]{2,1,0:T(8,128)S(1)}, u32[]{:S(2)}, u32[]{:S(2)}) collective-permute-start(f32[2,128,112]{2,1,0:T(8,128)S(1)} %shard_map.56.mine), channel_id=1, source_target_pairs={{0,1},{1,0},{2,3},{3,2},{4,5},{5,4},{6,7},{7,6},{8,9},{9,8},{10,11... | collective-permute-start | bytes 344072 | tf_op jit(solution)/shard_map/ppermute | solution.py:413
  99.5 1.0 collective-permute-done.16.there
  100.5 2.2 %shard_map.59 = (bf16[448,256]{1,0:T(8,128)(2,1)S(1)}, bf16[448,256]{1,0:T(8,128)(2,1)S(1)}) custom-call(s32[2]{0:T(128)S(1)} %pad_add_fusion.place, f32[2,128,112]{2,1,0:T(8,128)S(1)} %shard_map.56.mine, f32[2,128,112]{2,1,0:T(8,128)S(1)} %collective-permute-done.16.there, f32[448,3]{1,0:T(8,128)S(1)} %bitcast.6, ...), custom_call_target="tpu_custom_call" | custom-call | bytes 1611016 | tf_op jit(solution)/shard_map/pallas_call | solution.py:79
  102.7 4.9 %collective-permute-start.20 = (bf16[448,256]{1,0:T(8,128)(2,1)S(1)}, bf16[448,256]{1,0:T(8,128)(2,1)S(1)}, u32[]{:S(2)}, u32[]{:S(2)}) collective-permute-start(bf16[448,256]{1,0:T(8,128)(2,1)S(1)} %get-tuple-element.45), channel_id=1, source_target_pairs={{0,4},{1,5},{2,6},{3,7},{4,0},{5,1},{6,2},{7,3},{8,12},{9,13},{10,... | collective-permute-start | bytes 688136 | tf_op jit(solution)/shard_map/ppermute | solution.py:413
  107.6 0.4 collective-permute-start.21
  107.9 2.2 %shard_map.58 = (bf16[448,256]{1,0:T(8,128)(2,1)S(1)}, bf16[448,256]{1,0:T(8,128)(2,1)S(1)}) custom-call(s32[2]{0:T(128)S(1)} %pad_add_fusion.place, f32[2,128,112]{2,1,0:T(8,128)S(1)} %shard_map.56.mine, f32[2,128,112]{2,1,0:T(8,128)S(1)} %collective-permute-done.16.there, f32[448,3]{1,0:T(8,128)S(1)} %bitcast.7, ...), custom_call_target="tpu_custom_call" | custom-call | bytes 1611016 | tf_op jit(solution)/shard_map/pallas_call | solution.py:79
  110.1 1.2 %collective-permute-start.18 = (bf16[448,256]{1,0:T(8,128)(2,1)S(1)}, bf16[448,256]{1,0:T(8,128)(2,1)S(1)}, u32[]{:S(2)}, u32[]{:S(2)}) collective-permute-start(bf16[448,256]{1,0:T(8,128)(2,1)S(1)} %get-tuple-element.44), channel_id=1, source_target_pairs={{0,2},{1,3},{2,0},{3,1},{4,6},{5,7},{6,4},{7,5},{8,10},{9,11},{10,... | collective-permute-start | bytes 688136 | tf_op jit(solution)/shard_map/ppermute | solution.py:413
  111.4 7.0 %collective-permute-done.20.refs_2_ = bf16[448,256]{1,0:T(8,128)(2,1)S(1)} collective-permute-done((bf16[448,256]{1,0:T(8,128)(2,1)S(1)}, bf16[448,256]{1,0:T(8,128)(2,1)S(1)}, u32[]{:S(2)}, u32[]{:S(2)}) %collective-permute-start.20) | collective-permute-done | bytes 229408 | tf_op jit(solution)/shard_map/ppermute | solution.py:413
  118.4 1.3 %collective-permute-done.18.refs_1_ = bf16[448,256]{1,0:T(8,128)(2,1)S(1)} collective-permute-done((bf16[448,256]{1,0:T(8,128)(2,1)S(1)}, bf16[448,256]{1,0:T(8,128)(2,1)S(1)}, u32[]{:S(2)}, u32[]{:S(2)}) %collective-permute-start.18) | collective-permute-done | bytes 229408 | tf_op jit(solution)/shard_map/ppermute | solution.py:413
  119.7 2.0 %shard_map.60 = bf16[256,1792]{1,0:T(8,128)(2,1)} custom-call(s32[2]{0:T(128)S(1)} %pad_add_fusion.place, bf16[448,256]{1,0:T(8,128)(2,1)S(1)} %get-tuple-element.43.refs_0_, bf16[448,256]{1,0:T(8,128)(2,1)S(1)} %collective-permute-done.18.refs_1_, bf16[448,256]{1,0:T(8,128)(2,1)S(1)} %collective-permute-done.20.refs_2_, ...), custom_call_target="tpu_custom_call" | custom-call | bytes 917512 | tf_op jit(solution)/shard_map/pallas_call | solution.py:79
  (25 shorter events, 0.1 us)
Async XLA Ops:
  0.0 1.3 %copy-start.1 = (bf16[256,2240]{0,1:T(8,128)(2,1)S(1)}, bf16[256,2240]{0,1:T(8,128)(2,1)}, u32[]{:S(2)}) copy-start(bf16[256,2240]{0,1:T(8,128)(2,1)} %param.4) | copy-start | bytes 3440644
  1.3 4.8 %copy-start.2 = (bf16[112,2240]{1,0:T(8,128)(2,1)S(1)}, bf16[112,2240]{1,0:T(8,128)(2,1)}, u32[]{:S(2)}) copy-start(bf16[112,2240]{1,0:T(8,128)(2,1)} %w_keyval.1) | copy-start | bytes 1505284
  1.3 4.8 %copy-start.3 = (bf16[56,2240]{1,0:T(8,128)(2,1)S(1)}, bf16[56,2240]{1,0:T(8,128)(2,1)}, u32[]{:S(2)}) copy-start(bf16[56,2240]{1,0:T(8,128)(2,1)} %w_query.1) | copy-start | bytes 752644
  1.6 10.4 %copy-start.4 = (f32[3,1792]{1,0:T(4,128)S(1)}, f32[3,1792]{1,0:T(4,128)}, u32[]{:S(2)}) copy-start(f32[3,1792]{1,0:T(4,128)} %param.7) | copy-start | bytes 64516
  1.6 43.8 %collective-permute-start = (bf16[2240,256]{1,0:T(8,128)(2,1)S(1)}, bf16[2240,256]{1,0:T(8,128)(2,1)S(1)}, u32[]{:S(2)}, u32[]{:S(2)}) collective-permute-start(bf16[2240,256]{1,0:T(8,128)(2,1)S(1)} %shard_map.46.refs_0_.refs_2_.refs_3_), channel_id=1, source_target_pairs={{0,2},{1,3},{2,0},{3,1},{4,6},{5,7},{6,4},{7,5},{8,10},{9,11},{10,... | collective-permute-start | bytes 3440648 | tf_op jit(solution)/shard_map/ppermute | solution.py:413
  4.6 40.8 %collective-permute-start.1 = (bf16[2240,256]{1,0:T(8,128)(2,1)S(1)}, bf16[2240,256]{1,0:T(8,128)(2,1)S(1)}, u32[]{:S(2)}, u32[]{:S(2)}) collective-permute-start(bf16[2240,256]{1,0:T(8,128)(2,1)S(1)} %shard_map.46.refs_0_.refs_2_.refs_3_), channel_id=1, source_target_pairs={{0,4},{1,5},{2,6},{3,7},{4,0},{5,1},{6,2},{7,3},{8,12},{9,13},{10,... | collective-permute-start | bytes 3440648 | tf_op jit(solution)/shard_map/ppermute | solution.py:413
  7.7 35.3 %collective-permute-start.2 = (bf16[168,2240]{1,0:T(8,128)(2,1)}, bf16[168,2240]{1,0:T(8,128)(2,1)}, u32[]{:S(2)}, u32[]{:S(2)}) collective-permute-start(bf16[168,2240]{1,0:T(8,128)(2,1)} %shard_map.47.refs_0_), channel_id=1, source_target_pairs={{0,8},{1,9},{2,10},{3,11},{4,12},{5,13},{6,14},{7,15},{8,0},{9,1},... | collective-permute-start | bytes 2257928 | tf_op jit(solution)/shard_map/ppermute | solution.py:413
  9.3 36.0 %collective-permute-start.3 = (bf16[168,2240]{1,0:T(8,128)(2,1)}, bf16[168,2240]{1,0:T(8,128)(2,1)}, u32[]{:S(2)}, u32[]{:S(2)}) collective-permute-start(bf16[168,2240]{1,0:T(8,128)(2,1)} %shard_map.47.refs_0_), channel_id=1, source_target_pairs={{0,16},{1,17},{2,18},{3,19},{4,20},{5,21},{6,22},{7,23},{8,24},{9,... | collective-permute-start | bytes 2257928 | tf_op jit(solution)/shard_map/ppermute | solution.py:413
  11.9 33.5 %collective-permute-start.4 = (bf16[168,2240]{1,0:T(8,128)(2,1)}, bf16[168,2240]{1,0:T(8,128)(2,1)}, u32[]{:S(2)}, u32[]{:S(2)}) collective-permute-start(bf16[168,2240]{1,0:T(8,128)(2,1)} %shard_map.47.refs_0_), channel_id=1, source_target_pairs={{0,1},{1,0},{2,3},{3,2},{4,5},{5,4},{6,7},{7,6},{8,9},{9,8},{10,11... | collective-permute-start | bytes 2257928 | tf_op jit(solution)/shard_map/ppermute | solution.py:413
  46.0 23.1 %collective-permute-start.5 = (bf16[2240,256]{1,0:T(8,128)(2,1)S(1)}, bf16[2240,256]{1,0:T(8,128)(2,1)S(1)}, u32[]{:S(2)}, u32[]{:S(2)}) collective-permute-start(bf16[2240,256]{1,0:T(8,128)(2,1)S(1)} %shard_map.48), channel_id=1, source_target_pairs={{0,2},{1,5},{2,0},{3,7},{4,6},{5,1},{6,4},{7,3},{8,10},{9,13},{10,... | collective-permute-start | bytes 3440648 | tf_op jit(solution)/shard_map/ppermute | solution.py:413
  46.6 2.5 %collective-permute-start.8 = (bf16[168,2240]{1,0:T(8,128)(2,1)}, bf16[168,2240]{1,0:T(8,128)(2,1)S(1)}, u32[]{:S(2)}, u32[]{:S(2)}) collective-permute-start(bf16[168,2240]{1,0:T(8,128)(2,1)} %collective-permute-done.2.refs_1_), channel_id=1, source_target_pairs={{0,1},{1,0},{2,3},{3,2},{4,5},{5,4},{6,7},{7,6},{8,9},{9,8},{10,11... | collective-permute-start | bytes 2257928 | tf_op jit(solution)/shard_map/ppermute | solution.py:413
  46.6 3.6 %collective-permute-start.9 = (bf16[168,2240]{1,0:T(8,128)(2,1)}, bf16[168,2240]{1,0:T(8,128)(2,1)S(1)}, u32[]{:S(2)}, u32[]{:S(2)}) collective-permute-start(bf16[168,2240]{1,0:T(8,128)(2,1)} %collective-permute-done.3.refs_2_), channel_id=1, source_target_pairs={{0,1},{1,0},{2,3},{3,2},{4,5},{5,4},{6,7},{7,6},{8,9},{9,8},{10,11... | collective-permute-start | bytes 2257928 | tf_op jit(solution)/shard_map/ppermute | solution.py:413
  47.1 8.6 %collective-permute-start.6 = (bf16[168,2240]{1,0:T(8,128)(2,1)}, bf16[168,2240]{1,0:T(8,128)(2,1)S(1)}, u32[]{:S(2)}, u32[]{:S(2)}) collective-permute-start(bf16[168,2240]{1,0:T(8,128)(2,1)} %shard_map.47.refs_0_), channel_id=1, source_target_pairs={{8,16},{9,17},{10,18},{11,19},{12,20},{13,21},{14,22},{15,23},{16,... | collective-permute-start | bytes 2257928 | tf_op jit(solution)/shard_map/ppermute | solution.py:413
  47.8 21.3 %collective-permute-start.7 = (bf16[168,2240]{1,0:T(8,128)(2,1)}, bf16[168,2240]{1,0:T(8,128)(2,1)S(1)}, u32[]{:S(2)}, u32[]{:S(2)}) collective-permute-start(bf16[168,2240]{1,0:T(8,128)(2,1)} %collective-permute-done.3.refs_2_), channel_id=1, source_target_pairs={{8,0},{9,1},{10,2},{11,3},{12,4},{13,5},{14,6},{15,7},{16,24},{17,... | collective-permute-start | bytes 2257928 | tf_op jit(solution)/shard_map/ppermute | solution.py:413
  69.7 2.3 %collective-permute-start.10 = (bf16[168,2240]{1,0:T(8,128)(2,1)S(1)}, bf16[168,2240]{1,0:T(8,128)(2,1)S(1)}, u32[]{:S(2)}, u32[]{:S(2)}) collective-permute-start(bf16[168,2240]{1,0:T(8,128)(2,1)S(1)} %shard_map.51.refs_1_), channel_id=1, source_target_pairs={{0,1},{1,0},{2,3},{3,2},{4,5},{5,4},{6,7},{7,6},{8,9},{9,8},{10,11... | collective-permute-start | bytes 2257928 | tf_op jit(solution)/shard_map/ppermute | solution.py:413
  74.0 26.4 %collective-permute-start.19 = (bf16[448,512]{1,0:T(8,128)(2,1)S(1)}, bf16[448,512]{1,0:T(8,128)(2,1)S(1)}, u32[]{:S(2)}, u32[]{:S(2)}) collective-permute-start(bf16[448,512]{1,0:T(8,128)(2,1)S(1)} %shard_map.57.center.side), channel_id=1, source_target_pairs={{4,12},{5,13},{6,14},{7,15},{8,0},{9,1},{10,2},{11,3},{12,20},{13,... | collective-permute-start | bytes 1376264 | tf_op jit(solution)/shard_map/ppermute | solution.py:413
  77.3 30.6 %collective-permute-start.17 = (bf16[448,512]{1,0:T(8,128)(2,1)S(1)}, bf16[448,512]{1,0:T(8,128)(2,1)S(1)}, u32[]{:S(2)}, u32[]{:S(2)}) collective-permute-start(bf16[448,512]{1,0:T(8,128)(2,1)S(1)} %shard_map.53.side.center), channel_id=1, source_target_pairs={{0,8},{1,9},{2,10},{3,11},{8,16},{9,17},{10,18},{11,19},{12,4},{13... | collective-permute-start | bytes 1376264 | tf_op jit(solution)/shard_map/ppermute | solution.py:413
  84.3 16.1 %copy-start = (f32[3,4,1,112]{0,3,1,2:T(8,128)S(1)}, f32[3,4,1,112]{0,3,1,2:T(8,128)}, u32[]{:S(2)}) copy-start(f32[3,4,1,112]{0,3,1,2:T(8,128)} %copy.6) | copy-start | bytes 16132
  84.4 2.5 %collective-permute-start.11 = (f32[2,128,112]{2,1,0:T(8,128)S(1)}, f32[2,128,112]{2,1,0:T(8,128)S(1)}, u32[]{:S(2)}, u32[]{:S(2)}) collective-permute-start(f32[2,128,112]{2,1,0:T(8,128)S(1)} %shard_map.54), channel_id=1, source_target_pairs={{0,1},{1,0},{2,3},{3,2},{4,5},{5,4},{6,7},{7,6},{8,9},{9,8},{10,11... | collective-permute-start | bytes 344072 | tf_op jit(solution)/shard_map/ppermute | solution.py:413
  86.9 0.9 collective-permute-start.12
  87.8 4.6 %collective-permute-start.13 = (bf16[2,128,112]{2,1,0:T(8,128)(2,1)S(1)}, bf16[2,128,112]{2,1,0:T(8,128)(2,1)S(1)}, u32[]{:S(2)}, u32[]{:S(2)}) collective-permute-start(bf16[2,128,112]{2,1,0:T(8,128)(2,1)S(1)} %collective-permute-done.12.refs_0_), channel_id=1, source_target_pairs={{0,8},{1,9},{2,10},{3,11},{4,12},{5,13},{6,14},{7,15},{8,0},{9,1},... | collective-permute-start | bytes 172040 | tf_op jit(solution)/shard_map/ppermute | solution.py:413
  87.9 5.2 %collective-permute-start.14 = (bf16[2,128,112]{2,1,0:T(8,128)(2,1)S(1)}, bf16[2,128,112]{2,1,0:T(8,128)(2,1)S(1)}, u32[]{:S(2)}, u32[]{:S(2)}) collective-permute-start(bf16[2,128,112]{2,1,0:T(8,128)(2,1)S(1)} %collective-permute-done.12.refs_0_), channel_id=1, source_target_pairs={{0,16},{1,17},{2,18},{3,19},{4,20},{5,21},{6,22},{7,23},{8,24},{9,... | collective-permute-start | bytes 172040 | tf_op jit(solution)/shard_map/ppermute | solution.py:413
  88.6 6.7 %collective-permute-start.15 = (bf16[2,128,112]{2,1,0:T(8,128)(2,1)S(1)}, bf16[2,128,112]{2,1,0:T(8,128)(2,1)S(1)}, u32[]{:S(2)}, u32[]{:S(2)}) collective-permute-start(bf16[2,128,112]{2,1,0:T(8,128)(2,1)S(1)} %collective-permute-done.12.refs_0_), channel_id=1, source_target_pairs={{0,24},{1,25},{2,26},{3,27},{4,28},{5,29},{6,30},{7,31},{8,16},{9,... | collective-permute-start | bytes 172040 | tf_op jit(solution)/shard_map/ppermute | solution.py:413
  95.3 5.1 %collective-permute-start.16 = (f32[2,128,112]{2,1,0:T(8,128)S(1)}, f32[2,128,112]{2,1,0:T(8,128)S(1)}, u32[]{:S(2)}, u32[]{:S(2)}) collective-permute-start(f32[2,128,112]{2,1,0:T(8,128)S(1)} %shard_map.56.mine), channel_id=1, source_target_pairs={{0,1},{1,0},{2,3},{3,2},{4,5},{5,4},{6,7},{7,6},{8,9},{9,8},{10,11... | collective-permute-start | bytes 344072 | tf_op jit(solution)/shard_map/ppermute | solution.py:413
  102.7 15.7 %collective-permute-start.20 = (bf16[448,256]{1,0:T(8,128)(2,1)S(1)}, bf16[448,256]{1,0:T(8,128)(2,1)S(1)}, u32[]{:S(2)}, u32[]{:S(2)}) collective-permute-start(bf16[448,256]{1,0:T(8,128)(2,1)S(1)} %get-tuple-element.45), channel_id=1, source_target_pairs={{0,4},{1,5},{2,6},{3,7},{4,0},{5,1},{6,2},{7,3},{8,12},{9,13},{10,... | collective-permute-start | bytes 688136 | tf_op jit(solution)/shard_map/ppermute | solution.py:413
  107.6 10.8 %collective-permute-start.21 = (bf16[448,256]{1,0:T(8,128)(2,1)S(1)}, bf16[448,256]{1,0:T(8,128)(2,1)S(1)}, u32[]{:S(2)}, u32[]{:S(2)}) collective-permute-start(bf16[448,256]{1,0:T(8,128)(2,1)S(1)} %get-tuple-element.46), channel_id=1, source_target_pairs={{0,6},{1,7},{2,4},{3,5},{4,2},{5,3},{6,0},{7,1},{8,14},{9,15},{10,... | collective-permute-start | bytes 688136 | tf_op jit(solution)/shard_map/ppermute | solution.py:413
  110.1 9.6 %collective-permute-start.18 = (bf16[448,256]{1,0:T(8,128)(2,1)S(1)}, bf16[448,256]{1,0:T(8,128)(2,1)S(1)}, u32[]{:S(2)}, u32[]{:S(2)}) collective-permute-start(bf16[448,256]{1,0:T(8,128)(2,1)S(1)} %get-tuple-element.44), channel_id=1, source_target_pairs={{0,2},{1,3},{2,0},{3,1},{4,6},{5,7},{6,4},{7,5},{8,10},{9,11},{10,... | collective-permute-start | bytes 688136 | tf_op jit(solution)/shard_map/ppermute | solution.py:413

commit v4 on v3

--- a/solution.py
+++ b/solution.py
@@ -229,37 +229,27 @@
     )
 
 
-def late_kernel(core, place, part, *refs):
-    rows, last, *blocks, out, held, keys, values = refs
+def late_kernel(core, place, part, rows, last, *refs):
+    *blocks, out, held, keys, values = refs
     z = place[0]
     odd, keys_first = z % 2 == 1, z < 2
     held[:HDIM] = rows[:HDIM]
-    held[HDIM : 2 * HDIM] = last[:HDIM]
-    held[2 * HDIM :] = rows[HDIM:]
+    held[HDIM:] = last[:HDIM]
     tokens = blocks[0].shape[1]
     ones = (lax.broadcasted_iota(jnp.int32, (16, tokens), 0) == 0).astype(jnp.bfloat16)
-    contract = (((1,), (1,)), ((), ()))
     for k, block in enumerate(blocks):
-        final = k == len(blocks) - 1
-        weights = held[...] if final else held[: 2 * HDIM]
-        lin = jnp.dot(weights, block[...], preferred_element_type=jnp.float32)
+        lin = jnp.dot(held[...], block[...], preferred_element_type=jnp.float32)
         to = slice(tokens * k, tokens * (k + 1))
-        for i in range(2 if final else 1):
-            one, two = (lin[HDIM * j : HDIM * (j + 1)] for j in (2 * i, 2 * i + 1))
-            key = jnp.maximum(jnp.where(keys_first, one, two), 0.0).astype(jnp.bfloat16)
-            value = jnp.where(keys_first, two, one).astype(jnp.bfloat16)
-            if i == 0:
-                keys[:, to] = key
-                values[:HDIM, to] = value
-                values[HDIM:, to] = ones
-            else:
-                value = jnp.concatenate([value, ones], axis=0)
-                first = part[core] + lax.dot_general(
-                    value, key, contract, preferred_element_type=jnp.float32
-                )
-    total = lax.dot_general(values[...], keys[...], contract, preferred_element_type=jnp.float32)
-    out[0] = jnp.where(odd, total, first)
-    out[1] = jnp.where(odd, first, total)
+        one, two = lin[:HDIM], lin[HDIM:]
+        key = jnp.maximum(jnp.where(keys_first, one, two), 0.0)
+        keys[:, to] = key.astype(jnp.bfloat16)
+        values[:HDIM, to] = jnp.where(keys_first, two, one).astype(jnp.bfloat16)
+        values[HDIM:, to] = ones
+    total = lax.dot_general(
+        values[...], keys[...], (((1,), (1,)), ((), ())), preferred_element_type=jnp.float32
+    )
+    out[0] = jnp.where(odd, total, part[core])
+    out[1] = jnp.where(odd, part[core], total)
 
 
 def late_states(core, place, part, rows, last, blocks):
@@ -274,11 +264,11 @@
         last,
         *blocks,
         scratch=[
-            pltpu.VMEM((4 * HDIM, depth), jnp.bfloat16),
+            pltpu.VMEM((2 * HDIM, depth), jnp.bfloat16),
             pltpu.VMEM((HDIM, columns), jnp.bfloat16),
             pltpu.VMEM((HDIM + 16, columns), jnp.bfloat16),
         ],
-        flops=4 * HDIM * depth * (columns + tokens),
+        flops=4 * HDIM * depth * columns,
     )
 
 
@@ -293,37 +283,53 @@
     return kernel_call(sum_kernel, like(parts[0].shape, dtype), *parts, scalars=0)
 
 
-def query_kernel(place, *refs):
-    rows, last, last_there, block_0, block_1, out, held = refs
-    z = place[0]
+def query_heads(z, lin, first, one, two, out, columns):
     half = HDIM // 2
-    step = room_of(half)
-    for i, one in enumerate((last, last_there)):
-        at = LAYERS * step * i
-        held[at : at + 3 * step] = rows[3 * step * i : 3 * step * (i + 1)]
-        held[at + 3 * step : at + 4 * step] = spaced(one[HDIM:])
+    head = jnp.concatenate([lin[one : one + half], lin[two : two + half]], axis=0)
+    rows = pl.ds(pl.multiple_of((z ^ first) * HDIM, 16), HDIM)
+    out[rows, columns] = jnp.maximum(head, 0.0).astype(jnp.bfloat16)
+
+
+def near_query_kernel(place, rows, *refs):
+    *blocks, out = refs
+    step = rows.shape[0] // 6
+    tokens = blocks[0].shape[1]
+    for k, block in enumerate(blocks):
+        lin = jnp.dot(rows[...], block[...], preferred_element_type=jnp.float32)
+        for i in range(3):
+            columns = slice(tokens * k, tokens * (k + 1))
+            query_heads(place[0], lin, i, step * i, step * (3 + i), out, columns)
+
+
+def near_queries(place, rows, blocks):
+    tokens = blocks[0].shape[1]
+    return kernel_call(
+        near_query_kernel, like((LAYERS * HDIM, len(blocks) * tokens)), place, rows, *blocks
+    )
+
+
+def query_kernel(place, near, last, last_there, block_0, block_1, out, held):
+    step = held.shape[0] // 2
+    held[:step] = spaced(last[HDIM:])
+    held[step:] = spaced(last_there[HDIM:])
+    out[...] = near[...]
     tokens = block_0.shape[1]
     for k, block in enumerate((block_0, block_1)):
         lin = jnp.dot(held[...], block[...], preferred_element_type=jnp.float32)
-        for i in range(LAYERS):
-            one = lin[step * i : step * i + half]
-            two = lin[step * (LAYERS + i) : step * (LAYERS + i) + half]
-            head = jnp.maximum(jnp.concatenate([one, two], axis=0), 0.0).astype(jnp.bfloat16)
-            rows = pl.ds(pl.multiple_of((z ^ i) * HDIM, 16), HDIM)
-            out[rows, tokens * k : tokens * (k + 1)] = head
-
-
-def queries_of(place, rows, blocks):
-    depth, tokens = blocks[0].shape
-    height = 2 * LAYERS * room_of(HDIM // 2)
+        columns = slice(tokens * k, tokens * (k + 1))
+        query_heads(place[0], lin, 3, 0, step, out, columns)
+
+
+def queries_of(place, near, rows, blocks):
+    depth = blocks[0].shape[0]
     return kernel_call(
         query_kernel,
-        like((LAYERS * HDIM, 2 * tokens)),
+        like(near.shape),
         place,
+        near,
         *rows,
         *blocks,
-        scratch=[pltpu.VMEM((height, depth), jnp.bfloat16)],
-        flops=2 * height * depth * 2 * tokens,
+        scratch=[pltpu.VMEM((2 * room_of(HDIM // 2), depth), jnp.bfloat16)],
     )
 
 
@@ -454,24 +460,31 @@
     keyval, keyval_there, query = ready_rows(
         (weights, weights_1, weights_2), (weights_there, there_1, there_2)
     )
-    part = states_of(place, keyval, keyval_there, (own, beside, across))
-    diagonal, weights_inner, weights_outer, part = together(
-        diagonal, weights_inner, weights_outer, part
+    blocks = (own, beside, across, diagonal)
+    part = states_of(place, keyval, keyval_there, blocks)
+    near_here = near_queries(place, query, (own, beside))
+    near_there = near_queries(place, query, (across, diagonal))
+    diagonal, weights_inner, weights_outer, part, near_here, near_there = together(
+        diagonal, weights_inner, weights_outer, part, near_here, near_there
     )
 
     weights_3 = last_of(place, weights_inner, weights_outer)
     there_3 = swap(weights_3, 1)
-    blocks = (own, beside, across, diagonal)
     kept = late_states(0, place, part, keyval, weights_3, blocks)
-    rows = (query, weights_3, there_3)
-    here = queries_of(place, rows, (own, beside))
-    there = queries_of(place, rows, (across, diagonal))
-    there, part = together(there, part)
     given = late_states(1, place, part, keyval_there, there_3, blocks)
+    kept, given, near_here = together(kept, given, near_here)
+    rows = (weights_3, there_3)
+    here = queries_of(place, near_here, rows, (own, beside))
+    there = queries_of(place, near_there, rows, (across, diagonal))
     part = sum_of([kept, swap(given, 1)], STATE_SENT)
-    part = send(part, lambda z, slot: (z, 2 * (slot % 4) + slot // 4))
-    state = sum_of([part] + [between(part, cross[k]) for k in range(1, LAYERS)], jnp.float32)
-    state_there = swap(state, 1)
+    parts = [part] + [between(part, cross[k]) for k in range(1, LAYERS)]
+    here, parts[1] = together(here, parts[1])
+    there, *parts = together(there, *parts)
+    state = sum_of(parts, STATE_SENT)
+    state, state_there = (
+        send(state, lambda z, slot, flip=flip: (z, 2 * (slot % 4) + (slot // 4 ^ flip)))
+        for flip in range(2)
+    )
 
     def aside(value, row):
         def to(z, slot):

time: 122 us -> 113 us (0.926)
  starting transfers between devices: 33.8 us -> 28.6 us
  waiting for transfers between devices: 61.4 us -> 56.3 us
    ppermute x22, starting transfers between devices: 33.8 us -> 28.6 us  [send(): return lax.ppermute(value, 'frame', pairs)]
    ppermute x22, waiting for transfers between devices: 61.4 us -> 56.3 us  [send(): return lax.ppermute(value, 'frame', pairs)]
    pallas_call x14 -> x16, Pallas kernels: 22.3 us -> 23.5 us  [kernel_call(): pl.pallas_call(body, out_shape=outs, in_specs=[SMEM] * scalars + [VMEM] *...]
  transfers between devices with their start and end apart: 22 -> 22, of which waited for: 11 -> 12; matrix products, arithmetic and copies ran while one was open for 1% -> 1% of each run, Pallas kernels for 15% -> 17%
where the time goes in v4:
time: 113 us
  waiting for transfers between devices  56.3 us (50%)
  starting transfers between devices  28.6 us (25%)
  Pallas kernels  25.1 us (22%)
  local copies, waits for them, and re-layouts  2.23 us (2%)
    ppermute x22, waiting for transfers between devices, send(): return lax.ppermute(value, 'frame', pairs)  56.3 us
    ppermute x22, starting transfers between devices, send(): return lax.ppermute(value, 'frame', pairs)  28.6 us
    pallas_call x16, Pallas kernels, kernel_call(): pl.pallas_call(body, out_shape=outs, in_specs=[SMEM] * scalars + [VMEM] *...  23.5 us
  transfers between devices with their start and end apart: 22, of which 12 were waited for; matrix products, arithmetic and copies ran while one was open for 1% of the time, Pallas kernels for 17%

profile of v4, /device:TPU:0, one launch (start us, length us, event | category | flops | bytes accessed | tf_op | source)
XLA Modules:
  0.0 112.6 jit_solution(11354960731897332668)
XLA Ops:
  0.0 1.3 %copy-done.1 = bf16[256,2240]{0,1:T(8,128)(2,1)S(1)} copy-done((bf16[256,2240]{0,1:T(8,128)(2,1)S(1)}, bf16[256,2240]{0,1:T(8,128)(2,1)}, u32[]{:S(2)}) %copy-start.1) | copy-done | bytes 1146904
  1.3 0.3 shard_map.46.refs_0_.block_0
  1.6 3.0 %collective-permute-start = (bf16[2240,256]{1,0:T(8,128)(2,1)S(1)}, bf16[2240,256]{1,0:T(8,128)(2,1)S(1)}, u32[]{:S(2)}, u32[]{:S(2)}) collective-permute-start(bf16[2240,256]{1,0:T(8,128)(2,1)S(1)} %shard_map.46.refs_0_.block_0), channel_id=1, source_target_pairs={{0,2},{1,3},{2,0},{3,1},{4,6},{5,7},{6,4},{7,5},{8,10},{9,11},{10,... | collective-permute-start | bytes 3440648 | tf_op jit(solution)/shard_map/ppermute | solution.py:419
  4.6 1.5 %collective-permute-start.1 = (bf16[2240,256]{1,0:T(8,128)(2,1)S(1)}, bf16[2240,256]{1,0:T(8,128)(2,1)S(1)}, u32[]{:S(2)}, u32[]{:S(2)}) collective-permute-start(bf16[2240,256]{1,0:T(8,128)(2,1)S(1)} %shard_map.46.refs_0_.block_0), channel_id=1, source_target_pairs={{0,4},{1,5},{2,6},{3,7},{4,0},{5,1},{6,2},{7,3},{8,12},{9,13},{10,... | collective-permute-start | bytes 3440648 | tf_op jit(solution)/shard_map/ppermute | solution.py:419
  6.1 1.6 %shard_map.47.refs_0_ = bf16[168,2240]{1,0:T(8,128)(2,1)} custom-call(bf16[112,2240]{1,0:T(8,128)(2,1)S(1)} %copy-done.2, bf16[56,2240]{1,0:T(8,128)(2,1)S(1)} %copy-done.3), custom_call_target="tpu_custom_call" | custom-call | tf_op jit(solution)/shard_map/pallas_call | solution.py:148
  7.7 1.6 %collective-permute-start.2 = (bf16[168,2240]{1,0:T(8,128)(2,1)}, bf16[168,2240]{1,0:T(8,128)(2,1)}, u32[]{:S(2)}, u32[]{:S(2)}) collective-permute-start(bf16[168,2240]{1,0:T(8,128)(2,1)} %shard_map.47.refs_0_), channel_id=1, source_target_pairs={{0,8},{1,9},{2,10},{3,11},{4,12},{5,13},{6,14},{7,15},{8,0},{9,1},... | collective-permute-start | bytes 2257928 | tf_op jit(solution)/shard_map/ppermute | solution.py:419
  9.3 2.6 %collective-permute-start.3 = (bf16[168,2240]{1,0:T(8,128)(2,1)}, bf16[168,2240]{1,0:T(8,128)(2,1)}, u32[]{:S(2)}, u32[]{:S(2)}) collective-permute-start(bf16[168,2240]{1,0:T(8,128)(2,1)} %shard_map.47.refs_0_), channel_id=1, source_target_pairs={{0,16},{1,17},{2,18},{3,19},{4,20},{5,21},{6,22},{7,23},{8,24},{9,... | collective-permute-start | bytes 2257928 | tf_op jit(solution)/shard_map/ppermute | solution.py:419
  11.9 0.1 reshape.7
  12.0 0.8 copy.6
  12.9 0.1 pad_add_fusion.place
  13.0 30.0 %collective-permute-done.2.refs_1_ = bf16[168,2240]{1,0:T(8,128)(2,1)} collective-permute-done((bf16[168,2240]{1,0:T(8,128)(2,1)}, bf16[168,2240]{1,0:T(8,128)(2,1)}, u32[]{:S(2)}, u32[]{:S(2)}) %collective-permute-start.2) | collective-permute-done | bytes 752672 | tf_op jit(solution)/shard_map/ppermute | solution.py:419
  43.0 2.4 %collective-permute-done.3.refs_2_ = bf16[168,2240]{1,0:T(8,128)(2,1)} collective-permute-done((bf16[168,2240]{1,0:T(8,128)(2,1)}, bf16[168,2240]{1,0:T(8,128)(2,1)}, u32[]{:S(2)}, u32[]{:S(2)}) %collective-permute-start.3) | collective-permute-done | bytes 752672 | tf_op jit(solution)/shard_map/ppermute | solution.py:419
  45.4 0.6 shard_map.48
  46.0 0.6 collective-permute-start.5
  46.6 0.5 collective-permute-start.9
  47.1 0.7 collective-permute-start.6
  47.8 1.3 %collective-permute-start.7 = (bf16[168,2240]{1,0:T(8,128)(2,1)}, bf16[168,2240]{1,0:T(8,128)(2,1)S(1)}, u32[]{:S(2)}, u32[]{:S(2)}) collective-permute-start(bf16[168,2240]{1,0:T(8,128)(2,1)} %collective-permute-done.3.refs_2_), channel_id=1, source_target_pairs={{8,0},{9,1},{10,2},{11,3},{12,4},{13,5},{14,6},{15,7},{16,24},{17,... | collective-permute-start | bytes 2257928 | tf_op jit(solution)/shard_map/ppermute | solution.py:419
  49.1 1.1 collective-permute-done.9.refs_5_
  50.2 2.1 %shard_map.49 = (bf16[336,2240]{1,0:T(8,128)(2,1)S(1)}, bf16[336,2240]{1,0:T(8,128)(2,1)S(1)}, bf16[384,2240]{1,0:T(8,128)(2,1)S(1)}) custom-call(bf16[168,2240]{1,0:T(8,128)(2,1)} %shard_map.47.refs_0_, bf16[168,2240]{1,0:T(8,128)(2,1)} %collective-permute-done.2.refs_1_, bf16[168,2240]{1,0:T(8,128)(2,1)} %collective-permute-done.3.refs_2_, ...), custom_call_target="tpu_custom_call" | custom-call | bytes 4515840 | tf_op jit(solution)/shard_map/pallas_call | solution.py:79
  52.4 1.6 %shard_map.51.near = bf16[448,512]{1,0:T(8,128)(2,1)S(1)} custom-call(s32[2]{0:T(128)S(1)} %pad_add_fusion.place, bf16[384,2240]{1,0:T(8,128)(2,1)S(1)} %get-tuple-element.45.rows, bf16[2240,256]{1,0:T(8,128)(2,1)S(1)} %shard_map.46.refs_0_.block_0, bf16[2240,256]{1,0:T(8,128)(2,1)S(1)} %collective-permute-done.beside.refs_1_.block_1), custom_call_target="tpu_custom_call" | custom-call | bytes 4014088 | tf_op jit(solution)/shard_map/pallas_call | solution.py:79
  54.0 7.9 %collective-permute-done.5.refs_3_.refs_1_.block_1 = bf16[2240,256]{1,0:T(8,128)(2,1)S(1)} collective-permute-done((bf16[2240,256]{1,0:T(8,128)(2,1)S(1)}, bf16[2240,256]{1,0:T(8,128)(2,1)S(1)}, u32[]{:S(2)}, u32[]{:S(2)}) %collective-permute-start.5) | collective-permute-done | bytes 1146912 | tf_op jit(solution)/shard_map/ppermute | solution.py:419
  61.9 1.6 %shard_map.52.near = bf16[448,512]{1,0:T(8,128)(2,1)S(1)} custom-call(s32[2]{0:T(128)S(1)} %pad_add_fusion.place, bf16[384,2240]{1,0:T(8,128)(2,1)S(1)} %get-tuple-element.45.rows, bf16[2240,256]{1,0:T(8,128)(2,1)S(1)} %collective-permute-done.1.across.refs_2_.refs_0_.block_0, bf16[2240,256]{1,0:T(8,128)(2,1)S(1)} %collective-permute-done.5.refs_3_.refs_1_.block_1), custom_call_target="tpu_custom_call" | custom-call | bytes 4014088 | tf_op jit(solution)/shard_map/pallas_call | solution.py:79
  63.6 4.1 %shard_map.50.part = f32[2,128,112]{2,1,0:T(8,128)S(1)} custom-call(s32[2]{0:T(128)S(1)} %pad_add_fusion.place, bf16[336,2240]{1,0:T(8,128)(2,1)S(1)} %get-tuple-element.42.mine.rows, bf16[336,2240]{1,0:T(8,128)(2,1)S(1)} %get-tuple-element.43.there.rows, bf16[2240,256]{1,0:T(8,128)(2,1)S(1)} %shard_map.46.refs_0_.block_0, ...), custom_call_target="tpu_custom_call" | custom-call | flops 2055208960 | bytes 7598088 | tf_op jit(solution)/shard_map/pallas_call | solution.py:79
  67.7 1.5 %collective-permute-done.7.outer = bf16[168,2240]{1,0:T(8,128)(2,1)S(1)} collective-permute-done((bf16[168,2240]{1,0:T(8,128)(2,1)}, bf16[168,2240]{1,0:T(8,128)(2,1)S(1)}, u32[]{:S(2)}, u32[]{:S(2)}) %collective-permute-start.7) | collective-permute-done | bytes 752672 | tf_op jit(solution)/shard_map/ppermute | solution.py:419
  69.1 0.6 shard_map.53.last
  69.8 2.0 %shard_map.55.refs_0_ = f32[2,128,112]{2,1,0:T(8,128)S(1)} custom-call(s32[2]{0:T(128)S(1)} %pad_add_fusion.place, f32[2,128,112]{2,1,0:T(8,128)S(1)} %shard_map.50.part, bf16[336,2240]{1,0:T(8,128)(2,1)S(1)} %get-tuple-element.42.mine.rows, bf16[168,2240]{1,0:T(8,128)(2,1)S(1)} %shard_map.53.last, bf16[2240,256]{1,0:T(8,128)(2,1)S(1)} %shard_map.46.refs_0_.block_0, ...), custom_call_target="tpu_custom_call" | custom-call | flops 1027604480 | bytes 6960136 | tf_op jit(solution)/shard_map/pallas_call | solution.py:79
  71.8 0.2 collective-permute-done.10.last_there.last
  72.1 2.0 %shard_map.56 = f32[2,128,112]{2,1,0:T(8,128)S(1)} custom-call(s32[2]{0:T(128)S(1)} %pad_add_fusion.place, f32[2,128,112]{2,1,0:T(8,128)S(1)} %shard_map.50.part, bf16[336,2240]{1,0:T(8,128)(2,1)S(1)} %get-tuple-element.43.there.rows, bf16[168,2240]{1,0:T(8,128)(2,1)S(1)} %collective-permute-done.10.last_there.last, ...), custom_call_target="tpu_custom_call" | custom-call | flops 1027604480 | bytes 6960136 | tf_op jit(solution)/shard_map/pallas_call | solution.py:79
  74.1 0.3 collective-permute-start.11
  74.4 1.1 collective-permute-done.11.refs_1_
  75.6 3.0 %collective-permute-start.13 = (bf16[2,128,112]{2,1,0:T(8,128)(2,1)S(1)}, bf16[2,128,112]{2,1,0:T(8,128)(2,1)S(1)}, u32[]{:S(2)}, u32[]{:S(2)}) collective-permute-start(bf16[2,128,112]{2,1,0:T(8,128)(2,1)S(1)} %shard_map.57.refs_0_), channel_id=1, source_target_pairs={{0,16},{1,17},{2,18},{3,19},{4,20},{5,21},{6,22},{7,23},{8,24},{9,... | collective-permute-start | bytes 172040 | tf_op jit(solution)/shard_map/ppermute | solution.py:419
  78.6 1.4 %collective-permute-start.14 = (bf16[2,128,112]{2,1,0:T(8,128)(2,1)S(1)}, bf16[2,128,112]{2,1,0:T(8,128)(2,1)S(1)}, u32[]{:S(2)}, u32[]{:S(2)}) collective-permute-start(bf16[2,128,112]{2,1,0:T(8,128)(2,1)S(1)} %shard_map.57.refs_0_), channel_id=1, source_target_pairs={{0,24},{1,25},{2,26},{3,27},{4,28},{5,29},{6,30},{7,31},{8,16},{9,... | collective-permute-start | bytes 172040 | tf_op jit(solution)/shard_map/ppermute | solution.py:419
  80.0 1.0 shard_map.58.center.side
  81.0 1.0 shard_map.54.side.center
  82.1 1.3 %collective-permute-start.19 = (bf16[448,512]{1,0:T(8,128)(2,1)S(1)}, bf16[448,512]{1,0:T(8,128)(2,1)S(1)}, u32[]{:S(2)}, u32[]{:S(2)}) collective-permute-start(bf16[448,512]{1,0:T(8,128)(2,1)S(1)} %shard_map.58.center.side), channel_id=1, source_target_pairs={{4,12},{5,13},{6,14},{7,15},{8,0},{9,1},{10,2},{11,3},{12,20},{13,... | collective-permute-start | bytes 1376264 | tf_op jit(solution)/shard_map/ppermute | solution.py:419
  83.4 1.4 %collective-permute-done.14.refs_3_ = bf16[2,128,112]{2,1,0:T(8,128)(2,1)S(1)} collective-permute-done((bf16[2,128,112]{2,1,0:T(8,128)(2,1)S(1)}, bf16[2,128,112]{2,1,0:T(8,128)(2,1)S(1)}, u32[]{:S(2)}, u32[]{:S(2)}) %collective-permute-start.14) | collective-permute-done | bytes 57376 | tf_op jit(solution)/shard_map/ppermute | solution.py:419
  84.8 3.2 %collective-permute-start.17 = (bf16[448,512]{1,0:T(8,128)(2,1)S(1)}, bf16[448,512]{1,0:T(8,128)(2,1)S(1)}, u32[]{:S(2)}, u32[]{:S(2)}) collective-permute-start(bf16[448,512]{1,0:T(8,128)(2,1)S(1)} %shard_map.54.side.center), channel_id=1, source_target_pairs={{0,8},{1,9},{2,10},{3,11},{8,16},{9,17},{10,18},{11,19},{12,4},{13... | collective-permute-start | bytes 1376264 | tf_op jit(solution)/shard_map/ppermute | solution.py:419
  88.0 0.7 collective-permute-start.15
  88.7 3.1 %collective-permute-start.16 = (bf16[2,128,112]{2,1,0:T(8,128)(2,1)S(1)}, bf16[2,128,112]{2,1,0:T(8,128)(2,1)S(1)}, u32[]{:S(2)}, u32[]{:S(2)}) collective-permute-start(bf16[2,128,112]{2,1,0:T(8,128)(2,1)S(1)} %shard_map.59), channel_id=1, source_target_pairs={{0,1},{1,3},{2,5},{3,7},{4,0},{5,2},{6,4},{7,6},{8,9},{9,11},{10,1... | collective-permute-start | bytes 172040 | tf_op jit(solution)/shard_map/ppermute | solution.py:419
  91.8 1.6 %collective-permute-done.16.there = bf16[2,128,112]{2,1,0:T(8,128)(2,1)S(1)} collective-permute-done((bf16[2,128,112]{2,1,0:T(8,128)(2,1)S(1)}, bf16[2,128,112]{2,1,0:T(8,128)(2,1)S(1)}, u32[]{:S(2)}, u32[]{:S(2)}) %collective-permute-start.16) | collective-permute-done | bytes 57376 | tf_op jit(solution)/shard_map/ppermute | solution.py:419
  93.4 2.5 %collective-permute-done.19.halo = bf16[448,512]{1,0:T(8,128)(2,1)S(1)} collective-permute-done((bf16[448,512]{1,0:T(8,128)(2,1)S(1)}, bf16[448,512]{1,0:T(8,128)(2,1)S(1)}, u32[]{:S(2)}, u32[]{:S(2)}) %collective-permute-start.19) | collective-permute-done | bytes 458784 | tf_op jit(solution)/shard_map/ppermute | solution.py:419
  95.8 2.2 %shard_map.61 = (bf16[448,256]{1,0:T(8,128)(2,1)S(1)}, bf16[448,256]{1,0:T(8,128)(2,1)S(1)}) custom-call(s32[2]{0:T(128)S(1)} %pad_add_fusion.place, bf16[2,128,112]{2,1,0:T(8,128)(2,1)S(1)} %collective-permute-done.15.mine, bf16[2,128,112]{2,1,0:T(8,128)(2,1)S(1)} %collective-permute-done.16.there, f32[448,3]{1,0:T(8,128)S(1)} %bitcast.6, ...), custom_call_target="tpu_custom_call" | custom-call | bytes 1496328 | tf_op jit(solution)/shard_map/pallas_call | solution.py:79
  98.1 2.9 %collective-permute-start.21 = (bf16[448,256]{1,0:T(8,128)(2,1)S(1)}, bf16[448,256]{1,0:T(8,128)(2,1)S(1)}, u32[]{:S(2)}, u32[]{:S(2)}) collective-permute-start(bf16[448,256]{1,0:T(8,128)(2,1)S(1)} %get-tuple-element.66), channel_id=1, source_target_pairs={{0,6},{1,7},{2,4},{3,5},{4,2},{5,3},{6,0},{7,1},{8,14},{9,15},{10,... | collective-permute-start | bytes 688136 | tf_op jit(solution)/shard_map/ppermute | solution.py:419
  101.1 2.2 %shard_map.60 = (bf16[448,256]{1,0:T(8,128)(2,1)S(1)}, bf16[448,256]{1,0:T(8,128)(2,1)S(1)}) custom-call(s32[2]{0:T(128)S(1)} %pad_add_fusion.place, bf16[2,128,112]{2,1,0:T(8,128)(2,1)S(1)} %collective-permute-done.15.mine, bf16[2,128,112]{2,1,0:T(8,128)(2,1)S(1)} %collective-permute-done.16.there, f32[448,3]{1,0:T(8,128)S(1)} %bitcast.7, ...), custom_call_target="tpu_custom_call" | custom-call | bytes 1496328 | tf_op jit(solution)/shard_map/pallas_call | solution.py:79
  103.3 0.6 collective-permute-start.18
  103.9 5.4 %collective-permute-done.20.refs_2_ = bf16[448,256]{1,0:T(8,128)(2,1)S(1)} collective-permute-done((bf16[448,256]{1,0:T(8,128)(2,1)S(1)}, bf16[448,256]{1,0:T(8,128)(2,1)S(1)}, u32[]{:S(2)}, u32[]{:S(2)}) %collective-permute-start.20) | collective-permute-done | bytes 229408 | tf_op jit(solution)/shard_map/ppermute | solution.py:419
  109.3 1.3 %collective-permute-done.18.refs_1_ = bf16[448,256]{1,0:T(8,128)(2,1)S(1)} collective-permute-done((bf16[448,256]{1,0:T(8,128)(2,1)S(1)}, bf16[448,256]{1,0:T(8,128)(2,1)S(1)}, u32[]{:S(2)}, u32[]{:S(2)}) %collective-permute-start.18) | collective-permute-done | bytes 229408 | tf_op jit(solution)/shard_map/ppermute | solution.py:419
  110.6 2.0 %shard_map.62 = bf16[256,1792]{1,0:T(8,128)(2,1)} custom-call(s32[2]{0:T(128)S(1)} %pad_add_fusion.place, bf16[448,256]{1,0:T(8,128)(2,1)S(1)} %get-tuple-element.63.refs_0_, bf16[448,256]{1,0:T(8,128)(2,1)S(1)} %collective-permute-done.18.refs_1_, bf16[448,256]{1,0:T(8,128)(2,1)S(1)} %collective-permute-done.20.refs_2_, ...), custom_call_target="tpu_custom_call" | custom-call | bytes 917512 | tf_op jit(solution)/shard_map/pallas_call | solution.py:79
  (27 shorter events, 0.3 us)
Async XLA Ops:
  0.0 1.3 %copy-start.1 = (bf16[256,2240]{0,1:T(8,128)(2,1)S(1)}, bf16[256,2240]{0,1:T(8,128)(2,1)}, u32[]{:S(2)}) copy-start(bf16[256,2240]{0,1:T(8,128)(2,1)} %param.4) | copy-start | bytes 3440644
  1.3 4.8 %copy-start.2 = (bf16[112,2240]{1,0:T(8,128)(2,1)S(1)}, bf16[112,2240]{1,0:T(8,128)(2,1)}, u32[]{:S(2)}) copy-start(bf16[112,2240]{1,0:T(8,128)(2,1)} %w_keyval.1) | copy-start | bytes 1505284
  1.3 4.8 %copy-start.3 = (bf16[56,2240]{1,0:T(8,128)(2,1)S(1)}, bf16[56,2240]{1,0:T(8,128)(2,1)}, u32[]{:S(2)}) copy-start(bf16[56,2240]{1,0:T(8,128)(2,1)} %w_query.1) | copy-start | bytes 752644
  1.6 10.4 %copy-start.4 = (f32[3,1792]{1,0:T(4,128)S(1)}, f32[3,1792]{1,0:T(4,128)}, u32[]{:S(2)}) copy-start(f32[3,1792]{1,0:T(4,128)} %param.7) | copy-start | bytes 64516
  1.6 43.8 %collective-permute-start = (bf16[2240,256]{1,0:T(8,128)(2,1)S(1)}, bf16[2240,256]{1,0:T(8,128)(2,1)S(1)}, u32[]{:S(2)}, u32[]{:S(2)}) collective-permute-start(bf16[2240,256]{1,0:T(8,128)(2,1)S(1)} %shard_map.46.refs_0_.block_0), channel_id=1, source_target_pairs={{0,2},{1,3},{2,0},{3,1},{4,6},{5,7},{6,4},{7,5},{8,10},{9,11},{10,... | collective-permute-start | bytes 3440648 | tf_op jit(solution)/shard_map/ppermute | solution.py:419
  4.6 40.8 %collective-permute-start.1 = (bf16[2240,256]{1,0:T(8,128)(2,1)S(1)}, bf16[2240,256]{1,0:T(8,128)(2,1)S(1)}, u32[]{:S(2)}, u32[]{:S(2)}) collective-permute-start(bf16[2240,256]{1,0:T(8,128)(2,1)S(1)} %shard_map.46.refs_0_.block_0), channel_id=1, source_target_pairs={{0,4},{1,5},{2,6},{3,7},{4,0},{5,1},{6,2},{7,3},{8,12},{9,13},{10,... | collective-permute-start | bytes 3440648 | tf_op jit(solution)/shard_map/ppermute | solution.py:419
  7.7 35.3 %collective-permute-start.2 = (bf16[168,2240]{1,0:T(8,128)(2,1)}, bf16[168,2240]{1,0:T(8,128)(2,1)}, u32[]{:S(2)}, u32[]{:S(2)}) collective-permute-start(bf16[168,2240]{1,0:T(8,128)(2,1)} %shard_map.47.refs_0_), channel_id=1, source_target_pairs={{0,8},{1,9},{2,10},{3,11},{4,12},{5,13},{6,14},{7,15},{8,0},{9,1},... | collective-permute-start | bytes 2257928 | tf_op jit(solution)/shard_map/ppermute | solution.py:419
  9.3 36.0 %collective-permute-start.3 = (bf16[168,2240]{1,0:T(8,128)(2,1)}, bf16[168,2240]{1,0:T(8,128)(2,1)}, u32[]{:S(2)}, u32[]{:S(2)}) collective-permute-start(bf16[168,2240]{1,0:T(8,128)(2,1)} %shard_map.47.refs_0_), channel_id=1, source_target_pairs={{0,16},{1,17},{2,18},{3,19},{4,20},{5,21},{6,22},{7,23},{8,24},{9,... | collective-permute-start | bytes 2257928 | tf_op jit(solution)/shard_map/ppermute | solution.py:419
  11.9 33.5 %collective-permute-start.4 = (bf16[168,2240]{1,0:T(8,128)(2,1)}, bf16[168,2240]{1,0:T(8,128)(2,1)}, u32[]{:S(2)}, u32[]{:S(2)}) collective-permute-start(bf16[168,2240]{1,0:T(8,128)(2,1)} %shard_map.47.refs_0_), channel_id=1, source_target_pairs={{0,1},{1,0},{2,3},{3,2},{4,5},{5,4},{6,7},{7,6},{8,9},{9,8},{10,11... | collective-permute-start | bytes 2257928 | tf_op jit(solution)/shard_map/ppermute | solution.py:419
  46.0 15.9 %collective-permute-start.5 = (bf16[2240,256]{1,0:T(8,128)(2,1)S(1)}, bf16[2240,256]{1,0:T(8,128)(2,1)S(1)}, u32[]{:S(2)}, u32[]{:S(2)}) collective-permute-start(bf16[2240,256]{1,0:T(8,128)(2,1)S(1)} %shard_map.48), channel_id=1, source_target_pairs={{0,2},{1,5},{2,0},{3,7},{4,6},{5,1},{6,4},{7,3},{8,10},{9,13},{10,... | collective-permute-start | bytes 3440648 | tf_op jit(solution)/shard_map/ppermute | solution.py:419
  46.6 2.5 %collective-permute-start.8 = (bf16[168,2240]{1,0:T(8,128)(2,1)}, bf16[168,2240]{1,0:T(8,128)(2,1)S(1)}, u32[]{:S(2)}, u32[]{:S(2)}) collective-permute-start(bf16[168,2240]{1,0:T(8,128)(2,1)} %collective-permute-done.2.refs_1_), channel_id=1, source_target_pairs={{0,1},{1,0},{2,3},{3,2},{4,5},{5,4},{6,7},{7,6},{8,9},{9,8},{10,11... | collective-permute-start | bytes 2257928 | tf_op jit(solution)/shard_map/ppermute | solution.py:419
  46.6 3.6 %collective-permute-start.9 = (bf16[168,2240]{1,0:T(8,128)(2,1)}, bf16[168,2240]{1,0:T(8,128)(2,1)S(1)}, u32[]{:S(2)}, u32[]{:S(2)}) collective-permute-start(bf16[168,2240]{1,0:T(8,128)(2,1)} %collective-permute-done.3.refs_2_), channel_id=1, source_target_pairs={{0,1},{1,0},{2,3},{3,2},{4,5},{5,4},{6,7},{7,6},{8,9},{9,8},{10,11... | collective-permute-start | bytes 2257928 | tf_op jit(solution)/shard_map/ppermute | solution.py:419
  47.1 20.5 %collective-permute-start.6 = (bf16[168,2240]{1,0:T(8,128)(2,1)}, bf16[168,2240]{1,0:T(8,128)(2,1)S(1)}, u32[]{:S(2)}, u32[]{:S(2)}) collective-permute-start(bf16[168,2240]{1,0:T(8,128)(2,1)} %shard_map.47.refs_0_), channel_id=1, source_target_pairs={{8,16},{9,17},{10,18},{11,19},{12,20},{13,21},{14,22},{15,23},{16,... | collective-permute-start | bytes 2257928 | tf_op jit(solution)/shard_map/ppermute | solution.py:419
  47.8 21.3 %collective-permute-start.7 = (bf16[168,2240]{1,0:T(8,128)(2,1)}, bf16[168,2240]{1,0:T(8,128)(2,1)S(1)}, u32[]{:S(2)}, u32[]{:S(2)}) collective-permute-start(bf16[168,2240]{1,0:T(8,128)(2,1)} %collective-permute-done.3.refs_2_), channel_id=1, source_target_pairs={{8,0},{9,1},{10,2},{11,3},{12,4},{13,5},{14,6},{15,7},{16,24},{17,... | collective-permute-start | bytes 2257928 | tf_op jit(solution)/shard_map/ppermute | solution.py:419
  69.7 2.3 %collective-permute-start.10 = (bf16[168,2240]{1,0:T(8,128)(2,1)S(1)}, bf16[168,2240]{1,0:T(8,128)(2,1)S(1)}, u32[]{:S(2)}, u32[]{:S(2)}) collective-permute-start(bf16[168,2240]{1,0:T(8,128)(2,1)S(1)} %shard_map.53.last), channel_id=1, source_target_pairs={{0,1},{1,0},{2,3},{3,2},{4,5},{5,4},{6,7},{7,6},{8,9},{9,8},{10,11... | collective-permute-start | bytes 2257928 | tf_op jit(solution)/shard_map/ppermute | solution.py:419
  74.1 1.4 %collective-permute-start.11 = (f32[2,128,112]{2,1,0:T(8,128)S(1)}, f32[2,128,112]{2,1,0:T(8,128)S(1)}, u32[]{:S(2)}, u32[]{:S(2)}) collective-permute-start(f32[2,128,112]{2,1,0:T(8,128)S(1)} %shard_map.56), channel_id=1, source_target_pairs={{0,1},{1,0},{2,3},{3,2},{4,5},{5,4},{6,7},{7,6},{8,9},{9,8},{10,11... | collective-permute-start | bytes 344072 | tf_op jit(solution)/shard_map/ppermute | solution.py:419
  75.5 6.6 %collective-permute-start.12 = (bf16[2,128,112]{2,1,0:T(8,128)(2,1)S(1)}, bf16[2,128,112]{2,1,0:T(8,128)(2,1)S(1)}, u32[]{:S(2)}, u32[]{:S(2)}) collective-permute-start(bf16[2,128,112]{2,1,0:T(8,128)(2,1)S(1)} %shard_map.57.refs_0_), channel_id=1, source_target_pairs={{0,8},{1,9},{2,10},{3,11},{4,12},{5,13},{6,14},{7,15},{8,0},{9,1},... | collective-permute-start | bytes 172040 | tf_op jit(solution)/shard_map/ppermute | solution.py:419
  75.6 7.8 %collective-permute-start.13 = (bf16[2,128,112]{2,1,0:T(8,128)(2,1)S(1)}, bf16[2,128,112]{2,1,0:T(8,128)(2,1)S(1)}, u32[]{:S(2)}, u32[]{:S(2)}) collective-permute-start(bf16[2,128,112]{2,1,0:T(8,128)(2,1)S(1)} %shard_map.57.refs_0_), channel_id=1, source_target_pairs={{0,16},{1,17},{2,18},{3,19},{4,20},{5,21},{6,22},{7,23},{8,24},{9,... | collective-permute-start | bytes 172040 | tf_op jit(solution)/shard_map/ppermute | solution.py:419
  78.6 6.2 %collective-permute-start.14 = (bf16[2,128,112]{2,1,0:T(8,128)(2,1)S(1)}, bf16[2,128,112]{2,1,0:T(8,128)(2,1)S(1)}, u32[]{:S(2)}, u32[]{:S(2)}) collective-permute-start(bf16[2,128,112]{2,1,0:T(8,128)(2,1)S(1)} %shard_map.57.refs_0_), channel_id=1, source_target_pairs={{0,24},{1,25},{2,26},{3,27},{4,28},{5,29},{6,30},{7,31},{8,16},{9,... | collective-permute-start | bytes 172040 | tf_op jit(solution)/shard_map/ppermute | solution.py:419
  81.0 14.8 %copy-start = (f32[3,4,1,112]{0,3,1,2:T(8,128)S(1)}, f32[3,4,1,112]{0,3,1,2:T(8,128)}, u32[]{:S(2)}) copy-start(f32[3,4,1,112]{0,3,1,2:T(8,128)} %copy.6) | copy-start | bytes 16132
  82.1 13.7 %collective-permute-start.19 = (bf16[448,512]{1,0:T(8,128)(2,1)S(1)}, bf16[448,512]{1,0:T(8,128)(2,1)S(1)}, u32[]{:S(2)}, u32[]{:S(2)}) collective-permute-start(bf16[448,512]{1,0:T(8,128)(2,1)S(1)} %shard_map.58.center.side), channel_id=1, source_target_pairs={{4,12},{5,13},{6,14},{7,15},{8,0},{9,1},{10,2},{11,3},{12,20},{13,... | collective-permute-start | bytes 1376264 | tf_op jit(solution)/shard_map/ppermute | solution.py:419
  84.8 16.3 %collective-permute-start.17 = (bf16[448,512]{1,0:T(8,128)(2,1)S(1)}, bf16[448,512]{1,0:T(8,128)(2,1)S(1)}, u32[]{:S(2)}, u32[]{:S(2)}) collective-permute-start(bf16[448,512]{1,0:T(8,128)(2,1)S(1)} %shard_map.54.side.center), channel_id=1, source_target_pairs={{0,8},{1,9},{2,10},{3,11},{8,16},{9,17},{10,18},{11,19},{12,4},{13... | collective-permute-start | bytes 1376264 | tf_op jit(solution)/shard_map/ppermute | solution.py:419
  88.0 3.8 %collective-permute-start.15 = (bf16[2,128,112]{2,1,0:T(8,128)(2,1)S(1)}, bf16[2,128,112]{2,1,0:T(8,128)(2,1)S(1)}, u32[]{:S(2)}, u32[]{:S(2)}) collective-permute-start(bf16[2,128,112]{2,1,0:T(8,128)(2,1)S(1)} %shard_map.59), channel_id=1, source_target_pairs={{0,0},{1,2},{2,4},{3,6},{4,1},{5,3},{6,5},{7,7},{8,8},{9,10},{10,1... | collective-permute-start | bytes 172040 | tf_op jit(solution)/shard_map/ppermute | solution.py:419
  88.7 4.6 %collective-permute-start.16 = (bf16[2,128,112]{2,1,0:T(8,128)(2,1)S(1)}, bf16[2,128,112]{2,1,0:T(8,128)(2,1)S(1)}, u32[]{:S(2)}, u32[]{:S(2)}) collective-permute-start(bf16[2,128,112]{2,1,0:T(8,128)(2,1)S(1)} %shard_map.59), channel_id=1, source_target_pairs={{0,1},{1,3},{2,5},{3,7},{4,0},{5,2},{6,4},{7,6},{8,9},{9,11},{10,1... | collective-permute-start | bytes 172040 | tf_op jit(solution)/shard_map/ppermute | solution.py:419
  98.0 11.2 %collective-permute-start.20 = (bf16[448,256]{1,0:T(8,128)(2,1)S(1)}, bf16[448,256]{1,0:T(8,128)(2,1)S(1)}, u32[]{:S(2)}, u32[]{:S(2)}) collective-permute-start(bf16[448,256]{1,0:T(8,128)(2,1)S(1)} %get-tuple-element.65), channel_id=1, source_target_pairs={{0,4},{1,5},{2,6},{3,7},{4,0},{5,1},{6,2},{7,3},{8,12},{9,13},{10,... | collective-permute-start | bytes 688136 | tf_op jit(solution)/shard_map/ppermute | solution.py:419
  98.1 11.2 %collective-permute-start.21 = (bf16[448,256]{1,0:T(8,128)(2,1)S(1)}, bf16[448,256]{1,0:T(8,128)(2,1)S(1)}, u32[]{:S(2)}, u32[]{:S(2)}) collective-permute-start(bf16[448,256]{1,0:T(8,128)(2,1)S(1)} %get-tuple-element.66), channel_id=1, source_target_pairs={{0,6},{1,7},{2,4},{3,5},{4,2},{5,3},{6,0},{7,1},{8,14},{9,15},{10,... | collective-permute-start | bytes 688136 | tf_op jit(solution)/shard_map/ppermute | solution.py:419
  103.3 7.3 %collective-permute-start.18 = (bf16[448,256]{1,0:T(8,128)(2,1)S(1)}, bf16[448,256]{1,0:T(8,128)(2,1)S(1)}, u32[]{:S(2)}, u32[]{:S(2)}) collective-permute-start(bf16[448,256]{1,0:T(8,128)(2,1)S(1)} %get-tuple-element.64), channel_id=1, source_target_pairs={{0,2},{1,3},{2,0},{3,1},{4,6},{5,7},{6,4},{7,5},{8,10},{9,11},{10,... | collective-permute-start | bytes 688136 | tf_op jit(solution)/shard_map/ppermute | solution.py:419

commit v5 on v4

--- a/solution.py
+++ b/solution.py
@@ -283,10 +283,13 @@
     return kernel_call(sum_kernel, like(parts[0].shape, dtype), *parts, scalars=0)
 
 
-def query_heads(z, lin, first, one, two, out, columns):
+def query_heads(place, lin, first, one, two, out, columns):
     half = HDIM // 2
-    head = jnp.concatenate([lin[one : one + half], lin[two : two + half]], axis=0)
-    rows = pl.ds(pl.multiple_of((z ^ first) * HDIM, 16), HDIM)
+    one, two = lin[one : one + half], lin[two : two + half]
+    turned = place[1] % 2 == 1
+    head = [jnp.where(turned, two, one), jnp.where(turned, one, two)]
+    head = jnp.concatenate(head, axis=0)
+    rows = pl.ds(pl.multiple_of((place[0] ^ first) * HDIM, 16), HDIM)
     out[rows, columns] = jnp.maximum(head, 0.0).astype(jnp.bfloat16)
 
 
@@ -298,7 +301,7 @@
         lin = jnp.dot(rows[...], block[...], preferred_element_type=jnp.float32)
         for i in range(3):
             columns = slice(tokens * k, tokens * (k + 1))
-            query_heads(place[0], lin, i, step * i, step * (3 + i), out, columns)
+            query_heads(place, lin, i, step * i, step * (3 + i), out, columns)
 
 
 def near_queries(place, rows, blocks):
@@ -317,7 +320,7 @@
     for k, block in enumerate((block_0, block_1)):
         lin = jnp.dot(held[...], block[...], preferred_element_type=jnp.float32)
         columns = slice(tokens * k, tokens * (k + 1))
-        query_heads(place[0], lin, 3, 0, step, out, columns)
+        query_heads(place, lin, 3, 0, step, out, columns)
 
 
 def queries_of(place, near, rows, blocks):
@@ -333,29 +336,20 @@
     )
 
 
-def attend_kernel(row, place, mine, there, taps, center, side, halo, *outs):
+def attend_kernel(row, strip, place, mine, there, taps, center, side, halo, out):
     z, slot = place[0], place[1]
     y, core = slot // 4, slot % 2
-    tokens = outs[0].shape[1]
-    half = HDIM // 2
+    tokens = out.shape[1]
+    columns = slice(tokens * strip, tokens * (strip + 1))
     halo_later = y == row
     halo_there = jnp.where(halo_later, z < LAYERS - 1, z > 0)
-    to = lax.broadcasted_iota(jnp.int32, (HDIM, HDIM), 0)
-    column = lax.broadcasted_iota(jnp.int32, (HDIM, HDIM), 1)
-    turned = jnp.where(to < half, to + half, to - half)
-    order = (column == jnp.where(core == 0, to, turned)).astype(jnp.bfloat16)
     for m in range(LAYERS):
         own, other = mine[m // 2], there[m // 2]
-        state = jnp.where(core == m % 2, own, other)
-        high = state.astype(jnp.bfloat16)
-        low = (state - high.astype(jnp.float32)).astype(jnp.bfloat16)
-        both = jnp.concatenate([high, low], axis=0)
-        both = jnp.dot(both, order, preferred_element_type=jnp.float32).astype(jnp.bfloat16)
+        state = jnp.where(core == m % 2, own, other).astype(jnp.bfloat16)
         rows = pl.ds(HDIM * m, HDIM)
 
         def attended(frame):
-            sums = jnp.dot(both, frame[rows], preferred_element_type=jnp.float32)
-            sums = sums[: HDIM + 16] + sums[HDIM + 16 :]
+            sums = jnp.dot(state, frame[rows, columns], preferred_element_type=jnp.float32)
             result = sums[:HDIM] * (1.0 / (sums[HDIM : HDIM + 1] + epsilon))
             return result.astype(jnp.bfloat16).astype(jnp.float32)
 
@@ -364,15 +358,15 @@
         tap_halo = jnp.where(halo_later, tap[:, 2:3], tap[:, 0:1])
         mixed = tap_side * attended(side) + tap[:, 1:2] * attended(center)
         mixed += tap_halo * jnp.where(halo_there, attended(halo), 0.0)
-        for i, out in enumerate(outs):
-            out[rows] = mixed[:, tokens * i : tokens * (i + 1)].astype(jnp.bfloat16)
-
-
-def attend(row, place, mine, there, taps, *frames):
+        out[rows] = mixed.astype(jnp.bfloat16)
+
+
+def attend(row, strip, place, mine, there, taps, *frames):
     channels, tokens = frames[0].shape
-    outs = (like((channels, tokens // 2)),) * 2
-    body = functools.partial(attend_kernel, row)
-    return kernel_call(body, outs, place, mine, there, taps, *frames)
+    body = functools.partial(attend_kernel, row, strip)
+    return kernel_call(
+        body, like((channels, tokens // 2)), place, mine, there, taps, *frames
+    )
 
 
 def finish_kernel(place, *refs):
@@ -476,6 +470,7 @@
     rows = (weights_3, there_3)
     here = queries_of(place, near_here, rows, (own, beside))
     there = queries_of(place, near_there, rows, (across, diagonal))
+    kept, here = together(kept, here)
     part = sum_of([kept, swap(given, 1)], STATE_SENT)
     parts = [part] + [between(part, cross[k]) for k in range(1, LAYERS)]
     here, parts[1] = together(here, parts[1])
@@ -495,11 +490,14 @@
 
 
     halo_there, halo_here = aside(here, 1), aside(there, 0)
-    out_across = attend(0, place, state, state_there, tap, there, here, halo_there)
-    got_across = swap(out_across[0], 4), swap(out_across[1], 6)
-    out_here = attend(1, place, state, state_there, tap, here, there, halo_here)
-    got_beside = swap(out_here[1], 2)
-    return finish(place, [out_here[0], got_beside, *got_across])
+    states = (state, state_there, tap)
+    got_across = [
+        swap(attend(0, strip, place, *states, there, here, halo_there), 4 + 2 * strip)
+        for strip in range(2)
+    ]
+    got_beside = swap(attend(1, 1, place, *states, here, there, halo_here), 2)
+    kept_here = attend(1, 0, place, *states, here, there, halo_here)
+    return finish(place, [kept_here, got_beside, *got_across])
 
 
 def local(tokens, w_query, w_keyval, taps):

time: 113 us -> 111 us (0.982)
  waiting for transfers between devices: 56.3 us -> 54.4 us
    ppermute x22, waiting for transfers between devices: 56.3 us -> 54.4 us  [send(): return lax.ppermute(value, 'frame', pairs)]
    pallas_call x16 -> x18, Pallas kernels: 23.5 us -> 23.9 us  [kernel_call(): pl.pallas_call(body, out_shape=outs, in_specs=[SMEM] * scalars + [VMEM] *...]
  transfers between devices with their start and end apart: 22 -> 22, of which waited for: 12 -> 13; matrix products, arithmetic and copies ran while one was open for 1% -> 1% of each run, Pallas kernels for 17% -> 18%
where the time goes in v5:
time: 111 us
  waiting for transfers between devices  54.4 us (49%)
  starting transfers between devices  28.5 us (26%)
  Pallas kernels  25.5 us (23%)
  local copies, waits for them, and re-layouts  2.22 us (2%)
    ppermute x22, waiting for transfers between devices, send(): return lax.ppermute(value, 'frame', pairs)  54.4 us
    ppermute x22, starting transfers between devices, send(): return lax.ppermute(value, 'frame', pairs)  28.5 us
    pallas_call x18, Pallas kernels, kernel_call(): pl.pallas_call(body, out_shape=outs, in_specs=[SMEM] * scalars + [VMEM] *...  23.9 us
  transfers between devices with their start and end apart: 22, of which 13 were waited for; matrix products, arithmetic and copies ran while one was open for 1% of the time, Pallas kernels for 18%

profile of v5, /device:TPU:0, one launch (start us, length us, event | category | flops | bytes accessed | tf_op | source)
XLA Modules:
  0.0 111.0 jit_solution(11543210725864045966)
XLA Ops:
  0.0 1.3 %copy-done.1 = bf16[256,2240]{0,1:T(8,128)(2,1)S(1)} copy-done((bf16[256,2240]{0,1:T(8,128)(2,1)S(1)}, bf16[256,2240]{0,1:T(8,128)(2,1)}, u32[]{:S(2)}) %copy-start.1) | copy-done | bytes 1146904
  1.3 0.3 shard_map.46.refs_0_.block_0
  1.6 3.0 %collective-permute-start = (bf16[2240,256]{1,0:T(8,128)(2,1)S(1)}, bf16[2240,256]{1,0:T(8,128)(2,1)S(1)}, u32[]{:S(2)}, u32[]{:S(2)}) collective-permute-start(bf16[2240,256]{1,0:T(8,128)(2,1)S(1)} %shard_map.46.refs_0_.block_0), channel_id=1, source_target_pairs={{0,2},{1,3},{2,0},{3,1},{4,6},{5,7},{6,4},{7,5},{8,10},{9,11},{10,... | collective-permute-start | bytes 3440648 | tf_op jit(solution)/shard_map/ppermute | solution.py:413
  4.6 1.5 %collective-permute-start.1 = (bf16[2240,256]{1,0:T(8,128)(2,1)S(1)}, bf16[2240,256]{1,0:T(8,128)(2,1)S(1)}, u32[]{:S(2)}, u32[]{:S(2)}) collective-permute-start(bf16[2240,256]{1,0:T(8,128)(2,1)S(1)} %shard_map.46.refs_0_.block_0), channel_id=1, source_target_pairs={{0,4},{1,5},{2,6},{3,7},{4,0},{5,1},{6,2},{7,3},{8,12},{9,13},{10,... | collective-permute-start | bytes 3440648 | tf_op jit(solution)/shard_map/ppermute | solution.py:413
  6.1 1.6 %shard_map.47.refs_0_ = bf16[168,2240]{1,0:T(8,128)(2,1)} custom-call(bf16[112,2240]{1,0:T(8,128)(2,1)S(1)} %copy-done.2, bf16[56,2240]{1,0:T(8,128)(2,1)S(1)} %copy-done.3), custom_call_target="tpu_custom_call" | custom-call | tf_op jit(solution)/shard_map/pallas_call | solution.py:148
  7.7 1.6 %collective-permute-start.2 = (bf16[168,2240]{1,0:T(8,128)(2,1)}, bf16[168,2240]{1,0:T(8,128)(2,1)}, u32[]{:S(2)}, u32[]{:S(2)}) collective-permute-start(bf16[168,2240]{1,0:T(8,128)(2,1)} %shard_map.47.refs_0_), channel_id=1, source_target_pairs={{0,8},{1,9},{2,10},{3,11},{4,12},{5,13},{6,14},{7,15},{8,0},{9,1},... | collective-permute-start | bytes 2257928 | tf_op jit(solution)/shard_map/ppermute | solution.py:413
  9.3 2.6 %collective-permute-start.3 = (bf16[168,2240]{1,0:T(8,128)(2,1)}, bf16[168,2240]{1,0:T(8,128)(2,1)}, u32[]{:S(2)}, u32[]{:S(2)}) collective-permute-start(bf16[168,2240]{1,0:T(8,128)(2,1)} %shard_map.47.refs_0_), channel_id=1, source_target_pairs={{0,16},{1,17},{2,18},{3,19},{4,20},{5,21},{6,22},{7,23},{8,24},{9,... | collective-permute-start | bytes 2257928 | tf_op jit(solution)/shard_map/ppermute | solution.py:413
  12.0 0.8 copy.6
  13.0 30.0 %collective-permute-done.2.refs_1_ = bf16[168,2240]{1,0:T(8,128)(2,1)} collective-permute-done((bf16[168,2240]{1,0:T(8,128)(2,1)}, bf16[168,2240]{1,0:T(8,128)(2,1)}, u32[]{:S(2)}, u32[]{:S(2)}) %collective-permute-start.2) | collective-permute-done | bytes 752672 | tf_op jit(solution)/shard_map/ppermute | solution.py:413
  43.0 2.4 %collective-permute-done.3.refs_2_ = bf16[168,2240]{1,0:T(8,128)(2,1)} collective-permute-done((bf16[168,2240]{1,0:T(8,128)(2,1)}, bf16[168,2240]{1,0:T(8,128)(2,1)}, u32[]{:S(2)}, u32[]{:S(2)}) %collective-permute-start.3) | collective-permute-done | bytes 752672 | tf_op jit(solution)/shard_map/ppermute | solution.py:413
  45.4 0.6 shard_map.48
  46.0 0.6 collective-permute-start.5
  46.6 0.5 collective-permute-start.9
  47.1 0.7 collective-permute-start.6
  47.8 1.3 %collective-permute-start.7 = (bf16[168,2240]{1,0:T(8,128)(2,1)}, bf16[168,2240]{1,0:T(8,128)(2,1)S(1)}, u32[]{:S(2)}, u32[]{:S(2)}) collective-permute-start(bf16[168,2240]{1,0:T(8,128)(2,1)} %collective-permute-done.3.refs_2_), channel_id=1, source_target_pairs={{8,0},{9,1},{10,2},{11,3},{12,4},{13,5},{14,6},{15,7},{16,24},{17,... | collective-permute-start | bytes 2257928 | tf_op jit(solution)/shard_map/ppermute | solution.py:413
  49.1 1.1 collective-permute-done.9.refs_5_
  50.2 2.1 %shard_map.49 = (bf16[336,2240]{1,0:T(8,128)(2,1)S(1)}, bf16[336,2240]{1,0:T(8,128)(2,1)S(1)}, bf16[384,2240]{1,0:T(8,128)(2,1)S(1)}) custom-call(bf16[168,2240]{1,0:T(8,128)(2,1)} %shard_map.47.refs_0_, bf16[168,2240]{1,0:T(8,128)(2,1)} %collective-permute-done.2.refs_1_, bf16[168,2240]{1,0:T(8,128)(2,1)} %collective-permute-done.3.refs_2_, ...), custom_call_target="tpu_custom_call" | custom-call | bytes 4515840 | tf_op jit(solution)/shard_map/pallas_call | solution.py:79
  52.4 1.6 %shard_map.51.near = bf16[448,512]{1,0:T(8,128)(2,1)S(1)} custom-call(s32[2]{0:T(128)S(1)} %pad_add_fusion.place, bf16[384,2240]{1,0:T(8,128)(2,1)S(1)} %get-tuple-element.43.rows, bf16[2240,256]{1,0:T(8,128)(2,1)S(1)} %shard_map.46.refs_0_.block_0, bf16[2240,256]{1,0:T(8,128)(2,1)S(1)} %collective-permute-done.beside.refs_1_.block_1), custom_call_target="tpu_custom_call" | custom-call | bytes 4014088 | tf_op jit(solution)/shard_map/pallas_call | solution.py:79
  54.0 7.9 %collective-permute-done.5.refs_3_.refs_1_.block_1 = bf16[2240,256]{1,0:T(8,128)(2,1)S(1)} collective-permute-done((bf16[2240,256]{1,0:T(8,128)(2,1)S(1)}, bf16[2240,256]{1,0:T(8,128)(2,1)S(1)}, u32[]{:S(2)}, u32[]{:S(2)}) %collective-permute-start.5) | collective-permute-done | bytes 1146912 | tf_op jit(solution)/shard_map/ppermute | solution.py:413
  61.9 1.6 %shard_map.52.near = bf16[448,512]{1,0:T(8,128)(2,1)S(1)} custom-call(s32[2]{0:T(128)S(1)} %pad_add_fusion.place, bf16[384,2240]{1,0:T(8,128)(2,1)S(1)} %get-tuple-element.43.rows, bf16[2240,256]{1,0:T(8,128)(2,1)S(1)} %collective-permute-done.1.across.refs_2_.refs_0_.block_0, bf16[2240,256]{1,0:T(8,128)(2,1)S(1)} %collective-permute-done.5.refs_3_.refs_1_.block_1), custom_call_target="tpu_custom_call" | custom-call | bytes 4014088 | tf_op jit(solution)/shard_map/pallas_call | solution.py:79
  63.6 4.1 %shard_map.50.part = f32[2,128,112]{2,1,0:T(8,128)S(1)} custom-call(s32[2]{0:T(128)S(1)} %pad_add_fusion.place, bf16[336,2240]{1,0:T(8,128)(2,1)S(1)} %get-tuple-element.40.mine.rows, bf16[336,2240]{1,0:T(8,128)(2,1)S(1)} %get-tuple-element.41.there.rows, bf16[2240,256]{1,0:T(8,128)(2,1)S(1)} %shard_map.46.refs_0_.block_0, ...), custom_call_target="tpu_custom_call" | custom-call | flops 2055208960 | bytes 7598088 | tf_op jit(solution)/shard_map/pallas_call | solution.py:79
  67.7 1.4 %collective-permute-done.7.outer = bf16[168,2240]{1,0:T(8,128)(2,1)S(1)} collective-permute-done((bf16[168,2240]{1,0:T(8,128)(2,1)}, bf16[168,2240]{1,0:T(8,128)(2,1)S(1)}, u32[]{:S(2)}, u32[]{:S(2)}) %collective-permute-start.7) | collective-permute-done | bytes 752672 | tf_op jit(solution)/shard_map/ppermute | solution.py:413
  69.1 0.6 shard_map.53.last
  69.8 2.0 %shard_map.55.refs_0_ = f32[2,128,112]{2,1,0:T(8,128)S(1)} custom-call(s32[2]{0:T(128)S(1)} %pad_add_fusion.place, f32[2,128,112]{2,1,0:T(8,128)S(1)} %shard_map.50.part, bf16[336,2240]{1,0:T(8,128)(2,1)S(1)} %get-tuple-element.40.mine.rows, bf16[168,2240]{1,0:T(8,128)(2,1)S(1)} %shard_map.53.last, bf16[2240,256]{1,0:T(8,128)(2,1)S(1)} %shard_map.46.refs_0_.block_0, ...), custom_call_target="tpu_custom_call" | custom-call | flops 1027604480 | bytes 6960136 | tf_op jit(solution)/shard_map/pallas_call | solution.py:79
  71.8 0.2 collective-permute-done.10.last_there.last
  72.1 2.0 %shard_map.56 = f32[2,128,112]{2,1,0:T(8,128)S(1)} custom-call(s32[2]{0:T(128)S(1)} %pad_add_fusion.place, f32[2,128,112]{2,1,0:T(8,128)S(1)} %shard_map.50.part, bf16[336,2240]{1,0:T(8,128)(2,1)S(1)} %get-tuple-element.41.there.rows, bf16[168,2240]{1,0:T(8,128)(2,1)S(1)} %collective-permute-done.10.last_there.last, ...), custom_call_target="tpu_custom_call" | custom-call | flops 1027604480 | bytes 6960136 | tf_op jit(solution)/shard_map/pallas_call | solution.py:79
  74.1 0.3 collective-permute-start.11
  74.4 1.0 shard_map.57.center.side
  75.6 3.0 %collective-permute-start.13 = (bf16[2,128,112]{2,1,0:T(8,128)(2,1)S(1)}, bf16[2,128,112]{2,1,0:T(8,128)(2,1)S(1)}, u32[]{:S(2)}, u32[]{:S(2)}) collective-permute-start(bf16[2,128,112]{2,1,0:T(8,128)(2,1)S(1)} %shard_map.58.refs_0_), channel_id=1, source_target_pairs={{0,16},{1,17},{2,18},{3,19},{4,20},{5,21},{6,22},{7,23},{8,24},{9,... | collective-permute-start | bytes 172040 | tf_op jit(solution)/shard_map/ppermute | solution.py:413
  78.6 1.4 %collective-permute-start.14 = (bf16[2,128,112]{2,1,0:T(8,128)(2,1)S(1)}, bf16[2,128,112]{2,1,0:T(8,128)(2,1)S(1)}, u32[]{:S(2)}, u32[]{:S(2)}) collective-permute-start(bf16[2,128,112]{2,1,0:T(8,128)(2,1)S(1)} %shard_map.58.refs_0_), channel_id=1, source_target_pairs={{0,24},{1,25},{2,26},{3,27},{4,28},{5,29},{6,30},{7,31},{8,16},{9,... | collective-permute-start | bytes 172040 | tf_op jit(solution)/shard_map/ppermute | solution.py:413
  80.0 1.0 shard_map.54.side.center
  81.0 1.3 %collective-permute-start.19 = (bf16[448,512]{1,0:T(8,128)(2,1)S(1)}, bf16[448,512]{1,0:T(8,128)(2,1)S(1)}, u32[]{:S(2)}, u32[]{:S(2)}) collective-permute-start(bf16[448,512]{1,0:T(8,128)(2,1)S(1)} %shard_map.57.center.side), channel_id=1, source_target_pairs={{4,12},{5,13},{6,14},{7,15},{8,0},{9,1},{10,2},{11,3},{12,20},{13,... | collective-permute-start | bytes 1376264 | tf_op jit(solution)/shard_map/ppermute | solution.py:413
  82.3 0.3 collective-permute-done.13.refs_2_
  82.6 2.2 %collective-permute-done.14.refs_3_ = bf16[2,128,112]{2,1,0:T(8,128)(2,1)S(1)} collective-permute-done((bf16[2,128,112]{2,1,0:T(8,128)(2,1)S(1)}, bf16[2,128,112]{2,1,0:T(8,128)(2,1)S(1)}, u32[]{:S(2)}, u32[]{:S(2)}) %collective-permute-start.14) | collective-permute-done | bytes 57376 | tf_op jit(solution)/shard_map/ppermute | solution.py:413
  84.8 3.1 %collective-permute-start.17 = (bf16[448,512]{1,0:T(8,128)(2,1)S(1)}, bf16[448,512]{1,0:T(8,128)(2,1)S(1)}, u32[]{:S(2)}, u32[]{:S(2)}) collective-permute-start(bf16[448,512]{1,0:T(8,128)(2,1)S(1)} %shard_map.54.side.center), channel_id=1, source_target_pairs={{0,8},{1,9},{2,10},{3,11},{8,16},{9,17},{10,18},{11,19},{12,4},{13... | collective-permute-start | bytes 1376264 | tf_op jit(solution)/shard_map/ppermute | solution.py:413
  88.0 0.7 collective-permute-start.15
  88.6 3.1 %collective-permute-start.16 = (bf16[2,128,112]{2,1,0:T(8,128)(2,1)S(1)}, bf16[2,128,112]{2,1,0:T(8,128)(2,1)S(1)}, u32[]{:S(2)}, u32[]{:S(2)}) collective-permute-start(bf16[2,128,112]{2,1,0:T(8,128)(2,1)S(1)} %shard_map.59), channel_id=1, source_target_pairs={{0,1},{1,3},{2,5},{3,7},{4,0},{5,2},{6,4},{7,6},{8,9},{9,11},{10,1... | collective-permute-start | bytes 172040 | tf_op jit(solution)/shard_map/ppermute | solution.py:413
  91.7 1.4 %collective-permute-done.16.there = bf16[2,128,112]{2,1,0:T(8,128)(2,1)S(1)} collective-permute-done((bf16[2,128,112]{2,1,0:T(8,128)(2,1)S(1)}, bf16[2,128,112]{2,1,0:T(8,128)(2,1)S(1)}, u32[]{:S(2)}, u32[]{:S(2)}) %collective-permute-start.16) | collective-permute-done | bytes 57376 | tf_op jit(solution)/shard_map/ppermute | solution.py:413
  93.1 1.6 %collective-permute-done.19.halo = bf16[448,512]{1,0:T(8,128)(2,1)S(1)} collective-permute-done((bf16[448,512]{1,0:T(8,128)(2,1)S(1)}, bf16[448,512]{1,0:T(8,128)(2,1)S(1)}, u32[]{:S(2)}, u32[]{:S(2)}) %collective-permute-start.19) | collective-permute-done | bytes 458784 | tf_op jit(solution)/shard_map/ppermute | solution.py:413
  94.8 1.2 %shard_map.63 = bf16[448,256]{1,0:T(8,128)(2,1)S(1)} custom-call(s32[2]{0:T(128)S(1)} %pad_add_fusion.place, bf16[2,128,112]{2,1,0:T(8,128)(2,1)S(1)} %collective-permute-done.15.mine, bf16[2,128,112]{2,1,0:T(8,128)(2,1)S(1)} %collective-permute-done.16.there, f32[448,3]{1,0:T(8,128)S(1)} %bitcast.6, bf16[448,512]{1,0:T(8,128)(2,1)S(1)} %shard_map.54.side.center, ...), custom_call_target="tpu_custom_call" | custom-call | bytes 1496328 | tf_op jit(solution)/shard_map/pallas_call | solution.py:79
  96.1 1.2 %shard_map.62 = bf16[448,256]{1,0:T(8,128)(2,1)S(1)} custom-call(s32[2]{0:T(128)S(1)} %pad_add_fusion.place, bf16[2,128,112]{2,1,0:T(8,128)(2,1)S(1)} %collective-permute-done.15.mine, bf16[2,128,112]{2,1,0:T(8,128)(2,1)S(1)} %collective-permute-done.16.there, f32[448,3]{1,0:T(8,128)S(1)} %bitcast.7, bf16[448,512]{1,0:T(8,128)(2,1)S(1)} %shard_map.54.side.center, ...), custom_call_target="tpu_custom_call" | custom-call | bytes 1496328 | tf_op jit(solution)/shard_map/pallas_call | solution.py:79
  97.3 3.0 %collective-permute-start.20 = (bf16[448,256]{1,0:T(8,128)(2,1)S(1)}, bf16[448,256]{1,0:T(8,128)(2,1)S(1)}, u32[]{:S(2)}, u32[]{:S(2)}) collective-permute-start(bf16[448,256]{1,0:T(8,128)(2,1)S(1)} %shard_map.62), channel_id=1, source_target_pairs={{0,4},{1,5},{2,6},{3,7},{4,0},{5,1},{6,2},{7,3},{8,12},{9,13},{10,... | collective-permute-start | bytes 688136 | tf_op jit(solution)/shard_map/ppermute | solution.py:413
  100.3 1.2 %shard_map.61 = bf16[448,256]{1,0:T(8,128)(2,1)S(1)} custom-call(s32[2]{0:T(128)S(1)} %pad_add_fusion.place, bf16[2,128,112]{2,1,0:T(8,128)(2,1)S(1)} %collective-permute-done.15.mine, bf16[2,128,112]{2,1,0:T(8,128)(2,1)S(1)} %collective-permute-done.16.there, f32[448,3]{1,0:T(8,128)S(1)} %bitcast.8, bf16[448,512]{1,0:T(8,128)(2,1)S(1)} %shard_map.57.center.side, ...), custom_call_target="tpu_custom_call" | custom-call | bytes 1496328 | tf_op jit(solution)/shard_map/pallas_call | solution.py:79
  101.5 0.6 collective-permute-start.18
  102.1 1.2 %shard_map.60.refs_0_ = bf16[448,256]{1,0:T(8,128)(2,1)S(1)} custom-call(s32[2]{0:T(128)S(1)} %pad_add_fusion.place, bf16[2,128,112]{2,1,0:T(8,128)(2,1)S(1)} %collective-permute-done.15.mine, bf16[2,128,112]{2,1,0:T(8,128)(2,1)S(1)} %collective-permute-done.16.there, f32[448,3]{1,0:T(8,128)S(1)} %bitcast.9, bf16[448,512]{1,0:T(8,128)(2,1)S(1)} %shard_map.57.center.side, ...), custom_call_target="tpu_custom_call" | custom-call | bytes 1496328 | tf_op jit(solution)/shard_map/pallas_call | solution.py:79
  103.3 4.7 %collective-permute-done.20.refs_2_ = bf16[448,256]{1,0:T(8,128)(2,1)S(1)} collective-permute-done((bf16[448,256]{1,0:T(8,128)(2,1)S(1)}, bf16[448,256]{1,0:T(8,128)(2,1)S(1)}, u32[]{:S(2)}, u32[]{:S(2)}) %collective-permute-start.20) | collective-permute-done | bytes 229408 | tf_op jit(solution)/shard_map/ppermute | solution.py:413
  108.0 1.0 collective-permute-done.18.refs_1_
  109.0 2.0 %shard_map.64 = bf16[256,1792]{1,0:T(8,128)(2,1)} custom-call(s32[2]{0:T(128)S(1)} %pad_add_fusion.place, bf16[448,256]{1,0:T(8,128)(2,1)S(1)} %shard_map.60.refs_0_, bf16[448,256]{1,0:T(8,128)(2,1)S(1)} %collective-permute-done.18.refs_1_, bf16[448,256]{1,0:T(8,128)(2,1)S(1)} %collective-permute-done.20.refs_2_, ...), custom_call_target="tpu_custom_call" | custom-call | bytes 917512 | tf_op jit(solution)/shard_map/pallas_call | solution.py:79
  (29 shorter events, 0.6 us)
Async XLA Ops:
  0.0 1.3 %copy-start.1 = (bf16[256,2240]{0,1:T(8,128)(2,1)S(1)}, bf16[256,2240]{0,1:T(8,128)(2,1)}, u32[]{:S(2)}) copy-start(bf16[256,2240]{0,1:T(8,128)(2,1)} %param.4) | copy-start | bytes 3440644
  1.3 4.8 %copy-start.2 = (bf16[112,2240]{1,0:T(8,128)(2,1)S(1)}, bf16[112,2240]{1,0:T(8,128)(2,1)}, u32[]{:S(2)}) copy-start(bf16[112,2240]{1,0:T(8,128)(2,1)} %w_keyval.1) | copy-start | bytes 1505284
  1.3 4.8 %copy-start.3 = (bf16[56,2240]{1,0:T(8,128)(2,1)S(1)}, bf16[56,2240]{1,0:T(8,128)(2,1)}, u32[]{:S(2)}) copy-start(bf16[56,2240]{1,0:T(8,128)(2,1)} %w_query.1) | copy-start | bytes 752644
  1.6 10.4 %copy-start.4 = (f32[3,1792]{1,0:T(4,128)S(1)}, f32[3,1792]{1,0:T(4,128)}, u32[]{:S(2)}) copy-start(f32[3,1792]{1,0:T(4,128)} %param.7) | copy-start | bytes 64516
  1.6 43.8 %collective-permute-start = (bf16[2240,256]{1,0:T(8,128)(2,1)S(1)}, bf16[2240,256]{1,0:T(8,128)(2,1)S(1)}, u32[]{:S(2)}, u32[]{:S(2)}) collective-permute-start(bf16[2240,256]{1,0:T(8,128)(2,1)S(1)} %shard_map.46.refs_0_.block_0), channel_id=1, source_target_pairs={{0,2},{1,3},{2,0},{3,1},{4,6},{5,7},{6,4},{7,5},{8,10},{9,11},{10,... | collective-permute-start | bytes 3440648 | tf_op jit(solution)/shard_map/ppermute | solution.py:413
  4.6 40.8 %collective-permute-start.1 = (bf16[2240,256]{1,0:T(8,128)(2,1)S(1)}, bf16[2240,256]{1,0:T(8,128)(2,1)S(1)}, u32[]{:S(2)}, u32[]{:S(2)}) collective-permute-start(bf16[2240,256]{1,0:T(8,128)(2,1)S(1)} %shard_map.46.refs_0_.block_0), channel_id=1, source_target_pairs={{0,4},{1,5},{2,6},{3,7},{4,0},{5,1},{6,2},{7,3},{8,12},{9,13},{10,... | collective-permute-start | bytes 3440648 | tf_op jit(solution)/shard_map/ppermute | solution.py:413
  7.7 35.3 %collective-permute-start.2 = (bf16[168,2240]{1,0:T(8,128)(2,1)}, bf16[168,2240]{1,0:T(8,128)(2,1)}, u32[]{:S(2)}, u32[]{:S(2)}) collective-permute-start(bf16[168,2240]{1,0:T(8,128)(2,1)} %shard_map.47.refs_0_), channel_id=1, source_target_pairs={{0,8},{1,9},{2,10},{3,11},{4,12},{5,13},{6,14},{7,15},{8,0},{9,1},... | collective-permute-start | bytes 2257928 | tf_op jit(solution)/shard_map/ppermute | solution.py:413
  9.3 36.0 %collective-permute-start.3 = (bf16[168,2240]{1,0:T(8,128)(2,1)}, bf16[168,2240]{1,0:T(8,128)(2,1)}, u32[]{:S(2)}, u32[]{:S(2)}) collective-permute-start(bf16[168,2240]{1,0:T(8,128)(2,1)} %shard_map.47.refs_0_), channel_id=1, source_target_pairs={{0,16},{1,17},{2,18},{3,19},{4,20},{5,21},{6,22},{7,23},{8,24},{9,... | collective-permute-start | bytes 2257928 | tf_op jit(solution)/shard_map/ppermute | solution.py:413
  11.9 33.5 %collective-permute-start.4 = (bf16[168,2240]{1,0:T(8,128)(2,1)}, bf16[168,2240]{1,0:T(8,128)(2,1)}, u32[]{:S(2)}, u32[]{:S(2)}) collective-permute-start(bf16[168,2240]{1,0:T(8,128)(2,1)} %shard_map.47.refs_0_), channel_id=1, source_target_pairs={{0,1},{1,0},{2,3},{3,2},{4,5},{5,4},{6,7},{7,6},{8,9},{9,8},{10,11... | collective-permute-start | bytes 2257928 | tf_op jit(solution)/shard_map/ppermute | solution.py:413
  46.0 15.9 %collective-permute-start.5 = (bf16[2240,256]{1,0:T(8,128)(2,1)S(1)}, bf16[2240,256]{1,0:T(8,128)(2,1)S(1)}, u32[]{:S(2)}, u32[]{:S(2)}) collective-permute-start(bf16[2240,256]{1,0:T(8,128)(2,1)S(1)} %shard_map.48), channel_id=1, source_target_pairs={{0,2},{1,5},{2,0},{3,7},{4,6},{5,1},{6,4},{7,3},{8,10},{9,13},{10,... | collective-permute-start | bytes 3440648 | tf_op jit(solution)/shard_map/ppermute | solution.py:413
  46.6 2.5 %collective-permute-start.8 = (bf16[168,2240]{1,0:T(8,128)(2,1)}, bf16[168,2240]{1,0:T(8,128)(2,1)S(1)}, u32[]{:S(2)}, u32[]{:S(2)}) collective-permute-start(bf16[168,2240]{1,0:T(8,128)(2,1)} %collective-permute-done.2.refs_1_), channel_id=1, source_target_pairs={{0,1},{1,0},{2,3},{3,2},{4,5},{5,4},{6,7},{7,6},{8,9},{9,8},{10,11... | collective-permute-start | bytes 2257928 | tf_op jit(solution)/shard_map/ppermute | solution.py:413
  46.6 3.6 %collective-permute-start.9 = (bf16[168,2240]{1,0:T(8,128)(2,1)}, bf16[168,2240]{1,0:T(8,128)(2,1)S(1)}, u32[]{:S(2)}, u32[]{:S(2)}) collective-permute-start(bf16[168,2240]{1,0:T(8,128)(2,1)} %collective-permute-done.3.refs_2_), channel_id=1, source_target_pairs={{0,1},{1,0},{2,3},{3,2},{4,5},{5,4},{6,7},{7,6},{8,9},{9,8},{10,11... | collective-permute-start | bytes 2257928 | tf_op jit(solution)/shard_map/ppermute | solution.py:413
  47.1 20.5 %collective-permute-start.6 = (bf16[168,2240]{1,0:T(8,128)(2,1)}, bf16[168,2240]{1,0:T(8,128)(2,1)S(1)}, u32[]{:S(2)}, u32[]{:S(2)}) collective-permute-start(bf16[168,2240]{1,0:T(8,128)(2,1)} %shard_map.47.refs_0_), channel_id=1, source_target_pairs={{8,16},{9,17},{10,18},{11,19},{12,20},{13,21},{14,22},{15,23},{16,... | collective-permute-start | bytes 2257928 | tf_op jit(solution)/shard_map/ppermute | solution.py:413
  47.8 21.3 %collective-permute-start.7 = (bf16[168,2240]{1,0:T(8,128)(2,1)}, bf16[168,2240]{1,0:T(8,128)(2,1)S(1)}, u32[]{:S(2)}, u32[]{:S(2)}) collective-permute-start(bf16[168,2240]{1,0:T(8,128)(2,1)} %collective-permute-done.3.refs_2_), channel_id=1, source_target_pairs={{8,0},{9,1},{10,2},{11,3},{12,4},{13,5},{14,6},{15,7},{16,24},{17,... | collective-permute-start | bytes 2257928 | tf_op jit(solution)/shard_map/ppermute | solution.py:413
  69.7 2.3 %collective-permute-start.10 = (bf16[168,2240]{1,0:T(8,128)(2,1)S(1)}, bf16[168,2240]{1,0:T(8,128)(2,1)S(1)}, u32[]{:S(2)}, u32[]{:S(2)}) collective-permute-start(bf16[168,2240]{1,0:T(8,128)(2,1)S(1)} %shard_map.53.last), channel_id=1, source_target_pairs={{0,1},{1,0},{2,3},{3,2},{4,5},{5,4},{6,7},{7,6},{8,9},{9,8},{10,11... | collective-permute-start | bytes 2257928 | tf_op jit(solution)/shard_map/ppermute | solution.py:413
  74.1 1.4 %collective-permute-start.11 = (f32[2,128,112]{2,1,0:T(8,128)S(1)}, f32[2,128,112]{2,1,0:T(8,128)S(1)}, u32[]{:S(2)}, u32[]{:S(2)}) collective-permute-start(f32[2,128,112]{2,1,0:T(8,128)S(1)} %shard_map.56), channel_id=1, source_target_pairs={{0,1},{1,0},{2,3},{3,2},{4,5},{5,4},{6,7},{7,6},{8,9},{9,8},{10,11... | collective-permute-start | bytes 344072 | tf_op jit(solution)/shard_map/ppermute | solution.py:413
  75.5 19.3 %copy-start = (f32[3,4,1,112]{0,3,1,2:T(8,128)S(1)}, f32[3,4,1,112]{0,3,1,2:T(8,128)}, u32[]{:S(2)}) copy-start(f32[3,4,1,112]{0,3,1,2:T(8,128)} %copy.6) | copy-start | bytes 16132
  75.5 5.5 %collective-permute-start.12 = (bf16[2,128,112]{2,1,0:T(8,128)(2,1)S(1)}, bf16[2,128,112]{2,1,0:T(8,128)(2,1)S(1)}, u32[]{:S(2)}, u32[]{:S(2)}) collective-permute-start(bf16[2,128,112]{2,1,0:T(8,128)(2,1)S(1)} %shard_map.58.refs_0_), channel_id=1, source_target_pairs={{0,8},{1,9},{2,10},{3,11},{4,12},{5,13},{6,14},{7,15},{8,0},{9,1},... | collective-permute-start | bytes 172040 | tf_op jit(solution)/shard_map/ppermute | solution.py:413
  75.6 7.0 %collective-permute-start.13 = (bf16[2,128,112]{2,1,0:T(8,128)(2,1)S(1)}, bf16[2,128,112]{2,1,0:T(8,128)(2,1)S(1)}, u32[]{:S(2)}, u32[]{:S(2)}) collective-permute-start(bf16[2,128,112]{2,1,0:T(8,128)(2,1)S(1)} %shard_map.58.refs_0_), channel_id=1, source_target_pairs={{0,16},{1,17},{2,18},{3,19},{4,20},{5,21},{6,22},{7,23},{8,24},{9,... | collective-permute-start | bytes 172040 | tf_op jit(solution)/shard_map/ppermute | solution.py:413
  78.6 6.2 %collective-permute-start.14 = (bf16[2,128,112]{2,1,0:T(8,128)(2,1)S(1)}, bf16[2,128,112]{2,1,0:T(8,128)(2,1)S(1)}, u32[]{:S(2)}, u32[]{:S(2)}) collective-permute-start(bf16[2,128,112]{2,1,0:T(8,128)(2,1)S(1)} %shard_map.58.refs_0_), channel_id=1, source_target_pairs={{0,24},{1,25},{2,26},{3,27},{4,28},{5,29},{6,30},{7,31},{8,16},{9,... | collective-permute-start | bytes 172040 | tf_op jit(solution)/shard_map/ppermute | solution.py:413
  81.0 13.7 %collective-permute-start.19 = (bf16[448,512]{1,0:T(8,128)(2,1)S(1)}, bf16[448,512]{1,0:T(8,128)(2,1)S(1)}, u32[]{:S(2)}, u32[]{:S(2)}) collective-permute-start(bf16[448,512]{1,0:T(8,128)(2,1)S(1)} %shard_map.57.center.side), channel_id=1, source_target_pairs={{4,12},{5,13},{6,14},{7,15},{8,0},{9,1},{10,2},{11,3},{12,20},{13,... | collective-permute-start | bytes 1376264 | tf_op jit(solution)/shard_map/ppermute | solution.py:413
  84.8 15.5 %collective-permute-start.17 = (bf16[448,512]{1,0:T(8,128)(2,1)S(1)}, bf16[448,512]{1,0:T(8,128)(2,1)S(1)}, u32[]{:S(2)}, u32[]{:S(2)}) collective-permute-start(bf16[448,512]{1,0:T(8,128)(2,1)S(1)} %shard_map.54.side.center), channel_id=1, source_target_pairs={{0,8},{1,9},{2,10},{3,11},{8,16},{9,17},{10,18},{11,19},{12,4},{13... | collective-permute-start | bytes 1376264 | tf_op jit(solution)/shard_map/ppermute | solution.py:413
  88.0 3.8 %collective-permute-start.15 = (bf16[2,128,112]{2,1,0:T(8,128)(2,1)S(1)}, bf16[2,128,112]{2,1,0:T(8,128)(2,1)S(1)}, u32[]{:S(2)}, u32[]{:S(2)}) collective-permute-start(bf16[2,128,112]{2,1,0:T(8,128)(2,1)S(1)} %shard_map.59), channel_id=1, source_target_pairs={{0,0},{1,2},{2,4},{3,6},{4,1},{5,3},{6,5},{7,7},{8,8},{9,10},{10,1... | collective-permute-start | bytes 172040 | tf_op jit(solution)/shard_map/ppermute | solution.py:413
  88.6 4.5 %collective-permute-start.16 = (bf16[2,128,112]{2,1,0:T(8,128)(2,1)S(1)}, bf16[2,128,112]{2,1,0:T(8,128)(2,1)S(1)}, u32[]{:S(2)}, u32[]{:S(2)}) collective-permute-start(bf16[2,128,112]{2,1,0:T(8,128)(2,1)S(1)} %shard_map.59), channel_id=1, source_target_pairs={{0,1},{1,3},{2,5},{3,7},{4,0},{5,2},{6,4},{7,6},{8,9},{9,11},{10,1... | collective-permute-start | bytes 172040 | tf_op jit(solution)/shard_map/ppermute | solution.py:413
  96.0 7.3 %collective-permute-start.21 = (bf16[448,256]{1,0:T(8,128)(2,1)S(1)}, bf16[448,256]{1,0:T(8,128)(2,1)S(1)}, u32[]{:S(2)}, u32[]{:S(2)}) collective-permute-start(bf16[448,256]{1,0:T(8,128)(2,1)S(1)} %shard_map.63), channel_id=1, source_target_pairs={{0,6},{1,7},{2,4},{3,5},{4,2},{5,3},{6,0},{7,1},{8,14},{9,15},{10,... | collective-permute-start | bytes 688136 | tf_op jit(solution)/shard_map/ppermute | solution.py:413
  97.3 10.7 %collective-permute-start.20 = (bf16[448,256]{1,0:T(8,128)(2,1)S(1)}, bf16[448,256]{1,0:T(8,128)(2,1)S(1)}, u32[]{:S(2)}, u32[]{:S(2)}) collective-permute-start(bf16[448,256]{1,0:T(8,128)(2,1)S(1)} %shard_map.62), channel_id=1, source_target_pairs={{0,4},{1,5},{2,6},{3,7},{4,0},{5,1},{6,2},{7,3},{8,12},{9,13},{10,... | collective-permute-start | bytes 688136 | tf_op jit(solution)/shard_map/ppermute | solution.py:413
  101.5 7.6 %collective-permute-start.18 = (bf16[448,256]{1,0:T(8,128)(2,1)S(1)}, bf16[448,256]{1,0:T(8,128)(2,1)S(1)}, u32[]{:S(2)}, u32[]{:S(2)}) collective-permute-start(bf16[448,256]{1,0:T(8,128)(2,1)S(1)} %shard_map.61), channel_id=1, source_target_pairs={{0,2},{1,3},{2,0},{3,1},{4,6},{5,7},{6,4},{7,5},{8,10},{9,11},{10,... | collective-permute-start | bytes 688136 | tf_op jit(solution)/shard_map/ppermute | solution.py:413

commit v6 on v5

--- a/solution.py
+++ b/solution.py
@@ -69,7 +69,6 @@
 
 VMEM = pl.BlockSpec(memory_space=pltpu.VMEM)
 SMEM = pl.BlockSpec(memory_space=pltpu.SMEM)
-ANY = pl.BlockSpec(memory_space=pl.ANY)
 ANY = pl.BlockSpec(memory_space=pl.ANY)
 PARAMS = pltpu.CompilerParams(vmem_limit_bytes=16 * 2**20)
 
@@ -130,32 +129,14 @@
     return (rows + 15) // 16 * 16
 
 
-def weights_kernel(w_keyval, w_query, out, held, sems):
-    split = w_keyval.shape[0]
-    copies = [
-        pltpu.make_async_copy(w_keyval, out.at[pl.ds(0, split)], sems.at[0]),
-        pltpu.make_async_copy(w_query, held, sems.at[1]),
-    ]
-    for copy in copies:
-        copy.start()
-    copies[1].wait()
-    out[split:] = held[...]
-    copies[0].wait()
+def weights_kernel(w_keyval, w_query, out):
+    out[: w_keyval.shape[0]] = w_keyval[...]
+    out[w_keyval.shape[0] :] = w_query[...]
 
 
 def weights_of(w_keyval, w_query):
     rows, depth = w_keyval.shape[0] + w_query.shape[0], w_query.shape[1]
-    return pl.pallas_call(
-        weights_kernel,
-        out_shape=like((rows, depth)),
-        in_specs=[ANY, ANY],
-        out_specs=VMEM,
-        scratch_shapes=[
-            pltpu.VMEM(w_query.shape, w_query.dtype),
-            pltpu.SemaphoreType.DMA((2,)),
-        ],
-        compiler_params=PARAMS,
-    )(w_keyval, w_query)
+    return kernel_call(weights_kernel, like((rows, depth)), w_keyval, w_query, scalars=0)
 
 
 def last_kernel(place, inner, outer, out):
@@ -442,8 +423,8 @@
     own = begin(tokens.T)
     beside, across = swap(own, 2), swap(own, 4)
     weights_there = swap(weights, 1)
-    own, beside, across, weights, weights_1, weights_2, weights_there, tap = together(
-        own, beside, across, weights, weights_1, weights_2, weights_there, tap
+    weights_2, weights_1, weights, own, beside, across, weights_there, tap = together(
+        weights_2, weights_1, weights, own, beside, across, weights_there, tap
     )
 
     weights_inner = between(weights, inner)
@@ -472,8 +453,8 @@
     there = queries_of(place, near_there, rows, (across, diagonal))
     kept, here = together(kept, here)
     part = sum_of([kept, swap(given, 1)], STATE_SENT)
-    parts = [part] + [between(part, cross[k]) for k in range(1, LAYERS)]
-    here, parts[1] = together(here, parts[1])
+    parts = [part] + [between(part, cross[k]) for k in (2, 3, 1)]
+    here, parts[3] = together(here, parts[3])
     there, *parts = together(there, *parts)
     state = sum_of(parts, STATE_SENT)
     state, state_there = (

time: 111 us -> 110 us (level)
    pallas_call x1 -> x0, Pallas kernels: 1.58 us -> none  [weights_of(): pl.pallas_call(weights_kernel, out_shape=like((rows, depth)), in_specs=[A...]
    pallas_call x18 -> x19, Pallas kernels: 23.9 us -> 24.8 us  [kernel_call(): pl.pallas_call(body, out_shape=outs, in_specs=[SMEM] * scalars + [VMEM] *...]
  transfers between devices with their start and end apart: 22 -> 22, of which waited for: 13 -> 14; matrix products, arithmetic and copies ran while one was open for 1% -> 1% of each run, Pallas kernels for 18% -> 18%
where the time goes in v6:
time: 110 us
  waiting for transfers between devices  53.9 us (49%)
  starting transfers between devices  28.5 us (26%)
  Pallas kernels  24.8 us (23%)
  local copies, waits for them, and re-layouts  2.22 us (2%)
    ppermute x22, waiting for transfers between devices, send(): return lax.ppermute(value, 'frame', pairs)  53.9 us
    ppermute x22, starting transfers between devices, send(): return lax.ppermute(value, 'frame', pairs)  28.5 us
    pallas_call x19, Pallas kernels, kernel_call(): pl.pallas_call(body, out_shape=outs, in_specs=[SMEM] * scalars + [VMEM] *...  24.8 us
  transfers between devices with their start and end apart: 22, of which 14 were waited for; matrix products, arithmetic and copies ran while one was open for 1% of the time, Pallas kernels for 18%

profile of v6, /device:TPU:0, one launch (start us, length us, event | category | flops | bytes accessed | tf_op | source)
XLA Modules:
  0.0 109.8 jit_solution(14535958285888631073)
XLA Ops:
  0.0 1.3 %copy-done.1 = bf16[256,2240]{0,1:T(8,128)(2,1)S(1)} copy-done((bf16[256,2240]{0,1:T(8,128)(2,1)S(1)}, bf16[256,2240]{0,1:T(8,128)(2,1)}, u32[]{:S(2)}) %copy-start.1) | copy-done | bytes 1146904
  1.3 0.3 shard_map.47.refs_0_.block_0
  1.6 3.0 %collective-permute-start.2 = (bf16[2240,256]{1,0:T(8,128)(2,1)S(1)}, bf16[2240,256]{1,0:T(8,128)(2,1)S(1)}, u32[]{:S(2)}, u32[]{:S(2)}) collective-permute-start(bf16[2240,256]{1,0:T(8,128)(2,1)S(1)} %shard_map.47.refs_0_.block_0), channel_id=1, source_target_pairs={{0,2},{1,3},{2,0},{3,1},{4,6},{5,7},{6,4},{7,5},{8,10},{9,11},{10,... | collective-permute-start | bytes 3440648 | tf_op jit(solution)/shard_map/ppermute | solution.py:394
  4.6 1.5 %collective-permute-start.3 = (bf16[2240,256]{1,0:T(8,128)(2,1)S(1)}, bf16[2240,256]{1,0:T(8,128)(2,1)S(1)}, u32[]{:S(2)}, u32[]{:S(2)}) collective-permute-start(bf16[2240,256]{1,0:T(8,128)(2,1)S(1)} %shard_map.47.refs_0_.block_0), channel_id=1, source_target_pairs={{0,4},{1,5},{2,6},{3,7},{4,0},{5,1},{6,2},{7,3},{8,12},{9,13},{10,... | collective-permute-start | bytes 3440648 | tf_op jit(solution)/shard_map/ppermute | solution.py:394
  6.1 0.9 shard_map.46.refs_0_
  7.0 2.6 %collective-permute-start = (bf16[168,2240]{1,0:T(8,128)(2,1)}, bf16[168,2240]{1,0:T(8,128)(2,1)}, u32[]{:S(2)}, u32[]{:S(2)}) collective-permute-start(bf16[168,2240]{1,0:T(8,128)(2,1)} %shard_map.46.refs_0_), channel_id=1, source_target_pairs={{0,16},{1,17},{2,18},{3,19},{4,20},{5,21},{6,22},{7,23},{8,24},{9,... | collective-permute-start | bytes 2257928 | tf_op jit(solution)/shard_map/ppermute | solution.py:394
  9.6 1.6 %collective-permute-start.1 = (bf16[168,2240]{1,0:T(8,128)(2,1)}, bf16[168,2240]{1,0:T(8,128)(2,1)}, u32[]{:S(2)}, u32[]{:S(2)}) collective-permute-start(bf16[168,2240]{1,0:T(8,128)(2,1)} %shard_map.46.refs_0_), channel_id=1, source_target_pairs={{0,8},{1,9},{2,10},{3,11},{4,12},{5,13},{6,14},{7,15},{8,0},{9,1},... | collective-permute-start | bytes 2257928 | tf_op jit(solution)/shard_map/ppermute | solution.py:394
  11.3 0.8 copy.6
  12.2 31.2 %collective-permute-done.refs_2_ = bf16[168,2240]{1,0:T(8,128)(2,1)} collective-permute-done((bf16[168,2240]{1,0:T(8,128)(2,1)}, bf16[168,2240]{1,0:T(8,128)(2,1)}, u32[]{:S(2)}, u32[]{:S(2)}) %collective-permute-start) | collective-permute-done | bytes 752672 | tf_op jit(solution)/shard_map/ppermute | solution.py:394
  43.6 0.6 shard_map.48
  44.2 0.6 collective-permute-start.5
  44.8 0.5 collective-permute-start.9
  45.3 0.7 collective-permute-start.6
  46.0 1.3 %collective-permute-start.7 = (bf16[168,2240]{1,0:T(8,128)(2,1)}, bf16[168,2240]{1,0:T(8,128)(2,1)S(1)}, u32[]{:S(2)}, u32[]{:S(2)}) collective-permute-start(bf16[168,2240]{1,0:T(8,128)(2,1)} %collective-permute-done.refs_2_), channel_id=1, source_target_pairs={{8,0},{9,1},{10,2},{11,3},{12,4},{13,5},{14,6},{15,7},{16,24},{17,... | collective-permute-start | bytes 2257928 | tf_op jit(solution)/shard_map/ppermute | solution.py:394
  47.4 1.1 collective-permute-done.9.refs_5_
  48.4 2.1 %shard_map.49 = (bf16[336,2240]{1,0:T(8,128)(2,1)S(1)}, bf16[336,2240]{1,0:T(8,128)(2,1)S(1)}, bf16[384,2240]{1,0:T(8,128)(2,1)S(1)}) custom-call(bf16[168,2240]{1,0:T(8,128)(2,1)} %shard_map.46.refs_0_, bf16[168,2240]{1,0:T(8,128)(2,1)} %collective-permute-done.1.refs_1_, bf16[168,2240]{1,0:T(8,128)(2,1)} %collective-permute-done.refs_2_, ...), custom_call_target="tpu_custom_call" | custom-call | bytes 4515840 | tf_op jit(solution)/shard_map/pallas_call | solution.py:78
  50.6 1.6 %shard_map.51.near = bf16[448,512]{1,0:T(8,128)(2,1)S(1)} custom-call(s32[2]{0:T(128)S(1)} %pad_add_fusion.place, bf16[384,2240]{1,0:T(8,128)(2,1)S(1)} %get-tuple-element.43.rows, bf16[2240,256]{1,0:T(8,128)(2,1)S(1)} %shard_map.47.refs_0_.block_0, bf16[2240,256]{1,0:T(8,128)(2,1)S(1)} %collective-permute-done.2.beside.refs_1_.block_1), custom_call_target="tpu_custom_call" | custom-call | bytes 4014088 | tf_op jit(solution)/shard_map/pallas_call | solution.py:78
  52.2 7.9 %collective-permute-done.5.refs_3_.refs_1_.block_1 = bf16[2240,256]{1,0:T(8,128)(2,1)S(1)} collective-permute-done((bf16[2240,256]{1,0:T(8,128)(2,1)S(1)}, bf16[2240,256]{1,0:T(8,128)(2,1)S(1)}, u32[]{:S(2)}, u32[]{:S(2)}) %collective-permute-start.5) | collective-permute-done | bytes 1146912 | tf_op jit(solution)/shard_map/ppermute | solution.py:394
  60.1 1.6 %shard_map.52.near = bf16[448,512]{1,0:T(8,128)(2,1)S(1)} custom-call(s32[2]{0:T(128)S(1)} %pad_add_fusion.place, bf16[384,2240]{1,0:T(8,128)(2,1)S(1)} %get-tuple-element.43.rows, bf16[2240,256]{1,0:T(8,128)(2,1)S(1)} %collective-permute-done.3.across.refs_2_.refs_0_.block_0, bf16[2240,256]{1,0:T(8,128)(2,1)S(1)} %collective-permute-done.5.refs_3_.refs_1_.block_1), custom_call_target="tpu_custom_call" | custom-call | bytes 4014088 | tf_op jit(solution)/shard_map/pallas_call | solution.py:78
  61.8 4.1 %shard_map.50.part = f32[2,128,112]{2,1,0:T(8,128)S(1)} custom-call(s32[2]{0:T(128)S(1)} %pad_add_fusion.place, bf16[336,2240]{1,0:T(8,128)(2,1)S(1)} %get-tuple-element.40.mine.rows, bf16[336,2240]{1,0:T(8,128)(2,1)S(1)} %get-tuple-element.41.there.rows, bf16[2240,256]{1,0:T(8,128)(2,1)S(1)} %shard_map.47.refs_0_.block_0, ...), custom_call_target="tpu_custom_call" | custom-call | flops 2055208960 | bytes 7598088 | tf_op jit(solution)/shard_map/pallas_call | solution.py:78
  65.9 1.9 %collective-permute-done.7.outer = bf16[168,2240]{1,0:T(8,128)(2,1)S(1)} collective-permute-done((bf16[168,2240]{1,0:T(8,128)(2,1)}, bf16[168,2240]{1,0:T(8,128)(2,1)S(1)}, u32[]{:S(2)}, u32[]{:S(2)}) %collective-permute-start.7) | collective-permute-done | bytes 752672 | tf_op jit(solution)/shard_map/ppermute | solution.py:394
  67.8 0.6 shard_map.53.last
  68.5 2.0 %shard_map.55.refs_0_ = f32[2,128,112]{2,1,0:T(8,128)S(1)} custom-call(s32[2]{0:T(128)S(1)} %pad_add_fusion.place, f32[2,128,112]{2,1,0:T(8,128)S(1)} %shard_map.50.part, bf16[336,2240]{1,0:T(8,128)(2,1)S(1)} %get-tuple-element.40.mine.rows, bf16[168,2240]{1,0:T(8,128)(2,1)S(1)} %shard_map.53.last, bf16[2240,256]{1,0:T(8,128)(2,1)S(1)} %shard_map.47.refs_0_.block_0, ...), custom_call_target="tpu_custom_call" | custom-call | flops 1027604480 | bytes 6960136 | tf_op jit(solution)/shard_map/pallas_call | solution.py:78
  70.7 2.0 %shard_map.56 = f32[2,128,112]{2,1,0:T(8,128)S(1)} custom-call(s32[2]{0:T(128)S(1)} %pad_add_fusion.place, f32[2,128,112]{2,1,0:T(8,128)S(1)} %shard_map.50.part, bf16[336,2240]{1,0:T(8,128)(2,1)S(1)} %get-tuple-element.41.there.rows, bf16[168,2240]{1,0:T(8,128)(2,1)S(1)} %collective-permute-done.10.last_there.last, ...), custom_call_target="tpu_custom_call" | custom-call | flops 1027604480 | bytes 6960136 | tf_op jit(solution)/shard_map/pallas_call | solution.py:78
  72.7 0.3 collective-permute-start.11
  73.0 1.0 shard_map.57.center.side
  74.2 0.3 collective-permute-start.14
  74.5 3.0 %collective-permute-start.12 = (bf16[2,128,112]{2,1,0:T(8,128)(2,1)S(1)}, bf16[2,128,112]{2,1,0:T(8,128)(2,1)S(1)}, u32[]{:S(2)}, u32[]{:S(2)}) collective-permute-start(bf16[2,128,112]{2,1,0:T(8,128)(2,1)S(1)} %shard_map.58.refs_0_), channel_id=1, source_target_pairs={{0,16},{1,17},{2,18},{3,19},{4,20},{5,21},{6,22},{7,23},{8,24},{9,... | collective-permute-start | bytes 172040 | tf_op jit(solution)/shard_map/ppermute | solution.py:394
  77.6 1.1 collective-permute-start.13
  78.6 1.0 shard_map.54.side.center
  79.7 1.3 %collective-permute-start.19 = (bf16[448,512]{1,0:T(8,128)(2,1)S(1)}, bf16[448,512]{1,0:T(8,128)(2,1)S(1)}, u32[]{:S(2)}, u32[]{:S(2)}) collective-permute-start(bf16[448,512]{1,0:T(8,128)(2,1)S(1)} %shard_map.57.center.side), channel_id=1, source_target_pairs={{4,12},{5,13},{6,14},{7,15},{8,0},{9,1},{10,2},{11,3},{12,20},{13,... | collective-permute-start | bytes 1376264 | tf_op jit(solution)/shard_map/ppermute | solution.py:394
  81.0 0.6 collective-permute-done.12.refs_1_
  81.6 2.1 %collective-permute-done.13.refs_2_ = bf16[2,128,112]{2,1,0:T(8,128)(2,1)S(1)} collective-permute-done((bf16[2,128,112]{2,1,0:T(8,128)(2,1)S(1)}, bf16[2,128,112]{2,1,0:T(8,128)(2,1)S(1)}, u32[]{:S(2)}, u32[]{:S(2)}) %collective-permute-start.13) | collective-permute-done | bytes 57376 | tf_op jit(solution)/shard_map/ppermute | solution.py:394
  83.7 3.2 %collective-permute-start.17 = (bf16[448,512]{1,0:T(8,128)(2,1)S(1)}, bf16[448,512]{1,0:T(8,128)(2,1)S(1)}, u32[]{:S(2)}, u32[]{:S(2)}) collective-permute-start(bf16[448,512]{1,0:T(8,128)(2,1)S(1)} %shard_map.54.side.center), channel_id=1, source_target_pairs={{0,8},{1,9},{2,10},{3,11},{8,16},{9,17},{10,18},{11,19},{12,4},{13... | collective-permute-start | bytes 1376264 | tf_op jit(solution)/shard_map/ppermute | solution.py:394
  87.0 0.7 collective-permute-start.15
  87.6 3.1 %collective-permute-start.16 = (bf16[2,128,112]{2,1,0:T(8,128)(2,1)S(1)}, bf16[2,128,112]{2,1,0:T(8,128)(2,1)S(1)}, u32[]{:S(2)}, u32[]{:S(2)}) collective-permute-start(bf16[2,128,112]{2,1,0:T(8,128)(2,1)S(1)} %shard_map.59), channel_id=1, source_target_pairs={{0,1},{1,3},{2,5},{3,7},{4,0},{5,2},{6,4},{7,6},{8,9},{9,11},{10,1... | collective-permute-start | bytes 172040 | tf_op jit(solution)/shard_map/ppermute | solution.py:394
  90.7 1.4 %collective-permute-done.16.there = bf16[2,128,112]{2,1,0:T(8,128)(2,1)S(1)} collective-permute-done((bf16[2,128,112]{2,1,0:T(8,128)(2,1)S(1)}, bf16[2,128,112]{2,1,0:T(8,128)(2,1)S(1)}, u32[]{:S(2)}, u32[]{:S(2)}) %collective-permute-start.16) | collective-permute-done | bytes 57376 | tf_op jit(solution)/shard_map/ppermute | solution.py:394
  92.1 1.4 %collective-permute-done.19.halo = bf16[448,512]{1,0:T(8,128)(2,1)S(1)} collective-permute-done((bf16[448,512]{1,0:T(8,128)(2,1)S(1)}, bf16[448,512]{1,0:T(8,128)(2,1)S(1)}, u32[]{:S(2)}, u32[]{:S(2)}) %collective-permute-start.19) | collective-permute-done | bytes 458784 | tf_op jit(solution)/shard_map/ppermute | solution.py:394
  93.6 1.2 %shard_map.63 = bf16[448,256]{1,0:T(8,128)(2,1)S(1)} custom-call(s32[2]{0:T(128)S(1)} %pad_add_fusion.place, bf16[2,128,112]{2,1,0:T(8,128)(2,1)S(1)} %collective-permute-done.15.mine, bf16[2,128,112]{2,1,0:T(8,128)(2,1)S(1)} %collective-permute-done.16.there, f32[448,3]{1,0:T(8,128)S(1)} %bitcast.6, bf16[448,512]{1,0:T(8,128)(2,1)S(1)} %shard_map.54.side.center, ...), custom_call_target="tpu_custom_call" | custom-call | bytes 1496328 | tf_op jit(solution)/shard_map/pallas_call | solution.py:78
  94.8 1.2 %shard_map.62 = bf16[448,256]{1,0:T(8,128)(2,1)S(1)} custom-call(s32[2]{0:T(128)S(1)} %pad_add_fusion.place, bf16[2,128,112]{2,1,0:T(8,128)(2,1)S(1)} %collective-permute-done.15.mine, bf16[2,128,112]{2,1,0:T(8,128)(2,1)S(1)} %collective-permute-done.16.there, f32[448,3]{1,0:T(8,128)S(1)} %bitcast.7, bf16[448,512]{1,0:T(8,128)(2,1)S(1)} %shard_map.54.side.center, ...), custom_call_target="tpu_custom_call" | custom-call | bytes 1496328 | tf_op jit(solution)/shard_map/pallas_call | solution.py:78
  96.0 3.2 %collective-permute-start.20 = (bf16[448,256]{1,0:T(8,128)(2,1)S(1)}, bf16[448,256]{1,0:T(8,128)(2,1)S(1)}, u32[]{:S(2)}, u32[]{:S(2)}) collective-permute-start(bf16[448,256]{1,0:T(8,128)(2,1)S(1)} %shard_map.62), channel_id=1, source_target_pairs={{0,4},{1,5},{2,6},{3,7},{4,0},{5,1},{6,2},{7,3},{8,12},{9,13},{10,... | collective-permute-start | bytes 688136 | tf_op jit(solution)/shard_map/ppermute | solution.py:394
  99.2 1.2 %shard_map.61 = bf16[448,256]{1,0:T(8,128)(2,1)S(1)} custom-call(s32[2]{0:T(128)S(1)} %pad_add_fusion.place, bf16[2,128,112]{2,1,0:T(8,128)(2,1)S(1)} %collective-permute-done.15.mine, bf16[2,128,112]{2,1,0:T(8,128)(2,1)S(1)} %collective-permute-done.16.there, f32[448,3]{1,0:T(8,128)S(1)} %bitcast.8, bf16[448,512]{1,0:T(8,128)(2,1)S(1)} %shard_map.57.center.side, ...), custom_call_target="tpu_custom_call" | custom-call | bytes 1496328 | tf_op jit(solution)/shard_map/pallas_call | solution.py:78
  100.4 0.4 collective-permute-start.18
  100.8 1.2 %shard_map.60.refs_0_ = bf16[448,256]{1,0:T(8,128)(2,1)S(1)} custom-call(s32[2]{0:T(128)S(1)} %pad_add_fusion.place, bf16[2,128,112]{2,1,0:T(8,128)(2,1)S(1)} %collective-permute-done.15.mine, bf16[2,128,112]{2,1,0:T(8,128)(2,1)S(1)} %collective-permute-done.16.there, f32[448,3]{1,0:T(8,128)S(1)} %bitcast.9, bf16[448,512]{1,0:T(8,128)(2,1)S(1)} %shard_map.57.center.side, ...), custom_call_target="tpu_custom_call" | custom-call | bytes 1496328 | tf_op jit(solution)/shard_map/pallas_call | solution.py:78
  102.0 0.3 collective-permute-done.21.refs_3_
  102.3 4.7 %collective-permute-done.20.refs_2_ = bf16[448,256]{1,0:T(8,128)(2,1)S(1)} collective-permute-done((bf16[448,256]{1,0:T(8,128)(2,1)S(1)}, bf16[448,256]{1,0:T(8,128)(2,1)S(1)}, u32[]{:S(2)}, u32[]{:S(2)}) %collective-permute-start.20) | collective-permute-done | bytes 229408 | tf_op jit(solution)/shard_map/ppermute | solution.py:394
  107.0 0.8 collective-permute-done.18.refs_1_
  107.9 2.0 %shard_map.64 = bf16[256,1792]{1,0:T(8,128)(2,1)} custom-call(s32[2]{0:T(128)S(1)} %pad_add_fusion.place, bf16[448,256]{1,0:T(8,128)(2,1)S(1)} %shard_map.60.refs_0_, bf16[448,256]{1,0:T(8,128)(2,1)S(1)} %collective-permute-done.18.refs_1_, bf16[448,256]{1,0:T(8,128)(2,1)S(1)} %collective-permute-done.20.refs_2_, ...), custom_call_target="tpu_custom_call" | custom-call | bytes 917512 | tf_op jit(solution)/shard_map/pallas_call | solution.py:78
  (29 shorter events, 0.9 us)
Async XLA Ops:
  0.0 1.3 %copy-start.1 = (bf16[256,2240]{0,1:T(8,128)(2,1)S(1)}, bf16[256,2240]{0,1:T(8,128)(2,1)}, u32[]{:S(2)}) copy-start(bf16[256,2240]{0,1:T(8,128)(2,1)} %param.4) | copy-start | bytes 3440644
  1.3 4.8 %copy-start.2 = (bf16[112,2240]{1,0:T(8,128)(2,1)S(1)}, bf16[112,2240]{1,0:T(8,128)(2,1)}, u32[]{:S(2)}) copy-start(bf16[112,2240]{1,0:T(8,128)(2,1)} %w_keyval.1) | copy-start | bytes 1505284
  1.3 4.8 %copy-start.3 = (bf16[56,2240]{1,0:T(8,128)(2,1)S(1)}, bf16[56,2240]{1,0:T(8,128)(2,1)}, u32[]{:S(2)}) copy-start(bf16[56,2240]{1,0:T(8,128)(2,1)} %w_query.1) | copy-start | bytes 752644
  1.6 9.6 %copy-start.4 = (f32[3,1792]{1,0:T(4,128)S(1)}, f32[3,1792]{1,0:T(4,128)}, u32[]{:S(2)}) copy-start(f32[3,1792]{1,0:T(4,128)} %param.7) | copy-start | bytes 64516
  1.6 42.0 %collective-permute-start.2 = (bf16[2240,256]{1,0:T(8,128)(2,1)S(1)}, bf16[2240,256]{1,0:T(8,128)(2,1)S(1)}, u32[]{:S(2)}, u32[]{:S(2)}) collective-permute-start(bf16[2240,256]{1,0:T(8,128)(2,1)S(1)} %shard_map.47.refs_0_.block_0), channel_id=1, source_target_pairs={{0,2},{1,3},{2,0},{3,1},{4,6},{5,7},{6,4},{7,5},{8,10},{9,11},{10,... | collective-permute-start | bytes 3440648 | tf_op jit(solution)/shard_map/ppermute | solution.py:394
  4.6 39.0 %collective-permute-start.3 = (bf16[2240,256]{1,0:T(8,128)(2,1)S(1)}, bf16[2240,256]{1,0:T(8,128)(2,1)S(1)}, u32[]{:S(2)}, u32[]{:S(2)}) collective-permute-start(bf16[2240,256]{1,0:T(8,128)(2,1)S(1)} %shard_map.47.refs_0_.block_0), channel_id=1, source_target_pairs={{0,4},{1,5},{2,6},{3,7},{4,0},{5,1},{6,2},{7,3},{8,12},{9,13},{10,... | collective-permute-start | bytes 3440648 | tf_op jit(solution)/shard_map/ppermute | solution.py:394
  7.0 36.4 %collective-permute-start = (bf16[168,2240]{1,0:T(8,128)(2,1)}, bf16[168,2240]{1,0:T(8,128)(2,1)}, u32[]{:S(2)}, u32[]{:S(2)}) collective-permute-start(bf16[168,2240]{1,0:T(8,128)(2,1)} %shard_map.46.refs_0_), channel_id=1, source_target_pairs={{0,16},{1,17},{2,18},{3,19},{4,20},{5,21},{6,22},{7,23},{8,24},{9,... | collective-permute-start | bytes 2257928 | tf_op jit(solution)/shard_map/ppermute | solution.py:394
  9.6 34.0 %collective-permute-start.1 = (bf16[168,2240]{1,0:T(8,128)(2,1)}, bf16[168,2240]{1,0:T(8,128)(2,1)}, u32[]{:S(2)}, u32[]{:S(2)}) collective-permute-start(bf16[168,2240]{1,0:T(8,128)(2,1)} %shard_map.46.refs_0_), channel_id=1, source_target_pairs={{0,8},{1,9},{2,10},{3,11},{4,12},{5,13},{6,14},{7,15},{8,0},{9,1},... | collective-permute-start | bytes 2257928 | tf_op jit(solution)/shard_map/ppermute | solution.py:394
  11.2 32.4 %collective-permute-start.4 = (bf16[168,2240]{1,0:T(8,128)(2,1)}, bf16[168,2240]{1,0:T(8,128)(2,1)}, u32[]{:S(2)}, u32[]{:S(2)}) collective-permute-start(bf16[168,2240]{1,0:T(8,128)(2,1)} %shard_map.46.refs_0_), channel_id=1, source_target_pairs={{0,1},{1,0},{2,3},{3,2},{4,5},{5,4},{6,7},{7,6},{8,9},{9,8},{10,11... | collective-permute-start | bytes 2257928 | tf_op jit(solution)/shard_map/ppermute | solution.py:394
  44.2 15.9 %collective-permute-start.5 = (bf16[2240,256]{1,0:T(8,128)(2,1)S(1)}, bf16[2240,256]{1,0:T(8,128)(2,1)S(1)}, u32[]{:S(2)}, u32[]{:S(2)}) collective-permute-start(bf16[2240,256]{1,0:T(8,128)(2,1)S(1)} %shard_map.48), channel_id=1, source_target_pairs={{0,2},{1,5},{2,0},{3,7},{4,6},{5,1},{6,4},{7,3},{8,10},{9,13},{10,... | collective-permute-start | bytes 3440648 | tf_op jit(solution)/shard_map/ppermute | solution.py:394
  44.8 2.5 %collective-permute-start.8 = (bf16[168,2240]{1,0:T(8,128)(2,1)}, bf16[168,2240]{1,0:T(8,128)(2,1)S(1)}, u32[]{:S(2)}, u32[]{:S(2)}) collective-permute-start(bf16[168,2240]{1,0:T(8,128)(2,1)} %collective-permute-done.1.refs_1_), channel_id=1, source_target_pairs={{0,1},{1,0},{2,3},{3,2},{4,5},{5,4},{6,7},{7,6},{8,9},{9,8},{10,11... | collective-permute-start | bytes 2257928 | tf_op jit(solution)/shard_map/ppermute | solution.py:394
  44.8 3.6 %collective-permute-start.9 = (bf16[168,2240]{1,0:T(8,128)(2,1)}, bf16[168,2240]{1,0:T(8,128)(2,1)S(1)}, u32[]{:S(2)}, u32[]{:S(2)}) collective-permute-start(bf16[168,2240]{1,0:T(8,128)(2,1)} %collective-permute-done.refs_2_), channel_id=1, source_target_pairs={{0,1},{1,0},{2,3},{3,2},{4,5},{5,4},{6,7},{7,6},{8,9},{9,8},{10,11... | collective-permute-start | bytes 2257928 | tf_op jit(solution)/shard_map/ppermute | solution.py:394
  45.3 20.5 %collective-permute-start.6 = (bf16[168,2240]{1,0:T(8,128)(2,1)}, bf16[168,2240]{1,0:T(8,128)(2,1)S(1)}, u32[]{:S(2)}, u32[]{:S(2)}) collective-permute-start(bf16[168,2240]{1,0:T(8,128)(2,1)} %shard_map.46.refs_0_), channel_id=1, source_target_pairs={{8,16},{9,17},{10,18},{11,19},{12,20},{13,21},{14,22},{15,23},{16,... | collective-permute-start | bytes 2257928 | tf_op jit(solution)/shard_map/ppermute | solution.py:394
  46.0 21.7 %collective-permute-start.7 = (bf16[168,2240]{1,0:T(8,128)(2,1)}, bf16[168,2240]{1,0:T(8,128)(2,1)S(1)}, u32[]{:S(2)}, u32[]{:S(2)}) collective-permute-start(bf16[168,2240]{1,0:T(8,128)(2,1)} %collective-permute-done.refs_2_), channel_id=1, source_target_pairs={{8,0},{9,1},{10,2},{11,3},{12,4},{13,5},{14,6},{15,7},{16,24},{17,... | collective-permute-start | bytes 2257928 | tf_op jit(solution)/shard_map/ppermute | solution.py:394
  68.4 2.3 %collective-permute-start.10 = (bf16[168,2240]{1,0:T(8,128)(2,1)S(1)}, bf16[168,2240]{1,0:T(8,128)(2,1)S(1)}, u32[]{:S(2)}, u32[]{:S(2)}) collective-permute-start(bf16[168,2240]{1,0:T(8,128)(2,1)S(1)} %shard_map.53.last), channel_id=1, source_target_pairs={{0,1},{1,0},{2,3},{3,2},{4,5},{5,4},{6,7},{7,6},{8,9},{9,8},{10,11... | collective-permute-start | bytes 2257928 | tf_op jit(solution)/shard_map/ppermute | solution.py:394
  72.7 1.4 %collective-permute-start.11 = (f32[2,128,112]{2,1,0:T(8,128)S(1)}, f32[2,128,112]{2,1,0:T(8,128)S(1)}, u32[]{:S(2)}, u32[]{:S(2)}) collective-permute-start(f32[2,128,112]{2,1,0:T(8,128)S(1)} %shard_map.56), channel_id=1, source_target_pairs={{0,1},{1,0},{2,3},{3,2},{4,5},{5,4},{6,7},{7,6},{8,9},{9,8},{10,11... | collective-permute-start | bytes 344072 | tf_op jit(solution)/shard_map/ppermute | solution.py:394
  74.2 19.4 %copy-start = (f32[3,4,1,112]{0,3,1,2:T(8,128)S(1)}, f32[3,4,1,112]{0,3,1,2:T(8,128)}, u32[]{:S(2)}) copy-start(f32[3,4,1,112]{0,3,1,2:T(8,128)} %copy.6) | copy-start | bytes 16132
  74.2 5.5 %collective-permute-start.14 = (bf16[2,128,112]{2,1,0:T(8,128)(2,1)S(1)}, bf16[2,128,112]{2,1,0:T(8,128)(2,1)S(1)}, u32[]{:S(2)}, u32[]{:S(2)}) collective-permute-start(bf16[2,128,112]{2,1,0:T(8,128)(2,1)S(1)} %shard_map.58.refs_0_), channel_id=1, source_target_pairs={{0,8},{1,9},{2,10},{3,11},{4,12},{5,13},{6,14},{7,15},{8,0},{9,1},... | collective-permute-start | bytes 172040 | tf_op jit(solution)/shard_map/ppermute | solution.py:394
  74.5 7.1 %collective-permute-start.12 = (bf16[2,128,112]{2,1,0:T(8,128)(2,1)S(1)}, bf16[2,128,112]{2,1,0:T(8,128)(2,1)S(1)}, u32[]{:S(2)}, u32[]{:S(2)}) collective-permute-start(bf16[2,128,112]{2,1,0:T(8,128)(2,1)S(1)} %shard_map.58.refs_0_), channel_id=1, source_target_pairs={{0,16},{1,17},{2,18},{3,19},{4,20},{5,21},{6,22},{7,23},{8,24},{9,... | collective-permute-start | bytes 172040 | tf_op jit(solution)/shard_map/ppermute | solution.py:394
  77.6 6.2 %collective-permute-start.13 = (bf16[2,128,112]{2,1,0:T(8,128)(2,1)S(1)}, bf16[2,128,112]{2,1,0:T(8,128)(2,1)S(1)}, u32[]{:S(2)}, u32[]{:S(2)}) collective-permute-start(bf16[2,128,112]{2,1,0:T(8,128)(2,1)S(1)} %shard_map.58.refs_0_), channel_id=1, source_target_pairs={{0,24},{1,25},{2,26},{3,27},{4,28},{5,29},{6,30},{7,31},{8,16},{9,... | collective-permute-start | bytes 172040 | tf_op jit(solution)/shard_map/ppermute | solution.py:394
  79.7 13.9 %collective-permute-start.19 = (bf16[448,512]{1,0:T(8,128)(2,1)S(1)}, bf16[448,512]{1,0:T(8,128)(2,1)S(1)}, u32[]{:S(2)}, u32[]{:S(2)}) collective-permute-start(bf16[448,512]{1,0:T(8,128)(2,1)S(1)} %shard_map.57.center.side), channel_id=1, source_target_pairs={{4,12},{5,13},{6,14},{7,15},{8,0},{9,1},{10,2},{11,3},{12,20},{13,... | collective-permute-start | bytes 1376264 | tf_op jit(solution)/shard_map/ppermute | solution.py:394
  83.7 15.5 %collective-permute-start.17 = (bf16[448,512]{1,0:T(8,128)(2,1)S(1)}, bf16[448,512]{1,0:T(8,128)(2,1)S(1)}, u32[]{:S(2)}, u32[]{:S(2)}) collective-permute-start(bf16[448,512]{1,0:T(8,128)(2,1)S(1)} %shard_map.54.side.center), channel_id=1, source_target_pairs={{0,8},{1,9},{2,10},{3,11},{8,16},{9,17},{10,18},{11,19},{12,4},{13... | collective-permute-start | bytes 1376264 | tf_op jit(solution)/shard_map/ppermute | solution.py:394
  87.0 3.8 %collective-permute-start.15 = (bf16[2,128,112]{2,1,0:T(8,128)(2,1)S(1)}, bf16[2,128,112]{2,1,0:T(8,128)(2,1)S(1)}, u32[]{:S(2)}, u32[]{:S(2)}) collective-permute-start(bf16[2,128,112]{2,1,0:T(8,128)(2,1)S(1)} %shard_map.59), channel_id=1, source_target_pairs={{0,0},{1,2},{2,4},{3,6},{4,1},{5,3},{6,5},{7,7},{8,8},{9,10},{10,1... | collective-permute-start | bytes 172040 | tf_op jit(solution)/shard_map/ppermute | solution.py:394
  87.6 4.5 %collective-permute-start.16 = (bf16[2,128,112]{2,1,0:T(8,128)(2,1)S(1)}, bf16[2,128,112]{2,1,0:T(8,128)(2,1)S(1)}, u32[]{:S(2)}, u32[]{:S(2)}) collective-permute-start(bf16[2,128,112]{2,1,0:T(8,128)(2,1)S(1)} %shard_map.59), channel_id=1, source_target_pairs={{0,1},{1,3},{2,5},{3,7},{4,0},{5,2},{6,4},{7,6},{8,9},{9,11},{10,1... | collective-permute-start | bytes 172040 | tf_op jit(solution)/shard_map/ppermute | solution.py:394
  94.8 7.6 %collective-permute-start.21 = (bf16[448,256]{1,0:T(8,128)(2,1)S(1)}, bf16[448,256]{1,0:T(8,128)(2,1)S(1)}, u32[]{:S(2)}, u32[]{:S(2)}) collective-permute-start(bf16[448,256]{1,0:T(8,128)(2,1)S(1)} %shard_map.63), channel_id=1, source_target_pairs={{0,6},{1,7},{2,4},{3,5},{4,2},{5,3},{6,0},{7,1},{8,14},{9,15},{10,... | collective-permute-start | bytes 688136 | tf_op jit(solution)/shard_map/ppermute | solution.py:394
  96.0 11.0 %collective-permute-start.20 = (bf16[448,256]{1,0:T(8,128)(2,1)S(1)}, bf16[448,256]{1,0:T(8,128)(2,1)S(1)}, u32[]{:S(2)}, u32[]{:S(2)}) collective-permute-start(bf16[448,256]{1,0:T(8,128)(2,1)S(1)} %shard_map.62), channel_id=1, source_target_pairs={{0,4},{1,5},{2,6},{3,7},{4,0},{5,1},{6,2},{7,3},{8,12},{9,13},{10,... | collective-permute-start | bytes 688136 | tf_op jit(solution)/shard_map/ppermute | solution.py:394
  100.4 7.4 %collective-permute-start.18 = (bf16[448,256]{1,0:T(8,128)(2,1)S(1)}, bf16[448,256]{1,0:T(8,128)(2,1)S(1)}, u32[]{:S(2)}, u32[]{:S(2)}) collective-permute-start(bf16[448,256]{1,0:T(8,128)(2,1)S(1)} %shard_map.61), channel_id=1, source_target_pairs={{0,2},{1,3},{2,0},{3,1},{4,6},{5,7},{6,4},{7,5},{8,10},{9,11},{10,... | collective-permute-start | bytes 688136 | tf_op jit(solution)/shard_map/ppermute | solution.py:394

commit v7 on v6

--- a/solution.py
+++ b/solution.py
@@ -90,7 +90,7 @@
     return jax.ShapeDtypeStruct(shape, dtype)
 
 
-def begin_kernel(tokens, normed):
+def begin_kernel(tokens, low, high):
     depth = tokens.shape[0]
     step = depth // 10
     total = jnp.zeros((1, tokens.shape[1]), jnp.float32)
@@ -100,24 +100,42 @@
     scale_inv = lax.rsqrt(total / depth + epsilon)
     for start in range(0, depth, step):
         values = tokens[start : start + step].astype(jnp.float32)
-        normed[start : start + step] = (values * scale_inv).astype(jnp.bfloat16)
+        half, at = (low, start) if start < depth // 2 else (high, start - depth // 2)
+        half[at : at + step] = (values * scale_inv).astype(jnp.bfloat16)
 
 
 def begin(tokens):
-    return kernel_call(begin_kernel, like(tokens.shape), tokens, scalars=0)
-
-
-def relay_kernel(place, beside, across, out):
+    depth, count = tokens.shape
+    outs = (like((depth // 2, count)),) * 2
+    return kernel_call(begin_kernel, outs, tokens, scalars=0)
+
+
+def relay_kernel(place, *refs):
+    *halves, out = refs
     core = place[1] % 2
-    for k, block in enumerate((across, beside)):
+    depth = halves[0].shape[0]
+    for k, block in enumerate((halves[2:], halves[:2])):
 
         @pl.when(core == k)
         def _():
-            out[...] = block[...]
+            out[:depth] = block[0][...]
+            out[depth:] = block[1][...]
 
 
 def relay(place, beside, across):
-    return kernel_call(relay_kernel, like(beside.shape), place, beside, across)
+    depth, count = beside[0].shape
+    return kernel_call(relay_kernel, like((2 * depth, count)), place, *beside, *across)
+
+
+def whole_kernel(low, high, out):
+    depth = low.shape[0]
+    out[:depth] = low[...]
+    out[depth:] = high[...]
+
+
+def whole(halves):
+    depth, count = halves[0].shape
+    return kernel_call(whole_kernel, like((2 * depth, count)), *halves, scalars=0)
 
 
 def spaced(rows):
@@ -421,17 +439,19 @@
     weights_2 = between(weights, cross[2])
     weights_1 = between(weights, cross[1])
     own = begin(tokens.T)
-    beside, across = swap(own, 2), swap(own, 4)
+    beside, across = ([swap(half, bits) for half in own] for bits in (2, 4))
+    weights_2, weights_1, weights, *halves, tap = together(
+        weights_2, weights_1, weights, *own, *beside, *across, tap
+    )
+    own, beside, across = halves[:2], halves[2:4], halves[4:]
     weights_there = swap(weights, 1)
-    weights_2, weights_1, weights, own, beside, across, weights_there, tap = together(
-        weights_2, weights_1, weights, own, beside, across, weights_there, tap
-    )
 
     weights_inner = between(weights, inner)
     weights_outer = between(weights_2, outer)
     passed = relay(place, beside, across)
     diagonal = send(passed, lambda z, slot: (z, slot ^ (4 if slot % 2 else 2)))
     there_2, there_1 = swap(weights_2, 1), swap(weights_1, 1)
+    own, beside, across = whole(own), whole(beside), whole(across)
     keyval, keyval_there, query = ready_rows(
         (weights, weights_1, weights_2), (weights_there, there_1, there_2)
     )

time: 110 us -> 109 us (level)
  waiting for transfers between devices: 53.9 us -> 49.8 us
  starting transfers between devices: 28.5 us -> 31 us
  Pallas kernels: 24.8 us -> 26.2 us
    ppermute x22 -> x24, waiting for transfers between devices: 53.9 us -> 49.8 us  [send(): return lax.ppermute(value, 'frame', pairs)]
    ppermute x22 -> x24, starting transfers between devices: 28.5 us -> 31 us  [send(): return lax.ppermute(value, 'frame', pairs)]
    pallas_call x19 -> x22, Pallas kernels: 24.8 us -> 26.2 us  [kernel_call(): pl.pallas_call(body, out_shape=outs, in_specs=[SMEM] * scalars + [VMEM] *...]
  transfers between devices with their start and end apart: 22 -> 24, of which waited for: 14 -> 15; matrix products, arithmetic and copies ran while one was open for 1% -> 0% of each run, Pallas kernels for 18% -> 19%
where the time goes in v7:
time: 109 us
  waiting for transfers between devices  49.8 us (46%)
  starting transfers between devices  31 us (28%)
  Pallas kernels  26.2 us (24%)
  local copies, waits for them, and re-layouts  1.51 us (1%)
    ppermute x24, waiting for transfers between devices, send(): return lax.ppermute(value, 'frame', pairs)  49.8 us
    ppermute x24, starting transfers between devices, send(): return lax.ppermute(value, 'frame', pairs)  31 us
    pallas_call x22, Pallas kernels, kernel_call(): pl.pallas_call(body, out_shape=outs, in_specs=[SMEM] * scalars + [VMEM] *...  26.2 us
  transfers between devices with their start and end apart: 24, of which 15 were waited for; matrix products, arithmetic and copies ran while one was open for 0% of the time, Pallas kernels for 19%

profile of v7, /device:TPU:0, one launch (start us, length us, event | category | flops | bytes accessed | tf_op | source)
XLA Modules:
  0.0 108.8 jit_solution(9778756882086875440)
XLA Ops:
  0.0 1.3 %copy-done = bf16[256,2240]{0,1:T(8,128)(2,1)S(1)} copy-done((bf16[256,2240]{0,1:T(8,128)(2,1)S(1)}, bf16[256,2240]{0,1:T(8,128)(2,1)}, u32[]{:S(2)}) %copy-start) | copy-done | bytes 1146904
  1.3 1.2 %shard_map.47 = (bf16[1120,256]{1,0:T(8,128)(2,1)}, bf16[1120,256]{1,0:T(8,128)(2,1)}) custom-call(bf16[2240,256]{1,0:T(8,128)(2,1)S(1)} %bitcast.10), custom_call_target="tpu_custom_call" | custom-call | bytes 1146880 | tf_op jit(solution)/shard_map/pallas_call | solution.py:78
  2.5 2.9 %collective-permute-start.2 = (bf16[1120,256]{1,0:T(8,128)(2,1)}, bf16[1120,256]{1,0:T(8,128)(2,1)S(1)}, u32[]{:S(2)}, u32[]{:S(2)}) collective-permute-start(bf16[1120,256]{1,0:T(8,128)(2,1)} %get-tuple-element.49.low), channel_id=1, source_target_pairs={{0,2},{1,3},{2,0},{3,1},{4,6},{5,7},{6,4},{7,5},{8,10},{9,11},{10,... | collective-permute-start | bytes 1720328 | tf_op jit(solution)/shard_map/ppermute | solution.py:412
  5.5 2.7 %collective-permute-start = (bf16[168,2240]{1,0:T(8,128)(2,1)S(1)}, bf16[168,2240]{1,0:T(8,128)(2,1)}, u32[]{:S(2)}, u32[]{:S(2)}) collective-permute-start(bf16[168,2240]{1,0:T(8,128)(2,1)S(1)} %shard_map.46.refs_0_), channel_id=1, source_target_pairs={{0,16},{1,17},{2,18},{3,19},{4,20},{5,21},{6,22},{7,23},{8,24},{9,... | collective-permute-start | bytes 2257928 | tf_op jit(solution)/shard_map/ppermute | solution.py:412
  8.1 1.6 %collective-permute-start.1 = (bf16[168,2240]{1,0:T(8,128)(2,1)S(1)}, bf16[168,2240]{1,0:T(8,128)(2,1)}, u32[]{:S(2)}, u32[]{:S(2)}) collective-permute-start(bf16[168,2240]{1,0:T(8,128)(2,1)S(1)} %shard_map.46.refs_0_), channel_id=1, source_target_pairs={{0,8},{1,9},{2,10},{3,11},{4,12},{5,13},{6,14},{7,15},{8,0},{9,1},... | collective-permute-start | bytes 2257928 | tf_op jit(solution)/shard_map/ppermute | solution.py:412
  9.7 1.5 %collective-permute-start.4 = (bf16[1120,256]{1,0:T(8,128)(2,1)}, bf16[1120,256]{1,0:T(8,128)(2,1)S(1)}, u32[]{:S(2)}, u32[]{:S(2)}) collective-permute-start(bf16[1120,256]{1,0:T(8,128)(2,1)} %get-tuple-element.49.low), channel_id=1, source_target_pairs={{0,4},{1,5},{2,6},{3,7},{4,0},{5,1},{6,2},{7,3},{8,12},{9,13},{10,... | collective-permute-start | bytes 1720328 | tf_op jit(solution)/shard_map/ppermute | solution.py:412
  11.2 0.5 collective-permute-start.3
  11.7 7.7 %collective-permute-done.2.refs_0_.low = bf16[1120,256]{1,0:T(8,128)(2,1)S(1)} collective-permute-done((bf16[1120,256]{1,0:T(8,128)(2,1)}, bf16[1120,256]{1,0:T(8,128)(2,1)S(1)}, u32[]{:S(2)}, u32[]{:S(2)}) %collective-permute-start.2) | collective-permute-done | bytes 573472 | tf_op jit(solution)/shard_map/ppermute | solution.py:412
  19.4 2.1 %collective-permute-start.5 = (bf16[1120,256]{1,0:T(8,128)(2,1)}, bf16[1120,256]{1,0:T(8,128)(2,1)S(1)}, u32[]{:S(2)}, u32[]{:S(2)}) collective-permute-start(bf16[1120,256]{1,0:T(8,128)(2,1)} %get-tuple-element.50.high), channel_id=1, source_target_pairs={{0,4},{1,5},{2,6},{3,7},{4,0},{5,1},{6,2},{7,3},{8,12},{9,13},{10,... | collective-permute-start | bytes 1720328 | tf_op jit(solution)/shard_map/ppermute | solution.py:412
  21.8 9.1 %collective-permute-done.3.refs_1_.high = bf16[1120,256]{1,0:T(8,128)(2,1)S(1)} collective-permute-done((bf16[1120,256]{1,0:T(8,128)(2,1)}, bf16[1120,256]{1,0:T(8,128)(2,1)S(1)}, u32[]{:S(2)}, u32[]{:S(2)}) %collective-permute-start.3) | collective-permute-done | bytes 573472 | tf_op jit(solution)/shard_map/ppermute | solution.py:412
  30.9 5.2 %collective-permute-done.5.refs_3_.high = bf16[1120,256]{1,0:T(8,128)(2,1)S(1)} collective-permute-done((bf16[1120,256]{1,0:T(8,128)(2,1)}, bf16[1120,256]{1,0:T(8,128)(2,1)S(1)}, u32[]{:S(2)}, u32[]{:S(2)}) %collective-permute-start.5) | collective-permute-done | bytes 573472 | tf_op jit(solution)/shard_map/ppermute | solution.py:412
  36.1 5.9 %collective-permute-done.refs_2_ = bf16[168,2240]{1,0:T(8,128)(2,1)} collective-permute-done((bf16[168,2240]{1,0:T(8,128)(2,1)S(1)}, bf16[168,2240]{1,0:T(8,128)(2,1)}, u32[]{:S(2)}, u32[]{:S(2)}) %collective-permute-start) | collective-permute-done | bytes 752672 | tf_op jit(solution)/shard_map/ppermute | solution.py:412
  42.2 0.6 shard_map.48
  42.9 0.6 collective-permute-start.6
  43.4 1.3 %collective-permute-start.11 = (bf16[168,2240]{1,0:T(8,128)(2,1)}, bf16[168,2240]{1,0:T(8,128)(2,1)S(1)}, u32[]{:S(2)}, u32[]{:S(2)}) collective-permute-start(bf16[168,2240]{1,0:T(8,128)(2,1)} %collective-permute-done.refs_2_), channel_id=1, source_target_pairs={{0,1},{1,0},{2,3},{3,2},{4,5},{5,4},{6,7},{7,6},{8,9},{9,8},{10,11... | collective-permute-start | bytes 2257928 | tf_op jit(solution)/shard_map/ppermute | solution.py:412
  44.7 0.7 collective-permute-start.7
  45.4 1.3 %collective-permute-start.8 = (bf16[168,2240]{1,0:T(8,128)(2,1)}, bf16[168,2240]{1,0:T(8,128)(2,1)S(1)}, u32[]{:S(2)}, u32[]{:S(2)}) collective-permute-start(bf16[168,2240]{1,0:T(8,128)(2,1)} %collective-permute-done.refs_2_), channel_id=1, source_target_pairs={{8,0},{9,1},{10,2},{11,3},{12,4},{13,5},{14,6},{15,7},{16,24},{17,... | collective-permute-start | bytes 2257928 | tf_op jit(solution)/shard_map/ppermute | solution.py:412
  46.9 1.3 %shard_map.50.refs_0_.block_0 = bf16[2240,256]{1,0:T(8,128)(2,1)S(1)} custom-call(bf16[1120,256]{1,0:T(8,128)(2,1)} %get-tuple-element.49.low, bf16[1120,256]{1,0:T(8,128)(2,1)} %get-tuple-element.50.high), custom_call_target="tpu_custom_call" | custom-call | bytes 1146880 | tf_op jit(solution)/shard_map/pallas_call | solution.py:78
  48.2 1.9 %shard_map.49 = (bf16[336,2240]{1,0:T(8,128)(2,1)S(1)}, bf16[336,2240]{1,0:T(8,128)(2,1)S(1)}, bf16[384,2240]{1,0:T(8,128)(2,1)S(1)}) custom-call(bf16[168,2240]{1,0:T(8,128)(2,1)S(1)} %shard_map.46.refs_0_, bf16[168,2240]{1,0:T(8,128)(2,1)} %collective-permute-done.1.refs_1_, bf16[168,2240]{1,0:T(8,128)(2,1)} %collective-permute-done.refs_2_, ...), custom_call_target="tpu_custom_call" | custom-call | bytes 4515840 | tf_op jit(solution)/shard_map/pallas_call | solution.py:78
  50.1 1.6 %shard_map.54.near = bf16[448,512]{1,0:T(8,128)(2,1)S(1)} custom-call(s32[2]{0:T(128)S(1)} %pad_add_fusion.place, bf16[384,2240]{1,0:T(8,128)(2,1)S(1)} %get-tuple-element.51.rows, bf16[2240,256]{1,0:T(8,128)(2,1)S(1)} %shard_map.50.refs_0_.block_0, bf16[2240,256]{1,0:T(8,128)(2,1)S(1)} %shard_map.51.refs_1_.block_1), custom_call_target="tpu_custom_call" | custom-call | bytes 4014088 | tf_op jit(solution)/shard_map/pallas_call | solution.py:78
  51.8 7.0 %collective-permute-done.6.refs_3_.refs_1_.block_1 = bf16[2240,256]{1,0:T(8,128)(2,1)S(1)} collective-permute-done((bf16[2240,256]{1,0:T(8,128)(2,1)S(1)}, bf16[2240,256]{1,0:T(8,128)(2,1)S(1)}, u32[]{:S(2)}, u32[]{:S(2)}) %collective-permute-start.6) | collective-permute-done | bytes 1146912 | tf_op jit(solution)/shard_map/ppermute | solution.py:412
  58.8 1.6 %shard_map.55.near = bf16[448,512]{1,0:T(8,128)(2,1)S(1)} custom-call(s32[2]{0:T(128)S(1)} %pad_add_fusion.place, bf16[384,2240]{1,0:T(8,128)(2,1)S(1)} %get-tuple-element.51.rows, bf16[2240,256]{1,0:T(8,128)(2,1)S(1)} %shard_map.52.refs_2_.refs_0_.block_0, bf16[2240,256]{1,0:T(8,128)(2,1)S(1)} %collective-permute-done.6.refs_3_.refs_1_.block_1), custom_call_target="tpu_custom_call" | custom-call | bytes 4014088 | tf_op jit(solution)/shard_map/pallas_call | solution.py:78
  60.4 4.1 %shard_map.53.part = f32[2,128,112]{2,1,0:T(8,128)S(1)} custom-call(s32[2]{0:T(128)S(1)} %pad_add_fusion.place, bf16[336,2240]{1,0:T(8,128)(2,1)S(1)} %get-tuple-element.47.mine.rows, bf16[336,2240]{1,0:T(8,128)(2,1)S(1)} %get-tuple-element.48.there.rows, bf16[2240,256]{1,0:T(8,128)(2,1)S(1)} %shard_map.50.refs_0_.block_0, ...), custom_call_target="tpu_custom_call" | custom-call | flops 2055208960 | bytes 7598088 | tf_op jit(solution)/shard_map/pallas_call | solution.py:78
  64.5 3.1 %collective-permute-done.8.outer = bf16[168,2240]{1,0:T(8,128)(2,1)S(1)} collective-permute-done((bf16[168,2240]{1,0:T(8,128)(2,1)}, bf16[168,2240]{1,0:T(8,128)(2,1)S(1)}, u32[]{:S(2)}, u32[]{:S(2)}) %collective-permute-start.8) | collective-permute-done | bytes 752672 | tf_op jit(solution)/shard_map/ppermute | solution.py:412
  67.6 0.6 shard_map.56.last
  68.3 2.0 %shard_map.58.refs_0_ = f32[2,128,112]{2,1,0:T(8,128)S(1)} custom-call(s32[2]{0:T(128)S(1)} %pad_add_fusion.place, f32[2,128,112]{2,1,0:T(8,128)S(1)} %shard_map.53.part, bf16[336,2240]{1,0:T(8,128)(2,1)S(1)} %get-tuple-element.47.mine.rows, bf16[168,2240]{1,0:T(8,128)(2,1)S(1)} %shard_map.56.last, bf16[2240,256]{1,0:T(8,128)(2,1)S(1)} %shard_map.50.refs_0_.block_0, ...), custom_call_target="tpu_custom_call" | custom-call | flops 1027604480 | bytes 6960136 | tf_op jit(solution)/shard_map/pallas_call | solution.py:78
  70.6 2.0 %shard_map.59 = f32[2,128,112]{2,1,0:T(8,128)S(1)} custom-call(s32[2]{0:T(128)S(1)} %pad_add_fusion.place, f32[2,128,112]{2,1,0:T(8,128)S(1)} %shard_map.53.part, bf16[336,2240]{1,0:T(8,128)(2,1)S(1)} %get-tuple-element.48.there.rows, bf16[168,2240]{1,0:T(8,128)(2,1)S(1)} %collective-permute-done.12.last_there.last, ...), custom_call_target="tpu_custom_call" | custom-call | flops 1027604480 | bytes 6960136 | tf_op jit(solution)/shard_map/pallas_call | solution.py:78
  72.9 1.0 shard_map.60.center.side
  74.2 3.3 %collective-permute-start.14 = (bf16[2,128,112]{2,1,0:T(8,128)(2,1)S(1)}, bf16[2,128,112]{2,1,0:T(8,128)(2,1)S(1)}, u32[]{:S(2)}, u32[]{:S(2)}) collective-permute-start(bf16[2,128,112]{2,1,0:T(8,128)(2,1)S(1)} %shard_map.61.refs_0_), channel_id=1, source_target_pairs={{0,16},{1,17},{2,18},{3,19},{4,20},{5,21},{6,22},{7,23},{8,24},{9,... | collective-permute-start | bytes 172040 | tf_op jit(solution)/shard_map/ppermute | solution.py:412
  77.4 1.1 collective-permute-start.15
  78.5 1.1 shard_map.57.side.center
  79.6 1.3 %collective-permute-start.21 = (bf16[448,512]{1,0:T(8,128)(2,1)S(1)}, bf16[448,512]{1,0:T(8,128)(2,1)S(1)}, u32[]{:S(2)}, u32[]{:S(2)}) collective-permute-start(bf16[448,512]{1,0:T(8,128)(2,1)S(1)} %shard_map.60.center.side), channel_id=1, source_target_pairs={{4,12},{5,13},{6,14},{7,15},{8,0},{9,1},{10,2},{11,3},{12,20},{13,... | collective-permute-start | bytes 1376264 | tf_op jit(solution)/shard_map/ppermute | solution.py:412
  80.9 0.6 collective-permute-done.14.refs_1_
  81.5 2.1 %collective-permute-done.15.refs_2_ = bf16[2,128,112]{2,1,0:T(8,128)(2,1)S(1)} collective-permute-done((bf16[2,128,112]{2,1,0:T(8,128)(2,1)S(1)}, bf16[2,128,112]{2,1,0:T(8,128)(2,1)S(1)}, u32[]{:S(2)}, u32[]{:S(2)}) %collective-permute-start.15) | collective-permute-done | bytes 57376 | tf_op jit(solution)/shard_map/ppermute | solution.py:412
  83.5 3.2 %collective-permute-start.19 = (bf16[448,512]{1,0:T(8,128)(2,1)S(1)}, bf16[448,512]{1,0:T(8,128)(2,1)S(1)}, u32[]{:S(2)}, u32[]{:S(2)}) collective-permute-start(bf16[448,512]{1,0:T(8,128)(2,1)S(1)} %shard_map.57.side.center), channel_id=1, source_target_pairs={{0,8},{1,9},{2,10},{3,11},{8,16},{9,17},{10,18},{11,19},{12,4},{13... | collective-permute-start | bytes 1376264 | tf_op jit(solution)/shard_map/ppermute | solution.py:412
  86.8 0.7 collective-permute-start.17
  87.5 2.2 %collective-permute-start.18 = (bf16[2,128,112]{2,1,0:T(8,128)(2,1)S(1)}, bf16[2,128,112]{2,1,0:T(8,128)(2,1)S(1)}, u32[]{:S(2)}, u32[]{:S(2)}) collective-permute-start(bf16[2,128,112]{2,1,0:T(8,128)(2,1)S(1)} %shard_map.62), channel_id=1, source_target_pairs={{0,1},{1,3},{2,5},{3,7},{4,0},{5,2},{6,4},{7,6},{8,9},{9,11},{10,1... | collective-permute-start | bytes 172040 | tf_op jit(solution)/shard_map/ppermute | solution.py:412
  89.6 2.4 %collective-permute-done.18.there = bf16[2,128,112]{2,1,0:T(8,128)(2,1)S(1)} collective-permute-done((bf16[2,128,112]{2,1,0:T(8,128)(2,1)S(1)}, bf16[2,128,112]{2,1,0:T(8,128)(2,1)S(1)}, u32[]{:S(2)}, u32[]{:S(2)}) %collective-permute-start.18) | collective-permute-done | bytes 57376 | tf_op jit(solution)/shard_map/ppermute | solution.py:412
  92.0 1.4 %collective-permute-done.21.halo = bf16[448,512]{1,0:T(8,128)(2,1)S(1)} collective-permute-done((bf16[448,512]{1,0:T(8,128)(2,1)S(1)}, bf16[448,512]{1,0:T(8,128)(2,1)S(1)}, u32[]{:S(2)}, u32[]{:S(2)}) %collective-permute-start.21) | collective-permute-done | bytes 458784 | tf_op jit(solution)/shard_map/ppermute | solution.py:412
  93.4 1.2 %shard_map.66 = bf16[448,256]{1,0:T(8,128)(2,1)S(1)} custom-call(s32[2]{0:T(128)S(1)} %pad_add_fusion.place, bf16[2,128,112]{2,1,0:T(8,128)(2,1)S(1)} %collective-permute-done.17.mine, bf16[2,128,112]{2,1,0:T(8,128)(2,1)S(1)} %collective-permute-done.18.there, f32[448,3]{1,0:T(8,128)S(1)} %bitcast.6, bf16[448,512]{1,0:T(8,128)(2,1)S(1)} %shard_map.57.side.center, ...), custom_call_target="tpu_custom_call" | custom-call | bytes 1496328 | tf_op jit(solution)/shard_map/pallas_call | solution.py:78
  94.6 1.2 %shard_map.65 = bf16[448,256]{1,0:T(8,128)(2,1)S(1)} custom-call(s32[2]{0:T(128)S(1)} %pad_add_fusion.place, bf16[2,128,112]{2,1,0:T(8,128)(2,1)S(1)} %collective-permute-done.17.mine, bf16[2,128,112]{2,1,0:T(8,128)(2,1)S(1)} %collective-permute-done.18.there, f32[448,3]{1,0:T(8,128)S(1)} %bitcast.7, bf16[448,512]{1,0:T(8,128)(2,1)S(1)} %shard_map.57.side.center, ...), custom_call_target="tpu_custom_call" | custom-call | bytes 1496328 | tf_op jit(solution)/shard_map/pallas_call | solution.py:78
  95.8 2.3 %collective-permute-start.22 = (bf16[448,256]{1,0:T(8,128)(2,1)S(1)}, bf16[448,256]{1,0:T(8,128)(2,1)S(1)}, u32[]{:S(2)}, u32[]{:S(2)}) collective-permute-start(bf16[448,256]{1,0:T(8,128)(2,1)S(1)} %shard_map.65), channel_id=1, source_target_pairs={{0,4},{1,5},{2,6},{3,7},{4,0},{5,1},{6,2},{7,3},{8,12},{9,13},{10,... | collective-permute-start | bytes 688136 | tf_op jit(solution)/shard_map/ppermute | solution.py:412
  98.1 1.2 %shard_map.64 = bf16[448,256]{1,0:T(8,128)(2,1)S(1)} custom-call(s32[2]{0:T(128)S(1)} %pad_add_fusion.place, bf16[2,128,112]{2,1,0:T(8,128)(2,1)S(1)} %collective-permute-done.17.mine, bf16[2,128,112]{2,1,0:T(8,128)(2,1)S(1)} %collective-permute-done.18.there, f32[448,3]{1,0:T(8,128)S(1)} %bitcast.8, bf16[448,512]{1,0:T(8,128)(2,1)S(1)} %shard_map.60.center.side, ...), custom_call_target="tpu_custom_call" | custom-call | bytes 1496328 | tf_op jit(solution)/shard_map/pallas_call | solution.py:78
  99.3 1.3 %collective-permute-start.20 = (bf16[448,256]{1,0:T(8,128)(2,1)S(1)}, bf16[448,256]{1,0:T(8,128)(2,1)S(1)}, u32[]{:S(2)}, u32[]{:S(2)}) collective-permute-start(bf16[448,256]{1,0:T(8,128)(2,1)S(1)} %shard_map.64), channel_id=1, source_target_pairs={{0,2},{1,3},{2,0},{3,1},{4,6},{5,7},{6,4},{7,5},{8,10},{9,11},{10,... | collective-permute-start | bytes 688136 | tf_op jit(solution)/shard_map/ppermute | solution.py:412
  100.7 1.2 %shard_map.63.refs_0_ = bf16[448,256]{1,0:T(8,128)(2,1)S(1)} custom-call(s32[2]{0:T(128)S(1)} %pad_add_fusion.place, bf16[2,128,112]{2,1,0:T(8,128)(2,1)S(1)} %collective-permute-done.17.mine, bf16[2,128,112]{2,1,0:T(8,128)(2,1)S(1)} %collective-permute-done.18.there, f32[448,3]{1,0:T(8,128)S(1)} %bitcast.9, bf16[448,512]{1,0:T(8,128)(2,1)S(1)} %shard_map.60.center.side, ...), custom_call_target="tpu_custom_call" | custom-call | bytes 1496328 | tf_op jit(solution)/shard_map/pallas_call | solution.py:78
  101.9 0.5 collective-permute-done.23.refs_3_
  102.4 4.1 %collective-permute-done.22.refs_2_ = bf16[448,256]{1,0:T(8,128)(2,1)S(1)} collective-permute-done((bf16[448,256]{1,0:T(8,128)(2,1)S(1)}, bf16[448,256]{1,0:T(8,128)(2,1)S(1)}, u32[]{:S(2)}, u32[]{:S(2)}) %collective-permute-start.22) | collective-permute-done | bytes 229408 | tf_op jit(solution)/shard_map/ppermute | solution.py:412
  106.8 2.0 %shard_map.67 = bf16[256,1792]{1,0:T(8,128)(2,1)} custom-call(s32[2]{0:T(128)S(1)} %pad_add_fusion.place, bf16[448,256]{1,0:T(8,128)(2,1)S(1)} %shard_map.63.refs_0_, bf16[448,256]{1,0:T(8,128)(2,1)S(1)} %collective-permute-done.20.refs_1_, bf16[448,256]{1,0:T(8,128)(2,1)S(1)} %collective-permute-done.22.refs_2_, ...), custom_call_target="tpu_custom_call" | custom-call | bytes 917512 | tf_op jit(solution)/shard_map/pallas_call | solution.py:78
  (34 shorter events, 2.0 us)
Async XLA Ops:
  0.0 1.3 %copy-start = (bf16[256,2240]{0,1:T(8,128)(2,1)S(1)}, bf16[256,2240]{0,1:T(8,128)(2,1)}, u32[]{:S(2)}) copy-start(bf16[256,2240]{0,1:T(8,128)(2,1)} %param.4) | copy-start | bytes 3440644
  1.3 4.1 %copy-start.1 = (bf16[112,2240]{1,0:T(8,128)(2,1)S(1)}, bf16[112,2240]{1,0:T(8,128)(2,1)}, u32[]{:S(2)}) copy-start(bf16[112,2240]{1,0:T(8,128)(2,1)} %w_keyval.1) | copy-start | bytes 1505284
  1.3 4.1 %copy-start.2 = (bf16[56,2240]{1,0:T(8,128)(2,1)S(1)}, bf16[56,2240]{1,0:T(8,128)(2,1)}, u32[]{:S(2)}) copy-start(bf16[56,2240]{1,0:T(8,128)(2,1)} %w_query.1) | copy-start | bytes 752644
  1.3 20.2 %copy-start.3 = (f32[3,1792]{1,0:T(4,128)S(1)}, f32[3,1792]{1,0:T(4,128)}, u32[]{:S(2)}) copy-start(f32[3,1792]{1,0:T(4,128)} %param.7) | copy-start | bytes 64516
  2.5 17.0 %collective-permute-start.2 = (bf16[1120,256]{1,0:T(8,128)(2,1)}, bf16[1120,256]{1,0:T(8,128)(2,1)S(1)}, u32[]{:S(2)}, u32[]{:S(2)}) collective-permute-start(bf16[1120,256]{1,0:T(8,128)(2,1)} %get-tuple-element.49.low), channel_id=1, source_target_pairs={{0,2},{1,3},{2,0},{3,1},{4,6},{5,7},{6,4},{7,5},{8,10},{9,11},{10,... | collective-permute-start | bytes 1720328 | tf_op jit(solution)/shard_map/ppermute | solution.py:412
  5.5 36.5 %collective-permute-start = (bf16[168,2240]{1,0:T(8,128)(2,1)S(1)}, bf16[168,2240]{1,0:T(8,128)(2,1)}, u32[]{:S(2)}, u32[]{:S(2)}) collective-permute-start(bf16[168,2240]{1,0:T(8,128)(2,1)S(1)} %shard_map.46.refs_0_), channel_id=1, source_target_pairs={{0,16},{1,17},{2,18},{3,19},{4,20},{5,21},{6,22},{7,23},{8,24},{9,... | collective-permute-start | bytes 2257928 | tf_op jit(solution)/shard_map/ppermute | solution.py:412
  8.1 34.0 %collective-permute-start.1 = (bf16[168,2240]{1,0:T(8,128)(2,1)S(1)}, bf16[168,2240]{1,0:T(8,128)(2,1)}, u32[]{:S(2)}, u32[]{:S(2)}) collective-permute-start(bf16[168,2240]{1,0:T(8,128)(2,1)S(1)} %shard_map.46.refs_0_), channel_id=1, source_target_pairs={{0,8},{1,9},{2,10},{3,11},{4,12},{5,13},{6,14},{7,15},{8,0},{9,1},... | collective-permute-start | bytes 2257928 | tf_op jit(solution)/shard_map/ppermute | solution.py:412
  9.7 21.2 %collective-permute-start.4 = (bf16[1120,256]{1,0:T(8,128)(2,1)}, bf16[1120,256]{1,0:T(8,128)(2,1)S(1)}, u32[]{:S(2)}, u32[]{:S(2)}) collective-permute-start(bf16[1120,256]{1,0:T(8,128)(2,1)} %get-tuple-element.49.low), channel_id=1, source_target_pairs={{0,4},{1,5},{2,6},{3,7},{4,0},{5,1},{6,2},{7,3},{8,12},{9,13},{10,... | collective-permute-start | bytes 1720328 | tf_op jit(solution)/shard_map/ppermute | solution.py:412
  11.2 19.7 %collective-permute-start.3 = (bf16[1120,256]{1,0:T(8,128)(2,1)}, bf16[1120,256]{1,0:T(8,128)(2,1)S(1)}, u32[]{:S(2)}, u32[]{:S(2)}) collective-permute-start(bf16[1120,256]{1,0:T(8,128)(2,1)} %get-tuple-element.50.high), channel_id=1, source_target_pairs={{0,2},{1,3},{2,0},{3,1},{4,6},{5,7},{6,4},{7,5},{8,10},{9,11},{10,... | collective-permute-start | bytes 1720328 | tf_op jit(solution)/shard_map/ppermute | solution.py:412
  19.4 16.7 %collective-permute-start.5 = (bf16[1120,256]{1,0:T(8,128)(2,1)}, bf16[1120,256]{1,0:T(8,128)(2,1)S(1)}, u32[]{:S(2)}, u32[]{:S(2)}) collective-permute-start(bf16[1120,256]{1,0:T(8,128)(2,1)} %get-tuple-element.50.high), channel_id=1, source_target_pairs={{0,4},{1,5},{2,6},{3,7},{4,0},{5,1},{6,2},{7,3},{8,12},{9,13},{10,... | collective-permute-start | bytes 1720328 | tf_op jit(solution)/shard_map/ppermute | solution.py:412
  42.2 3.2 %collective-permute-start.10 = (bf16[168,2240]{1,0:T(8,128)(2,1)}, bf16[168,2240]{1,0:T(8,128)(2,1)}, u32[]{:S(2)}, u32[]{:S(2)}) collective-permute-start(bf16[168,2240]{1,0:T(8,128)(2,1)} %collective-permute-done.1.refs_1_), channel_id=1, source_target_pairs={{0,1},{1,0},{2,3},{3,2},{4,5},{5,4},{6,7},{7,6},{8,9},{9,8},{10,11... | collective-permute-start | bytes 2257928 | tf_op jit(solution)/shard_map/ppermute | solution.py:412
  42.9 15.9 %collective-permute-start.6 = (bf16[2240,256]{1,0:T(8,128)(2,1)S(1)}, bf16[2240,256]{1,0:T(8,128)(2,1)S(1)}, u32[]{:S(2)}, u32[]{:S(2)}) collective-permute-start(bf16[2240,256]{1,0:T(8,128)(2,1)S(1)} %shard_map.48), channel_id=1, source_target_pairs={{0,2},{1,5},{2,0},{3,7},{4,6},{5,1},{6,4},{7,3},{8,10},{9,13},{10,... | collective-permute-start | bytes 3440648 | tf_op jit(solution)/shard_map/ppermute | solution.py:412
  43.4 4.8 %collective-permute-start.11 = (bf16[168,2240]{1,0:T(8,128)(2,1)}, bf16[168,2240]{1,0:T(8,128)(2,1)S(1)}, u32[]{:S(2)}, u32[]{:S(2)}) collective-permute-start(bf16[168,2240]{1,0:T(8,128)(2,1)} %collective-permute-done.refs_2_), channel_id=1, source_target_pairs={{0,1},{1,0},{2,3},{3,2},{4,5},{5,4},{6,7},{7,6},{8,9},{9,8},{10,11... | collective-permute-start | bytes 2257928 | tf_op jit(solution)/shard_map/ppermute | solution.py:412
  44.7 3.5 %collective-permute-start.9 = (bf16[168,2240]{1,0:T(8,128)(2,1)S(1)}, bf16[168,2240]{1,0:T(8,128)(2,1)S(1)}, u32[]{:S(2)}, u32[]{:S(2)}) collective-permute-start(bf16[168,2240]{1,0:T(8,128)(2,1)S(1)} %shard_map.46.refs_0_), channel_id=1, source_target_pairs={{0,1},{1,0},{2,3},{3,2},{4,5},{5,4},{6,7},{7,6},{8,9},{9,8},{10,11... | collective-permute-start | bytes 2257928 | tf_op jit(solution)/shard_map/ppermute | solution.py:412
  44.7 19.8 %collective-permute-start.7 = (bf16[168,2240]{1,0:T(8,128)(2,1)S(1)}, bf16[168,2240]{1,0:T(8,128)(2,1)S(1)}, u32[]{:S(2)}, u32[]{:S(2)}) collective-permute-start(bf16[168,2240]{1,0:T(8,128)(2,1)S(1)} %shard_map.46.refs_0_), channel_id=1, source_target_pairs={{8,16},{9,17},{10,18},{11,19},{12,20},{13,21},{14,22},{15,23},{16,... | collective-permute-start | bytes 2257928 | tf_op jit(solution)/shard_map/ppermute | solution.py:412
  45.4 22.2 %collective-permute-start.8 = (bf16[168,2240]{1,0:T(8,128)(2,1)}, bf16[168,2240]{1,0:T(8,128)(2,1)S(1)}, u32[]{:S(2)}, u32[]{:S(2)}) collective-permute-start(bf16[168,2240]{1,0:T(8,128)(2,1)} %collective-permute-done.refs_2_), channel_id=1, source_target_pairs={{8,0},{9,1},{10,2},{11,3},{12,4},{13,5},{14,6},{15,7},{16,24},{17,... | collective-permute-start | bytes 2257928 | tf_op jit(solution)/shard_map/ppermute | solution.py:412
  68.2 2.3 %collective-permute-start.12 = (bf16[168,2240]{1,0:T(8,128)(2,1)S(1)}, bf16[168,2240]{1,0:T(8,128)(2,1)S(1)}, u32[]{:S(2)}, u32[]{:S(2)}) collective-permute-start(bf16[168,2240]{1,0:T(8,128)(2,1)S(1)} %shard_map.56.last), channel_id=1, source_target_pairs={{0,1},{1,0},{2,3},{3,2},{4,5},{5,4},{6,7},{7,6},{8,9},{9,8},{10,11... | collective-permute-start | bytes 2257928 | tf_op jit(solution)/shard_map/ppermute | solution.py:412
  72.6 1.4 %collective-permute-start.13 = (f32[2,128,112]{2,1,0:T(8,128)S(1)}, f32[2,128,112]{2,1,0:T(8,128)S(1)}, u32[]{:S(2)}, u32[]{:S(2)}) collective-permute-start(f32[2,128,112]{2,1,0:T(8,128)S(1)} %shard_map.59), channel_id=1, source_target_pairs={{0,1},{1,0},{2,3},{3,2},{4,5},{5,4},{6,7},{7,6},{8,9},{9,8},{10,11... | collective-permute-start | bytes 344072 | tf_op jit(solution)/shard_map/ppermute | solution.py:412
  74.0 5.5 %collective-permute-start.16 = (bf16[2,128,112]{2,1,0:T(8,128)(2,1)S(1)}, bf16[2,128,112]{2,1,0:T(8,128)(2,1)S(1)}, u32[]{:S(2)}, u32[]{:S(2)}) collective-permute-start(bf16[2,128,112]{2,1,0:T(8,128)(2,1)S(1)} %shard_map.61.refs_0_), channel_id=1, source_target_pairs={{0,8},{1,9},{2,10},{3,11},{4,12},{5,13},{6,14},{7,15},{8,0},{9,1},... | collective-permute-start | bytes 172040 | tf_op jit(solution)/shard_map/ppermute | solution.py:412
  74.2 7.3 %collective-permute-start.14 = (bf16[2,128,112]{2,1,0:T(8,128)(2,1)S(1)}, bf16[2,128,112]{2,1,0:T(8,128)(2,1)S(1)}, u32[]{:S(2)}, u32[]{:S(2)}) collective-permute-start(bf16[2,128,112]{2,1,0:T(8,128)(2,1)S(1)} %shard_map.61.refs_0_), channel_id=1, source_target_pairs={{0,16},{1,17},{2,18},{3,19},{4,20},{5,21},{6,22},{7,23},{8,24},{9,... | collective-permute-start | bytes 172040 | tf_op jit(solution)/shard_map/ppermute | solution.py:412
  77.4 6.1 %collective-permute-start.15 = (bf16[2,128,112]{2,1,0:T(8,128)(2,1)S(1)}, bf16[2,128,112]{2,1,0:T(8,128)(2,1)S(1)}, u32[]{:S(2)}, u32[]{:S(2)}) collective-permute-start(bf16[2,128,112]{2,1,0:T(8,128)(2,1)S(1)} %shard_map.61.refs_0_), channel_id=1, source_target_pairs={{0,24},{1,25},{2,26},{3,27},{4,28},{5,29},{6,30},{7,31},{8,16},{9,... | collective-permute-start | bytes 172040 | tf_op jit(solution)/shard_map/ppermute | solution.py:412
  79.6 13.8 %collective-permute-start.21 = (bf16[448,512]{1,0:T(8,128)(2,1)S(1)}, bf16[448,512]{1,0:T(8,128)(2,1)S(1)}, u32[]{:S(2)}, u32[]{:S(2)}) collective-permute-start(bf16[448,512]{1,0:T(8,128)(2,1)S(1)} %shard_map.60.center.side), channel_id=1, source_target_pairs={{4,12},{5,13},{6,14},{7,15},{8,0},{9,1},{10,2},{11,3},{12,20},{13,... | collective-permute-start | bytes 1376264 | tf_op jit(solution)/shard_map/ppermute | solution.py:412
  83.5 14.6 %collective-permute-start.19 = (bf16[448,512]{1,0:T(8,128)(2,1)S(1)}, bf16[448,512]{1,0:T(8,128)(2,1)S(1)}, u32[]{:S(2)}, u32[]{:S(2)}) collective-permute-start(bf16[448,512]{1,0:T(8,128)(2,1)S(1)} %shard_map.57.side.center), channel_id=1, source_target_pairs={{0,8},{1,9},{2,10},{3,11},{8,16},{9,17},{10,18},{11,19},{12,4},{13... | collective-permute-start | bytes 1376264 | tf_op jit(solution)/shard_map/ppermute | solution.py:412
  86.8 2.8 %collective-permute-start.17 = (bf16[2,128,112]{2,1,0:T(8,128)(2,1)S(1)}, bf16[2,128,112]{2,1,0:T(8,128)(2,1)S(1)}, u32[]{:S(2)}, u32[]{:S(2)}) collective-permute-start(bf16[2,128,112]{2,1,0:T(8,128)(2,1)S(1)} %shard_map.62), channel_id=1, source_target_pairs={{0,0},{1,2},{2,4},{3,6},{4,1},{5,3},{6,5},{7,7},{8,8},{9,10},{10,1... | collective-permute-start | bytes 172040 | tf_op jit(solution)/shard_map/ppermute | solution.py:412
  87.5 4.5 %collective-permute-start.18 = (bf16[2,128,112]{2,1,0:T(8,128)(2,1)S(1)}, bf16[2,128,112]{2,1,0:T(8,128)(2,1)S(1)}, u32[]{:S(2)}, u32[]{:S(2)}) collective-permute-start(bf16[2,128,112]{2,1,0:T(8,128)(2,1)S(1)} %shard_map.62), channel_id=1, source_target_pairs={{0,1},{1,3},{2,5},{3,7},{4,0},{5,2},{6,4},{7,6},{8,9},{9,11},{10,1... | collective-permute-start | bytes 172040 | tf_op jit(solution)/shard_map/ppermute | solution.py:412
  94.6 7.8 %collective-permute-start.23 = (bf16[448,256]{1,0:T(8,128)(2,1)S(1)}, bf16[448,256]{1,0:T(8,128)(2,1)S(1)}, u32[]{:S(2)}, u32[]{:S(2)}) collective-permute-start(bf16[448,256]{1,0:T(8,128)(2,1)S(1)} %shard_map.66), channel_id=1, source_target_pairs={{0,6},{1,7},{2,4},{3,5},{4,2},{5,3},{6,0},{7,1},{8,14},{9,15},{10,... | collective-permute-start | bytes 688136 | tf_op jit(solution)/shard_map/ppermute | solution.py:412
  95.8 10.7 %collective-permute-start.22 = (bf16[448,256]{1,0:T(8,128)(2,1)S(1)}, bf16[448,256]{1,0:T(8,128)(2,1)S(1)}, u32[]{:S(2)}, u32[]{:S(2)}) collective-permute-start(bf16[448,256]{1,0:T(8,128)(2,1)S(1)} %shard_map.65), channel_id=1, source_target_pairs={{0,4},{1,5},{2,6},{3,7},{4,0},{5,1},{6,2},{7,3},{8,12},{9,13},{10,... | collective-permute-start | bytes 688136 | tf_op jit(solution)/shard_map/ppermute | solution.py:412
  99.3 7.5 %collective-permute-start.20 = (bf16[448,256]{1,0:T(8,128)(2,1)S(1)}, bf16[448,256]{1,0:T(8,128)(2,1)S(1)}, u32[]{:S(2)}, u32[]{:S(2)}) collective-permute-start(bf16[448,256]{1,0:T(8,128)(2,1)S(1)} %shard_map.64), channel_id=1, source_target_pairs={{0,2},{1,3},{2,0},{3,1},{4,6},{5,7},{6,4},{7,5},{8,10},{9,11},{10,... | collective-permute-start | bytes 688136 | tf_op jit(solution)/shard_map/ppermute | solution.py:412

commit v8 on v7

--- a/solution.py
+++ b/solution.py
@@ -100,31 +100,33 @@
     scale_inv = lax.rsqrt(total / depth + epsilon)
     for start in range(0, depth, step):
         values = tokens[start : start + step].astype(jnp.float32)
-        half, at = (low, start) if start < depth // 2 else (high, start - depth // 2)
+        half, at = (low, start) if start < depth * 2 // 5 else (high, start - depth * 2 // 5)
         half[at : at + step] = (values * scale_inv).astype(jnp.bfloat16)
 
 
 def begin(tokens):
     depth, count = tokens.shape
-    outs = (like((depth // 2, count)),) * 2
-    return kernel_call(begin_kernel, outs, tokens, scalars=0)
+    cut = depth * 2 // 5
+    return kernel_call(
+        begin_kernel, (like((cut, count)), like((depth - cut, count))), tokens, scalars=0
+    )
 
 
 def relay_kernel(place, *refs):
     *halves, out = refs
     core = place[1] % 2
-    depth = halves[0].shape[0]
+    cut = halves[0].shape[0]
     for k, block in enumerate((halves[2:], halves[:2])):
 
         @pl.when(core == k)
         def _():
-            out[:depth] = block[0][...]
-            out[depth:] = block[1][...]
+            out[:cut] = block[0][...]
+            out[cut:] = block[1][...]
 
 
 def relay(place, beside, across):
-    depth, count = beside[0].shape
-    return kernel_call(relay_kernel, like((2 * depth, count)), place, *beside, *across)
+    depth, count = (sum(half.shape[0] for half in beside), beside[0].shape[1])
+    return kernel_call(relay_kernel, like((depth, count)), place, *beside, *across)
 
 
 def whole_kernel(low, high, out):
@@ -134,8 +136,8 @@
 
 
 def whole(halves):
-    depth, count = halves[0].shape
-    return kernel_call(whole_kernel, like((2 * depth, count)), *halves, scalars=0)
+    depth, count = (sum(half.shape[0] for half in halves), halves[0].shape[1])
+    return kernel_call(whole_kernel, like((depth, count)), *halves, scalars=0)
 
 
 def spaced(rows):

time: 109 us -> 109 us (level)
  transfers between devices with their start and end apart: 24 -> 24, of which waited for: 15 -> 14; matrix products, arithmetic and copies ran while one was open for 0% -> 0% of each run, Pallas kernels for 19% -> 19%
where the time goes in v8:
time: 109 us
  waiting for transfers between devices  49.8 us (46%)
  starting transfers between devices  30.9 us (28%)
  Pallas kernels  26.1 us (24%)
  local copies, waits for them, and re-layouts  1.51 us (1%)
    ppermute x24, waiting for transfers between devices, send(): return lax.ppermute(value, 'frame', pairs)  49.8 us
    ppermute x24, starting transfers between devices, send(): return lax.ppermute(value, 'frame', pairs)  30.9 us
    pallas_call x22, Pallas kernels, kernel_call(): pl.pallas_call(body, out_shape=outs, in_specs=[SMEM] * scalars + [VMEM] *...  26.1 us
  transfers between devices with their start and end apart: 24, of which 14 were waited for; matrix products, arithmetic and copies ran while one was open for 0% of the time, Pallas kernels for 19%

profile of v8, /device:TPU:0, one launch (start us, length us, event | category | flops | bytes accessed | tf_op | source)
XLA Modules:
  0.0 108.7 jit_solution(12451165651546725123)
XLA Ops:
  0.0 1.3 %copy-done = bf16[256,2240]{0,1:T(8,128)(2,1)S(1)} copy-done((bf16[256,2240]{0,1:T(8,128)(2,1)S(1)}, bf16[256,2240]{0,1:T(8,128)(2,1)}, u32[]{:S(2)}) %copy-start) | copy-done | bytes 1146904
  1.3 1.2 %shard_map.47 = (bf16[896,256]{1,0:T(8,128)(2,1)}, bf16[1344,256]{1,0:T(8,128)(2,1)}) custom-call(bf16[2240,256]{1,0:T(8,128)(2,1)S(1)} %bitcast.10), custom_call_target="tpu_custom_call" | custom-call | bytes 1146880 | tf_op jit(solution)/shard_map/pallas_call | solution.py:78
  2.4 2.9 %collective-permute-start.2 = (bf16[896,256]{1,0:T(8,128)(2,1)}, bf16[896,256]{1,0:T(8,128)(2,1)S(1)}, u32[]{:S(2)}, u32[]{:S(2)}) collective-permute-start(bf16[896,256]{1,0:T(8,128)(2,1)} %get-tuple-element.49.low), channel_id=1, source_target_pairs={{0,2},{1,3},{2,0},{3,1},{4,6},{5,7},{6,4},{7,5},{8,10},{9,11},{10,... | collective-permute-start | bytes 1376264 | tf_op jit(solution)/shard_map/ppermute | solution.py:414
  5.4 2.7 %collective-permute-start = (bf16[168,2240]{1,0:T(8,128)(2,1)S(1)}, bf16[168,2240]{1,0:T(8,128)(2,1)}, u32[]{:S(2)}, u32[]{:S(2)}) collective-permute-start(bf16[168,2240]{1,0:T(8,128)(2,1)S(1)} %shard_map.46.refs_0_), channel_id=1, source_target_pairs={{0,16},{1,17},{2,18},{3,19},{4,20},{5,21},{6,22},{7,23},{8,24},{9,... | collective-permute-start | bytes 2257928 | tf_op jit(solution)/shard_map/ppermute | solution.py:414
  8.1 1.6 %collective-permute-start.1 = (bf16[168,2240]{1,0:T(8,128)(2,1)S(1)}, bf16[168,2240]{1,0:T(8,128)(2,1)}, u32[]{:S(2)}, u32[]{:S(2)}) collective-permute-start(bf16[168,2240]{1,0:T(8,128)(2,1)S(1)} %shard_map.46.refs_0_), channel_id=1, source_target_pairs={{0,8},{1,9},{2,10},{3,11},{4,12},{5,13},{6,14},{7,15},{8,0},{9,1},... | collective-permute-start | bytes 2257928 | tf_op jit(solution)/shard_map/ppermute | solution.py:414
  9.7 0.5 collective-permute-start.3
  10.2 1.5 %collective-permute-start.5 = (bf16[1344,256]{1,0:T(8,128)(2,1)}, bf16[1344,256]{1,0:T(8,128)(2,1)S(1)}, u32[]{:S(2)}, u32[]{:S(2)}) collective-permute-start(bf16[1344,256]{1,0:T(8,128)(2,1)} %get-tuple-element.50.high), channel_id=1, source_target_pairs={{0,4},{1,5},{2,6},{3,7},{4,0},{5,1},{6,2},{7,3},{8,12},{9,13},{10,... | collective-permute-start | bytes 2064392 | tf_op jit(solution)/shard_map/ppermute | solution.py:414
  11.7 5.2 %collective-permute-done.2.refs_0_.low = bf16[896,256]{1,0:T(8,128)(2,1)S(1)} collective-permute-done((bf16[896,256]{1,0:T(8,128)(2,1)}, bf16[896,256]{1,0:T(8,128)(2,1)S(1)}, u32[]{:S(2)}, u32[]{:S(2)}) %collective-permute-start.2) | collective-permute-done | bytes 458784 | tf_op jit(solution)/shard_map/ppermute | solution.py:414
  16.9 2.1 %collective-permute-start.4 = (bf16[896,256]{1,0:T(8,128)(2,1)}, bf16[896,256]{1,0:T(8,128)(2,1)S(1)}, u32[]{:S(2)}, u32[]{:S(2)}) collective-permute-start(bf16[896,256]{1,0:T(8,128)(2,1)} %get-tuple-element.49.low), channel_id=1, source_target_pairs={{0,4},{1,5},{2,6},{3,7},{4,0},{5,1},{6,2},{7,3},{8,12},{9,13},{10,... | collective-permute-start | bytes 1376264 | tf_op jit(solution)/shard_map/ppermute | solution.py:414
  19.3 17.0 %collective-permute-done.4.refs_2_.low = bf16[896,256]{1,0:T(8,128)(2,1)S(1)} collective-permute-done((bf16[896,256]{1,0:T(8,128)(2,1)}, bf16[896,256]{1,0:T(8,128)(2,1)S(1)}, u32[]{:S(2)}, u32[]{:S(2)}) %collective-permute-start.4) | collective-permute-done | bytes 458784 | tf_op jit(solution)/shard_map/ppermute | solution.py:414
  36.3 5.6 %collective-permute-done.refs_2_ = bf16[168,2240]{1,0:T(8,128)(2,1)} collective-permute-done((bf16[168,2240]{1,0:T(8,128)(2,1)S(1)}, bf16[168,2240]{1,0:T(8,128)(2,1)}, u32[]{:S(2)}, u32[]{:S(2)}) %collective-permute-start) | collective-permute-done | bytes 752672 | tf_op jit(solution)/shard_map/ppermute | solution.py:414
  42.2 0.6 shard_map.48
  42.8 0.6 collective-permute-start.6
  43.4 1.3 %collective-permute-start.11 = (bf16[168,2240]{1,0:T(8,128)(2,1)}, bf16[168,2240]{1,0:T(8,128)(2,1)S(1)}, u32[]{:S(2)}, u32[]{:S(2)}) collective-permute-start(bf16[168,2240]{1,0:T(8,128)(2,1)} %collective-permute-done.refs_2_), channel_id=1, source_target_pairs={{0,1},{1,0},{2,3},{3,2},{4,5},{5,4},{6,7},{7,6},{8,9},{9,8},{10,11... | collective-permute-start | bytes 2257928 | tf_op jit(solution)/shard_map/ppermute | solution.py:414
  44.7 0.7 collective-permute-start.7
  45.4 1.3 %collective-permute-start.8 = (bf16[168,2240]{1,0:T(8,128)(2,1)}, bf16[168,2240]{1,0:T(8,128)(2,1)S(1)}, u32[]{:S(2)}, u32[]{:S(2)}) collective-permute-start(bf16[168,2240]{1,0:T(8,128)(2,1)} %collective-permute-done.refs_2_), channel_id=1, source_target_pairs={{8,0},{9,1},{10,2},{11,3},{12,4},{13,5},{14,6},{15,7},{16,24},{17,... | collective-permute-start | bytes 2257928 | tf_op jit(solution)/shard_map/ppermute | solution.py:414
  46.8 1.3 %shard_map.50.refs_0_.block_0 = bf16[2240,256]{1,0:T(8,128)(2,1)S(1)} custom-call(bf16[896,256]{1,0:T(8,128)(2,1)} %get-tuple-element.49.low, bf16[1344,256]{1,0:T(8,128)(2,1)} %get-tuple-element.50.high), custom_call_target="tpu_custom_call" | custom-call | bytes 1146880 | tf_op jit(solution)/shard_map/pallas_call | solution.py:78
  48.2 1.9 %shard_map.49 = (bf16[336,2240]{1,0:T(8,128)(2,1)S(1)}, bf16[336,2240]{1,0:T(8,128)(2,1)S(1)}, bf16[384,2240]{1,0:T(8,128)(2,1)S(1)}) custom-call(bf16[168,2240]{1,0:T(8,128)(2,1)S(1)} %shard_map.46.refs_0_, bf16[168,2240]{1,0:T(8,128)(2,1)} %collective-permute-done.1.refs_1_, bf16[168,2240]{1,0:T(8,128)(2,1)} %collective-permute-done.refs_2_, ...), custom_call_target="tpu_custom_call" | custom-call | bytes 4515840 | tf_op jit(solution)/shard_map/pallas_call | solution.py:78
  50.1 1.6 %shard_map.54.near = bf16[448,512]{1,0:T(8,128)(2,1)S(1)} custom-call(s32[2]{0:T(128)S(1)} %pad_add_fusion.place, bf16[384,2240]{1,0:T(8,128)(2,1)S(1)} %get-tuple-element.51.rows, bf16[2240,256]{1,0:T(8,128)(2,1)S(1)} %shard_map.50.refs_0_.block_0, bf16[2240,256]{1,0:T(8,128)(2,1)S(1)} %shard_map.51.refs_1_.block_1), custom_call_target="tpu_custom_call" | custom-call | bytes 4014088 | tf_op jit(solution)/shard_map/pallas_call | solution.py:78
  51.7 7.0 %collective-permute-done.6.refs_3_.refs_1_.block_1 = bf16[2240,256]{1,0:T(8,128)(2,1)S(1)} collective-permute-done((bf16[2240,256]{1,0:T(8,128)(2,1)S(1)}, bf16[2240,256]{1,0:T(8,128)(2,1)S(1)}, u32[]{:S(2)}, u32[]{:S(2)}) %collective-permute-start.6) | collective-permute-done | bytes 1146912 | tf_op jit(solution)/shard_map/ppermute | solution.py:414
  58.8 1.6 %shard_map.55.near = bf16[448,512]{1,0:T(8,128)(2,1)S(1)} custom-call(s32[2]{0:T(128)S(1)} %pad_add_fusion.place, bf16[384,2240]{1,0:T(8,128)(2,1)S(1)} %get-tuple-element.51.rows, bf16[2240,256]{1,0:T(8,128)(2,1)S(1)} %shard_map.52.refs_2_.refs_0_.block_0, bf16[2240,256]{1,0:T(8,128)(2,1)S(1)} %collective-permute-done.6.refs_3_.refs_1_.block_1), custom_call_target="tpu_custom_call" | custom-call | bytes 4014088 | tf_op jit(solution)/shard_map/pallas_call | solution.py:78
  60.4 4.1 %shard_map.53.part = f32[2,128,112]{2,1,0:T(8,128)S(1)} custom-call(s32[2]{0:T(128)S(1)} %pad_add_fusion.place, bf16[336,2240]{1,0:T(8,128)(2,1)S(1)} %get-tuple-element.47.mine.rows, bf16[336,2240]{1,0:T(8,128)(2,1)S(1)} %get-tuple-element.48.there.rows, bf16[2240,256]{1,0:T(8,128)(2,1)S(1)} %shard_map.50.refs_0_.block_0, ...), custom_call_target="tpu_custom_call" | custom-call | flops 2055208960 | bytes 7598088 | tf_op jit(solution)/shard_map/pallas_call | solution.py:78
  64.5 3.1 %collective-permute-done.8.outer = bf16[168,2240]{1,0:T(8,128)(2,1)S(1)} collective-permute-done((bf16[168,2240]{1,0:T(8,128)(2,1)}, bf16[168,2240]{1,0:T(8,128)(2,1)S(1)}, u32[]{:S(2)}, u32[]{:S(2)}) %collective-permute-start.8) | collective-permute-done | bytes 752672 | tf_op jit(solution)/shard_map/ppermute | solution.py:414
  67.6 0.6 shard_map.56.last
  68.3 2.0 %shard_map.58.refs_0_ = f32[2,128,112]{2,1,0:T(8,128)S(1)} custom-call(s32[2]{0:T(128)S(1)} %pad_add_fusion.place, f32[2,128,112]{2,1,0:T(8,128)S(1)} %shard_map.53.part, bf16[336,2240]{1,0:T(8,128)(2,1)S(1)} %get-tuple-element.47.mine.rows, bf16[168,2240]{1,0:T(8,128)(2,1)S(1)} %shard_map.56.last, bf16[2240,256]{1,0:T(8,128)(2,1)S(1)} %shard_map.50.refs_0_.block_0, ...), custom_call_target="tpu_custom_call" | custom-call | flops 1027604480 | bytes 6960136 | tf_op jit(solution)/shard_map/pallas_call | solution.py:78
  70.5 2.0 %shard_map.59 = f32[2,128,112]{2,1,0:T(8,128)S(1)} custom-call(s32[2]{0:T(128)S(1)} %pad_add_fusion.place, f32[2,128,112]{2,1,0:T(8,128)S(1)} %shard_map.53.part, bf16[336,2240]{1,0:T(8,128)(2,1)S(1)} %get-tuple-element.48.there.rows, bf16[168,2240]{1,0:T(8,128)(2,1)S(1)} %collective-permute-done.12.last_there.last, ...), custom_call_target="tpu_custom_call" | custom-call | flops 1027604480 | bytes 6960136 | tf_op jit(solution)/shard_map/pallas_call | solution.py:78
  72.6 0.3 collective-permute-start.13
  72.9 1.0 shard_map.60.center.side
  74.1 3.3 %collective-permute-start.14 = (bf16[2,128,112]{2,1,0:T(8,128)(2,1)S(1)}, bf16[2,128,112]{2,1,0:T(8,128)(2,1)S(1)}, u32[]{:S(2)}, u32[]{:S(2)}) collective-permute-start(bf16[2,128,112]{2,1,0:T(8,128)(2,1)S(1)} %shard_map.61.refs_0_), channel_id=1, source_target_pairs={{0,16},{1,17},{2,18},{3,19},{4,20},{5,21},{6,22},{7,23},{8,24},{9,... | collective-permute-start | bytes 172040 | tf_op jit(solution)/shard_map/ppermute | solution.py:414
  77.4 1.1 collective-permute-start.15
  78.5 1.0 shard_map.57.side.center
  79.5 1.3 %collective-permute-start.21 = (bf16[448,512]{1,0:T(8,128)(2,1)S(1)}, bf16[448,512]{1,0:T(8,128)(2,1)S(1)}, u32[]{:S(2)}, u32[]{:S(2)}) collective-permute-start(bf16[448,512]{1,0:T(8,128)(2,1)S(1)} %shard_map.60.center.side), channel_id=1, source_target_pairs={{4,12},{5,13},{6,14},{7,15},{8,0},{9,1},{10,2},{11,3},{12,20},{13,... | collective-permute-start | bytes 1376264 | tf_op jit(solution)/shard_map/ppermute | solution.py:414
  80.8 0.6 collective-permute-done.14.refs_1_
  81.4 2.1 %collective-permute-done.15.refs_2_ = bf16[2,128,112]{2,1,0:T(8,128)(2,1)S(1)} collective-permute-done((bf16[2,128,112]{2,1,0:T(8,128)(2,1)S(1)}, bf16[2,128,112]{2,1,0:T(8,128)(2,1)S(1)}, u32[]{:S(2)}, u32[]{:S(2)}) %collective-permute-start.15) | collective-permute-done | bytes 57376 | tf_op jit(solution)/shard_map/ppermute | solution.py:414
  83.5 3.2 %collective-permute-start.19 = (bf16[448,512]{1,0:T(8,128)(2,1)S(1)}, bf16[448,512]{1,0:T(8,128)(2,1)S(1)}, u32[]{:S(2)}, u32[]{:S(2)}) collective-permute-start(bf16[448,512]{1,0:T(8,128)(2,1)S(1)} %shard_map.57.side.center), channel_id=1, source_target_pairs={{0,8},{1,9},{2,10},{3,11},{8,16},{9,17},{10,18},{11,19},{12,4},{13... | collective-permute-start | bytes 1376264 | tf_op jit(solution)/shard_map/ppermute | solution.py:414
  86.8 0.7 collective-permute-start.17
  87.5 2.2 %collective-permute-start.18 = (bf16[2,128,112]{2,1,0:T(8,128)(2,1)S(1)}, bf16[2,128,112]{2,1,0:T(8,128)(2,1)S(1)}, u32[]{:S(2)}, u32[]{:S(2)}) collective-permute-start(bf16[2,128,112]{2,1,0:T(8,128)(2,1)S(1)} %shard_map.62), channel_id=1, source_target_pairs={{0,1},{1,3},{2,5},{3,7},{4,0},{5,2},{6,4},{7,6},{8,9},{9,11},{10,1... | collective-permute-start | bytes 172040 | tf_op jit(solution)/shard_map/ppermute | solution.py:414
  89.6 2.3 %collective-permute-done.18.there = bf16[2,128,112]{2,1,0:T(8,128)(2,1)S(1)} collective-permute-done((bf16[2,128,112]{2,1,0:T(8,128)(2,1)S(1)}, bf16[2,128,112]{2,1,0:T(8,128)(2,1)S(1)}, u32[]{:S(2)}, u32[]{:S(2)}) %collective-permute-start.18) | collective-permute-done | bytes 57376 | tf_op jit(solution)/shard_map/ppermute | solution.py:414
  92.0 1.4 %collective-permute-done.21.halo = bf16[448,512]{1,0:T(8,128)(2,1)S(1)} collective-permute-done((bf16[448,512]{1,0:T(8,128)(2,1)S(1)}, bf16[448,512]{1,0:T(8,128)(2,1)S(1)}, u32[]{:S(2)}, u32[]{:S(2)}) %collective-permute-start.21) | collective-permute-done | bytes 458784 | tf_op jit(solution)/shard_map/ppermute | solution.py:414
  93.4 1.2 %shard_map.66 = bf16[448,256]{1,0:T(8,128)(2,1)S(1)} custom-call(s32[2]{0:T(128)S(1)} %pad_add_fusion.place, bf16[2,128,112]{2,1,0:T(8,128)(2,1)S(1)} %collective-permute-done.17.mine, bf16[2,128,112]{2,1,0:T(8,128)(2,1)S(1)} %collective-permute-done.18.there, f32[448,3]{1,0:T(8,128)S(1)} %bitcast.6, bf16[448,512]{1,0:T(8,128)(2,1)S(1)} %shard_map.57.side.center, ...), custom_call_target="tpu_custom_call" | custom-call | bytes 1496328 | tf_op jit(solution)/shard_map/pallas_call | solution.py:78
  94.7 1.2 %shard_map.65 = bf16[448,256]{1,0:T(8,128)(2,1)S(1)} custom-call(s32[2]{0:T(128)S(1)} %pad_add_fusion.place, bf16[2,128,112]{2,1,0:T(8,128)(2,1)S(1)} %collective-permute-done.17.mine, bf16[2,128,112]{2,1,0:T(8,128)(2,1)S(1)} %collective-permute-done.18.there, f32[448,3]{1,0:T(8,128)S(1)} %bitcast.7, bf16[448,512]{1,0:T(8,128)(2,1)S(1)} %shard_map.57.side.center, ...), custom_call_target="tpu_custom_call" | custom-call | bytes 1496328 | tf_op jit(solution)/shard_map/pallas_call | solution.py:78
  95.9 2.2 %collective-permute-start.22 = (bf16[448,256]{1,0:T(8,128)(2,1)S(1)}, bf16[448,256]{1,0:T(8,128)(2,1)S(1)}, u32[]{:S(2)}, u32[]{:S(2)}) collective-permute-start(bf16[448,256]{1,0:T(8,128)(2,1)S(1)} %shard_map.65), channel_id=1, source_target_pairs={{0,4},{1,5},{2,6},{3,7},{4,0},{5,1},{6,2},{7,3},{8,12},{9,13},{10,... | collective-permute-start | bytes 688136 | tf_op jit(solution)/shard_map/ppermute | solution.py:414
  98.1 1.2 %shard_map.64 = bf16[448,256]{1,0:T(8,128)(2,1)S(1)} custom-call(s32[2]{0:T(128)S(1)} %pad_add_fusion.place, bf16[2,128,112]{2,1,0:T(8,128)(2,1)S(1)} %collective-permute-done.17.mine, bf16[2,128,112]{2,1,0:T(8,128)(2,1)S(1)} %collective-permute-done.18.there, f32[448,3]{1,0:T(8,128)S(1)} %bitcast.8, bf16[448,512]{1,0:T(8,128)(2,1)S(1)} %shard_map.60.center.side, ...), custom_call_target="tpu_custom_call" | custom-call | bytes 1496328 | tf_op jit(solution)/shard_map/pallas_call | solution.py:78
  99.3 1.4 %collective-permute-start.20 = (bf16[448,256]{1,0:T(8,128)(2,1)S(1)}, bf16[448,256]{1,0:T(8,128)(2,1)S(1)}, u32[]{:S(2)}, u32[]{:S(2)}) collective-permute-start(bf16[448,256]{1,0:T(8,128)(2,1)S(1)} %shard_map.64), channel_id=1, source_target_pairs={{0,2},{1,3},{2,0},{3,1},{4,6},{5,7},{6,4},{7,5},{8,10},{9,11},{10,... | collective-permute-start | bytes 688136 | tf_op jit(solution)/shard_map/ppermute | solution.py:414
  100.7 1.2 %shard_map.63.refs_0_ = bf16[448,256]{1,0:T(8,128)(2,1)S(1)} custom-call(s32[2]{0:T(128)S(1)} %pad_add_fusion.place, bf16[2,128,112]{2,1,0:T(8,128)(2,1)S(1)} %collective-permute-done.17.mine, bf16[2,128,112]{2,1,0:T(8,128)(2,1)S(1)} %collective-permute-done.18.there, f32[448,3]{1,0:T(8,128)S(1)} %bitcast.9, bf16[448,512]{1,0:T(8,128)(2,1)S(1)} %shard_map.60.center.side, ...), custom_call_target="tpu_custom_call" | custom-call | bytes 1496328 | tf_op jit(solution)/shard_map/pallas_call | solution.py:78
  101.9 0.7 collective-permute-done.23.refs_3_
  102.6 4.0 %collective-permute-done.22.refs_2_ = bf16[448,256]{1,0:T(8,128)(2,1)S(1)} collective-permute-done((bf16[448,256]{1,0:T(8,128)(2,1)S(1)}, bf16[448,256]{1,0:T(8,128)(2,1)S(1)}, u32[]{:S(2)}, u32[]{:S(2)}) %collective-permute-start.22) | collective-permute-done | bytes 229408 | tf_op jit(solution)/shard_map/ppermute | solution.py:414
  106.8 2.0 %shard_map.67 = bf16[256,1792]{1,0:T(8,128)(2,1)} custom-call(s32[2]{0:T(128)S(1)} %pad_add_fusion.place, bf16[448,256]{1,0:T(8,128)(2,1)S(1)} %shard_map.63.refs_0_, bf16[448,256]{1,0:T(8,128)(2,1)S(1)} %collective-permute-done.20.refs_1_, bf16[448,256]{1,0:T(8,128)(2,1)S(1)} %collective-permute-done.22.refs_2_, ...), custom_call_target="tpu_custom_call" | custom-call | bytes 917512 | tf_op jit(solution)/shard_map/pallas_call | solution.py:78
  (34 shorter events, 1.5 us)
Async XLA Ops:
  0.0 1.3 %copy-start = (bf16[256,2240]{0,1:T(8,128)(2,1)S(1)}, bf16[256,2240]{0,1:T(8,128)(2,1)}, u32[]{:S(2)}) copy-start(bf16[256,2240]{0,1:T(8,128)(2,1)} %param.4) | copy-start | bytes 3440644
  1.3 4.1 %copy-start.1 = (bf16[112,2240]{1,0:T(8,128)(2,1)S(1)}, bf16[112,2240]{1,0:T(8,128)(2,1)}, u32[]{:S(2)}) copy-start(bf16[112,2240]{1,0:T(8,128)(2,1)} %w_keyval.1) | copy-start | bytes 1505284
  1.3 4.1 %copy-start.2 = (bf16[56,2240]{1,0:T(8,128)(2,1)S(1)}, bf16[56,2240]{1,0:T(8,128)(2,1)}, u32[]{:S(2)}) copy-start(bf16[56,2240]{1,0:T(8,128)(2,1)} %w_query.1) | copy-start | bytes 752644
  1.3 17.7 %copy-start.3 = (f32[3,1792]{1,0:T(4,128)S(1)}, f32[3,1792]{1,0:T(4,128)}, u32[]{:S(2)}) copy-start(f32[3,1792]{1,0:T(4,128)} %param.7) | copy-start | bytes 64516
  2.4 14.5 %collective-permute-start.2 = (bf16[896,256]{1,0:T(8,128)(2,1)}, bf16[896,256]{1,0:T(8,128)(2,1)S(1)}, u32[]{:S(2)}, u32[]{:S(2)}) collective-permute-start(bf16[896,256]{1,0:T(8,128)(2,1)} %get-tuple-element.49.low), channel_id=1, source_target_pairs={{0,2},{1,3},{2,0},{3,1},{4,6},{5,7},{6,4},{7,5},{8,10},{9,11},{10,... | collective-permute-start | bytes 1376264 | tf_op jit(solution)/shard_map/ppermute | solution.py:414
  5.4 36.5 %collective-permute-start = (bf16[168,2240]{1,0:T(8,128)(2,1)S(1)}, bf16[168,2240]{1,0:T(8,128)(2,1)}, u32[]{:S(2)}, u32[]{:S(2)}) collective-permute-start(bf16[168,2240]{1,0:T(8,128)(2,1)S(1)} %shard_map.46.refs_0_), channel_id=1, source_target_pairs={{0,16},{1,17},{2,18},{3,19},{4,20},{5,21},{6,22},{7,23},{8,24},{9,... | collective-permute-start | bytes 2257928 | tf_op jit(solution)/shard_map/ppermute | solution.py:414
  8.1 34.0 %collective-permute-start.1 = (bf16[168,2240]{1,0:T(8,128)(2,1)S(1)}, bf16[168,2240]{1,0:T(8,128)(2,1)}, u32[]{:S(2)}, u32[]{:S(2)}) collective-permute-start(bf16[168,2240]{1,0:T(8,128)(2,1)S(1)} %shard_map.46.refs_0_), channel_id=1, source_target_pairs={{0,8},{1,9},{2,10},{3,11},{4,12},{5,13},{6,14},{7,15},{8,0},{9,1},... | collective-permute-start | bytes 2257928 | tf_op jit(solution)/shard_map/ppermute | solution.py:414
  9.7 26.6 %collective-permute-start.3 = (bf16[1344,256]{1,0:T(8,128)(2,1)}, bf16[1344,256]{1,0:T(8,128)(2,1)S(1)}, u32[]{:S(2)}, u32[]{:S(2)}) collective-permute-start(bf16[1344,256]{1,0:T(8,128)(2,1)} %get-tuple-element.50.high), channel_id=1, source_target_pairs={{0,2},{1,3},{2,0},{3,1},{4,6},{5,7},{6,4},{7,5},{8,10},{9,11},{10,... | collective-permute-start | bytes 2064392 | tf_op jit(solution)/shard_map/ppermute | solution.py:414
  10.2 26.1 %collective-permute-start.5 = (bf16[1344,256]{1,0:T(8,128)(2,1)}, bf16[1344,256]{1,0:T(8,128)(2,1)S(1)}, u32[]{:S(2)}, u32[]{:S(2)}) collective-permute-start(bf16[1344,256]{1,0:T(8,128)(2,1)} %get-tuple-element.50.high), channel_id=1, source_target_pairs={{0,4},{1,5},{2,6},{3,7},{4,0},{5,1},{6,2},{7,3},{8,12},{9,13},{10,... | collective-permute-start | bytes 2064392 | tf_op jit(solution)/shard_map/ppermute | solution.py:414
  16.9 19.4 %collective-permute-start.4 = (bf16[896,256]{1,0:T(8,128)(2,1)}, bf16[896,256]{1,0:T(8,128)(2,1)S(1)}, u32[]{:S(2)}, u32[]{:S(2)}) collective-permute-start(bf16[896,256]{1,0:T(8,128)(2,1)} %get-tuple-element.49.low), channel_id=1, source_target_pairs={{0,4},{1,5},{2,6},{3,7},{4,0},{5,1},{6,2},{7,3},{8,12},{9,13},{10,... | collective-permute-start | bytes 1376264 | tf_op jit(solution)/shard_map/ppermute | solution.py:414
  42.1 3.2 %collective-permute-start.10 = (bf16[168,2240]{1,0:T(8,128)(2,1)}, bf16[168,2240]{1,0:T(8,128)(2,1)}, u32[]{:S(2)}, u32[]{:S(2)}) collective-permute-start(bf16[168,2240]{1,0:T(8,128)(2,1)} %collective-permute-done.1.refs_1_), channel_id=1, source_target_pairs={{0,1},{1,0},{2,3},{3,2},{4,5},{5,4},{6,7},{7,6},{8,9},{9,8},{10,11... | collective-permute-start | bytes 2257928 | tf_op jit(solution)/shard_map/ppermute | solution.py:414
  42.8 15.9 %collective-permute-start.6 = (bf16[2240,256]{1,0:T(8,128)(2,1)S(1)}, bf16[2240,256]{1,0:T(8,128)(2,1)S(1)}, u32[]{:S(2)}, u32[]{:S(2)}) collective-permute-start(bf16[2240,256]{1,0:T(8,128)(2,1)S(1)} %shard_map.48), channel_id=1, source_target_pairs={{0,2},{1,5},{2,0},{3,7},{4,6},{5,1},{6,4},{7,3},{8,10},{9,13},{10,... | collective-permute-start | bytes 3440648 | tf_op jit(solution)/shard_map/ppermute | solution.py:414
  43.4 4.8 %collective-permute-start.11 = (bf16[168,2240]{1,0:T(8,128)(2,1)}, bf16[168,2240]{1,0:T(8,128)(2,1)S(1)}, u32[]{:S(2)}, u32[]{:S(2)}) collective-permute-start(bf16[168,2240]{1,0:T(8,128)(2,1)} %collective-permute-done.refs_2_), channel_id=1, source_target_pairs={{0,1},{1,0},{2,3},{3,2},{4,5},{5,4},{6,7},{7,6},{8,9},{9,8},{10,11... | collective-permute-start | bytes 2257928 | tf_op jit(solution)/shard_map/ppermute | solution.py:414
  44.6 3.5 %collective-permute-start.9 = (bf16[168,2240]{1,0:T(8,128)(2,1)S(1)}, bf16[168,2240]{1,0:T(8,128)(2,1)S(1)}, u32[]{:S(2)}, u32[]{:S(2)}) collective-permute-start(bf16[168,2240]{1,0:T(8,128)(2,1)S(1)} %shard_map.46.refs_0_), channel_id=1, source_target_pairs={{0,1},{1,0},{2,3},{3,2},{4,5},{5,4},{6,7},{7,6},{8,9},{9,8},{10,11... | collective-permute-start | bytes 2257928 | tf_op jit(solution)/shard_map/ppermute | solution.py:414
  44.7 19.8 %collective-permute-start.7 = (bf16[168,2240]{1,0:T(8,128)(2,1)S(1)}, bf16[168,2240]{1,0:T(8,128)(2,1)S(1)}, u32[]{:S(2)}, u32[]{:S(2)}) collective-permute-start(bf16[168,2240]{1,0:T(8,128)(2,1)S(1)} %shard_map.46.refs_0_), channel_id=1, source_target_pairs={{8,16},{9,17},{10,18},{11,19},{12,20},{13,21},{14,22},{15,23},{16,... | collective-permute-start | bytes 2257928 | tf_op jit(solution)/shard_map/ppermute | solution.py:414
  45.4 22.2 %collective-permute-start.8 = (bf16[168,2240]{1,0:T(8,128)(2,1)}, bf16[168,2240]{1,0:T(8,128)(2,1)S(1)}, u32[]{:S(2)}, u32[]{:S(2)}) collective-permute-start(bf16[168,2240]{1,0:T(8,128)(2,1)} %collective-permute-done.refs_2_), channel_id=1, source_target_pairs={{8,0},{9,1},{10,2},{11,3},{12,4},{13,5},{14,6},{15,7},{16,24},{17,... | collective-permute-start | bytes 2257928 | tf_op jit(solution)/shard_map/ppermute | solution.py:414
  68.2 2.3 %collective-permute-start.12 = (bf16[168,2240]{1,0:T(8,128)(2,1)S(1)}, bf16[168,2240]{1,0:T(8,128)(2,1)S(1)}, u32[]{:S(2)}, u32[]{:S(2)}) collective-permute-start(bf16[168,2240]{1,0:T(8,128)(2,1)S(1)} %shard_map.56.last), channel_id=1, source_target_pairs={{0,1},{1,0},{2,3},{3,2},{4,5},{5,4},{6,7},{7,6},{8,9},{9,8},{10,11... | collective-permute-start | bytes 2257928 | tf_op jit(solution)/shard_map/ppermute | solution.py:414
  72.6 1.4 %collective-permute-start.13 = (f32[2,128,112]{2,1,0:T(8,128)S(1)}, f32[2,128,112]{2,1,0:T(8,128)S(1)}, u32[]{:S(2)}, u32[]{:S(2)}) collective-permute-start(f32[2,128,112]{2,1,0:T(8,128)S(1)} %shard_map.59), channel_id=1, source_target_pairs={{0,1},{1,0},{2,3},{3,2},{4,5},{5,4},{6,7},{7,6},{8,9},{9,8},{10,11... | collective-permute-start | bytes 344072 | tf_op jit(solution)/shard_map/ppermute | solution.py:414
  74.0 5.5 %collective-permute-start.16 = (bf16[2,128,112]{2,1,0:T(8,128)(2,1)S(1)}, bf16[2,128,112]{2,1,0:T(8,128)(2,1)S(1)}, u32[]{:S(2)}, u32[]{:S(2)}) collective-permute-start(bf16[2,128,112]{2,1,0:T(8,128)(2,1)S(1)} %shard_map.61.refs_0_), channel_id=1, source_target_pairs={{0,8},{1,9},{2,10},{3,11},{4,12},{5,13},{6,14},{7,15},{8,0},{9,1},... | collective-permute-start | bytes 172040 | tf_op jit(solution)/shard_map/ppermute | solution.py:414
  74.1 7.3 %collective-permute-start.14 = (bf16[2,128,112]{2,1,0:T(8,128)(2,1)S(1)}, bf16[2,128,112]{2,1,0:T(8,128)(2,1)S(1)}, u32[]{:S(2)}, u32[]{:S(2)}) collective-permute-start(bf16[2,128,112]{2,1,0:T(8,128)(2,1)S(1)} %shard_map.61.refs_0_), channel_id=1, source_target_pairs={{0,16},{1,17},{2,18},{3,19},{4,20},{5,21},{6,22},{7,23},{8,24},{9,... | collective-permute-start | bytes 172040 | tf_op jit(solution)/shard_map/ppermute | solution.py:414
  77.4 6.2 %collective-permute-start.15 = (bf16[2,128,112]{2,1,0:T(8,128)(2,1)S(1)}, bf16[2,128,112]{2,1,0:T(8,128)(2,1)S(1)}, u32[]{:S(2)}, u32[]{:S(2)}) collective-permute-start(bf16[2,128,112]{2,1,0:T(8,128)(2,1)S(1)} %shard_map.61.refs_0_), channel_id=1, source_target_pairs={{0,24},{1,25},{2,26},{3,27},{4,28},{5,29},{6,30},{7,31},{8,16},{9,... | collective-permute-start | bytes 172040 | tf_op jit(solution)/shard_map/ppermute | solution.py:414
  79.5 13.9 %collective-permute-start.21 = (bf16[448,512]{1,0:T(8,128)(2,1)S(1)}, bf16[448,512]{1,0:T(8,128)(2,1)S(1)}, u32[]{:S(2)}, u32[]{:S(2)}) collective-permute-start(bf16[448,512]{1,0:T(8,128)(2,1)S(1)} %shard_map.60.center.side), channel_id=1, source_target_pairs={{4,12},{5,13},{6,14},{7,15},{8,0},{9,1},{10,2},{11,3},{12,20},{13,... | collective-permute-start | bytes 1376264 | tf_op jit(solution)/shard_map/ppermute | solution.py:414
  83.5 14.5 %collective-permute-start.19 = (bf16[448,512]{1,0:T(8,128)(2,1)S(1)}, bf16[448,512]{1,0:T(8,128)(2,1)S(1)}, u32[]{:S(2)}, u32[]{:S(2)}) collective-permute-start(bf16[448,512]{1,0:T(8,128)(2,1)S(1)} %shard_map.57.side.center), channel_id=1, source_target_pairs={{0,8},{1,9},{2,10},{3,11},{8,16},{9,17},{10,18},{11,19},{12,4},{13... | collective-permute-start | bytes 1376264 | tf_op jit(solution)/shard_map/ppermute | solution.py:414
  86.8 2.8 %collective-permute-start.17 = (bf16[2,128,112]{2,1,0:T(8,128)(2,1)S(1)}, bf16[2,128,112]{2,1,0:T(8,128)(2,1)S(1)}, u32[]{:S(2)}, u32[]{:S(2)}) collective-permute-start(bf16[2,128,112]{2,1,0:T(8,128)(2,1)S(1)} %shard_map.62), channel_id=1, source_target_pairs={{0,0},{1,2},{2,4},{3,6},{4,1},{5,3},{6,5},{7,7},{8,8},{9,10},{10,1... | collective-permute-start | bytes 172040 | tf_op jit(solution)/shard_map/ppermute | solution.py:414
  87.5 4.5 %collective-permute-start.18 = (bf16[2,128,112]{2,1,0:T(8,128)(2,1)S(1)}, bf16[2,128,112]{2,1,0:T(8,128)(2,1)S(1)}, u32[]{:S(2)}, u32[]{:S(2)}) collective-permute-start(bf16[2,128,112]{2,1,0:T(8,128)(2,1)S(1)} %shard_map.62), channel_id=1, source_target_pairs={{0,1},{1,3},{2,5},{3,7},{4,0},{5,2},{6,4},{7,6},{8,9},{9,11},{10,1... | collective-permute-start | bytes 172040 | tf_op jit(solution)/shard_map/ppermute | solution.py:414
  94.6 8.0 %collective-permute-start.23 = (bf16[448,256]{1,0:T(8,128)(2,1)S(1)}, bf16[448,256]{1,0:T(8,128)(2,1)S(1)}, u32[]{:S(2)}, u32[]{:S(2)}) collective-permute-start(bf16[448,256]{1,0:T(8,128)(2,1)S(1)} %shard_map.66), channel_id=1, source_target_pairs={{0,6},{1,7},{2,4},{3,5},{4,2},{5,3},{6,0},{7,1},{8,14},{9,15},{10,... | collective-permute-start | bytes 688136 | tf_op jit(solution)/shard_map/ppermute | solution.py:414
  95.9 10.7 %collective-permute-start.22 = (bf16[448,256]{1,0:T(8,128)(2,1)S(1)}, bf16[448,256]{1,0:T(8,128)(2,1)S(1)}, u32[]{:S(2)}, u32[]{:S(2)}) collective-permute-start(bf16[448,256]{1,0:T(8,128)(2,1)S(1)} %shard_map.65), channel_id=1, source_target_pairs={{0,4},{1,5},{2,6},{3,7},{4,0},{5,1},{6,2},{7,3},{8,12},{9,13},{10,... | collective-permute-start | bytes 688136 | tf_op jit(solution)/shard_map/ppermute | solution.py:414
  99.3 7.5 %collective-permute-start.20 = (bf16[448,256]{1,0:T(8,128)(2,1)S(1)}, bf16[448,256]{1,0:T(8,128)(2,1)S(1)}, u32[]{:S(2)}, u32[]{:S(2)}) collective-permute-start(bf16[448,256]{1,0:T(8,128)(2,1)S(1)} %shard_map.64), channel_id=1, source_target_pairs={{0,2},{1,3},{2,0},{3,1},{4,6},{5,7},{6,4},{7,5},{8,10},{9,11},{10,... | collective-permute-start | bytes 688136 | tf_op jit(solution)/shard_map/ppermute | solution.py:414

commit v9 on v7

--- a/solution.py
+++ b/solution.py
@@ -492,11 +492,13 @@
 
     halo_there, halo_here = aside(here, 1), aside(there, 0)
     states = (state, state_there, tap)
-    got_across = [
-        swap(attend(0, strip, place, *states, there, here, halo_there), 4 + 2 * strip)
-        for strip in range(2)
-    ]
-    got_beside = swap(attend(1, 1, place, *states, here, there, halo_here), 2)
+    corner = attend(0, 1, place, *states, there, here, halo_there)
+    got_corner = swap(corner, 6)
+    beside_out = attend(1, 1, place, *states, here, there, halo_here)
+    across_out = attend(0, 0, place, *states, there, here, halo_there)
+    across_out, beside_out = together(across_out, beside_out)
+    got_across = [swap(across_out, 4), got_corner]
+    got_beside = swap(beside_out, 2)
     kept_here = attend(1, 0, place, *states, here, there, halo_here)
     return finish(place, [kept_here, got_beside, *got_across])
 

time: 109 us -> 109 us (level)
  transfers between devices with their start and end apart: 24 -> 24, of which waited for: 15 -> 14; matrix products, arithmetic and copies ran while one was open for 0% -> 0% of each run, Pallas kernels for 19% -> 19%
where the time goes in v9:
time: 109 us
  waiting for transfers between devices  49.8 us (46%)
  starting transfers between devices  30.9 us (28%)
  Pallas kernels  26.2 us (24%)
  local copies, waits for them, and re-layouts  1.51 us (1%)
    ppermute x24, waiting for transfers between devices, send(): return lax.ppermute(value, 'frame', pairs)  49.8 us
    ppermute x24, starting transfers between devices, send(): return lax.ppermute(value, 'frame', pairs)  30.9 us
    pallas_call x22, Pallas kernels, kernel_call(): pl.pallas_call(body, out_shape=outs, in_specs=[SMEM] * scalars + [VMEM] *...  26.2 us
  transfers between devices with their start and end apart: 24, of which 14 were waited for; matrix products, arithmetic and copies ran while one was open for 0% of the time, Pallas kernels for 19%

profile of v9, /device:TPU:0, one launch (start us, length us, event | category | flops | bytes accessed | tf_op | source)
XLA Modules:
  0.0 108.7 jit_solution(9844430172611735856)
XLA Ops:
  0.0 1.3 %copy-done = bf16[256,2240]{0,1:T(8,128)(2,1)S(1)} copy-done((bf16[256,2240]{0,1:T(8,128)(2,1)S(1)}, bf16[256,2240]{0,1:T(8,128)(2,1)}, u32[]{:S(2)}) %copy-start) | copy-done | bytes 1146904
  1.3 1.2 %shard_map.47 = (bf16[1120,256]{1,0:T(8,128)(2,1)}, bf16[1120,256]{1,0:T(8,128)(2,1)}) custom-call(bf16[2240,256]{1,0:T(8,128)(2,1)S(1)} %bitcast.10), custom_call_target="tpu_custom_call" | custom-call | bytes 1146880 | tf_op jit(solution)/shard_map/pallas_call | solution.py:78
  2.5 2.9 %collective-permute-start.2 = (bf16[1120,256]{1,0:T(8,128)(2,1)}, bf16[1120,256]{1,0:T(8,128)(2,1)S(1)}, u32[]{:S(2)}, u32[]{:S(2)}) collective-permute-start(bf16[1120,256]{1,0:T(8,128)(2,1)} %get-tuple-element.51.low), channel_id=1, source_target_pairs={{0,2},{1,3},{2,0},{3,1},{4,6},{5,7},{6,4},{7,5},{8,10},{9,11},{10,... | collective-permute-start | bytes 1720328 | tf_op jit(solution)/shard_map/ppermute | solution.py:412
  5.5 2.7 %collective-permute-start = (bf16[168,2240]{1,0:T(8,128)(2,1)S(1)}, bf16[168,2240]{1,0:T(8,128)(2,1)}, u32[]{:S(2)}, u32[]{:S(2)}) collective-permute-start(bf16[168,2240]{1,0:T(8,128)(2,1)S(1)} %shard_map.46.refs_0_), channel_id=1, source_target_pairs={{0,16},{1,17},{2,18},{3,19},{4,20},{5,21},{6,22},{7,23},{8,24},{9,... | collective-permute-start | bytes 2257928 | tf_op jit(solution)/shard_map/ppermute | solution.py:412
  8.1 1.6 %collective-permute-start.1 = (bf16[168,2240]{1,0:T(8,128)(2,1)S(1)}, bf16[168,2240]{1,0:T(8,128)(2,1)}, u32[]{:S(2)}, u32[]{:S(2)}) collective-permute-start(bf16[168,2240]{1,0:T(8,128)(2,1)S(1)} %shard_map.46.refs_0_), channel_id=1, source_target_pairs={{0,8},{1,9},{2,10},{3,11},{4,12},{5,13},{6,14},{7,15},{8,0},{9,1},... | collective-permute-start | bytes 2257928 | tf_op jit(solution)/shard_map/ppermute | solution.py:412
  9.7 1.5 %collective-permute-start.4 = (bf16[1120,256]{1,0:T(8,128)(2,1)}, bf16[1120,256]{1,0:T(8,128)(2,1)S(1)}, u32[]{:S(2)}, u32[]{:S(2)}) collective-permute-start(bf16[1120,256]{1,0:T(8,128)(2,1)} %get-tuple-element.51.low), channel_id=1, source_target_pairs={{0,4},{1,5},{2,6},{3,7},{4,0},{5,1},{6,2},{7,3},{8,12},{9,13},{10,... | collective-permute-start | bytes 1720328 | tf_op jit(solution)/shard_map/ppermute | solution.py:412
  11.2 0.5 collective-permute-start.3
  11.7 7.7 %collective-permute-done.2.refs_0_.low = bf16[1120,256]{1,0:T(8,128)(2,1)S(1)} collective-permute-done((bf16[1120,256]{1,0:T(8,128)(2,1)}, bf16[1120,256]{1,0:T(8,128)(2,1)S(1)}, u32[]{:S(2)}, u32[]{:S(2)}) %collective-permute-start.2) | collective-permute-done | bytes 573472 | tf_op jit(solution)/shard_map/ppermute | solution.py:412
  19.4 2.1 %collective-permute-start.5 = (bf16[1120,256]{1,0:T(8,128)(2,1)}, bf16[1120,256]{1,0:T(8,128)(2,1)S(1)}, u32[]{:S(2)}, u32[]{:S(2)}) collective-permute-start(bf16[1120,256]{1,0:T(8,128)(2,1)} %get-tuple-element.52.high), channel_id=1, source_target_pairs={{0,4},{1,5},{2,6},{3,7},{4,0},{5,1},{6,2},{7,3},{8,12},{9,13},{10,... | collective-permute-start | bytes 1720328 | tf_op jit(solution)/shard_map/ppermute | solution.py:412
  21.8 9.1 %collective-permute-done.3.refs_1_.high = bf16[1120,256]{1,0:T(8,128)(2,1)S(1)} collective-permute-done((bf16[1120,256]{1,0:T(8,128)(2,1)}, bf16[1120,256]{1,0:T(8,128)(2,1)S(1)}, u32[]{:S(2)}, u32[]{:S(2)}) %collective-permute-start.3) | collective-permute-done | bytes 573472 | tf_op jit(solution)/shard_map/ppermute | solution.py:412
  30.9 5.2 %collective-permute-done.5.refs_3_.high = bf16[1120,256]{1,0:T(8,128)(2,1)S(1)} collective-permute-done((bf16[1120,256]{1,0:T(8,128)(2,1)}, bf16[1120,256]{1,0:T(8,128)(2,1)S(1)}, u32[]{:S(2)}, u32[]{:S(2)}) %collective-permute-start.5) | collective-permute-done | bytes 573472 | tf_op jit(solution)/shard_map/ppermute | solution.py:412
  36.1 5.9 %collective-permute-done.refs_2_ = bf16[168,2240]{1,0:T(8,128)(2,1)} collective-permute-done((bf16[168,2240]{1,0:T(8,128)(2,1)S(1)}, bf16[168,2240]{1,0:T(8,128)(2,1)}, u32[]{:S(2)}, u32[]{:S(2)}) %collective-permute-start) | collective-permute-done | bytes 752672 | tf_op jit(solution)/shard_map/ppermute | solution.py:412
  42.2 0.6 shard_map.48
  42.9 0.6 collective-permute-start.6
  43.4 1.3 %collective-permute-start.11 = (bf16[168,2240]{1,0:T(8,128)(2,1)}, bf16[168,2240]{1,0:T(8,128)(2,1)S(1)}, u32[]{:S(2)}, u32[]{:S(2)}) collective-permute-start(bf16[168,2240]{1,0:T(8,128)(2,1)} %collective-permute-done.refs_2_), channel_id=1, source_target_pairs={{0,1},{1,0},{2,3},{3,2},{4,5},{5,4},{6,7},{7,6},{8,9},{9,8},{10,11... | collective-permute-start | bytes 2257928 | tf_op jit(solution)/shard_map/ppermute | solution.py:412
  44.7 0.7 collective-permute-start.7
  45.4 1.3 %collective-permute-start.8 = (bf16[168,2240]{1,0:T(8,128)(2,1)}, bf16[168,2240]{1,0:T(8,128)(2,1)S(1)}, u32[]{:S(2)}, u32[]{:S(2)}) collective-permute-start(bf16[168,2240]{1,0:T(8,128)(2,1)} %collective-permute-done.refs_2_), channel_id=1, source_target_pairs={{8,0},{9,1},{10,2},{11,3},{12,4},{13,5},{14,6},{15,7},{16,24},{17,... | collective-permute-start | bytes 2257928 | tf_op jit(solution)/shard_map/ppermute | solution.py:412
  46.9 1.3 %shard_map.50.refs_0_.block_0 = bf16[2240,256]{1,0:T(8,128)(2,1)S(1)} custom-call(bf16[1120,256]{1,0:T(8,128)(2,1)} %get-tuple-element.51.low, bf16[1120,256]{1,0:T(8,128)(2,1)} %get-tuple-element.52.high), custom_call_target="tpu_custom_call" | custom-call | bytes 1146880 | tf_op jit(solution)/shard_map/pallas_call | solution.py:78
  48.2 1.9 %shard_map.49 = (bf16[336,2240]{1,0:T(8,128)(2,1)S(1)}, bf16[336,2240]{1,0:T(8,128)(2,1)S(1)}, bf16[384,2240]{1,0:T(8,128)(2,1)S(1)}) custom-call(bf16[168,2240]{1,0:T(8,128)(2,1)S(1)} %shard_map.46.refs_0_, bf16[168,2240]{1,0:T(8,128)(2,1)} %collective-permute-done.1.refs_1_, bf16[168,2240]{1,0:T(8,128)(2,1)} %collective-permute-done.refs_2_, ...), custom_call_target="tpu_custom_call" | custom-call | bytes 4515840 | tf_op jit(solution)/shard_map/pallas_call | solution.py:78
  50.1 1.6 %shard_map.54.near = bf16[448,512]{1,0:T(8,128)(2,1)S(1)} custom-call(s32[2]{0:T(128)S(1)} %pad_add_fusion.place, bf16[384,2240]{1,0:T(8,128)(2,1)S(1)} %get-tuple-element.53.rows, bf16[2240,256]{1,0:T(8,128)(2,1)S(1)} %shard_map.50.refs_0_.block_0, bf16[2240,256]{1,0:T(8,128)(2,1)S(1)} %shard_map.51.refs_1_.block_1), custom_call_target="tpu_custom_call" | custom-call | bytes 4014088 | tf_op jit(solution)/shard_map/pallas_call | solution.py:78
  51.8 7.0 %collective-permute-done.6.refs_3_.refs_1_.block_1 = bf16[2240,256]{1,0:T(8,128)(2,1)S(1)} collective-permute-done((bf16[2240,256]{1,0:T(8,128)(2,1)S(1)}, bf16[2240,256]{1,0:T(8,128)(2,1)S(1)}, u32[]{:S(2)}, u32[]{:S(2)}) %collective-permute-start.6) | collective-permute-done | bytes 1146912 | tf_op jit(solution)/shard_map/ppermute | solution.py:412
  58.8 1.6 %shard_map.55.near = bf16[448,512]{1,0:T(8,128)(2,1)S(1)} custom-call(s32[2]{0:T(128)S(1)} %pad_add_fusion.place, bf16[384,2240]{1,0:T(8,128)(2,1)S(1)} %get-tuple-element.53.rows, bf16[2240,256]{1,0:T(8,128)(2,1)S(1)} %shard_map.52.refs_2_.refs_0_.block_0, bf16[2240,256]{1,0:T(8,128)(2,1)S(1)} %collective-permute-done.6.refs_3_.refs_1_.block_1), custom_call_target="tpu_custom_call" | custom-call | bytes 4014088 | tf_op jit(solution)/shard_map/pallas_call | solution.py:78
  60.4 4.1 %shard_map.53.part = f32[2,128,112]{2,1,0:T(8,128)S(1)} custom-call(s32[2]{0:T(128)S(1)} %pad_add_fusion.place, bf16[336,2240]{1,0:T(8,128)(2,1)S(1)} %get-tuple-element.49.mine.rows, bf16[336,2240]{1,0:T(8,128)(2,1)S(1)} %get-tuple-element.50.there.rows, bf16[2240,256]{1,0:T(8,128)(2,1)S(1)} %shard_map.50.refs_0_.block_0, ...), custom_call_target="tpu_custom_call" | custom-call | flops 2055208960 | bytes 7598088 | tf_op jit(solution)/shard_map/pallas_call | solution.py:78
  64.5 3.1 %collective-permute-done.8.outer = bf16[168,2240]{1,0:T(8,128)(2,1)S(1)} collective-permute-done((bf16[168,2240]{1,0:T(8,128)(2,1)}, bf16[168,2240]{1,0:T(8,128)(2,1)S(1)}, u32[]{:S(2)}, u32[]{:S(2)}) %collective-permute-start.8) | collective-permute-done | bytes 752672 | tf_op jit(solution)/shard_map/ppermute | solution.py:412
  67.6 0.6 shard_map.56.last
  68.3 2.0 %shard_map.58.refs_0_ = f32[2,128,112]{2,1,0:T(8,128)S(1)} custom-call(s32[2]{0:T(128)S(1)} %pad_add_fusion.place, f32[2,128,112]{2,1,0:T(8,128)S(1)} %shard_map.53.part, bf16[336,2240]{1,0:T(8,128)(2,1)S(1)} %get-tuple-element.49.mine.rows, bf16[168,2240]{1,0:T(8,128)(2,1)S(1)} %shard_map.56.last, bf16[2240,256]{1,0:T(8,128)(2,1)S(1)} %shard_map.50.refs_0_.block_0, ...), custom_call_target="tpu_custom_call" | custom-call | flops 1027604480 | bytes 6960136 | tf_op jit(solution)/shard_map/pallas_call | solution.py:78
  70.6 2.0 %shard_map.59 = f32[2,128,112]{2,1,0:T(8,128)S(1)} custom-call(s32[2]{0:T(128)S(1)} %pad_add_fusion.place, f32[2,128,112]{2,1,0:T(8,128)S(1)} %shard_map.53.part, bf16[336,2240]{1,0:T(8,128)(2,1)S(1)} %get-tuple-element.50.there.rows, bf16[168,2240]{1,0:T(8,128)(2,1)S(1)} %collective-permute-done.12.last_there.last, ...), custom_call_target="tpu_custom_call" | custom-call | flops 1027604480 | bytes 6960136 | tf_op jit(solution)/shard_map/pallas_call | solution.py:78
  72.9 1.0 shard_map.60.center.side
  74.2 3.3 %collective-permute-start.14 = (bf16[2,128,112]{2,1,0:T(8,128)(2,1)S(1)}, bf16[2,128,112]{2,1,0:T(8,128)(2,1)S(1)}, u32[]{:S(2)}, u32[]{:S(2)}) collective-permute-start(bf16[2,128,112]{2,1,0:T(8,128)(2,1)S(1)} %shard_map.61.refs_0_), channel_id=1, source_target_pairs={{0,16},{1,17},{2,18},{3,19},{4,20},{5,21},{6,22},{7,23},{8,24},{9,... | collective-permute-start | bytes 172040 | tf_op jit(solution)/shard_map/ppermute | solution.py:412
  77.4 1.1 collective-permute-start.15
  78.5 1.1 shard_map.57.side.center
  79.6 1.3 %collective-permute-start.20 = (bf16[448,512]{1,0:T(8,128)(2,1)S(1)}, bf16[448,512]{1,0:T(8,128)(2,1)S(1)}, u32[]{:S(2)}, u32[]{:S(2)}) collective-permute-start(bf16[448,512]{1,0:T(8,128)(2,1)S(1)} %shard_map.60.center.side), channel_id=1, source_target_pairs={{4,12},{5,13},{6,14},{7,15},{8,0},{9,1},{10,2},{11,3},{12,20},{13,... | collective-permute-start | bytes 1376264 | tf_op jit(solution)/shard_map/ppermute | solution.py:412
  80.9 0.6 collective-permute-done.14.refs_1_
  81.5 2.1 %collective-permute-done.15.refs_2_ = bf16[2,128,112]{2,1,0:T(8,128)(2,1)S(1)} collective-permute-done((bf16[2,128,112]{2,1,0:T(8,128)(2,1)S(1)}, bf16[2,128,112]{2,1,0:T(8,128)(2,1)S(1)}, u32[]{:S(2)}, u32[]{:S(2)}) %collective-permute-start.15) | collective-permute-done | bytes 57376 | tf_op jit(solution)/shard_map/ppermute | solution.py:412
  83.5 3.2 %collective-permute-start.19 = (bf16[448,512]{1,0:T(8,128)(2,1)S(1)}, bf16[448,512]{1,0:T(8,128)(2,1)S(1)}, u32[]{:S(2)}, u32[]{:S(2)}) collective-permute-start(bf16[448,512]{1,0:T(8,128)(2,1)S(1)} %shard_map.57.side.center), channel_id=1, source_target_pairs={{0,8},{1,9},{2,10},{3,11},{8,16},{9,17},{10,18},{11,19},{12,4},{13... | collective-permute-start | bytes 1376264 | tf_op jit(solution)/shard_map/ppermute | solution.py:412
  86.8 0.7 collective-permute-start.17
  87.5 2.2 %collective-permute-start.18 = (bf16[2,128,112]{2,1,0:T(8,128)(2,1)S(1)}, bf16[2,128,112]{2,1,0:T(8,128)(2,1)S(1)}, u32[]{:S(2)}, u32[]{:S(2)}) collective-permute-start(bf16[2,128,112]{2,1,0:T(8,128)(2,1)S(1)} %shard_map.62), channel_id=1, source_target_pairs={{0,1},{1,3},{2,5},{3,7},{4,0},{5,2},{6,4},{7,6},{8,9},{9,11},{10,1... | collective-permute-start | bytes 172040 | tf_op jit(solution)/shard_map/ppermute | solution.py:412
  89.6 2.4 %collective-permute-done.18.there = bf16[2,128,112]{2,1,0:T(8,128)(2,1)S(1)} collective-permute-done((bf16[2,128,112]{2,1,0:T(8,128)(2,1)S(1)}, bf16[2,128,112]{2,1,0:T(8,128)(2,1)S(1)}, u32[]{:S(2)}, u32[]{:S(2)}) %collective-permute-start.18) | collective-permute-done | bytes 57376 | tf_op jit(solution)/shard_map/ppermute | solution.py:412
  92.0 1.4 %collective-permute-done.20.halo = bf16[448,512]{1,0:T(8,128)(2,1)S(1)} collective-permute-done((bf16[448,512]{1,0:T(8,128)(2,1)S(1)}, bf16[448,512]{1,0:T(8,128)(2,1)S(1)}, u32[]{:S(2)}, u32[]{:S(2)}) %collective-permute-start.20) | collective-permute-done | bytes 458784 | tf_op jit(solution)/shard_map/ppermute | solution.py:412
  93.4 1.2 %shard_map.66 = bf16[448,256]{1,0:T(8,128)(2,1)S(1)} custom-call(s32[2]{0:T(128)S(1)} %pad_add_fusion.place, bf16[2,128,112]{2,1,0:T(8,128)(2,1)S(1)} %collective-permute-done.17.mine, bf16[2,128,112]{2,1,0:T(8,128)(2,1)S(1)} %collective-permute-done.18.there, f32[448,3]{1,0:T(8,128)S(1)} %bitcast.6, bf16[448,512]{1,0:T(8,128)(2,1)S(1)} %shard_map.57.side.center, ...), custom_call_target="tpu_custom_call" | custom-call | bytes 1496328 | tf_op jit(solution)/shard_map/pallas_call | solution.py:78
  94.6 1.2 %shard_map.64 = bf16[448,256]{1,0:T(8,128)(2,1)S(1)} custom-call(s32[2]{0:T(128)S(1)} %pad_add_fusion.place, bf16[2,128,112]{2,1,0:T(8,128)(2,1)S(1)} %collective-permute-done.17.mine, bf16[2,128,112]{2,1,0:T(8,128)(2,1)S(1)} %collective-permute-done.18.there, f32[448,3]{1,0:T(8,128)S(1)} %bitcast.7, bf16[448,512]{1,0:T(8,128)(2,1)S(1)} %shard_map.57.side.center, ...), custom_call_target="tpu_custom_call" | custom-call | bytes 1496328 | tf_op jit(solution)/shard_map/pallas_call | solution.py:78
  95.9 1.2 %shard_map.65 = bf16[448,256]{1,0:T(8,128)(2,1)S(1)} custom-call(s32[2]{0:T(128)S(1)} %pad_add_fusion.place, bf16[2,128,112]{2,1,0:T(8,128)(2,1)S(1)} %collective-permute-done.17.mine, bf16[2,128,112]{2,1,0:T(8,128)(2,1)S(1)} %collective-permute-done.18.there, f32[448,3]{1,0:T(8,128)S(1)} %bitcast.8, bf16[448,512]{1,0:T(8,128)(2,1)S(1)} %shard_map.60.center.side, ...), custom_call_target="tpu_custom_call" | custom-call | bytes 1496328 | tf_op jit(solution)/shard_map/pallas_call | solution.py:78
  97.1 1.4 %collective-permute-start.21 = (bf16[448,256]{1,0:T(8,128)(2,1)S(1)}, bf16[448,256]{1,0:T(8,128)(2,1)S(1)}, u32[]{:S(2)}, u32[]{:S(2)}) collective-permute-start(bf16[448,256]{1,0:T(8,128)(2,1)S(1)} %shard_map.65), channel_id=1, source_target_pairs={{0,2},{1,3},{2,0},{3,1},{4,6},{5,7},{6,4},{7,5},{8,10},{9,11},{10,... | collective-permute-start | bytes 688136 | tf_op jit(solution)/shard_map/ppermute | solution.py:412
  98.4 2.2 %collective-permute-start.22 = (bf16[448,256]{1,0:T(8,128)(2,1)S(1)}, bf16[448,256]{1,0:T(8,128)(2,1)S(1)}, u32[]{:S(2)}, u32[]{:S(2)}) collective-permute-start(bf16[448,256]{1,0:T(8,128)(2,1)S(1)} %shard_map.64), channel_id=1, source_target_pairs={{0,4},{1,5},{2,6},{3,7},{4,0},{5,1},{6,2},{7,3},{8,12},{9,13},{10,... | collective-permute-start | bytes 688136 | tf_op jit(solution)/shard_map/ppermute | solution.py:412
  100.6 1.2 %shard_map.63.refs_0_ = bf16[448,256]{1,0:T(8,128)(2,1)S(1)} custom-call(s32[2]{0:T(128)S(1)} %pad_add_fusion.place, bf16[2,128,112]{2,1,0:T(8,128)(2,1)S(1)} %collective-permute-done.17.mine, bf16[2,128,112]{2,1,0:T(8,128)(2,1)S(1)} %collective-permute-done.18.there, f32[448,3]{1,0:T(8,128)S(1)} %bitcast.9, bf16[448,512]{1,0:T(8,128)(2,1)S(1)} %shard_map.60.center.side, ...), custom_call_target="tpu_custom_call" | custom-call | bytes 1496328 | tf_op jit(solution)/shard_map/pallas_call | solution.py:78
  101.8 0.5 collective-permute-done.23.refs_3_
  102.4 4.4 %collective-permute-done.21.refs_1_ = bf16[448,256]{1,0:T(8,128)(2,1)S(1)} collective-permute-done((bf16[448,256]{1,0:T(8,128)(2,1)S(1)}, bf16[448,256]{1,0:T(8,128)(2,1)S(1)}, u32[]{:S(2)}, u32[]{:S(2)}) %collective-permute-start.21) | collective-permute-done | bytes 229408 | tf_op jit(solution)/shard_map/ppermute | solution.py:412
  106.8 2.0 %shard_map.67 = bf16[256,1792]{1,0:T(8,128)(2,1)} custom-call(s32[2]{0:T(128)S(1)} %pad_add_fusion.place, bf16[448,256]{1,0:T(8,128)(2,1)S(1)} %shard_map.63.refs_0_, bf16[448,256]{1,0:T(8,128)(2,1)S(1)} %collective-permute-done.21.refs_1_, bf16[448,256]{1,0:T(8,128)(2,1)S(1)} %collective-permute-done.22.refs_2_, ...), custom_call_target="tpu_custom_call" | custom-call | bytes 917512 | tf_op jit(solution)/shard_map/pallas_call | solution.py:78
  (34 shorter events, 1.7 us)
Async XLA Ops:
  0.0 1.3 %copy-start = (bf16[256,2240]{0,1:T(8,128)(2,1)S(1)}, bf16[256,2240]{0,1:T(8,128)(2,1)}, u32[]{:S(2)}) copy-start(bf16[256,2240]{0,1:T(8,128)(2,1)} %param.4) | copy-start | bytes 3440644
  1.3 4.1 %copy-start.1 = (bf16[112,2240]{1,0:T(8,128)(2,1)S(1)}, bf16[112,2240]{1,0:T(8,128)(2,1)}, u32[]{:S(2)}) copy-start(bf16[112,2240]{1,0:T(8,128)(2,1)} %w_keyval.1) | copy-start | bytes 1505284
  1.3 4.1 %copy-start.2 = (bf16[56,2240]{1,0:T(8,128)(2,1)S(1)}, bf16[56,2240]{1,0:T(8,128)(2,1)}, u32[]{:S(2)}) copy-start(bf16[56,2240]{1,0:T(8,128)(2,1)} %w_query.1) | copy-start | bytes 752644
  1.3 20.2 %copy-start.3 = (f32[3,1792]{1,0:T(4,128)S(1)}, f32[3,1792]{1,0:T(4,128)}, u32[]{:S(2)}) copy-start(f32[3,1792]{1,0:T(4,128)} %param.7) | copy-start | bytes 64516
  2.5 17.0 %collective-permute-start.2 = (bf16[1120,256]{1,0:T(8,128)(2,1)}, bf16[1120,256]{1,0:T(8,128)(2,1)S(1)}, u32[]{:S(2)}, u32[]{:S(2)}) collective-permute-start(bf16[1120,256]{1,0:T(8,128)(2,1)} %get-tuple-element.51.low), channel_id=1, source_target_pairs={{0,2},{1,3},{2,0},{3,1},{4,6},{5,7},{6,4},{7,5},{8,10},{9,11},{10,... | collective-permute-start | bytes 1720328 | tf_op jit(solution)/shard_map/ppermute | solution.py:412
  5.5 36.5 %collective-permute-start = (bf16[168,2240]{1,0:T(8,128)(2,1)S(1)}, bf16[168,2240]{1,0:T(8,128)(2,1)}, u32[]{:S(2)}, u32[]{:S(2)}) collective-permute-start(bf16[168,2240]{1,0:T(8,128)(2,1)S(1)} %shard_map.46.refs_0_), channel_id=1, source_target_pairs={{0,16},{1,17},{2,18},{3,19},{4,20},{5,21},{6,22},{7,23},{8,24},{9,... | collective-permute-start | bytes 2257928 | tf_op jit(solution)/shard_map/ppermute | solution.py:412
  8.1 34.0 %collective-permute-start.1 = (bf16[168,2240]{1,0:T(8,128)(2,1)S(1)}, bf16[168,2240]{1,0:T(8,128)(2,1)}, u32[]{:S(2)}, u32[]{:S(2)}) collective-permute-start(bf16[168,2240]{1,0:T(8,128)(2,1)S(1)} %shard_map.46.refs_0_), channel_id=1, source_target_pairs={{0,8},{1,9},{2,10},{3,11},{4,12},{5,13},{6,14},{7,15},{8,0},{9,1},... | collective-permute-start | bytes 2257928 | tf_op jit(solution)/shard_map/ppermute | solution.py:412
  9.7 21.2 %collective-permute-start.4 = (bf16[1120,256]{1,0:T(8,128)(2,1)}, bf16[1120,256]{1,0:T(8,128)(2,1)S(1)}, u32[]{:S(2)}, u32[]{:S(2)}) collective-permute-start(bf16[1120,256]{1,0:T(8,128)(2,1)} %get-tuple-element.51.low), channel_id=1, source_target_pairs={{0,4},{1,5},{2,6},{3,7},{4,0},{5,1},{6,2},{7,3},{8,12},{9,13},{10,... | collective-permute-start | bytes 1720328 | tf_op jit(solution)/shard_map/ppermute | solution.py:412
  11.2 19.7 %collective-permute-start.3 = (bf16[1120,256]{1,0:T(8,128)(2,1)}, bf16[1120,256]{1,0:T(8,128)(2,1)S(1)}, u32[]{:S(2)}, u32[]{:S(2)}) collective-permute-start(bf16[1120,256]{1,0:T(8,128)(2,1)} %get-tuple-element.52.high), channel_id=1, source_target_pairs={{0,2},{1,3},{2,0},{3,1},{4,6},{5,7},{6,4},{7,5},{8,10},{9,11},{10,... | collective-permute-start | bytes 1720328 | tf_op jit(solution)/shard_map/ppermute | solution.py:412
  19.4 16.7 %collective-permute-start.5 = (bf16[1120,256]{1,0:T(8,128)(2,1)}, bf16[1120,256]{1,0:T(8,128)(2,1)S(1)}, u32[]{:S(2)}, u32[]{:S(2)}) collective-permute-start(bf16[1120,256]{1,0:T(8,128)(2,1)} %get-tuple-element.52.high), channel_id=1, source_target_pairs={{0,4},{1,5},{2,6},{3,7},{4,0},{5,1},{6,2},{7,3},{8,12},{9,13},{10,... | collective-permute-start | bytes 1720328 | tf_op jit(solution)/shard_map/ppermute | solution.py:412
  42.2 3.2 %collective-permute-start.10 = (bf16[168,2240]{1,0:T(8,128)(2,1)}, bf16[168,2240]{1,0:T(8,128)(2,1)}, u32[]{:S(2)}, u32[]{:S(2)}) collective-permute-start(bf16[168,2240]{1,0:T(8,128)(2,1)} %collective-permute-done.1.refs_1_), channel_id=1, source_target_pairs={{0,1},{1,0},{2,3},{3,2},{4,5},{5,4},{6,7},{7,6},{8,9},{9,8},{10,11... | collective-permute-start | bytes 2257928 | tf_op jit(solution)/shard_map/ppermute | solution.py:412
  42.9 15.9 %collective-permute-start.6 = (bf16[2240,256]{1,0:T(8,128)(2,1)S(1)}, bf16[2240,256]{1,0:T(8,128)(2,1)S(1)}, u32[]{:S(2)}, u32[]{:S(2)}) collective-permute-start(bf16[2240,256]{1,0:T(8,128)(2,1)S(1)} %shard_map.48), channel_id=1, source_target_pairs={{0,2},{1,5},{2,0},{3,7},{4,6},{5,1},{6,4},{7,3},{8,10},{9,13},{10,... | collective-permute-start | bytes 3440648 | tf_op jit(solution)/shard_map/ppermute | solution.py:412
  43.4 4.8 %collective-permute-start.11 = (bf16[168,2240]{1,0:T(8,128)(2,1)}, bf16[168,2240]{1,0:T(8,128)(2,1)S(1)}, u32[]{:S(2)}, u32[]{:S(2)}) collective-permute-start(bf16[168,2240]{1,0:T(8,128)(2,1)} %collective-permute-done.refs_2_), channel_id=1, source_target_pairs={{0,1},{1,0},{2,3},{3,2},{4,5},{5,4},{6,7},{7,6},{8,9},{9,8},{10,11... | collective-permute-start | bytes 2257928 | tf_op jit(solution)/shard_map/ppermute | solution.py:412
  44.7 3.5 %collective-permute-start.9 = (bf16[168,2240]{1,0:T(8,128)(2,1)S(1)}, bf16[168,2240]{1,0:T(8,128)(2,1)S(1)}, u32[]{:S(2)}, u32[]{:S(2)}) collective-permute-start(bf16[168,2240]{1,0:T(8,128)(2,1)S(1)} %shard_map.46.refs_0_), channel_id=1, source_target_pairs={{0,1},{1,0},{2,3},{3,2},{4,5},{5,4},{6,7},{7,6},{8,9},{9,8},{10,11... | collective-permute-start | bytes 2257928 | tf_op jit(solution)/shard_map/ppermute | solution.py:412
  44.7 19.8 %collective-permute-start.7 = (bf16[168,2240]{1,0:T(8,128)(2,1)S(1)}, bf16[168,2240]{1,0:T(8,128)(2,1)S(1)}, u32[]{:S(2)}, u32[]{:S(2)}) collective-permute-start(bf16[168,2240]{1,0:T(8,128)(2,1)S(1)} %shard_map.46.refs_0_), channel_id=1, source_target_pairs={{8,16},{9,17},{10,18},{11,19},{12,20},{13,21},{14,22},{15,23},{16,... | collective-permute-start | bytes 2257928 | tf_op jit(solution)/shard_map/ppermute | solution.py:412
  45.4 22.2 %collective-permute-start.8 = (bf16[168,2240]{1,0:T(8,128)(2,1)}, bf16[168,2240]{1,0:T(8,128)(2,1)S(1)}, u32[]{:S(2)}, u32[]{:S(2)}) collective-permute-start(bf16[168,2240]{1,0:T(8,128)(2,1)} %collective-permute-done.refs_2_), channel_id=1, source_target_pairs={{8,0},{9,1},{10,2},{11,3},{12,4},{13,5},{14,6},{15,7},{16,24},{17,... | collective-permute-start | bytes 2257928 | tf_op jit(solution)/shard_map/ppermute | solution.py:412
  68.2 2.3 %collective-permute-start.12 = (bf16[168,2240]{1,0:T(8,128)(2,1)S(1)}, bf16[168,2240]{1,0:T(8,128)(2,1)S(1)}, u32[]{:S(2)}, u32[]{:S(2)}) collective-permute-start(bf16[168,2240]{1,0:T(8,128)(2,1)S(1)} %shard_map.56.last), channel_id=1, source_target_pairs={{0,1},{1,0},{2,3},{3,2},{4,5},{5,4},{6,7},{7,6},{8,9},{9,8},{10,11... | collective-permute-start | bytes 2257928 | tf_op jit(solution)/shard_map/ppermute | solution.py:412
  72.6 1.4 %collective-permute-start.13 = (f32[2,128,112]{2,1,0:T(8,128)S(1)}, f32[2,128,112]{2,1,0:T(8,128)S(1)}, u32[]{:S(2)}, u32[]{:S(2)}) collective-permute-start(f32[2,128,112]{2,1,0:T(8,128)S(1)} %shard_map.59), channel_id=1, source_target_pairs={{0,1},{1,0},{2,3},{3,2},{4,5},{5,4},{6,7},{7,6},{8,9},{9,8},{10,11... | collective-permute-start | bytes 344072 | tf_op jit(solution)/shard_map/ppermute | solution.py:412
  74.0 5.5 %collective-permute-start.16 = (bf16[2,128,112]{2,1,0:T(8,128)(2,1)S(1)}, bf16[2,128,112]{2,1,0:T(8,128)(2,1)S(1)}, u32[]{:S(2)}, u32[]{:S(2)}) collective-permute-start(bf16[2,128,112]{2,1,0:T(8,128)(2,1)S(1)} %shard_map.61.refs_0_), channel_id=1, source_target_pairs={{0,8},{1,9},{2,10},{3,11},{4,12},{5,13},{6,14},{7,15},{8,0},{9,1},... | collective-permute-start | bytes 172040 | tf_op jit(solution)/shard_map/ppermute | solution.py:412
  74.2 7.3 %collective-permute-start.14 = (bf16[2,128,112]{2,1,0:T(8,128)(2,1)S(1)}, bf16[2,128,112]{2,1,0:T(8,128)(2,1)S(1)}, u32[]{:S(2)}, u32[]{:S(2)}) collective-permute-start(bf16[2,128,112]{2,1,0:T(8,128)(2,1)S(1)} %shard_map.61.refs_0_), channel_id=1, source_target_pairs={{0,16},{1,17},{2,18},{3,19},{4,20},{5,21},{6,22},{7,23},{8,24},{9,... | collective-permute-start | bytes 172040 | tf_op jit(solution)/shard_map/ppermute | solution.py:412
  77.4 6.1 %collective-permute-start.15 = (bf16[2,128,112]{2,1,0:T(8,128)(2,1)S(1)}, bf16[2,128,112]{2,1,0:T(8,128)(2,1)S(1)}, u32[]{:S(2)}, u32[]{:S(2)}) collective-permute-start(bf16[2,128,112]{2,1,0:T(8,128)(2,1)S(1)} %shard_map.61.refs_0_), channel_id=1, source_target_pairs={{0,24},{1,25},{2,26},{3,27},{4,28},{5,29},{6,30},{7,31},{8,16},{9,... | collective-permute-start | bytes 172040 | tf_op jit(solution)/shard_map/ppermute | solution.py:412
  79.6 13.8 %collective-permute-start.20 = (bf16[448,512]{1,0:T(8,128)(2,1)S(1)}, bf16[448,512]{1,0:T(8,128)(2,1)S(1)}, u32[]{:S(2)}, u32[]{:S(2)}) collective-permute-start(bf16[448,512]{1,0:T(8,128)(2,1)S(1)} %shard_map.60.center.side), channel_id=1, source_target_pairs={{4,12},{5,13},{6,14},{7,15},{8,0},{9,1},{10,2},{11,3},{12,20},{13,... | collective-permute-start | bytes 1376264 | tf_op jit(solution)/shard_map/ppermute | solution.py:412
  83.5 12.3 %collective-permute-start.19 = (bf16[448,512]{1,0:T(8,128)(2,1)S(1)}, bf16[448,512]{1,0:T(8,128)(2,1)S(1)}, u32[]{:S(2)}, u32[]{:S(2)}) collective-permute-start(bf16[448,512]{1,0:T(8,128)(2,1)S(1)} %shard_map.57.side.center), channel_id=1, source_target_pairs={{0,8},{1,9},{2,10},{3,11},{8,16},{9,17},{10,18},{11,19},{12,4},{13... | collective-permute-start | bytes 1376264 | tf_op jit(solution)/shard_map/ppermute | solution.py:412
  86.8 2.8 %collective-permute-start.17 = (bf16[2,128,112]{2,1,0:T(8,128)(2,1)S(1)}, bf16[2,128,112]{2,1,0:T(8,128)(2,1)S(1)}, u32[]{:S(2)}, u32[]{:S(2)}) collective-permute-start(bf16[2,128,112]{2,1,0:T(8,128)(2,1)S(1)} %shard_map.62), channel_id=1, source_target_pairs={{0,0},{1,2},{2,4},{3,6},{4,1},{5,3},{6,5},{7,7},{8,8},{9,10},{10,1... | collective-permute-start | bytes 172040 | tf_op jit(solution)/shard_map/ppermute | solution.py:412
  87.5 4.5 %collective-permute-start.18 = (bf16[2,128,112]{2,1,0:T(8,128)(2,1)S(1)}, bf16[2,128,112]{2,1,0:T(8,128)(2,1)S(1)}, u32[]{:S(2)}, u32[]{:S(2)}) collective-permute-start(bf16[2,128,112]{2,1,0:T(8,128)(2,1)S(1)} %shard_map.62), channel_id=1, source_target_pairs={{0,1},{1,3},{2,5},{3,7},{4,0},{5,2},{6,4},{7,6},{8,9},{9,11},{10,1... | collective-permute-start | bytes 172040 | tf_op jit(solution)/shard_map/ppermute | solution.py:412
  94.6 7.8 %collective-permute-start.23 = (bf16[448,256]{1,0:T(8,128)(2,1)S(1)}, bf16[448,256]{1,0:T(8,128)(2,1)S(1)}, u32[]{:S(2)}, u32[]{:S(2)}) collective-permute-start(bf16[448,256]{1,0:T(8,128)(2,1)S(1)} %shard_map.66), channel_id=1, source_target_pairs={{0,6},{1,7},{2,4},{3,5},{4,2},{5,3},{6,0},{7,1},{8,14},{9,15},{10,... | collective-permute-start | bytes 688136 | tf_op jit(solution)/shard_map/ppermute | solution.py:412
  97.1 9.7 %collective-permute-start.21 = (bf16[448,256]{1,0:T(8,128)(2,1)S(1)}, bf16[448,256]{1,0:T(8,128)(2,1)S(1)}, u32[]{:S(2)}, u32[]{:S(2)}) collective-permute-start(bf16[448,256]{1,0:T(8,128)(2,1)S(1)} %shard_map.65), channel_id=1, source_target_pairs={{0,2},{1,3},{2,0},{3,1},{4,6},{5,7},{6,4},{7,5},{8,10},{9,11},{10,... | collective-permute-start | bytes 688136 | tf_op jit(solution)/shard_map/ppermute | solution.py:412
  98.4 8.3 %collective-permute-start.22 = (bf16[448,256]{1,0:T(8,128)(2,1)S(1)}, bf16[448,256]{1,0:T(8,128)(2,1)S(1)}, u32[]{:S(2)}, u32[]{:S(2)}) collective-permute-start(bf16[448,256]{1,0:T(8,128)(2,1)S(1)} %shard_map.64), channel_id=1, source_target_pairs={{0,4},{1,5},{2,6},{3,7},{4,0},{5,1},{6,2},{7,3},{8,12},{9,13},{10,... | collective-permute-start | bytes 688136 | tf_op jit(solution)/shard_map/ppermute | solution.py:412
